TPU v7x, 32 devices: a whole 2x2x4 slice. The times are simulated.
32 devices in a mesh: row: 4 (over x, core), col: 8 (over z, y).
Axes of the slice: x: 2, y: 2, z: 4, core: 2. Of those that a mesh axis runs over, the one named last changes fastest.
Arguments:
- history: bfloat16 [4, 16, 4096], P(None, None, ('col', 'row')), may hold values from -6 to 6
- incident: float32 [16, 4096], P(None, ('col', 'row')), may hold values from -6 to 6
- centroids: float32 [3, 4096], replicated, may hold values from 0 to 1
- moments: float32 [4, 4096], replicated, may hold values from -4 to 4
- dual_moments: float32 [3, 4096], replicated, may hold values from -4 to 4
- shell: int32 [32, 32], P('row', 'col'), may hold values from 0 to 3
- near_mask: int32 [32, 32], P('row', 'col'), may hold values 0 or 1
- neighbours: int32 [4, 4096], P(None, 'row'), may hold values from 0 to 4095, as said below
- gram_diag: float32 [4096], P('row'), may hold values from 2 to 3
- gram_off: float32 [4, 4096], P(None, 'row'), may hold values from -0.45 to 0.45, as said below
Outputs:
- march_rhs: float32 [16, 4096], P(None, ('col', 'row'))
- dual_field: float32 [16, 4096], P(None, ('row', 'col'))
Inputs may be any that keep to these rules, and one draw needn't show every extreme that they name: neighbours[m, i] differs from i by 1 to 32; the first row is i + 32 (i - 32 where that leaves the range), the second i - 32 (i + 32 where that leaves the range). `gram_off`: each entry's magnitude is 0.25 to 0.45.
All inputs are finite; a program needn't handle non-finite values. No bound on the sum of `near_mask` on one device may be relied on, other than what follows from the above.
Results may differ from a plain program's by a relative error of at most 0.008.
Values may be sent and summed in bfloat16 or wider, within the bound.
No kernel may reach another device: no remote copies, remote signals or barrier semaphores. Data moves between devices by JAX's collectives and lax.ppermute only.
A program may use at most 64 MiB of HBM per device.

v0:
```python
import math

import jax
import jax.numpy as jnp
from jax import lax
from jax.sharding import PartitionSpec as P

SWEEPS = 2
W = 32


SOFT_T = 0.05
SOFT_S = 0.1
NEAR_GAIN = 2.0
NEAR_REACH = 0.5


def extended_2(block, sides, width):
    for axis, dim in sides:
        count = lax.axis_size(axis)
        forward = [(i, i + 1) for i in range(count - 1)]
        backward = [(target, source) for source, target in forward]
        low = lax.ppermute(
            lax.slice_in_dim(block, block.shape[dim] - width, None, axis=dim), axis, forward
        )
        high = lax.ppermute(lax.slice_in_dim(block, 0, width, axis=dim), axis, backward)
        block = jnp.concatenate([low, block, high], axis=dim)
    return block


def distances(row_xyz, col_xyz):
    delta_x = row_xyz[0][:, None] - col_xyz[0][None, :]
    delta_y = row_xyz[1][:, None] - col_xyz[1][None, :]
    delta_z = row_xyz[2][:, None] - col_xyz[2][None, :]
    return jnp.sqrt(delta_x * delta_x + delta_y * delta_y + delta_z * delta_z)


def apply_t_tiles(row_xyz, row_weights, col_xyz, scaled, shell_rows, mask_rows, tile_len):
    tile_rows = shell_rows.shape[0]
    col_count = col_xyz.shape[1]
    spacing = distances(row_xyz, col_xyz).reshape(tile_rows, tile_len, col_count)
    kernel = (
        1.0 / (spacing + SOFT_T)
        + NEAR_GAIN * mask_rows[:, None, :].astype(jnp.float32) * jnp.exp(-spacing / NEAR_REACH)
    ).astype(jnp.bfloat16)
    picked = jnp.zeros((tile_rows,) + scaled.shape[1:], jnp.bfloat16)
    for slot_id in range(scaled.shape[0]):
        picked = jnp.where((shell_rows == slot_id)[:, None, None, :], scaled[slot_id][None], picked)
    products = jnp.einsum("tqk,tabk->abtq", kernel, picked, preferred_element_type=jnp.float32)
    products = products.reshape(products.shape[0], products.shape[1], tile_rows * tile_len)
    return jnp.sum(row_weights[:, None, :] * products, axis=0)


def apply_s_tiles(row_xyz, row_dual, col_xyz, scaled_dual):
    kernel = (1.0 / (distances(row_xyz, col_xyz) + SOFT_S)).astype(jnp.bfloat16)
    products = jnp.einsum("qk,abk->abq", kernel, scaled_dual, preferred_element_type=jnp.float32)
    return jnp.sum(row_dual[:, None, :] * products, axis=0)


def sweep_mass(field_sum, diag, off_diag, links, base, extend):
    dual_iter = field_sum / diag[None, :]
    length = field_sum.shape[1]
    local_index = (links - base + W).reshape(-1)
    for sweep_id in range(SWEEPS):
        extended = extend(dual_iter)
        nearby = jnp.take(extended, local_index, axis=1).reshape(
            field_sum.shape[0], links.shape[0], length
        )
        coupling = jnp.sum(off_diag[None] * nearby, axis=1)
        dual_iter = (field_sum - coupling) / diag[None, :]
    return dual_iter


def per_device(
    history,
    incident,
    centroids,
    moments,
    dual_moments,
    shell,
    near_mask,
    neighbours,
    gram_diag,
    gram_off,
):
    row_devices = lax.axis_size("row")
    col_devices = lax.axis_size("col")
    row_id = lax.axis_index("row")
    col_id = lax.axis_index("col")
    shard_len = history.shape[2]
    excitations = history.shape[1]
    rows_t = shard_len * col_devices
    cols_t = shard_len * row_devices
    total_rwg = rows_t * row_devices
    tile_len = rows_t // shell.shape[0]
    norm_scale = 1.0 / math.sqrt(total_rwg)
    row_start = row_id * rows_t
    col_start = col_id * cols_t
    weights = jnp.concatenate([moments[:3], -moments[3:]], axis=0)
    t_block = math.gcd(rows_t, 512)
    t_tiles = t_block // tile_len
    row_xyz = lax.dynamic_slice_in_dim(centroids, row_start, rows_t, 1)
    row_weights = lax.dynamic_slice_in_dim(weights, row_start, rows_t, 1)
    shell_wide = jnp.repeat(shell, tile_len, axis=1)
    mask_wide = jnp.repeat(near_mask, tile_len, axis=1)
    hist_piece = lax.all_gather(history, "row", axis=2, tiled=True)
    col_count = hist_piece.shape[2]
    col_first = col_start
    col_xyz = lax.dynamic_slice_in_dim(centroids, col_first, col_count, 1)
    col_moments = lax.dynamic_slice_in_dim(moments, col_first, col_count, 1)
    scaled = (col_moments[None, :, None, :] * hist_piece[:, None, :, :].astype(jnp.float32)).astype(
        jnp.bfloat16
    )

    def one_block(block_id):
        row_lo = block_id * t_block
        return apply_t_tiles(
            lax.dynamic_slice_in_dim(row_xyz, row_lo, t_block, 1),
            lax.dynamic_slice_in_dim(row_weights, row_lo, t_block, 1),
            col_xyz,
            scaled,
            lax.dynamic_slice_in_dim(shell_wide, block_id * t_tiles, t_tiles, 0),
            lax.dynamic_slice_in_dim(mask_wide, block_id * t_tiles, t_tiles, 0),
            tile_len,
        )

    block_out = lax.map(one_block, jnp.arange(rows_t // t_block, dtype=jnp.int32))
    partial_field = jnp.moveaxis(block_out, 0, 1).reshape(excitations, rows_t)
    partial_field = partial_field * norm_scale
    s_block = math.gcd(cols_t, 512)
    srow_xyz = lax.dynamic_slice_in_dim(centroids, col_start, cols_t, 1)
    srow_dual = lax.dynamic_slice_in_dim(dual_moments, col_start, cols_t, 1)
    share_sum = lax.psum_scatter(partial_field, "col", scatter_dimension=1, tiled=True)
    shard_offset = col_id * shard_len
    own_dual = sweep_mass(
        share_sum,
        lax.dynamic_slice_in_dim(gram_diag, shard_offset, shard_len, 0),
        lax.dynamic_slice_in_dim(gram_off, shard_offset, shard_len, 1),
        lax.dynamic_slice_in_dim(neighbours, shard_offset, shard_len, 1),
        row_start + shard_offset,
        lambda values: extended_2(values, ((("row", "col"), 1),), W),
    )
    dual_piece = lax.all_gather(own_dual, "col", axis=1, tiled=True)
    col_count = dual_piece.shape[1]
    col_first = row_start
    add_col_xyz = lax.dynamic_slice_in_dim(centroids, col_first, col_count, 1)
    col_dual = lax.dynamic_slice_in_dim(dual_moments, col_first, col_count, 1)
    scaled_dual = (col_dual[:, None, :] * dual_piece[None]).astype(jnp.bfloat16)

    def one_block(block_id):
        row_lo = block_id * s_block
        return apply_s_tiles(
            lax.dynamic_slice_in_dim(srow_xyz, row_lo, s_block, 1),
            lax.dynamic_slice_in_dim(srow_dual, row_lo, s_block, 1),
            add_col_xyz,
            scaled_dual,
        )

    block_out = lax.map(one_block, jnp.arange(cols_t // s_block, dtype=jnp.int32))
    partial_terms = jnp.moveaxis(block_out, 0, 1).reshape(excitations, cols_t)
    potential = lax.psum_scatter(partial_terms, "row", scatter_dimension=1, tiled=True)
    march_rhs = incident - potential * norm_scale
    return (march_rhs, own_dual)


def solution(mesh):
    placed = (
        P(None, None, ("col", "row")),
        P(None, ("col", "row")),
        P(),
        P(),
        P(),
        P("row", "col"),
        P("row", "col"),
        P(None, "row"),
        P("row"),
        P(None, "row"),
    )
    return jax.shard_map(
        per_device,
        mesh=mesh,
        in_specs=placed,
        out_specs=(P(None, ("col", "row")), P(None, ("row", "col"))),
        check_vma=False,
    )
```

profile of v0, /device:TPU:0, one launch (start us, length us, event | category | flops | bytes accessed | tf_op | source)
XLA Modules:
  0.0 171.9 jit_solution(8131669916985676429)
XLA Ops:
  7.2 0.0 copy-start
  7.2 0.0 copy-start.2
  7.2 0.0 copy-start.5
  7.2 0.0 copy-start.4
  7.2 0.0 reduce-scatter.3.cloned.1.call-start
  7.3 0.9 slice_negate_fusion
  8.1 0.7 constant_dynamic-slice_fusion.7
  8.8 6.4 %all_gather.6 = bf16[4,16,512]{2,1,0:T(8,128)(2,1)S(1)} all-gather(bf16[4,16,128]{2,1,0:T(8,128)(2,1)} %param.14), channel_id=1, replica_groups=mesh['row'=4,'col'=8] {'row'}, dimensions={2}, use_global_device_ids=true | all-gather | bytes 81920 | tf_op jit(solution)/shard_map/all_gather | solution.py:106
  15.3 0.7 constant_dynamic-slice_fusion.5
  16.0 0.7 constant_dynamic-slice_fusion.6
  16.8 0.0 copy-done.2
  16.8 0.1 fusion.44
  16.9 0.0 copy-done.5
  16.9 0.0 copy-done.4
  16.9 0.1 broadcast_bitcast_fusion
  17.0 6.4 %while.2 = (s32[]{:T(128)}, f32[2,16,512]{2,1,0:T(8,128)S(1)}, s32[2]{0:T(128)S(1)}, f32[4,1024]{1,0:T(4,128)S(1)}, s32[8,512]{1,0:T(8,128)S(1)}, /*index=5*/bf1...) while((s32[]{:T(128)}, f32[2,16,512]{2,1,0:T(8,128)S(1)}, ...), condition=%wide.region_2.3_spmd, body=%wide.region_0.2_spmd.sunk | while | flops 38080524 | bytes 1126713 | solution.py:127
  17.0 0.6 dynamic_slice.98
  18.2 0.1 constant_dynamic-slice_fusion.11
  19.0 1.0 fusion.58
  20.2 0.6 dynamic_slice.98
  21.4 0.1 constant_dynamic-slice_fusion.11
  22.2 1.0 fusion.58
  23.4 1.0 copy.35
  24.4 0.0 reduce-scatter.3.cloned.1.call-update
  24.4 0.0 reduce-scatter.5.cloned.1.call-start
  24.5 0.0 copy-done
  24.5 0.9 constant_dynamic-slice_fusion.1
  25.4 0.7 compare_and_fusion
  26.1 0.8 dynamic_slice.59
  26.9 61.3 %reduce-scatter.3.cloned.1.call-done = f32[16,128]{0,1:T(8,128)} async-done(((f32[16,1024]{0,1:T(8,128)}), f32[16,128]{0,1:T(8,128)}) %reduce-scatter.3.cloned.1.call-update) | async-done | bytes 8208 | tf_op jit(solution)/shard_map/reduce_scatter | solution.py:133
  88.2 0.9 broadcast_divide_fusion
  89.1 3.2 %collective-permute-start = (f32[16,32]{0,1:T(8,128)S(1)}, f32[16,32]{0,1:T(8,128)S(1)}, u32[]{:S(2)}, u32[]{:S(2)}) collective-permute-start(f32[16,32]{0,1:T(8,128)S(1)} %get-tuple-element.114), channel_id=1, source_target_pairs={{0,1},{1,2},{2,3},{3,4},{4,5},{5,6},{6,7},{7,8},{8,9},{9,10},{10,1... | collective-permute-start | bytes 6152 | tf_op jit(solution)/shard_map/ppermute | solution.py:23
  92.4 1.3 collective-permute-start.1
  93.7 0.7 constant_dynamic-slice_fusion.4
  94.4 0.0 collective-permute-done
  94.4 3.6 %collective-permute-done.1 = f32[16,32]{0,1:T(8,128)S(1)} collective-permute-done((f32[16,32]{0,1:T(8,128)S(1)}, f32[16,32]{0,1:T(8,128)S(1)}, u32[]{:S(2)}, u32[]{:S(2)}) %collective-permute-start.1) | collective-permute-done | bytes 2080 | tf_op jit(solution)/shard_map/ppermute | solution.py:26
  98.0 0.0 copy-start.1
  98.0 1.0 gather_fusion
  99.1 0.1 broadcast_select_fusion.1
  99.2 0.1 multiply_reduce_fusion.1
  99.4 0.0 copy-done.1
  99.4 0.1 subtract_divide_fusion.1
  99.5 4.3 %collective-permute-start.2 = (f32[16,32]{0,1:T(8,128)S(1)}, f32[16,32]{0,1:T(8,128)S(1)}, u32[]{:S(2)}, u32[]{:S(2)}) collective-permute-start(f32[16,32]{0,1:T(8,128)S(1)} %get-tuple-element.112), channel_id=1, source_target_pairs={{0,1},{1,2},{2,3},{3,4},{4,5},{5,6},{6,7},{7,8},{8,9},{9,10},{10,1... | collective-permute-start | bytes 6152 | tf_op jit(solution)/shard_map/ppermute | solution.py:23
  103.8 1.3 collective-permute-start.3
  105.1 0.9 constant_dynamic-slice_fusion.2
  106.0 0.0 collective-permute-done.2
  106.0 3.4 %collective-permute-done.3 = f32[16,32]{0,1:T(8,128)S(1)} collective-permute-done((f32[16,32]{0,1:T(8,128)S(1)}, f32[16,32]{0,1:T(8,128)S(1)}, u32[]{:S(2)}, u32[]{:S(2)}) %collective-permute-start.3) | collective-permute-done | bytes 2080 | tf_op jit(solution)/shard_map/ppermute | solution.py:26
  109.5 1.0 gather_fusion.1
  110.5 0.1 broadcast_select_fusion
  110.6 0.1 multiply_reduce_fusion
  110.8 0.1 subtract_divide_fusion
  110.9 31.6 %all_gather.7 = f32[16,1024]{0,1:T(8,128)S(1)} all-gather(f32[16,128]{0,1:T(8,128)S(1)} %subtract_divide_fusion), channel_id=1, replica_groups=mesh['row'=4,'col'=8] {'col'}, dimensions={1}, use_global_device_ids=true | all-gather | bytes 73728 | tf_op jit(solution)/shard_map/all_gather | solution.py:143
  142.5 0.2 copy.36
  142.7 0.0 copy-start.3
  142.7 2.1 %fusion.31 = f32[16,512]{1,0:T(8,128)} fusion(f32[1024]{0:T(1024)S(1)} %bitcast.92, f32[512]{0:T(512)S(1)} %bitcast.95, f32[1024]{0:T(1024)S(1)} %bitcast.93, f32[512]{0:T(512)S(1)} %bitcast.96, f32[1024]{0:T(1024)S(1)} %bitcast.91, f32[512]{0:T(512)S(1)} %bitcast.94, f32[16,1024]{1,0:T(8,128)S(1)} %copy.36, ...), kind=kOutput, calls=%fused_computation.48 | convolution fusion | flops 56238080 | bytes 135168 | tf_op jit(solution)/shard_map/while/body/eval_jaxpr/qk,abk->abq/dot_general | solution.py:56
  144.7 0.0 reduce-scatter.5.cloned.1.call-update
  144.7 0.7 copy.37
  145.4 18.4 %reduce-scatter.5.cloned.1.call-done = f32[16,128]{1,0:T(8,128)} async-done(((f32[16,512]{1,0:T(8,128)}), f32[16,128]{1,0:T(8,128)}) %reduce-scatter.5.cloned.1.call-update) | async-done | bytes 8208 | tf_op jit(solution)/shard_map/reduce_scatter | solution.py:161
  163.8 0.0 copy-done.3
  163.8 1.3 multiply_subtract_fusion
  (26 shorter events, 0.3 us)
Async XLA Ops:
  7.2 17.3 %copy-start = (f32[3,4096]{1,0:T(4,128)S(1)}, f32[3,4096]{1,0:T(4,128)}, u32[]{:S(2)}) copy-start(f32[3,4096]{1,0:T(4,128)} %param.18) | copy-start | bytes 147460
  7.2 9.6 %copy-start.2 = (f32[4,4096]{1,0:T(4,128)S(1)}, f32[4,4096]{1,0:T(4,128)}, u32[]{:S(2)}) copy-start(f32[4,4096]{1,0:T(4,128)} %param.17) | copy-start | bytes 196612
  7.2 9.7 %copy-start.5 = (s32[8,4]{0,1:T(4,128)S(1)}, s32[8,4]{0,1:T(4,128)}, u32[]{:S(2)}) copy-start(s32[8,4]{0,1:T(4,128)} %param.19) | copy-start | bytes 388
  7.2 9.7 %copy-start.4 = (s32[8,4]{0,1:T(4,128)S(1)}, s32[8,4]{0,1:T(4,128)}, u32[]{:S(2)}) copy-start(s32[8,4]{0,1:T(4,128)} %param.20) | copy-start | bytes 388
  7.2 81.0 %reduce-scatter.3.cloned.1.call-start = ((), (), s32[]{:S(2)}) async-start(), calls=%async_computation.2 | async-start | bytes 589824 | tf_op jit(solution)/shard_map/reduce_scatter | solution.py:133
  24.4 139.4 %reduce-scatter.5.cloned.1.call-start = ((), (), s32[]{:S(2)}) async-start(), calls=%async_computation.3 | async-start | bytes 40960 | tf_op jit(solution)/shard_map/reduce_scatter | solution.py:161
  89.1 5.2 %collective-permute-start = (f32[16,32]{0,1:T(8,128)S(1)}, f32[16,32]{0,1:T(8,128)S(1)}, u32[]{:S(2)}, u32[]{:S(2)}) collective-permute-start(f32[16,32]{0,1:T(8,128)S(1)} %get-tuple-element.114), channel_id=1, source_target_pairs={{0,1},{1,2},{2,3},{3,4},{4,5},{5,6},{6,7},{7,8},{8,9},{9,10},{10,1... | collective-permute-start | bytes 6152 | tf_op jit(solution)/shard_map/ppermute | solution.py:23
  92.4 5.6 %collective-permute-start.1 = (f32[16,32]{0,1:T(8,128)S(1)}, f32[16,32]{0,1:T(8,128)S(1)}, u32[]{:S(2)}, u32[]{:S(2)}) collective-permute-start(f32[16,32]{0,1:T(8,128)S(1)} %get-tuple-element.115), channel_id=1, source_target_pairs={{1,0},{2,1},{3,2},{4,3},{5,4},{6,5},{7,6},{8,7},{9,8},{10,9},{11,1... | collective-permute-start | bytes 6152 | tf_op jit(solution)/shard_map/ppermute | solution.py:26
  98.0 1.3 copy-start.1
  99.5 6.5 %collective-permute-start.2 = (f32[16,32]{0,1:T(8,128)S(1)}, f32[16,32]{0,1:T(8,128)S(1)}, u32[]{:S(2)}, u32[]{:S(2)}) collective-permute-start(f32[16,32]{0,1:T(8,128)S(1)} %get-tuple-element.112), channel_id=1, source_target_pairs={{0,1},{1,2},{2,3},{3,4},{4,5},{5,6},{6,7},{7,8},{8,9},{9,10},{10,1... | collective-permute-start | bytes 6152 | tf_op jit(solution)/shard_map/ppermute | solution.py:23
  103.8 5.6 %collective-permute-start.3 = (f32[16,32]{0,1:T(8,128)S(1)}, f32[16,32]{0,1:T(8,128)S(1)}, u32[]{:S(2)}, u32[]{:S(2)}) collective-permute-start(f32[16,32]{0,1:T(8,128)S(1)} %get-tuple-element.113), channel_id=1, source_target_pairs={{1,0},{2,1},{3,2},{4,3},{5,4},{6,5},{7,6},{8,7},{9,8},{10,9},{11,1... | collective-permute-start | bytes 6152 | tf_op jit(solution)/shard_map/ppermute | solution.py:26
  142.7 21.1 %copy-start.3 = (f32[16,128]{1,0:T(8,128)S(1)}, f32[16,128]{1,0:T(8,128)}, u32[]{:S(2)}) copy-start(f32[16,128]{1,0:T(8,128)} %param.15) | copy-start | bytes 24580
Sparse Core Ops, SparseCore 0:
  24.5 63.6 reduce-scatter.2
  144.9 18.8 reduce-scatter.4
where the time goes:
time: 173 us; the launch traced here: 172 us
  waiting for transfers between devices  86.8 us (50%)
  blocking collectives  38 us (22%)
  between operations  14.3 us (8%)
  local copies, waits for them, and re-layouts  10.9 us (6%)
  starting transfers between devices  10.2 us (6%)
  other arithmetic  4.72 us (3%)
  matrix products  4.13 us (2%)
  loops' own time  2.77 us (2%)
    reduce_scatter x1, waiting for transfers between devices, per_device(): lax.psum_scatter(partial_field, 'col', scatter_dimension=1, tiled=True)  61.3 us
    all_gather x1, blocking collectives, per_device(): dual_piece = lax.all_gather(own_dual, 'col', axis=1, tiled=True)  31.6 us
    reduce_scatter x1, waiting for transfers between devices, per_device(): lax.psum_scatter(partial_terms, 'row', scatter_dimension=1, tiled=True)  18.4 us
    ppermute x2, starting transfers between devices, extended_2(): lax.ppermute(lax.slice_in_dim(block, block.shape[dim] - width, None, axis...  7.56 us
    ppermute x2, waiting for transfers between devices, extended_2(): lax.ppermute(lax.slice_in_dim(block, 0, width, axis=dim), axis, backward)  7.07 us
    all_gather x1, blocking collectives, per_device(): hist_piece = lax.all_gather(history, 'row', axis=2, tiled=True)  6.43 us
  transfers between devices with their start and end apart: 6, of which 4 were waited for; matrix products, arithmetic and copies ran while one was open for 3% of the time, Pallas kernels for 0%

commit v1 on v0

--- a/solution.py
+++ b/solution.py
@@ -49,12 +49,6 @@
     products = jnp.einsum("tqk,tabk->abtq", kernel, picked, preferred_element_type=jnp.float32)
     products = products.reshape(products.shape[0], products.shape[1], tile_rows * tile_len)
     return jnp.sum(row_weights[:, None, :] * products, axis=0)
-
-
-def apply_s_tiles(row_xyz, row_dual, col_xyz, scaled_dual):
-    kernel = (1.0 / (distances(row_xyz, col_xyz) + SOFT_S)).astype(jnp.bfloat16)
-    products = jnp.einsum("qk,abk->abq", kernel, scaled_dual, preferred_element_type=jnp.float32)
-    return jnp.sum(row_dual[:, None, :] * products, axis=0)
 
 
 def sweep_mass(field_sum, diag, off_diag, links, base, extend):
@@ -127,10 +121,9 @@
     block_out = lax.map(one_block, jnp.arange(rows_t // t_block, dtype=jnp.int32))
     partial_field = jnp.moveaxis(block_out, 0, 1).reshape(excitations, rows_t)
     partial_field = partial_field * norm_scale
-    s_block = math.gcd(cols_t, 512)
-    srow_xyz = lax.dynamic_slice_in_dim(centroids, col_start, cols_t, 1)
-    srow_dual = lax.dynamic_slice_in_dim(dual_moments, col_start, cols_t, 1)
-    share_sum = lax.psum_scatter(partial_field, "col", scatter_dimension=1, tiled=True)
+    pieces = partial_field.reshape(excitations, col_devices, shard_len).transpose(1, 0, 2)
+    pieces = lax.all_to_all(pieces, "col", 0, 0)
+    share_sum = jnp.sum(pieces, axis=0)
     shard_offset = col_id * shard_len
     own_dual = sweep_mass(
         share_sum,
@@ -140,25 +133,19 @@
         row_start + shard_offset,
         lambda values: extended_2(values, ((("row", "col"), 1),), W),
     )
-    dual_piece = lax.all_gather(own_dual, "col", axis=1, tiled=True)
-    col_count = dual_piece.shape[1]
-    col_first = row_start
-    add_col_xyz = lax.dynamic_slice_in_dim(centroids, col_first, col_count, 1)
-    col_dual = lax.dynamic_slice_in_dim(dual_moments, col_first, col_count, 1)
-    scaled_dual = (col_dual[:, None, :] * dual_piece[None]).astype(jnp.bfloat16)
-
-    def one_block(block_id):
-        row_lo = block_id * s_block
-        return apply_s_tiles(
-            lax.dynamic_slice_in_dim(srow_xyz, row_lo, s_block, 1),
-            lax.dynamic_slice_in_dim(srow_dual, row_lo, s_block, 1),
-            add_col_xyz,
-            scaled_dual,
-        )
-
-    block_out = lax.map(one_block, jnp.arange(cols_t // s_block, dtype=jnp.int32))
-    partial_terms = jnp.moveaxis(block_out, 0, 1).reshape(excitations, cols_t)
-    potential = lax.psum_scatter(partial_terms, "row", scatter_dimension=1, tiled=True)
+    devices = row_devices * col_devices
+    sent = jnp.broadcast_to(own_dual.astype(jnp.bfloat16)[None], (devices, excitations, shard_len))
+    dual_all = lax.all_to_all(sent, ("row", "col"), 0, 0)
+    scaled_dual = (
+        dual_moments.reshape(3, devices, 1, shard_len) * dual_all[None].astype(jnp.float32)
+    ).astype(jnp.bfloat16)
+    out_start = (col_id * row_devices + row_id) * shard_len
+    srow_xyz = lax.dynamic_slice_in_dim(centroids, out_start, shard_len, 1)
+    srow_dual = lax.dynamic_slice_in_dim(dual_moments, out_start, shard_len, 1)
+    kernel = (1.0 / (distances(srow_xyz, centroids) + SOFT_S)).astype(jnp.bfloat16)
+    kernel = kernel.reshape(shard_len, devices, shard_len)
+    products = jnp.einsum("qdk,adbk->abq", kernel, scaled_dual, preferred_element_type=jnp.float32)
+    potential = jnp.sum(srow_dual[:, None, :] * products, axis=0)
     march_rhs = incident - potential * norm_scale
     return (march_rhs, own_dual)
 

time: 173 us -> 71.8 us (0.42)
  waiting for transfers between devices: 86.8 us -> 21.5 us
  blocking collectives: 38 us -> 6.43 us
  starting transfers between devices: 10.2 us -> 24.5 us
  between operations: 14.3 us -> 0.98 us
  local copies, waits for them, and re-layouts: 10.9 us -> 7.82 us
    reduce_scatter x2 -> x0, waiting for transfers between devices: 79.7 us -> none  [the longest x1 61.3 us: per_device(): lax.psum_scatter(partial_field, 'col', scatter_dimension=1, tiled=True)]
    all_gather x1 -> x0, blocking collectives: 31.6 us -> none  [per_device(): dual_piece = lax.all_gather(own_dual, 'col', axis=1, tiled=True)]
    all_to_all x0 -> x2, starting transfers between devices: none -> 15.6 us  [the longest x1 9.24 us: per_device(): dual_all = lax.all_to_all(sent, ('row', 'col'), 0, 0)]
    all_to_all x0 -> x2, waiting for transfers between devices: none -> 13.1 us  [the longest x1 7.68 us: per_device(): dual_all = lax.all_to_all(sent, ('row', 'col'), 0, 0)]
    slice x4 -> x3, local copies, waits for them, and re-layouts: 1.99 us -> 0.21 us  [distances(): delta_x = row_xyz[0][:, None] - col_xyz[0][None, :]]
  transfers between devices with their start and end apart: 6 -> 6, of which waited for: 4 -> 4; matrix products, arithmetic and copies ran while one was open for 3% -> 2% of each run, Pallas kernels for 0% -> 0%
where the time goes in v1:
time: 71.8 us; the launch traced here: 71.3 us
  starting transfers between devices  24.5 us (34%)
  waiting for transfers between devices  21.5 us (30%)
  local copies, waits for them, and re-layouts  7.82 us (11%)
  blocking collectives  6.43 us (9%)
  other arithmetic  3.76 us (5%)
  matrix products  3.49 us (5%)
  loops' own time  2.77 us (4%)
  between operations  0.98 us (1%)
    all_to_all x1, starting transfers between devices, per_device(): dual_all = lax.all_to_all(sent, ('row', 'col'), 0, 0)  9.24 us
    ppermute x2, waiting for transfers between devices, extended_2(): lax.ppermute(lax.slice_in_dim(block, 0, width, axis=dim), axis, backward)  8.39 us
    all_to_all x1, waiting for transfers between devices, per_device(): dual_all = lax.all_to_all(sent, ('row', 'col'), 0, 0)  7.68 us
    all_gather x1, blocking collectives, per_device(): hist_piece = lax.all_gather(history, 'row', axis=2, tiled=True)  6.43 us
    ppermute x2, starting transfers between devices, extended_2(): lax.ppermute(lax.slice_in_dim(block, block.shape[dim] - width, None, axis...  6.38 us
    all_to_all x1, starting transfers between devices, per_device(): pieces = lax.all_to_all(pieces, 'col', 0, 0)  6.31 us
    all_to_all x1, waiting for transfers between devices, per_device(): pieces = lax.all_to_all(pieces, 'col', 0, 0)  5.4 us
    another operation x1, loops' own time, per_device(): lax.map(one_block, jnp.arange(rows_t // t_block, dtype=jnp.int32))  2.77 us
  transfers between devices with their start and end apart: 6, of which 4 were waited for; matrix products, arithmetic and copies ran while one was open for 2% of the time, Pallas kernels for 0%

profile of v1, /device:TPU:0, one launch (start us, length us, event | category | flops | bytes accessed | tf_op | source)
XLA Modules:
  0.0 71.3 jit_solution(10083132448612401100)
XLA Ops:
  0.6 0.0 copy-start
  0.6 0.0 copy-start.2
  0.7 0.9 %slice_negate_fusion = f32[1,4096]{1,0:T(1,128)S(1)} fusion(f32[4,4096]{1,0:T(4,128)} %param.17), kind=kLoop, calls=%fused_computation.74 | loop fusion | flops 4096 | bytes 32768 | tf_op jit(solution)/shard_map/neg | solution.py:93
  1.6 0.7 constant_dynamic-slice_fusion.6
  2.3 6.4 %all_gather.3 = bf16[4,16,512]{2,1,0:T(8,128)(2,1)S(1)} all-gather(bf16[4,16,128]{2,1,0:T(8,128)(2,1)} %param.14), channel_id=1, replica_groups=mesh['row'=4,'col'=8] {'row'}, dimensions={2}, use_global_device_ids=true | all-gather | bytes 81920 | tf_op jit(solution)/shard_map/all_gather | solution.py:100
  8.7 0.0 copy-done.2
  8.7 0.0 copy-start.1
  8.8 0.0 copy-start.5
  8.8 0.0 copy-start.6
  8.9 0.7 %copy-done.1 = f32[4,4096]{1,0:T(4,128)S(1)} copy-done((f32[4,4096]{1,0:T(4,128)S(1)}, f32[4,4096]{1,0:T(4,128)}, u32[]{:S(2)}) %copy-start.1) | copy-done | bytes 65560
  9.6 0.1 fusion.45
  9.7 0.0 copy-done.5
  9.7 0.0 copy-done.6
  9.7 0.1 broadcast_bitcast_fusion
  9.8 6.4 %while.10 = (s32[]{:T(128)}, f32[2,16,512]{2,1,0:T(8,128)S(1)}, s32[2]{0:T(128)S(1)}, f32[4,1024]{1,0:T(4,128)S(1)}, s32[8,512]{1,0:T(8,128)S(1)}, /*index=5*/bf...) while((s32[]{:T(128)}, f32[2,16,512]{2,1,0:T(8,128)S(1)}, ...), condition=%wide.region_2.3_spmd, body=%wide.region_0.2_spmd.sunk | while | flops 38080524 | bytes 1126713 | solution.py:121
  9.8 0.6 dynamic_slice.89
  11.0 0.1 constant_dynamic-slice_fusion.9
  11.8 1.0 %fusion.61 = f32[16,4,128]{2,0,1:T(8,128)S(1)} fusion(f32[4,512]{1,0:T(4,128)S(1)} %convert_multiply_fusion.2, f32[512]{0:T(512)S(1)} %bitcast.104, f32[4,128]{1,0:T(4,128)S(1)} %bitcast.102, f32[512]{0:T(512)S(1)} %bitcast.103, f32[4,128]{1,0:T(4,128)S(1)} %bitcast.101, f32[512]{0:T(512)S(1)} %bitcast.105, f32[4,128]{1,0:T(4,128)S(1)} %bitcast.100, ...), kind=kOutput, calls=%fused_computation.4.clone.1 | convolution fusion | flops 38068224 | bytes 331776 | tf_op jit(solution)/shard_map/while/body/eval_jaxpr/tqk,tabk->abtq/dot_general | solution.py:49
  13.0 0.6 dynamic_slice.89
  14.2 0.1 constant_dynamic-slice_fusion.9
  15.0 1.0 %fusion.61 = f32[16,4,128]{2,0,1:T(8,128)S(1)} fusion(f32[4,512]{1,0:T(4,128)S(1)} %convert_multiply_fusion.2, f32[512]{0:T(512)S(1)} %bitcast.104, f32[4,128]{1,0:T(4,128)S(1)} %bitcast.102, f32[512]{0:T(512)S(1)} %bitcast.103, f32[4,128]{1,0:T(4,128)S(1)} %bitcast.101, f32[512]{0:T(512)S(1)} %bitcast.105, f32[4,128]{1,0:T(4,128)S(1)} %bitcast.100, ...), kind=kOutput, calls=%fused_computation.4.clone.1 | convolution fusion | flops 38068224 | bytes 331776 | tf_op jit(solution)/shard_map/while/body/eval_jaxpr/tqk,tabk->abtq/dot_general | solution.py:49
  16.2 0.1 copy.29
  16.2 0.1 mul.157
  16.3 0.6 copy.30
  16.9 6.3 %all-to-all-start = ((f32[8,16,128]{2,1,0:T(8,128)}), f32[8,16,128]{2,1,0:T(8,128)S(1)}, u32[]{:S(2)}, u32[]{:S(2)}) async-start(f32[8,16,128]{2,1,0:T(8,128)} %copy.30), calls=%async_computation | async-start | bytes 131072 | tf_op jit(solution)/shard_map/all_to_all | solution.py:125
  23.3 0.7 compare_and_fusion
  24.0 0.8 %dynamic_slice.49 = f32[128]{0:T(128)S(1)} dynamic-slice(f32[1024]{0:T(1024)} %param.22, s32[]{:T(128)S(6)} %select_n.48), dynamic_slice_sizes={128} | dynamic-slice | bytes 1028 | tf_op jit(solution)/shard_map/dynamic_slice | solution.py:130
  24.7 5.4 %all-to-all-done = f32[8,16,128]{2,1,0:T(8,128)S(1)} async-done(((f32[8,16,128]{2,1,0:T(8,128)}), f32[8,16,128]{2,1,0:T(8,128)S(1)}, u32[]{:S(2)}, u32[]{:S(2)}) %all-to-all-start) | async-done | bytes 65568 | tf_op jit(solution)/shard_map/all_to_all | solution.py:125
  30.2 0.1 fusion.55
  30.2 2.3 %collective-permute-start = (f32[16,32]{1,0:T(8,128)S(1)}, f32[16,32]{1,0:T(8,128)S(1)}, u32[]{:S(2)}, u32[]{:S(2)}) collective-permute-start(f32[16,32]{1,0:T(8,128)S(1)} %get-tuple-element.99), channel_id=1, source_target_pairs={{0,1},{1,2},{2,3},{3,4},{4,5},{5,6},{6,7},{7,8},{8,9},{9,10},{10,1... | collective-permute-start | bytes 6152 | tf_op jit(solution)/shard_map/ppermute | solution.py:23
  32.5 1.3 %collective-permute-start.1 = (f32[16,32]{1,0:T(8,128)S(1)}, f32[16,32]{1,0:T(8,128)S(1)}, u32[]{:S(2)}, u32[]{:S(2)}) collective-permute-start(f32[16,32]{1,0:T(8,128)S(1)} %get-tuple-element.100), channel_id=1, source_target_pairs={{1,0},{2,1},{3,2},{4,3},{5,4},{6,5},{7,6},{8,7},{9,8},{10,9},{11,1... | collective-permute-start | bytes 6152 | tf_op jit(solution)/shard_map/ppermute | solution.py:26
  33.8 0.0 copy-done
  33.9 0.0 collective-permute-done
  33.9 4.2 %collective-permute-done.1 = f32[16,32]{1,0:T(8,128)S(1)} collective-permute-done((f32[16,32]{1,0:T(8,128)S(1)}, f32[16,32]{1,0:T(8,128)S(1)}, u32[]{:S(2)}, u32[]{:S(2)}) %collective-permute-start.1) | collective-permute-done | bytes 2080 | tf_op jit(solution)/shard_map/ppermute | solution.py:26
  38.1 0.1 pad_maximum_fusion
  38.1 0.1 copy.32
  38.3 1.0 %gather_fusion = f32[512,16]{1,0:T(8,128)S(1)} fusion(f32[16,192]{0,1:T(8,128)S(1)} %copy.32, s32[1024]{0:T(1024)S(1)} %pad_clamp_fusion), kind=kCustom, calls=%fused_computation.clone | custom fusion | bytes 67584 | tf_op jit(solution)/shard_map/jit(_take)/gather | solution.py:60
  39.3 0.1 broadcast_select_fusion.1
  39.4 0.1 multiply_reduce_fusion.1
  39.6 0.1 copy.33
  39.6 0.1 fusion.54
  39.7 4.1 %collective-permute-start.2 = (f32[16,32]{1,0:T(8,128)S(1)}, f32[16,32]{1,0:T(8,128)S(1)}, u32[]{:S(2)}, u32[]{:S(2)}) collective-permute-start(f32[16,32]{1,0:T(8,128)S(1)} %get-tuple-element.97), channel_id=1, source_target_pairs={{0,1},{1,2},{2,3},{3,4},{4,5},{5,6},{6,7},{7,8},{8,9},{9,10},{10,1... | collective-permute-start | bytes 6152 | tf_op jit(solution)/shard_map/ppermute | solution.py:23
  43.8 1.3 %collective-permute-start.3 = (f32[16,32]{1,0:T(8,128)S(1)}, f32[16,32]{1,0:T(8,128)S(1)}, u32[]{:S(2)}, u32[]{:S(2)}) collective-permute-start(f32[16,32]{1,0:T(8,128)S(1)} %get-tuple-element.98), channel_id=1, source_target_pairs={{1,0},{2,1},{3,2},{4,3},{5,4},{6,5},{7,6},{8,7},{9,8},{10,9},{11,1... | collective-permute-start | bytes 6152 | tf_op jit(solution)/shard_map/ppermute | solution.py:26
  45.1 0.0 collective-permute-done.2
  45.2 4.2 %collective-permute-done.3 = f32[16,32]{1,0:T(8,128)S(1)} collective-permute-done((f32[16,32]{1,0:T(8,128)S(1)}, f32[16,32]{1,0:T(8,128)S(1)}, u32[]{:S(2)}, u32[]{:S(2)}) %collective-permute-start.3) | collective-permute-done | bytes 2080 | tf_op jit(solution)/shard_map/ppermute | solution.py:26
  49.4 0.1 pad_maximum_fusion.1
  49.5 0.1 copy.34
  49.6 1.0 %gather_fusion.1 = f32[512,16]{1,0:T(8,128)S(1)} fusion(f32[16,192]{0,1:T(8,128)S(1)} %copy.34, s32[1024]{0:T(1024)S(1)} %pad_clamp_fusion), kind=kCustom, calls=%fused_computation.1.clone | custom fusion | bytes 67584 | tf_op jit(solution)/shard_map/jit(_take)/gather | solution.py:60
  50.6 0.1 broadcast_select_fusion
  50.7 0.1 multiply_reduce_fusion
  50.9 0.0 copy-start.3
  50.9 0.1 copy.35
  50.9 0.6 fusion.51
  51.6 0.7 broadcast_in_dim.100
  52.2 9.2 %all-to-all-start.1 = ((bf16[32,16,128]{2,1,0:T(8,128)(2,1)}), bf16[32,16,128]{2,1,0:T(8,128)(2,1)S(1)}, u32[]{:S(2)}, u32[]{:S(2)}) async-start(bf16[32,16,128]{2,1,0:T(8,128)(2,1)} %broadcast_in_dim.100), calls=%async_computation.1 | async-start | bytes 262144 | tf_op jit(solution)/shard_map/all_to_all | solution.py:138
  61.5 0.0 copy-done.3
  61.5 7.7 %all-to-all-done.1 = bf16[32,16,128]{2,1,0:T(8,128)(2,1)S(1)} async-done(((bf16[32,16,128]{2,1,0:T(8,128)(2,1)}), bf16[32,16,128]{2,1,0:T(8,128)(2,1)S(1)}, u32[]{:S(2)}, u32[]{:S(2)}) %all-to-all-start.1) | async-done | bytes 131104 | tf_op jit(solution)/shard_map/all_to_all | solution.py:138
  69.2 0.0 copy-start.4
  69.3 1.4 %fusion.32 = f32[16,128]{1,0:T(8,128)S(1)} fusion(f32[32,128]{1,0:T(8,128)S(1)} %bitcast.108, f32[128]{0:T(128)S(1)} %get-tuple-element.102, f32[32,128]{1,0:T(8,128)S(1)} %bitcast.109, f32[128]{0:T(128)S(1)} %get-tuple-element.103, f32[32,128]{1,0:T(8,128)S(1)} %bitcast.107, f32[128]{0:T(128)S(1)} %get-tuple-element.101, ...), kind=kOutput, calls=%fused_computation.49 | convolution fusion | flops 56502272 | bytes 371712 | tf_op jit(solution)/shard_map/qdk,adbk->abq/dot_general | solution.py:147
  70.7 0.0 copy-done.4
  70.7 0.6 multiply_subtract_fusion
  (32 shorter events, 0.4 us)
Async XLA Ops:
  0.6 33.2 %copy-start = (f32[4,1024]{1,0:T(4,128)S(1)}, f32[4,1024]{1,0:T(4,128)}, u32[]{:S(2)}) copy-start(f32[4,1024]{1,0:T(4,128)} %param.23) | copy-start | bytes 49156
  0.6 8.1 %copy-start.2 = (f32[3,4096]{1,0:T(4,128)S(1)}, f32[3,4096]{1,0:T(4,128)}, u32[]{:S(2)}) copy-start(f32[3,4096]{1,0:T(4,128)} %param.16) | copy-start | bytes 147460
  8.7 0.8 %copy-start.1 = (f32[4,4096]{1,0:T(4,128)S(1)}, f32[4,4096]{1,0:T(4,128)}, u32[]{:S(2)}) copy-start(f32[4,4096]{1,0:T(4,128)} %param.17) | copy-start | bytes 196612
  8.8 0.9 %copy-start.5 = (s32[8,4]{0,1:T(4,128)S(1)}, s32[8,4]{0,1:T(4,128)}, u32[]{:S(2)}) copy-start(s32[8,4]{0,1:T(4,128)} %param.20) | copy-start | bytes 388
  8.8 0.9 %copy-start.6 = (s32[8,4]{0,1:T(4,128)S(1)}, s32[8,4]{0,1:T(4,128)}, u32[]{:S(2)}) copy-start(s32[8,4]{0,1:T(4,128)} %param.19) | copy-start | bytes 388
  16.9 13.2 %all-to-all-start = ((f32[8,16,128]{2,1,0:T(8,128)}), f32[8,16,128]{2,1,0:T(8,128)S(1)}, u32[]{:S(2)}, u32[]{:S(2)}) async-start(f32[8,16,128]{2,1,0:T(8,128)} %copy.30), calls=%async_computation | async-start | bytes 131072 | tf_op jit(solution)/shard_map/all_to_all | solution.py:125
  30.2 3.6 %collective-permute-start = (f32[16,32]{1,0:T(8,128)S(1)}, f32[16,32]{1,0:T(8,128)S(1)}, u32[]{:S(2)}, u32[]{:S(2)}) collective-permute-start(f32[16,32]{1,0:T(8,128)S(1)} %get-tuple-element.99), channel_id=1, source_target_pairs={{0,1},{1,2},{2,3},{3,4},{4,5},{5,6},{6,7},{7,8},{8,9},{9,10},{10,1... | collective-permute-start | bytes 6152 | tf_op jit(solution)/shard_map/ppermute | solution.py:23
  32.5 5.5 %collective-permute-start.1 = (f32[16,32]{1,0:T(8,128)S(1)}, f32[16,32]{1,0:T(8,128)S(1)}, u32[]{:S(2)}, u32[]{:S(2)}) collective-permute-start(f32[16,32]{1,0:T(8,128)S(1)} %get-tuple-element.100), channel_id=1, source_target_pairs={{1,0},{2,1},{3,2},{4,3},{5,4},{6,5},{7,6},{8,7},{9,8},{10,9},{11,1... | collective-permute-start | bytes 6152 | tf_op jit(solution)/shard_map/ppermute | solution.py:26
  39.7 5.5 %collective-permute-start.2 = (f32[16,32]{1,0:T(8,128)S(1)}, f32[16,32]{1,0:T(8,128)S(1)}, u32[]{:S(2)}, u32[]{:S(2)}) collective-permute-start(f32[16,32]{1,0:T(8,128)S(1)} %get-tuple-element.97), channel_id=1, source_target_pairs={{0,1},{1,2},{2,3},{3,4},{4,5},{5,6},{6,7},{7,8},{8,9},{9,10},{10,1... | collective-permute-start | bytes 6152 | tf_op jit(solution)/shard_map/ppermute | solution.py:23
  43.8 5.5 %collective-permute-start.3 = (f32[16,32]{1,0:T(8,128)S(1)}, f32[16,32]{1,0:T(8,128)S(1)}, u32[]{:S(2)}, u32[]{:S(2)}) collective-permute-start(f32[16,32]{1,0:T(8,128)S(1)} %get-tuple-element.98), channel_id=1, source_target_pairs={{1,0},{2,1},{3,2},{4,3},{5,4},{6,5},{7,6},{8,7},{9,8},{10,9},{11,1... | collective-permute-start | bytes 6152 | tf_op jit(solution)/shard_map/ppermute | solution.py:26
  50.9 10.6 %copy-start.3 = (f32[3,4096]{1,0:T(4,128)S(1)}, f32[3,4096]{1,0:T(4,128)}, u32[]{:S(2)}) copy-start(f32[3,4096]{1,0:T(4,128)} %param.18) | copy-start | bytes 147460
  52.2 17.0 %all-to-all-start.1 = ((bf16[32,16,128]{2,1,0:T(8,128)(2,1)}), bf16[32,16,128]{2,1,0:T(8,128)(2,1)S(1)}, u32[]{:S(2)}, u32[]{:S(2)}) async-start(bf16[32,16,128]{2,1,0:T(8,128)(2,1)} %broadcast_in_dim.100), calls=%async_computation.1 | async-start | bytes 262144 | tf_op jit(solution)/shard_map/all_to_all | solution.py:138
  69.2 1.4 %copy-start.4 = (f32[16,128]{1,0:T(8,128)S(1)}, f32[16,128]{1,0:T(8,128)}, u32[]{:S(2)}) copy-start(f32[16,128]{1,0:T(8,128)} %param.15) | copy-start | bytes 24580

commit v2 on v1

v2 whole, which is shorter than its diff:
```python
import functools
import math

import jax
import jax.numpy as jnp
from jax import lax
from jax.experimental import pallas as pl
from jax.experimental.pallas import tpu as pltpu
from jax.sharding import PartitionSpec as P

SWEEPS = 2

SOFT_T = 0.05
SOFT_S = 0.1
NEAR_GAIN = 2.0
NEAR_REACH = 0.5

LANES = 128
HALF = LANES // 2
CHUNK = 64

VMEM = pl.BlockSpec(memory_space=pltpu.VMEM)
SMEM = pl.BlockSpec(memory_space=pltpu.SMEM)
PARAMS = pltpu.CompilerParams(vmem_limit_bytes=56 * 1024 * 1024)


def lane_ids(rows=1):
    return lax.broadcasted_iota(jnp.int32, (rows, LANES), 1)


def tile_at(start):
    return pl.ds(pl.multiple_of(start, LANES), LANES)


def edges(ref, row, length):
    first = ref[row : row + 1, :LANES]
    last = ref[row : row + 1, length - LANES :]
    return jnp.where(lane_ids() < HALF, first, last)


def split3(value):
    high = value.astype(jnp.bfloat16).astype(jnp.float32)
    rest = value - high
    middle = rest.astype(jnp.bfloat16).astype(jnp.float32)
    return [high, middle, rest - middle]


def stack_rows(rows, height):
    row_ids = lax.broadcasted_iota(jnp.int32, (height, LANES), 0)
    out = jnp.zeros((height, LANES), jnp.float32)
    for position, row in enumerate(rows):
        out = jnp.where(row_ids == position, row, out)
    return out


def pack_kernel(history_ref, shell_ref, near_ref, diag_ref, off_ref, links_ref, out_ref):
    slots, excitations = history_ref.shape[:2]
    length = diag_ref.shape[1]
    tiles = shell_ref.shape[1]
    lanes = lane_ids()
    rows = []
    for tile in (0, tiles - 1):
        code = jnp.zeros((1, LANES), jnp.float32)
        for j in range(shell_ref.shape[0]):
            value = (shell_ref[j, tile] + slots * near_ref[j, tile]).astype(jnp.float32)
            code = jnp.where(lanes == j, value, code)
        rows.append(code)
    here = lax.axis_index("row") * length + jnp.where(lanes < HALF, lanes, length - LANES + lanes)
    for m in range(links_ref.shape[0]):
        rows.append((edges(links_ref, m, length) - here).astype(jnp.float32))
    rows += split3(edges(diag_ref, 0, length))
    coupling = []
    for m in range(off_ref.shape[0]):
        coupling += split3(edges(off_ref, m, length))
    out_ref[:slots] = history_ref[...]
    out_ref[slots] = stack_rows(rows, excitations).astype(jnp.bfloat16)
    out_ref[slots + 1] = stack_rows(coupling, excitations).astype(jnp.bfloat16)


def halo_row(packed_ref, row_count, plane, row):
    me = lax.axis_index("row")
    right = lax.rem(me + 1, row_count)
    left = lax.rem(me + row_count - 1, row_count)
    right_row = packed_ref[plane, :, tile_at(right * LANES)].astype(jnp.float32)[row : row + 1]
    left_row = packed_ref[plane, :, tile_at(left * LANES)].astype(jnp.float32)[row : row + 1]
    return right_row, left_row


def column_coords(centroids_ref, start, store):
    for axis in range(3):
        line = centroids_ref[axis : axis + 1, tile_at(start)]
        store(axis, jnp.broadcast_to(line, (LANES, LANES)).T)


def t_kernel(
    packed_ref, centroids_ref, moments_ref, shell_ref, near_ref, out_ref, scaled_ref, column_ref, tile_ref, norm, slots
):
    q_tiles, p_tiles = shell_ref.shape
    row_count = packed_ref.shape[2] // LANES
    excitations = packed_ref.shape[1]
    kinds = moments_ref.shape[0]
    copies = out_ref.shape[0]
    total = centroids_ref.shape[1]
    length = p_tiles * LANES
    row_start = lax.axis_index("row") * length
    col_start = lax.axis_index("col") * (q_tiles * LANES)
    low = lane_ids() < HALF

    code_right, code_left = halo_row(packed_ref, row_count, slots, 0)[0], halo_row(packed_ref, row_count, slots, 1)[1]
    near_right = jnp.where(code_right >= slots, 1.0, 0.0)
    near_left = jnp.where(code_left >= slots, 1.0, 0.0)
    slot_right = code_right - slots * near_right
    slot_left = code_left - slots * near_left

    for j in range(q_tiles):
        lanes = slice(j * LANES, (j + 1) * LANES)
        weights = [moments_ref[a : a + 1, tile_at(col_start + j * LANES)] for a in range(kinds)]
        picked = [packed_ref[s, :, lanes].astype(jnp.float32) for s in range(slots)]
        for code in (slot_right, slot_left):
            choice = jnp.broadcast_to(code[:, j : j + 1], (excitations, LANES))
            value = picked[0]
            for s in range(1, slots):
                value = jnp.where(choice == s, picked[s], value)
            picked.append(value)
        for s, value in enumerate(picked):
            for a in range(kinds):
                scaled_ref[s, a * excitations : (a + 1) * excitations, lanes] = (weights[a] * value).astype(jnp.bfloat16)

        def store(axis, value, j=j):
            column_ref[axis, j * LANES : (j + 1) * LANES, :] = value

        column_coords(centroids_ref, col_start + j * LANES, store)

    def fill(line, gain_of):
        for j in range(q_tiles):
            gain = gain_of(j)
            for k in range(LANES // CHUNK):
                at = slice(j * LANES + k * CHUNK, j * LANES + (k + 1) * CHUNK)
                dx = line[0] - column_ref[0, at, :]
                dy = line[1] - column_ref[1, at, :]
                dz = line[2] - column_ref[2, at, :]
                spacing = jnp.sqrt(dx * dx + dy * dy + dz * dz)
                tile_ref[at, :] = (
                    1.0 / (spacing + SOFT_T) + gain * jnp.exp(spacing * (-1.0 / NEAR_REACH))
                ).astype(jnp.bfloat16)

    def products(lhs):
        return jnp.dot(lhs, tile_ref[...], preferred_element_type=jnp.float32)

    def weighted(product, weights):
        field = weights[0] * product[:excitations]
        for a in range(1, kinds):
            term = weights[a] * product[a * excitations : (a + 1) * excitations]
            field = field + term if a < kinds - 1 else field - term
        return (field * norm).astype(jnp.bfloat16)

    def one_tile(t, carry):
        start = row_start + t * LANES
        line = [centroids_ref[axis : axis + 1, tile_at(start)] for axis in range(3)]
        fill(line, lambda j: NEAR_GAIN * near_ref[j, t].astype(jnp.float32))
        lhs = jnp.concatenate(
            [scaled_ref[shell_ref[j, t], :, j * LANES : (j + 1) * LANES] for j in range(q_tiles)], axis=1
        )
        weights = [moments_ref[a : a + 1, tile_at(start)] for a in range(kinds)]
        field = weighted(products(lhs), weights)
        for copy in range(copies):
            out_ref[copy, :, tile_at(t * LANES)] = field
        return carry

    lax.fori_loop(0, p_tiles, one_tile, 0)

    right_start = lax.rem(row_start + length, total)
    left_start = lax.rem(row_start + total - LANES, total)

    def halo(ref, row):
        return jnp.where(low, ref[row : row + 1, tile_at(right_start)], ref[row : row + 1, tile_at(left_start)])

    gains = NEAR_GAIN * jnp.where(low, 1.0, 0.0), NEAR_GAIN * jnp.where(low, 0.0, 1.0)
    fill(
        [halo(centroids_ref, axis) for axis in range(3)],
        lambda j: gains[0] * near_right[:, j : j + 1] + gains[1] * near_left[:, j : j + 1],
    )
    product = jnp.where(low, products(scaled_ref[slots]), products(scaled_ref[slots + 1]))
    field = weighted(product, [halo(moments_ref, a) for a in range(kinds)])
    for copy in range(copies):
        out_ref[copy, :, length:] = field


def s_tiles_kernel(centroids_ref, out_ref, column_ref):
    length, width = out_ref.shape
    row_start = lax.axis_index("row") * length
    col_start = lax.axis_index("col") * width

    def one_tile(t, carry):
        def store(axis, value):
            column_ref[axis] = value

        column_coords(centroids_ref, row_start + t * LANES, store)
        for k in range(width // LANES):
            line = [centroids_ref[axis : axis + 1, tile_at(col_start + k * LANES)] for axis in range(3)]
            for piece in range(LANES // CHUNK):
                at = slice(piece * CHUNK, (piece + 1) * CHUNK)
                dx = line[0] - column_ref[0, at, :]
                dy = line[1] - column_ref[1, at, :]
                dz = line[2] - column_ref[2, at, :]
                spacing = jnp.sqrt(dx * dx + dy * dy + dz * dz)
                rows = pl.ds(pl.multiple_of(t * LANES + piece * CHUNK, CHUNK), CHUNK)
                out_ref[rows, k * LANES : (k + 1) * LANES] = (1.0 / (spacing + SOFT_S)).astype(jnp.bfloat16)
        return carry

    lax.fori_loop(0, length // LANES, one_tile, 0)


def sweep_kernel(
    parts_ref, packed_ref, diag_ref, off_ref, links_ref, tiles_ref, dual_moments_ref, dual_ref, out_ref, iter_ref, scaled_ref, slots
):
    length = diag_ref.shape[1]
    tiles = length // LANES
    row_count = packed_ref.shape[2] // LANES
    excitations = parts_ref.shape[1]
    link_count = links_ref.shape[0]
    kinds = dual_moments_ref.shape[0]
    row_start = lax.axis_index("row") * length
    col_start = lax.axis_index("col") * tiles_ref.shape[1]
    lanes = lane_ids()
    low = lanes < HALF

    def halo(plane, row):
        return jnp.where(low, *halo_row(packed_ref, row_count, plane, row))

    def sum3(plane, row):
        return halo(plane, row) + halo(plane, row + 1) + halo(plane, row + 2)

    def tile(t):
        return slice(t * LANES, (t + 1) * LANES)

    field, diag = [], []
    for t in range(tiles + 1):
        total = parts_ref[0, :, tile(t)].astype(jnp.float32)
        for c in range(1, parts_ref.shape[0]):
            total = total + parts_ref[c, :, tile(t)].astype(jnp.float32)
        field.append(total)
        diag.append(diag_ref[:, tile(t)] if t < tiles else sum3(slots, 2 + link_count))

    dual = [f / d for f, d in zip(field, diag)]
    for sweep_id in range(SWEEPS):
        last = sweep_id == SWEEPS - 1
        updated = []
        for t in range(tiles if last else tiles + 1):
            around = jnp.where(low, dual[(t + 1) % (tiles + 1)], dual[t - 1])
            coupled = jnp.zeros_like(field[t])
            for m in range(link_count):
                if t < tiles:
                    source = links_ref[m : m + 1, tile(t)] - (row_start + t * LANES)
                    gram = off_ref[m : m + 1, tile(t)]
                else:
                    source = halo(slots, 2 + m).astype(jnp.int32) + lanes
                    gram = sum3(slots + 1, 3 * m)
                inside = (source >= 0) & (source < LANES)
                index = jnp.broadcast_to(source & (LANES - 1), (excitations, LANES))
                here = jnp.take_along_axis(dual[t], index, axis=1)
                beside = jnp.take_along_axis(around, index, axis=1)
                coupled = coupled + gram * jnp.where(inside, here, beside)
            updated.append((field[t] - coupled) / diag[t])
        dual = updated

    for t in range(tiles):
        iter_ref[t] = dual[t]
        for a in range(kinds):
            weight = dual_moments_ref[a : a + 1, tile_at(row_start + t * LANES)]
            scaled_ref[a * excitations : (a + 1) * excitations, tile(t)] = (weight * dual[t]).astype(jnp.bfloat16)
    dual_ref[...] = iter_ref[lax.axis_index("col")]
    product = jnp.dot(scaled_ref[...], tiles_ref[...], preferred_element_type=jnp.float32)
    for k in range(out_ref.shape[0]):
        term = jnp.zeros((excitations, LANES), jnp.float32)
        for a in range(kinds):
            weight = dual_moments_ref[a : a + 1, tile_at(col_start + k * LANES)]
            term = term + weight * product[a * excitations : (a + 1) * excitations, tile(k)]
        out_ref[k] = term.astype(jnp.bfloat16)


def final_kernel(shares_ref, incident_ref, out_ref, norm):
    me = lax.axis_index("row")
    total = jnp.zeros(out_ref.shape, jnp.float32)
    for share in range(shares_ref.shape[2] // LANES):
        total = total + shares_ref[me, :, share * LANES : (share + 1) * LANES].astype(jnp.float32)
    out_ref[...] = incident_ref[...] - total * norm


def per_device(
    history,
    incident,
    centroids,
    moments,
    dual_moments,
    shell,
    near_mask,
    neighbours,
    gram_diag,
    gram_off,
):
    col_devices = lax.axis_size("col")
    slots, excitations, shard_len = history.shape
    p_tiles, q_tiles = shell.shape
    rows_t = gram_diag.shape[0]
    cols_t = q_tiles * LANES
    norm = 1.0 / math.sqrt(centroids.shape[1])
    shell, near_mask = shell.T, near_mask.T
    gram_diag = gram_diag.reshape(1, rows_t)

    packed = pl.pallas_call(
        pack_kernel,
        out_shape=jax.ShapeDtypeStruct((slots + 2, excitations, shard_len), jnp.bfloat16),
        in_specs=[VMEM, SMEM, SMEM, VMEM, VMEM, VMEM],
        out_specs=VMEM,
        compiler_params=PARAMS,
    )(history, shell, near_mask, gram_diag, gram_off, neighbours)
    packed = lax.all_gather(packed, "row", axis=2, tiled=True)

    parts = pl.pallas_call(
        functools.partial(t_kernel, norm=norm, slots=slots),
        out_shape=jax.ShapeDtypeStruct((col_devices, excitations, rows_t + LANES), jnp.bfloat16),
        in_specs=[VMEM, VMEM, VMEM, SMEM, SMEM],
        out_specs=VMEM,
        scratch_shapes=[
            pltpu.VMEM((slots + 2, moments.shape[0] * excitations, cols_t), jnp.bfloat16),
            pltpu.VMEM((3, cols_t, LANES), jnp.float32),
            pltpu.VMEM((cols_t, LANES), jnp.bfloat16),
        ],
        compiler_params=PARAMS,
    )(packed, centroids, moments, shell, near_mask)
    parts, late_centroids = lax.optimization_barrier((parts, centroids))
    parts = lax.all_to_all(parts, "col", 0, 0)

    entries = rows_t * cols_t
    s_tiles = pl.pallas_call(
        s_tiles_kernel,
        out_shape=jax.ShapeDtypeStruct((rows_t, cols_t), jnp.bfloat16),
        in_specs=[VMEM],
        out_specs=VMEM,
        scratch_shapes=[pltpu.VMEM((3, LANES, LANES), jnp.float32)],
        compiler_params=PARAMS,
        cost_estimate=pl.CostEstimate(flops=12 * entries, bytes_accessed=2 * entries, transcendentals=2 * entries),
    )(late_centroids)

    own_dual, potential = pl.pallas_call(
        functools.partial(sweep_kernel, slots=slots),
        out_shape=(
            jax.ShapeDtypeStruct((excitations, shard_len), jnp.float32),
            jax.ShapeDtypeStruct((q_tiles, excitations, LANES), jnp.bfloat16),
        ),
        in_specs=[VMEM] * 7,
        out_specs=(VMEM, VMEM),
        scratch_shapes=[
            pltpu.VMEM((p_tiles, excitations, LANES), jnp.float32),
            pltpu.VMEM((dual_moments.shape[0] * excitations, rows_t), jnp.bfloat16),
        ],
        compiler_params=PARAMS,
    )(parts, packed, gram_diag, gram_off, neighbours, s_tiles, dual_moments)
    shares = lax.all_gather(potential, "row", axis=2, tiled=True)
    march_rhs = pl.pallas_call(
        functools.partial(final_kernel, norm=norm),
        out_shape=jax.ShapeDtypeStruct(incident.shape, jnp.float32),
        in_specs=[VMEM, VMEM],
        out_specs=VMEM,
        compiler_params=PARAMS,
    )(shares, incident)
    return (march_rhs, own_dual)


def solution(mesh):
    placed = (
        P(None, None, ("col", "row")),
        P(None, ("col", "row")),
        P(),
        P(),
        P(),
        P("row", "col"),
        P("row", "col"),
        P(None, "row"),
        P("row"),
        P(None, "row"),
    )
    return jax.shard_map(
        per_device,
        mesh=mesh,
        in_specs=placed,
        out_specs=(P(None, ("col", "row")), P(None, ("row", "col"))),
        check_vma=False,
    )
```

time: 71.8 us -> 43.3 us (0.60)
  starting transfers between devices: 24.5 us -> 5.84 us
  waiting for transfers between devices: 21.5 us -> 6.38 us
  Pallas kernels: 0 us -> 15.1 us
  blocking collectives: 6.43 us -> 14.2 us
  local copies, waits for them, and re-layouts: 7.82 us -> 0.7 us
  other arithmetic: 3.76 us -> 0 us
  matrix products: 3.49 us -> 0 us
  loops' own time: 2.77 us -> 0 us
    pallas_call x0 -> x5, Pallas kernels: none -> 15.1 us  [the longest x1 5.65 us: per_device(): pl.pallas_call(functools.partial(t_kernel, norm=norm, slots=slots), out_s...]
    all_to_all x2 -> x1, starting transfers between devices: 15.6 us -> 5.84 us  [per_device(): parts = lax.all_to_all(parts, 'col', 0, 0)]
    ppermute x4 -> x0, starting transfers between devices: 8.97 us -> none  [the longest x2 6.38 us: extended_2(): lax.ppermute(lax.slice_in_dim(block, block.shape[dim] - width, None, axis...]
    ppermute x4 -> x0, waiting for transfers between devices: 8.43 us -> none  [the longest x2 8.39 us: extended_2(): lax.ppermute(lax.slice_in_dim(block, 0, width, axis=dim), axis, backward)]
    all_gather x1 -> x2, blocking collectives: 6.43 us -> 14.2 us  [the longest x1 8.25 us: per_device(): packed = lax.all_gather(packed, 'row', axis=2, tiled=True)]
    all_to_all x2 -> x1, waiting for transfers between devices: 13.1 us -> 6.38 us  [per_device(): parts = lax.all_to_all(parts, 'col', 0, 0)]
    dot_general x3 -> x0, matrix products: 3.49 us -> none  [the longest x2 2.07 us: apply_t_tiles(): jnp.einsum('tqk,tabk->abtq', kernel, picked, preferred_element_type=jnp.f...]
    another operation x1 -> x0, loops' own time: 2.77 us -> none  [per_device(): lax.map(one_block, jnp.arange(rows_t // t_block, dtype=jnp.int32))]
  transfers between devices with their start and end apart: 6 -> 1, of which waited for: 4 -> 1; matrix products, arithmetic and copies ran while one was open for 2% -> 0% of each run, Pallas kernels for 0% -> 9%
where the time goes in v2:
time: 43.3 us; the launch traced here: 42.8 us
  Pallas kernels  15.1 us (35%)
  blocking collectives  14.2 us (33%)
  waiting for transfers between devices  6.38 us (15%)
  starting transfers between devices  5.84 us (13%)
  local copies, waits for them, and re-layouts  0.7 us (2%)
  between operations  0.63 us (1%)
    all_gather x1, blocking collectives, per_device(): packed = lax.all_gather(packed, 'row', axis=2, tiled=True)  8.25 us
    all_to_all x1, waiting for transfers between devices, per_device(): parts = lax.all_to_all(parts, 'col', 0, 0)  6.38 us
    all_gather x1, blocking collectives, per_device(): shares = lax.all_gather(potential, 'row', axis=2, tiled=True)  5.91 us
    all_to_all x1, starting transfers between devices, per_device(): parts = lax.all_to_all(parts, 'col', 0, 0)  5.84 us
    pallas_call x1, Pallas kernels, per_device(): pl.pallas_call(functools.partial(t_kernel, norm=norm, slots=slots), out_s...  5.65 us
    pallas_call x1, Pallas kernels, per_device(): pl.pallas_call(s_tiles_kernel, out_shape=jax.ShapeDtypeStruct((rows_t, co...  3.69 us
    pallas_call x1, Pallas kernels, per_device(): pl.pallas_call(functools.partial(sweep_kernel, slots=slots), out_shape=(j...  2.79 us
    pallas_call x1, Pallas kernels, per_device(): pl.pallas_call(pack_kernel, out_shape=jax.ShapeDtypeStruct((slots + 2, ex...  1.49 us
  transfers between devices with their start and end apart: 1, of which 1 were waited for; matrix products, arithmetic and copies ran while one was open for 0% of the time, Pallas kernels for 9%

profile of v2, /device:TPU:0, one launch (start us, length us, event | category | flops | bytes accessed | tf_op | source)
XLA Modules:
  0.0 42.8 jit_solution(15684544496818237768)
XLA Ops:
  0.6 1.5 %shard_map.113 = bf16[6,16,128]{2,1,0:T(8,128)(2,1)} custom-call(bf16[4,16,128]{2,1,0:T(8,128)(2,1)} %history_ref.1, s32[4,8]{1,0:T(4,128)} %bitcast.5, s32[4,8]{1,0:T(4,128)} %bitcast.7, f32[1,1024]{1,0:T(1,128)} %bitcast.3, f32[4,1024]{1,0:T(4,128)} %off_ref.3, s32[4,1024]{1,0:T(4,128)} %links_ref.3), custom_call_target="tpu_custom_call" | custom-call | tf_op jit(solution)/shard_map/pallas_call | solution.py:311
  2.1 8.2 %all_gather.6.packed_ref = bf16[6,16,512]{2,1,0:T(8,128)(2,1)} all-gather(bf16[6,16,128]{2,1,0:T(8,128)(2,1)} %shard_map.113), channel_id=1, replica_groups=mesh['row'=4,'col'=8] {'row'}, dimensions={2}, use_global_device_ids=true | all-gather | bytes 122880 | tf_op jit(solution)/shard_map/all_gather | solution.py:318
  10.4 5.7 %shard_map.114 = bf16[8,16,1152]{2,1,0:T(8,128)(2,1)} custom-call(bf16[6,16,512]{2,1,0:T(8,128)(2,1)} %all_gather.6.packed_ref, f32[3,4096]{1,0:T(4,128)} %centroids_ref.2, f32[4,4096]{1,0:T(4,128)} %moments_ref.1, s32[4,8]{1,0:T(4,128)} %bitcast.6, s32[4,8]{1,0:T(4,128)} %bitcast.8), custom_call_target="tpu_custom_call" | custom-call | tf_op jit(solution)/shard_map/pallas_call | solution.py:320
  16.0 5.8 %all-to-all-start = ((bf16[8,16,1152]{2,1,0:T(8,128)(2,1)}), bf16[8,16,1152]{2,1,0:T(8,128)(2,1)S(1)}, u32[]{:S(2)}, u32[]{:S(2)}) async-start(bf16[8,16,1152]{2,1,0:T(8,128)(2,1)} %shard_map.114), calls=%async_computation | async-start | bytes 589824 | tf_op jit(solution)/shard_map/all_to_all | solution.py:333
  21.9 3.7 %shard_map.115.tiles_ref = bf16[1024,512]{1,0:T(8,128)(2,1)} custom-call(f32[3,4096]{1,0:T(4,128)} %centroids_ref.2), custom_call_target="tpu_custom_call" | custom-call | flops 6291456 | bytes 1048576 | tf_op jit(solution)/shard_map/pallas_call | solution.py:336
  25.5 6.4 %all-to-all-done.parts_ref = bf16[8,16,1152]{2,1,0:T(8,128)(2,1)S(1)} async-done(((bf16[8,16,1152]{2,1,0:T(8,128)(2,1)}), bf16[8,16,1152]{2,1,0:T(8,128)(2,1)S(1)}, u32[]{:S(2)}, u32[]{:S(2)}) %all-to-all-start) | async-done | bytes 294944 | tf_op jit(solution)/shard_map/all_to_all | solution.py:333
  31.9 0.0 copy-start
  31.9 0.7 %copy-done = bf16[8,16,1152]{2,1,0:T(8,128)(2,1)} copy-done((bf16[8,16,1152]{2,1,0:T(8,128)(2,1)}, bf16[8,16,1152]{2,1,0:T(8,128)(2,1)S(1)}, u32[]{:S(2)}) %copy-start) | copy-done | bytes 294936
  32.6 2.8 %shard_map.116 = (f32[16,128]{1,0:T(8,128)}, bf16[4,16,128]{2,1,0:T(8,128)(2,1)}) custom-call(bf16[8,16,1152]{2,1,0:T(8,128)(2,1)} %copy-done, bf16[6,16,512]{2,1,0:T(8,128)(2,1)} %all_gather.6.packed_ref, f32[1,1024]{1,0:T(1,128)} %bitcast.4, f32[4,1024]{1,0:T(4,128)} %off_ref.3, s32[4,1024]{1,0:T(4,128)} %links_ref.3, ...), custom_call_target="tpu_custom_call" | custom-call | tf_op jit(solution)/shard_map/pallas_call | solution.py:346
  35.4 5.9 %all_gather.7.shares_ref = bf16[4,16,512]{2,1,0:T(8,128)(2,1)} all-gather(bf16[4,16,128]{2,1,0:T(8,128)(2,1)} %get-tuple-element.8), channel_id=1, replica_groups=mesh['row'=4,'col'=8] {'row'}, dimensions={2}, use_global_device_ids=true | all-gather | bytes 81920 | tf_op jit(solution)/shard_map/all_gather | solution.py:360
  41.3 1.4 %shard_map.117 = f32[16,128]{1,0:T(8,128)} custom-call(bf16[4,16,512]{2,1,0:T(8,128)(2,1)} %all_gather.7.shares_ref, f32[16,128]{1,0:T(8,128)} %incident_ref.1), custom_call_target="tpu_custom_call" | custom-call | tf_op jit(solution)/shard_map/pallas_call | solution.py:361
Async XLA Ops:
  16.0 15.9 %all-to-all-start = ((bf16[8,16,1152]{2,1,0:T(8,128)(2,1)}), bf16[8,16,1152]{2,1,0:T(8,128)(2,1)S(1)}, u32[]{:S(2)}, u32[]{:S(2)}) async-start(bf16[8,16,1152]{2,1,0:T(8,128)(2,1)} %shard_map.114), calls=%async_computation | async-start | bytes 589824 | tf_op jit(solution)/shard_map/all_to_all | solution.py:333
  31.9 0.7 %copy-start = (bf16[8,16,1152]{2,1,0:T(8,128)(2,1)}, bf16[8,16,1152]{2,1,0:T(8,128)(2,1)S(1)}, u32[]{:S(2)}) copy-start(bf16[8,16,1152]{2,1,0:T(8,128)(2,1)S(1)} %all-to-all-done.parts_ref) | copy-start | bytes 884740

commit v3 on v2

--- a/solution.py
+++ b/solution.py
@@ -21,7 +21,28 @@
 
 VMEM = pl.BlockSpec(memory_space=pltpu.VMEM)
 SMEM = pl.BlockSpec(memory_space=pltpu.SMEM)
-PARAMS = pltpu.CompilerParams(vmem_limit_bytes=56 * 1024 * 1024)
+LOG2_E = 1.4426950408889634
+TINY = 1e-30
+MIB = 1024 * 1024
+
+
+def grant(*shapes):
+    total = 0
+    for shape in shapes:
+        size = 4
+        for extent in shape[:-2] + (-(-shape[-2] // 8) * 8, shape[-1]):
+            size *= extent
+        total += size
+    return pltpu.CompilerParams(vmem_limit_bytes=min(56 * MIB, 2 * total + 2 * MIB))
+
+
+def root(square):
+    square = jnp.maximum(square, TINY)
+    return square * lax.rsqrt(square)
+
+
+def inverse(value):
+    return pl.reciprocal(value, approx=True)
 
 
 def lane_ids(rows=1):
@@ -99,7 +120,6 @@
     row_count = packed_ref.shape[2] // LANES
     excitations = packed_ref.shape[1]
     kinds = moments_ref.shape[0]
-    copies = out_ref.shape[0]
     total = centroids_ref.shape[1]
     length = p_tiles * LANES
     row_start = lax.axis_index("row") * length
@@ -131,7 +151,7 @@
 
         column_coords(centroids_ref, col_start + j * LANES, store)
 
-    def fill(line, gain_of):
+    def fill(slot, line, gain_of):
         for j in range(q_tiles):
             gain = gain_of(j)
             for k in range(LANES // CHUNK):
@@ -139,13 +159,13 @@
                 dx = line[0] - column_ref[0, at, :]
                 dy = line[1] - column_ref[1, at, :]
                 dz = line[2] - column_ref[2, at, :]
-                spacing = jnp.sqrt(dx * dx + dy * dy + dz * dz)
-                tile_ref[at, :] = (
-                    1.0 / (spacing + SOFT_T) + gain * jnp.exp(spacing * (-1.0 / NEAR_REACH))
+                spacing = root(dx * dx + dy * dy + dz * dz)
+                tile_ref[slot, at, :] = (
+                    inverse(spacing + SOFT_T) + gain * jnp.exp2(spacing * (-LOG2_E / NEAR_REACH))
                 ).astype(jnp.bfloat16)
 
-    def products(lhs):
-        return jnp.dot(lhs, tile_ref[...], preferred_element_type=jnp.float32)
+    def products(slot, lhs):
+        return jnp.dot(lhs, tile_ref[slot], preferred_element_type=jnp.float32)
 
     def weighted(product, weights):
         field = weights[0] * product[:excitations]
@@ -154,20 +174,24 @@
             field = field + term if a < kinds - 1 else field - term
         return (field * norm).astype(jnp.bfloat16)
 
-    def one_tile(t, carry):
-        start = row_start + t * LANES
-        line = [centroids_ref[axis : axis + 1, tile_at(start)] for axis in range(3)]
-        fill(line, lambda j: NEAR_GAIN * near_ref[j, t].astype(jnp.float32))
-        lhs = jnp.concatenate(
-            [scaled_ref[shell_ref[j, t], :, j * LANES : (j + 1) * LANES] for j in range(q_tiles)], axis=1
-        )
-        weights = [moments_ref[a : a + 1, tile_at(start)] for a in range(kinds)]
-        field = weighted(products(lhs), weights)
-        for copy in range(copies):
-            out_ref[copy, :, tile_at(t * LANES)] = field
+    group = max(1, 16 // q_tiles)
+    while p_tiles % group:
+        group -= 1
+
+    def one_group(g, carry):
+        for k in range(group):
+            t = g * group + k
+            start = row_start + t * LANES
+            line = [centroids_ref[axis : axis + 1, tile_at(start)] for axis in range(3)]
+            fill(k % 2, line, lambda j: NEAR_GAIN * near_ref[j, t].astype(jnp.float32))
+            lhs = jnp.concatenate(
+                [scaled_ref[shell_ref[j, t], :, j * LANES : (j + 1) * LANES] for j in range(q_tiles)], axis=1
+            )
+            weights = [moments_ref[a : a + 1, tile_at(start)] for a in range(kinds)]
+            out_ref[:, tile_at(t * LANES)] = weighted(products(k % 2, lhs), weights)
         return carry
 
-    lax.fori_loop(0, p_tiles, one_tile, 0)
+    lax.fori_loop(0, p_tiles // group, one_group, 0)
 
     right_start = lax.rem(row_start + length, total)
     left_start = lax.rem(row_start + total - LANES, total)
@@ -177,13 +201,12 @@
 
     gains = NEAR_GAIN * jnp.where(low, 1.0, 0.0), NEAR_GAIN * jnp.where(low, 0.0, 1.0)
     fill(
+        0,
         [halo(centroids_ref, axis) for axis in range(3)],
         lambda j: gains[0] * near_right[:, j : j + 1] + gains[1] * near_left[:, j : j + 1],
     )
-    product = jnp.where(low, products(scaled_ref[slots]), products(scaled_ref[slots + 1]))
-    field = weighted(product, [halo(moments_ref, a) for a in range(kinds)])
-    for copy in range(copies):
-        out_ref[copy, :, length:] = field
+    product = jnp.where(low, products(0, scaled_ref[slots]), products(0, scaled_ref[slots + 1]))
+    out_ref[:, length:] = weighted(product, [halo(moments_ref, a) for a in range(kinds)])
 
 
 def s_tiles_kernel(centroids_ref, out_ref, column_ref):
@@ -203,9 +226,9 @@
                 dx = line[0] - column_ref[0, at, :]
                 dy = line[1] - column_ref[1, at, :]
                 dz = line[2] - column_ref[2, at, :]
-                spacing = jnp.sqrt(dx * dx + dy * dy + dz * dz)
+                spacing = root(dx * dx + dy * dy + dz * dz)
                 rows = pl.ds(pl.multiple_of(t * LANES + piece * CHUNK, CHUNK), CHUNK)
-                out_ref[rows, k * LANES : (k + 1) * LANES] = (1.0 / (spacing + SOFT_S)).astype(jnp.bfloat16)
+                out_ref[rows, k * LANES : (k + 1) * LANES] = inverse(spacing + SOFT_S).astype(jnp.bfloat16)
         return carry
 
     lax.fori_loop(0, length // LANES, one_tile, 0)
@@ -279,14 +302,6 @@
         out_ref[k] = term.astype(jnp.bfloat16)
 
 
-def final_kernel(shares_ref, incident_ref, out_ref, norm):
-    me = lax.axis_index("row")
-    total = jnp.zeros(out_ref.shape, jnp.float32)
-    for share in range(shares_ref.shape[2] // LANES):
-        total = total + shares_ref[me, :, share * LANES : (share + 1) * LANES].astype(jnp.float32)
-    out_ref[...] = incident_ref[...] - total * norm
-
-
 def per_device(
     history,
     incident,
@@ -299,7 +314,6 @@
     gram_diag,
     gram_off,
 ):
-    col_devices = lax.axis_size("col")
     slots, excitations, shard_len = history.shape
     p_tiles, q_tiles = shell.shape
     rows_t = gram_diag.shape[0]
@@ -313,24 +327,24 @@
         out_shape=jax.ShapeDtypeStruct((slots + 2, excitations, shard_len), jnp.bfloat16),
         in_specs=[VMEM, SMEM, SMEM, VMEM, VMEM, VMEM],
         out_specs=VMEM,
-        compiler_params=PARAMS,
+        compiler_params=grant(history.shape, gram_diag.shape, gram_off.shape, neighbours.shape),
     )(history, shell, near_mask, gram_diag, gram_off, neighbours)
     packed = lax.all_gather(packed, "row", axis=2, tiled=True)
 
     parts = pl.pallas_call(
         functools.partial(t_kernel, norm=norm, slots=slots),
-        out_shape=jax.ShapeDtypeStruct((col_devices, excitations, rows_t + LANES), jnp.bfloat16),
+        out_shape=jax.ShapeDtypeStruct((excitations, rows_t + LANES), jnp.bfloat16),
         in_specs=[VMEM, VMEM, VMEM, SMEM, SMEM],
         out_specs=VMEM,
         scratch_shapes=[
             pltpu.VMEM((slots + 2, moments.shape[0] * excitations, cols_t), jnp.bfloat16),
             pltpu.VMEM((3, cols_t, LANES), jnp.float32),
-            pltpu.VMEM((cols_t, LANES), jnp.bfloat16),
+            pltpu.VMEM((2, cols_t, LANES), jnp.bfloat16),
         ],
-        compiler_params=PARAMS,
+        compiler_params=grant((excitations, rows_t), (slots + 2, moments.shape[0] * excitations, cols_t), (5, cols_t, LANES), moments.shape, centroids.shape),
     )(packed, centroids, moments, shell, near_mask)
     parts, late_centroids = lax.optimization_barrier((parts, centroids))
-    parts = lax.all_to_all(parts, "col", 0, 0)
+    parts = lax.all_gather(parts, "col")
 
     entries = rows_t * cols_t
     s_tiles = pl.pallas_call(
@@ -339,7 +353,7 @@
         in_specs=[VMEM],
         out_specs=VMEM,
         scratch_shapes=[pltpu.VMEM((3, LANES, LANES), jnp.float32)],
-        compiler_params=PARAMS,
+        compiler_params=grant((rows_t, cols_t // 2), centroids.shape),
         cost_estimate=pl.CostEstimate(flops=12 * entries, bytes_accessed=2 * entries, transcendentals=2 * entries),
     )(late_centroids)
 
@@ -355,16 +369,11 @@
             pltpu.VMEM((p_tiles, excitations, LANES), jnp.float32),
             pltpu.VMEM((dual_moments.shape[0] * excitations, rows_t), jnp.bfloat16),
         ],
-        compiler_params=PARAMS,
+        compiler_params=grant(parts.shape, (rows_t, cols_t // 2), (excitations, 8 * rows_t)),
     )(parts, packed, gram_diag, gram_off, neighbours, s_tiles, dual_moments)
-    shares = lax.all_gather(potential, "row", axis=2, tiled=True)
-    march_rhs = pl.pallas_call(
-        functools.partial(final_kernel, norm=norm),
-        out_shape=jax.ShapeDtypeStruct(incident.shape, jnp.float32),
-        in_specs=[VMEM, VMEM],
-        out_specs=VMEM,
-        compiler_params=PARAMS,
-    )(shares, incident)
+    shares = lax.all_gather(potential, "row")
+    share = lax.dynamic_index_in_dim(shares, lax.axis_index("row"), 1, keepdims=False)
+    march_rhs = incident - jnp.sum(share.astype(jnp.float32), axis=0) * norm
     return (march_rhs, own_dual)
 
 

time: 43.3 us -> 57 us (1.32)
  blocking collectives: 14.2 us -> 43.5 us
  Pallas kernels: 15.1 us -> 6.71 us
  waiting for transfers between devices: 6.38 us -> 0 us
  starting transfers between devices: 5.84 us -> 0 us
  local copies, waits for them, and re-layouts: 0.7 us -> 4.92 us
  other arithmetic: 0 us -> 0.61 us
    all_gather x1 -> x2, blocking collectives: 5.91 us -> 37 us  [the longest x1 31.8 us: per_device(): parts = lax.all_gather(parts, 'col')]
    all_to_all x1 -> x0, waiting for transfers between devices: 6.38 us -> none  [per_device(): parts = lax.all_to_all(parts, 'col', 0, 0)]
    all_to_all x1 -> x0, starting transfers between devices: 5.84 us -> none  [per_device(): parts = lax.all_to_all(parts, 'col', 0, 0)]
    unnamed x2 -> x28, local copies, waits for them, and re-layouts: 0.7 us -> 4.92 us
    pallas_call x1, Pallas kernels: 5.65 us -> 3.12 us  [per_device(): pl.pallas_call(functools.partial(t_kernel, norm=norm, slots=slots), out_s...]
    pallas_call x1, Pallas kernels: 3.69 us -> 1.66 us  [per_device(): pl.pallas_call(s_tiles_kernel, out_shape=jax.ShapeDtypeStruct((rows_t, co...]
    all_gather x1, blocking collectives: 8.25 us -> 6.46 us  [per_device(): packed = lax.all_gather(packed, 'row', axis=2, tiled=True)]
    pallas_call x1, Pallas kernels: 2.79 us -> 1.32 us  [per_device(): pl.pallas_call(functools.partial(sweep_kernel, slots=slots), out_shape=(j...]
  transfers between devices with their start and end apart: 1 -> 0, of which waited for: 1 -> 0; matrix products, arithmetic and copies ran while one was open for 0% -> 0% of each run, Pallas kernels for 9% -> 0%
where the time goes in v3:
time: 57 us; the launch traced here: 56.4 us
  blocking collectives  43.5 us (76%)
  Pallas kernels  6.71 us (12%)
  local copies, waits for them, and re-layouts  4.92 us (9%)
  between operations  0.72 us (1%)
  other arithmetic  0.61 us (1%)
    all_gather x1, blocking collectives, per_device(): parts = lax.all_gather(parts, 'col')  31.8 us
    all_gather x1, blocking collectives, per_device(): packed = lax.all_gather(packed, 'row', axis=2, tiled=True)  6.46 us
    all_gather x1, blocking collectives, per_device(): shares = lax.all_gather(potential, 'row')  5.23 us
    unnamed x28, local copies, waits for them, and re-layouts  4.92 us
    pallas_call x1, Pallas kernels, per_device(): pl.pallas_call(functools.partial(t_kernel, norm=norm, slots=slots), out_s...  3.12 us
    pallas_call x1, Pallas kernels, per_device(): pl.pallas_call(s_tiles_kernel, out_shape=jax.ShapeDtypeStruct((rows_t, co...  1.66 us
    pallas_call x1, Pallas kernels, per_device(): pl.pallas_call(functools.partial(sweep_kernel, slots=slots), out_shape=(j...  1.32 us

profile of v3, /device:TPU:0, one launch (start us, length us, event | category | flops | bytes accessed | tf_op | source)
XLA Modules:
  0.0 56.4 jit_solution(6151612815087170434)
XLA Ops:
  0.6 0.0 copy-start.7
  0.6 0.7 %copy-done.7 = f32[1024]{0:T(1024)S(1)} copy-done((f32[1024]{0:T(1024)S(1)}, f32[1024]{0:T(1024)}, u32[]{:S(2)}) %copy-start.7) | copy-done | bytes 4120
  1.3 0.0 copy-start
  1.3 0.7 %copy-done = f32[4,1024]{1,0:T(4,128)S(1)} copy-done((f32[4,1024]{1,0:T(4,128)S(1)}, f32[4,1024]{1,0:T(4,128)}, u32[]{:S(2)}) %copy-start) | copy-done | bytes 16408
  2.0 0.0 copy-start.2
  2.0 0.7 %copy-done.2 = s32[4,1024]{1,0:T(4,128)S(1)} copy-done((s32[4,1024]{1,0:T(4,128)S(1)}, s32[4,1024]{1,0:T(4,128)}, u32[]{:S(2)}) %copy-start.2) | copy-done | bytes 16408
  2.8 0.0 copy-start.8
  2.8 0.7 %copy-done.8 = bf16[4,16,128]{2,1,0:T(8,128)(2,1)S(1)} copy-done((bf16[4,16,128]{2,1,0:T(8,128)(2,1)S(1)}, bf16[4,16,128]{2,1,0:T(8,128)(2,1)}, u32[]{:S(2)}) %copy-start.8) | copy-done | bytes 16408
  3.5 0.0 copy-start.9
  3.5 0.7 %copy-done.9 = s32[8,4]{0,1:T(4,128)S(1)} copy-done((s32[8,4]{0,1:T(4,128)S(1)}, s32[8,4]{0,1:T(4,128)}, u32[]{:S(2)}) %copy-start.9) | copy-done | bytes 152
  4.2 0.0 copy-start.11
  4.2 0.7 %copy-done.11 = s32[8,4]{0,1:T(4,128)S(1)} copy-done((s32[8,4]{0,1:T(4,128)S(1)}, s32[8,4]{0,1:T(4,128)}, u32[]{:S(2)}) %copy-start.11) | copy-done | bytes 152
  4.8 0.0 copy-start.6
  4.8 0.6 %shard_map.113 = bf16[6,16,128]{2,1,0:T(8,128)(2,1)S(1)} custom-call(bf16[4,16,128]{2,1,0:T(8,128)(2,1)S(1)} %copy-done.8, s32[4,8]{1,0:T(4,128)S(1)} %bitcast.8, s32[4,8]{1,0:T(4,128)S(1)} %bitcast.10, f32[1,1024]{1,0:T(1,128)S(1)} %bitcast.6, f32[4,1024]{1,0:T(4,128)S(1)} %copy-done, s32[4,1024]{1,0:T(4,128)S(1)} %copy-done.2), custom_call_target="tpu_custom_call" | custom-call | tf_op jit(solution)/shard_map/pallas_call | solution.py:325
  5.5 0.0 copy-start.5
  5.5 0.0 copy-start.10
  5.5 0.0 copy-start.12
  5.5 6.5 %all_gather.15.packed_ref = bf16[6,16,512]{2,1,0:T(8,128)(2,1)S(1)} all-gather(bf16[6,16,128]{2,1,0:T(8,128)(2,1)S(1)} %shard_map.113), channel_id=1, replica_groups=mesh['row'=4,'col'=8] {'row'}, dimensions={2}, use_global_device_ids=true | all-gather | bytes 122880 | tf_op jit(solution)/shard_map/all_gather | solution.py:332
  12.0 0.0 copy-done.6
  12.0 0.0 copy-done.5
  12.0 0.0 copy-done.10
  12.0 0.0 copy-done.12
  12.0 3.1 %shard_map.114 = bf16[16,1152]{1,0:T(8,128)(2,1)S(1)} custom-call(bf16[6,16,512]{2,1,0:T(8,128)(2,1)S(1)} %all_gather.15.packed_ref, f32[3,4096]{1,0:T(4,128)S(1)} %copy-done.6, f32[4,4096]{1,0:T(4,128)S(1)} %copy-done.5, s32[4,8]{1,0:T(4,128)S(1)} %bitcast.9, s32[4,8]{1,0:T(4,128)S(1)} %bitcast.11), custom_call_target="tpu_custom_call" | custom-call | tf_op jit(solution)/shard_map/pallas_call | solution.py:334
  15.1 31.8 %all-gather = bf16[128,1152]{1,0:T(8,128)(2,1)S(1)} all-gather(bf16[16,1152]{1,0:T(8,128)(2,1)S(1)} %shard_map.114), channel_id=2, replica_groups=mesh['row'=4,'col'=8] {'col'}, dimensions={0}, use_global_device_ids=true | all-gather | bytes 331776 | tf_op jit(solution)/shard_map/all_gather | solution.py:347
  46.9 0.0 copy-start.1
  46.9 0.0 copy-start.3
  46.9 0.0 copy-start.4
  46.9 1.7 %shard_map.115.tiles_ref = bf16[1024,512]{1,0:T(8,128)(2,1)S(1)} custom-call(f32[3,4096]{1,0:T(4,128)S(1)} %copy-done.6), custom_call_target="tpu_custom_call" | custom-call | flops 6291456 | bytes 1048576 | tf_op jit(solution)/shard_map/pallas_call | solution.py:350
  48.5 0.0 copy-done.1
  48.5 0.0 copy-done.3
  48.6 0.0 copy-done.4
  48.6 1.3 %shard_map.116 = (f32[16,128]{1,0:T(8,128)}, bf16[4,16,128]{2,1,0:T(8,128)(2,1)S(1)}) custom-call(bf16[8,16,1152]{2,1,0:T(8,128)(2,1)S(1)} %bitcast.5, bf16[6,16,512]{2,1,0:T(8,128)(2,1)S(1)} %all_gather.15.packed_ref, f32[1,1024]{1,0:T(1,128)S(1)} %bitcast.7, f32[4,1024]{1,0:T(4,128)S(1)} %copy-done.1, s32[4,1024]{1,0:T(4,128)S(1)} %copy-done.3, ...), custom_call_target="tpu_custom_call" | custom-call | tf_op jit(solution)/shard_map/pallas_call | solution.py:360
  49.9 5.2 %all-gather.1 = bf16[16,16,128]{2,1,0:T(8,128)(2,1)S(1)} all-gather(bf16[4,16,128]{2,1,0:T(8,128)(2,1)S(1)} %get-tuple-element.8), channel_id=3, replica_groups=mesh['row'=4,'col'=8] {'row'}, dimensions={0}, use_global_device_ids=true | all-gather | bytes 81920 | tf_op jit(solution)/shard_map/all_gather | solution.py:374
  55.1 0.0 copy-start.13
  55.1 0.7 %copy-done.13 = f32[16,128]{1,0:T(8,128)S(1)} copy-done((f32[16,128]{1,0:T(8,128)S(1)}, f32[16,128]{1,0:T(8,128)}, u32[]{:S(2)}) %copy-start.13) | copy-done | bytes 8216
  55.8 0.6 %multiply_subtract_fusion = f32[16,128]{1,0:T(8,128)} fusion(f32[16,128]{1,0:T(8,128)S(1)} %copy-done.13, f32[16,128]{1,0:T(8,128)S(1)} %convert_reduce_fusion), kind=kLoop, calls=%fused_computation.1 | loop fusion | flops 4096 | bytes 24576 | tf_op jit(solution)/shard_map/sub | solution.py:376
  (1 shorter events, 0.0 us)
Async XLA Ops:
  0.6 0.7 %copy-start.7 = (f32[1024]{0:T(1024)S(1)}, f32[1024]{0:T(1024)}, u32[]{:S(2)}) copy-start(f32[1024]{0:T(1024)} %param.18) | copy-start | bytes 12292
  1.3 0.7 %copy-start = (f32[4,1024]{1,0:T(4,128)S(1)}, f32[4,1024]{1,0:T(4,128)}, u32[]{:S(2)}) copy-start(f32[4,1024]{1,0:T(4,128)} %off_ref.3) | copy-start | bytes 49156
  2.0 0.7 %copy-start.2 = (s32[4,1024]{1,0:T(4,128)S(1)}, s32[4,1024]{1,0:T(4,128)}, u32[]{:S(2)}) copy-start(s32[4,1024]{1,0:T(4,128)} %links_ref.3) | copy-start | bytes 49156
  2.8 0.7 %copy-start.8 = (bf16[4,16,128]{2,1,0:T(8,128)(2,1)S(1)}, bf16[4,16,128]{2,1,0:T(8,128)(2,1)}, u32[]{:S(2)}) copy-start(bf16[4,16,128]{2,1,0:T(8,128)(2,1)} %history_ref.1) | copy-start | bytes 49156
  3.5 0.7 %copy-start.9 = (s32[8,4]{0,1:T(4,128)S(1)}, s32[8,4]{0,1:T(4,128)}, u32[]{:S(2)}) copy-start(s32[8,4]{0,1:T(4,128)} %param.15) | copy-start | bytes 388
  4.2 0.7 %copy-start.11 = (s32[8,4]{0,1:T(4,128)S(1)}, s32[8,4]{0,1:T(4,128)}, u32[]{:S(2)}) copy-start(s32[8,4]{0,1:T(4,128)} %param.16) | copy-start | bytes 388
  4.8 7.1 %copy-start.6 = (f32[3,4096]{1,0:T(4,128)S(1)}, f32[3,4096]{1,0:T(4,128)}, u32[]{:S(2)}) copy-start(f32[3,4096]{1,0:T(4,128)} %centroids_ref.2) | copy-start | bytes 147460
  5.5 6.5 %copy-start.5 = (f32[4,4096]{1,0:T(4,128)S(1)}, f32[4,4096]{1,0:T(4,128)}, u32[]{:S(2)}) copy-start(f32[4,4096]{1,0:T(4,128)} %moments_ref.1) | copy-start | bytes 196612
  5.5 6.5 %copy-start.10 = (s32[8,4]{0,1:T(4,128)S(1)}, s32[8,4]{0,1:T(4,128)}, u32[]{:S(2)}) copy-start(s32[8,4]{0,1:T(4,128)} %param.15) | copy-start | bytes 388
  5.5 6.5 %copy-start.12 = (s32[8,4]{0,1:T(4,128)S(1)}, s32[8,4]{0,1:T(4,128)}, u32[]{:S(2)}) copy-start(s32[8,4]{0,1:T(4,128)} %param.16) | copy-start | bytes 388
  46.9 1.7 %copy-start.1 = (f32[4,1024]{1,0:T(4,128)S(1)}, f32[4,1024]{1,0:T(4,128)}, u32[]{:S(2)}) copy-start(f32[4,1024]{1,0:T(4,128)} %off_ref.3) | copy-start | bytes 49156
  46.9 1.7 %copy-start.3 = (s32[4,1024]{1,0:T(4,128)S(1)}, s32[4,1024]{1,0:T(4,128)}, u32[]{:S(2)}) copy-start(s32[4,1024]{1,0:T(4,128)} %links_ref.3) | copy-start | bytes 49156
  46.9 1.7 %copy-start.4 = (f32[3,4096]{1,0:T(4,128)S(1)}, f32[3,4096]{1,0:T(4,128)}, u32[]{:S(2)}) copy-start(f32[3,4096]{1,0:T(4,128)} %dual_moments_ref.1) | copy-start | bytes 147460
  55.1 0.7 %copy-start.13 = (f32[16,128]{1,0:T(8,128)S(1)}, f32[16,128]{1,0:T(8,128)}, u32[]{:S(2)}) copy-start(f32[16,128]{1,0:T(8,128)} %param.11) | copy-start | bytes 24580

commit v4 on v3

--- a/solution.py
+++ b/solution.py
@@ -174,6 +174,10 @@
             field = field + term if a < kinds - 1 else field - term
         return (field * norm).astype(jnp.bfloat16)
 
+    def emit(lanes, field):
+        for copy in range(out_ref.shape[0]):
+            out_ref[copy, :, lanes] = field
+
     group = max(1, 16 // q_tiles)
     while p_tiles % group:
         group -= 1
@@ -188,7 +192,7 @@
                 [scaled_ref[shell_ref[j, t], :, j * LANES : (j + 1) * LANES] for j in range(q_tiles)], axis=1
             )
             weights = [moments_ref[a : a + 1, tile_at(start)] for a in range(kinds)]
-            out_ref[:, tile_at(t * LANES)] = weighted(products(k % 2, lhs), weights)
+            emit(tile_at(t * LANES), weighted(products(k % 2, lhs), weights))
         return carry
 
     lax.fori_loop(0, p_tiles // group, one_group, 0)
@@ -206,7 +210,7 @@
         lambda j: gains[0] * near_right[:, j : j + 1] + gains[1] * near_left[:, j : j + 1],
     )
     product = jnp.where(low, products(0, scaled_ref[slots]), products(0, scaled_ref[slots + 1]))
-    out_ref[:, length:] = weighted(product, [halo(moments_ref, a) for a in range(kinds)])
+    emit(slice(length, length + LANES), weighted(product, [halo(moments_ref, a) for a in range(kinds)]))
 
 
 def s_tiles_kernel(centroids_ref, out_ref, column_ref):
@@ -302,6 +306,14 @@
         out_ref[k] = term.astype(jnp.bfloat16)
 
 
+def final_kernel(shares_ref, incident_ref, out_ref, norm):
+    me = lax.axis_index("row")
+    total = shares_ref[0, me].astype(jnp.float32)
+    for share in range(1, shares_ref.shape[0]):
+        total = total + shares_ref[share, me].astype(jnp.float32)
+    out_ref[...] = incident_ref[...] - total * norm
+
+
 def per_device(
     history,
     incident,
@@ -314,6 +326,7 @@
     gram_diag,
     gram_off,
 ):
+    col_devices = lax.axis_size("col")
     slots, excitations, shard_len = history.shape
     p_tiles, q_tiles = shell.shape
     rows_t = gram_diag.shape[0]
@@ -327,13 +340,13 @@
         out_shape=jax.ShapeDtypeStruct((slots + 2, excitations, shard_len), jnp.bfloat16),
         in_specs=[VMEM, SMEM, SMEM, VMEM, VMEM, VMEM],
         out_specs=VMEM,
-        compiler_params=grant(history.shape, gram_diag.shape, gram_off.shape, neighbours.shape),
+        compiler_params=pltpu.CompilerParams(vmem_limit_bytes=56 * MIB),
     )(history, shell, near_mask, gram_diag, gram_off, neighbours)
     packed = lax.all_gather(packed, "row", axis=2, tiled=True)
 
     parts = pl.pallas_call(
         functools.partial(t_kernel, norm=norm, slots=slots),
-        out_shape=jax.ShapeDtypeStruct((excitations, rows_t + LANES), jnp.bfloat16),
+        out_shape=jax.ShapeDtypeStruct((col_devices, excitations, rows_t + LANES), jnp.bfloat16),
         in_specs=[VMEM, VMEM, VMEM, SMEM, SMEM],
         out_specs=VMEM,
         scratch_shapes=[
@@ -341,10 +354,10 @@
             pltpu.VMEM((3, cols_t, LANES), jnp.float32),
             pltpu.VMEM((2, cols_t, LANES), jnp.bfloat16),
         ],
-        compiler_params=grant((excitations, rows_t), (slots + 2, moments.shape[0] * excitations, cols_t), (5, cols_t, LANES), moments.shape, centroids.shape),
+        compiler_params=grant((col_devices, excitations, rows_t // 2), (slots + 2, moments.shape[0] * excitations, cols_t), (5, cols_t, LANES), moments.shape, centroids.shape),
     )(packed, centroids, moments, shell, near_mask)
     parts, late_centroids = lax.optimization_barrier((parts, centroids))
-    parts = lax.all_gather(parts, "col")
+    parts = lax.all_to_all(parts, "col", 0, 0)
 
     entries = rows_t * cols_t
     s_tiles = pl.pallas_call(
@@ -372,8 +385,13 @@
         compiler_params=grant(parts.shape, (rows_t, cols_t // 2), (excitations, 8 * rows_t)),
     )(parts, packed, gram_diag, gram_off, neighbours, s_tiles, dual_moments)
     shares = lax.all_gather(potential, "row")
-    share = lax.dynamic_index_in_dim(shares, lax.axis_index("row"), 1, keepdims=False)
-    march_rhs = incident - jnp.sum(share.astype(jnp.float32), axis=0) * norm
+    march_rhs = pl.pallas_call(
+        functools.partial(final_kernel, norm=norm),
+        out_shape=jax.ShapeDtypeStruct(incident.shape, jnp.float32),
+        in_specs=[VMEM, VMEM],
+        out_specs=VMEM,
+        compiler_params=grant(shares.shape),
+    )(shares, incident)
     return (march_rhs, own_dual)
 
 

time: 57 us -> 36.7 us (0.64)
  blocking collectives: 43.5 us -> 12.1 us
  waiting for transfers between devices: 0 us -> 8.37 us
  starting transfers between devices: 0 us -> 6.3 us
  local copies, waits for them, and re-layouts: 4.92 us -> 0.04 us
  Pallas kernels: 6.71 us -> 8.89 us
  other arithmetic: 0.61 us -> 0 us
    all_gather x1 -> x0, blocking collectives: 31.8 us -> none  [per_device(): parts = lax.all_gather(parts, 'col')]
    all_to_all x0 -> x1, waiting for transfers between devices: none -> 8.37 us  [per_device(): parts = lax.all_to_all(parts, 'col', 0, 0)]
    all_to_all x0 -> x1, starting transfers between devices: none -> 6.3 us  [per_device(): parts = lax.all_to_all(parts, 'col', 0, 0)]
    unnamed x28 -> x18, local copies, waits for them, and re-layouts: 4.92 us -> 0.04 us
    pallas_call x1, Pallas kernels: 0.62 us -> 1.49 us  [per_device(): pl.pallas_call(pack_kernel, out_shape=jax.ShapeDtypeStruct((slots + 2, ex...]
    pallas_call x1, Pallas kernels: 3.12 us -> 3.83 us  [per_device(): pl.pallas_call(functools.partial(t_kernel, norm=norm, slots=slots), out_s...]
    pallas_call x0 -> x1, Pallas kernels: none -> 0.61 us  [per_device(): pl.pallas_call(functools.partial(final_kernel, norm=norm), out_shape=jax....]
    sub x1 -> x0, other arithmetic: 0.6 us -> none  [per_device(): march_rhs = incident - jnp.sum(share.astype(jnp.float32), axis=0) * norm]
  transfers between devices with their start and end apart: 0 -> 1, of which waited for: 0 -> 1; matrix products, arithmetic and copies ran while one was open for 0% -> 0% of each run, Pallas kernels for 0% -> 5%
where the time goes in v4:
time: 36.7 us; the launch traced here: 36.4 us
  blocking collectives  12.1 us (33%)
  Pallas kernels  8.89 us (24%)
  waiting for transfers between devices  8.37 us (23%)
  starting transfers between devices  6.3 us (17%)
  between operations  0.71 us (2%)
    all_to_all x1, waiting for transfers between devices, per_device(): parts = lax.all_to_all(parts, 'col', 0, 0)  8.37 us
    all_gather x1, blocking collectives, per_device(): packed = lax.all_gather(packed, 'row', axis=2, tiled=True)  6.69 us
    all_to_all x1, starting transfers between devices, per_device(): parts = lax.all_to_all(parts, 'col', 0, 0)  6.3 us
    all_gather x1, blocking collectives, per_device(): shares = lax.all_gather(potential, 'row')  5.36 us
    pallas_call x1, Pallas kernels, per_device(): pl.pallas_call(functools.partial(t_kernel, norm=norm, slots=slots), out_s...  3.83 us
    pallas_call x1, Pallas kernels, per_device(): pl.pallas_call(s_tiles_kernel, out_shape=jax.ShapeDtypeStruct((rows_t, co...  1.66 us
    pallas_call x1, Pallas kernels, per_device(): pl.pallas_call(pack_kernel, out_shape=jax.ShapeDtypeStruct((slots + 2, ex...  1.49 us
    pallas_call x1, Pallas kernels, per_device(): pl.pallas_call(functools.partial(sweep_kernel, slots=slots), out_shape=(j...  1.31 us
  transfers between devices with their start and end apart: 1, of which 1 were waited for; matrix products, arithmetic and copies ran while one was open for 0% of the time, Pallas kernels for 5%

profile of v4, /device:TPU:0, one launch (start us, length us, event | category | flops | bytes accessed | tf_op | source)
XLA Modules:
  0.0 36.4 jit_solution(14461956303815010388)
XLA Ops:
  0.6 0.0 copy-start.4
  0.6 1.5 %shard_map.113 = bf16[6,16,128]{2,1,0:T(8,128)(2,1)} custom-call(bf16[4,16,128]{2,1,0:T(8,128)(2,1)} %history_ref.1, s32[4,8]{1,0:T(4,128)} %bitcast.7, s32[4,8]{1,0:T(4,128)} %bitcast.9, f32[1,1024]{1,0:T(1,128)} %bitcast.5, f32[4,1024]{1,0:T(4,128)} %off_ref.3, s32[4,1024]{1,0:T(4,128)} %links_ref.3), custom_call_target="tpu_custom_call" | custom-call | tf_op jit(solution)/shard_map/pallas_call | solution.py:338
  2.1 0.0 copy-start.3
  2.1 0.0 copy-start.6
  2.1 0.0 copy-start.7
  2.1 6.7 %all_gather.9.packed_ref = bf16[6,16,512]{2,1,0:T(8,128)(2,1)S(1)} all-gather(bf16[6,16,128]{2,1,0:T(8,128)(2,1)} %shard_map.113), channel_id=1, replica_groups=mesh['row'=4,'col'=8] {'row'}, dimensions={2}, use_global_device_ids=true | all-gather | bytes 122880 | tf_op jit(solution)/shard_map/all_gather | solution.py:345
  8.8 0.0 copy-done.4
  8.8 0.0 copy-done.3
  8.8 0.0 copy-done.6
  8.8 0.0 copy-done.7
  8.8 3.8 %shard_map.114 = bf16[8,16,1152]{2,1,0:T(8,128)(2,1)} custom-call(bf16[6,16,512]{2,1,0:T(8,128)(2,1)S(1)} %all_gather.9.packed_ref, f32[3,4096]{1,0:T(4,128)S(1)} %copy-done.4, f32[4,4096]{1,0:T(4,128)S(1)} %copy-done.3, s32[4,8]{1,0:T(4,128)S(1)} %bitcast.8, s32[4,8]{1,0:T(4,128)S(1)} %bitcast.10), custom_call_target="tpu_custom_call" | custom-call | tf_op jit(solution)/shard_map/pallas_call | solution.py:347
  12.7 6.3 %all-to-all-start = ((bf16[8,16,1152]{2,1,0:T(8,128)(2,1)}), bf16[8,16,1152]{2,1,0:T(8,128)(2,1)S(1)}, u32[]{:S(2)}, u32[]{:S(2)}) async-start(bf16[8,16,1152]{2,1,0:T(8,128)(2,1)} %shard_map.114), calls=%async_computation | async-start | bytes 589824 | tf_op jit(solution)/shard_map/all_to_all | solution.py:360
  19.0 0.0 copy-start
  19.0 0.0 copy-start.1
  19.0 0.0 copy-start.2
  19.0 0.0 copy-start.5
  19.0 1.7 %shard_map.115.tiles_ref = bf16[1024,512]{1,0:T(8,128)(2,1)S(1)} custom-call(f32[3,4096]{1,0:T(4,128)S(1)} %copy-done.4), custom_call_target="tpu_custom_call" | custom-call | flops 6291456 | bytes 1048576 | tf_op jit(solution)/shard_map/pallas_call | solution.py:363
  20.7 8.4 %all-to-all-done.parts_ref = bf16[8,16,1152]{2,1,0:T(8,128)(2,1)S(1)} async-done(((bf16[8,16,1152]{2,1,0:T(8,128)(2,1)}), bf16[8,16,1152]{2,1,0:T(8,128)(2,1)S(1)}, u32[]{:S(2)}, u32[]{:S(2)}) %all-to-all-start) | async-done | bytes 294944 | tf_op jit(solution)/shard_map/all_to_all | solution.py:360
  29.1 0.0 copy-done
  29.1 0.0 copy-done.1
  29.1 0.0 copy-done.2
  29.1 0.0 copy-done.5
  29.1 1.3 %shard_map.116 = (f32[16,128]{1,0:T(8,128)}, bf16[4,16,128]{2,1,0:T(8,128)(2,1)S(1)}) custom-call(bf16[8,16,1152]{2,1,0:T(8,128)(2,1)S(1)} %all-to-all-done.parts_ref, bf16[6,16,512]{2,1,0:T(8,128)(2,1)S(1)} %all_gather.9.packed_ref, f32[1,1024]{1,0:T(1,128)S(1)} %bitcast.6, f32[4,1024]{1,0:T(4,128)S(1)} %copy-done, s32[4,1024]{1,0:T(4,128)S(1)} %copy-done.1, ...), custom_call_target="tpu_custom_call" | custom-call | tf_op jit(solution)/shard_map/pallas_call | solution.py:373
  30.4 0.0 copy-start.8
  30.4 5.4 %all-gather = bf16[16,16,128]{2,1,0:T(8,128)(2,1)S(1)} all-gather(bf16[4,16,128]{2,1,0:T(8,128)(2,1)S(1)} %get-tuple-element.8), channel_id=2, replica_groups=mesh['row'=4,'col'=8] {'row'}, dimensions={0}, use_global_device_ids=true | all-gather | bytes 81920 | tf_op jit(solution)/shard_map/all_gather | solution.py:387
  35.7 0.0 copy-done.8
  35.7 0.6 %shard_map.117 = f32[16,128]{1,0:T(8,128)} custom-call(bf16[4,4,16,128]{3,2,1,0:T(8,128)(2,1)S(1)} %bitcast.4, f32[16,128]{1,0:T(8,128)S(1)} %copy-done.8), custom_call_target="tpu_custom_call" | custom-call | tf_op jit(solution)/shard_map/pallas_call | solution.py:388
Async XLA Ops:
  0.6 8.2 %copy-start.4 = (f32[3,4096]{1,0:T(4,128)S(1)}, f32[3,4096]{1,0:T(4,128)}, u32[]{:S(2)}) copy-start(f32[3,4096]{1,0:T(4,128)} %centroids_ref.2) | copy-start | bytes 147460
  2.1 6.7 %copy-start.3 = (f32[4,4096]{1,0:T(4,128)S(1)}, f32[4,4096]{1,0:T(4,128)}, u32[]{:S(2)}) copy-start(f32[4,4096]{1,0:T(4,128)} %moments_ref.1) | copy-start | bytes 196612
  2.1 6.7 %copy-start.6 = (s32[8,4]{0,1:T(4,128)S(1)}, s32[8,4]{0,1:T(4,128)}, u32[]{:S(2)}) copy-start(s32[8,4]{0,1:T(4,128)} %param.15) | copy-start | bytes 388
  2.1 6.7 %copy-start.7 = (s32[8,4]{0,1:T(4,128)S(1)}, s32[8,4]{0,1:T(4,128)}, u32[]{:S(2)}) copy-start(s32[8,4]{0,1:T(4,128)} %param.16) | copy-start | bytes 388
  12.7 16.4 %all-to-all-start = ((bf16[8,16,1152]{2,1,0:T(8,128)(2,1)}), bf16[8,16,1152]{2,1,0:T(8,128)(2,1)S(1)}, u32[]{:S(2)}, u32[]{:S(2)}) async-start(bf16[8,16,1152]{2,1,0:T(8,128)(2,1)} %shard_map.114), calls=%async_computation | async-start | bytes 589824 | tf_op jit(solution)/shard_map/all_to_all | solution.py:360
  19.0 10.1 %copy-start = (f32[4,1024]{1,0:T(4,128)S(1)}, f32[4,1024]{1,0:T(4,128)}, u32[]{:S(2)}) copy-start(f32[4,1024]{1,0:T(4,128)} %off_ref.3) | copy-start | bytes 49156
  19.0 10.1 %copy-start.1 = (s32[4,1024]{1,0:T(4,128)S(1)}, s32[4,1024]{1,0:T(4,128)}, u32[]{:S(2)}) copy-start(s32[4,1024]{1,0:T(4,128)} %links_ref.3) | copy-start | bytes 49156
  19.0 10.1 %copy-start.2 = (f32[3,4096]{1,0:T(4,128)S(1)}, f32[3,4096]{1,0:T(4,128)}, u32[]{:S(2)}) copy-start(f32[3,4096]{1,0:T(4,128)} %dual_moments_ref.1) | copy-start | bytes 147460
  19.0 10.1 %copy-start.5 = (f32[1024]{0:T(1024)S(1)}, f32[1024]{0:T(1024)}, u32[]{:S(2)}) copy-start(f32[1024]{0:T(1024)} %param.18) | copy-start | bytes 12292
  30.4 5.4 %copy-start.8 = (f32[16,128]{1,0:T(8,128)S(1)}, f32[16,128]{1,0:T(8,128)}, u32[]{:S(2)}) copy-start(f32[16,128]{1,0:T(8,128)} %incident_ref.1) | copy-start | bytes 24580

commit v5 on v4

--- a/solution.py
+++ b/solution.py
@@ -174,10 +174,6 @@
             field = field + term if a < kinds - 1 else field - term
         return (field * norm).astype(jnp.bfloat16)
 
-    def emit(lanes, field):
-        for copy in range(out_ref.shape[0]):
-            out_ref[copy, :, lanes] = field
-
     group = max(1, 16 // q_tiles)
     while p_tiles % group:
         group -= 1
@@ -192,7 +188,7 @@
                 [scaled_ref[shell_ref[j, t], :, j * LANES : (j + 1) * LANES] for j in range(q_tiles)], axis=1
             )
             weights = [moments_ref[a : a + 1, tile_at(start)] for a in range(kinds)]
-            emit(tile_at(t * LANES), weighted(products(k % 2, lhs), weights))
+            out_ref[:, tile_at(t * LANES)] = weighted(products(k % 2, lhs), weights)
         return carry
 
     lax.fori_loop(0, p_tiles // group, one_group, 0)
@@ -210,7 +206,7 @@
         lambda j: gains[0] * near_right[:, j : j + 1] + gains[1] * near_left[:, j : j + 1],
     )
     product = jnp.where(low, products(0, scaled_ref[slots]), products(0, scaled_ref[slots + 1]))
-    emit(slice(length, length + LANES), weighted(product, [halo(moments_ref, a) for a in range(kinds)]))
+    out_ref[:, length:] = weighted(product, [halo(moments_ref, a) for a in range(kinds)])
 
 
 def s_tiles_kernel(centroids_ref, out_ref, column_ref):
@@ -238,13 +234,14 @@
     lax.fori_loop(0, length // LANES, one_tile, 0)
 
 
-def sweep_kernel(
-    parts_ref, packed_ref, diag_ref, off_ref, links_ref, tiles_ref, dual_moments_ref, dual_ref, out_ref, iter_ref, scaled_ref, slots
-):
+def sweep_kernel(*refs, slots, part_count):
+    parts = refs[:part_count]
+    packed_ref, diag_ref, off_ref, links_ref, tiles_ref, dual_moments_ref = refs[part_count:-4]
+    dual_ref, out_ref, iter_ref, scaled_ref = refs[-4:]
     length = diag_ref.shape[1]
     tiles = length // LANES
     row_count = packed_ref.shape[2] // LANES
-    excitations = parts_ref.shape[1]
+    excitations = parts[0].shape[0]
     link_count = links_ref.shape[0]
     kinds = dual_moments_ref.shape[0]
     row_start = lax.axis_index("row") * length
@@ -263,9 +260,9 @@
 
     field, diag = [], []
     for t in range(tiles + 1):
-        total = parts_ref[0, :, tile(t)].astype(jnp.float32)
-        for c in range(1, parts_ref.shape[0]):
-            total = total + parts_ref[c, :, tile(t)].astype(jnp.float32)
+        total = parts[0][:, tile(t)].astype(jnp.float32)
+        for part in parts[1:]:
+            total = total + part[:, tile(t)].astype(jnp.float32)
         field.append(total)
         diag.append(diag_ref[:, tile(t)] if t < tiles else sum3(slots, 2 + link_count))
 
@@ -314,6 +311,16 @@
     out_ref[...] = incident_ref[...] - total * norm
 
 
+def exchange(value, axis):
+    count = lax.axis_size(axis)
+    pairwise = count & (count - 1) == 0
+    values = [value]
+    for step in range(count - 1, 0, -1):
+        pairs = [(i, i ^ step if pairwise else (i + step) % count) for i in range(count)]
+        values.append(lax.ppermute(value, axis, pairs))
+    return values
+
+
 def per_device(
     history,
     incident,
@@ -346,7 +353,7 @@
 
     parts = pl.pallas_call(
         functools.partial(t_kernel, norm=norm, slots=slots),
-        out_shape=jax.ShapeDtypeStruct((col_devices, excitations, rows_t + LANES), jnp.bfloat16),
+        out_shape=jax.ShapeDtypeStruct((excitations, rows_t + LANES), jnp.bfloat16),
         in_specs=[VMEM, VMEM, VMEM, SMEM, SMEM],
         out_specs=VMEM,
         scratch_shapes=[
@@ -354,10 +361,10 @@
             pltpu.VMEM((3, cols_t, LANES), jnp.float32),
             pltpu.VMEM((2, cols_t, LANES), jnp.bfloat16),
         ],
-        compiler_params=grant((col_devices, excitations, rows_t // 2), (slots + 2, moments.shape[0] * excitations, cols_t), (5, cols_t, LANES), moments.shape, centroids.shape),
+        compiler_params=grant((excitations, rows_t), (slots + 2, moments.shape[0] * excitations, cols_t), (5, cols_t, LANES), moments.shape, centroids.shape),
     )(packed, centroids, moments, shell, near_mask)
     parts, late_centroids = lax.optimization_barrier((parts, centroids))
-    parts = lax.all_to_all(parts, "col", 0, 0)
+    parts = exchange(parts, "col")
 
     entries = rows_t * cols_t
     s_tiles = pl.pallas_call(
@@ -371,19 +378,19 @@
     )(late_centroids)
 
     own_dual, potential = pl.pallas_call(
-        functools.partial(sweep_kernel, slots=slots),
+        functools.partial(sweep_kernel, slots=slots, part_count=col_devices),
         out_shape=(
             jax.ShapeDtypeStruct((excitations, shard_len), jnp.float32),
             jax.ShapeDtypeStruct((q_tiles, excitations, LANES), jnp.bfloat16),
         ),
-        in_specs=[VMEM] * 7,
+        in_specs=[VMEM] * (col_devices + 6),
         out_specs=(VMEM, VMEM),
         scratch_shapes=[
             pltpu.VMEM((p_tiles, excitations, LANES), jnp.float32),
             pltpu.VMEM((dual_moments.shape[0] * excitations, rows_t), jnp.bfloat16),
         ],
-        compiler_params=grant(parts.shape, (rows_t, cols_t // 2), (excitations, 8 * rows_t)),
-    )(parts, packed, gram_diag, gram_off, neighbours, s_tiles, dual_moments)
+        compiler_params=grant((col_devices, excitations, rows_t), (rows_t, cols_t // 2), (excitations, 8 * rows_t)),
+    )(*parts, packed, gram_diag, gram_off, neighbours, s_tiles, dual_moments)
     shares = lax.all_gather(potential, "row")
     march_rhs = pl.pallas_call(
         functools.partial(final_kernel, norm=norm),

time: 36.7 us -> 37.8 us (1.030)
  starting transfers between devices: 6.3 us -> 11.5 us
  waiting for transfers between devices: 8.37 us -> 4.97 us
  Pallas kernels: 8.89 us -> 8.19 us
    ppermute x0 -> x7, starting transfers between devices: none -> 11.5 us  [exchange(): values.append(lax.ppermute(value, axis, pairs))]
    all_to_all x1 -> x0, waiting for transfers between devices: 8.37 us -> none  [per_device(): parts = lax.all_to_all(parts, 'col', 0, 0)]
    all_to_all x1 -> x0, starting transfers between devices: 6.3 us -> none  [per_device(): parts = lax.all_to_all(parts, 'col', 0, 0)]
    ppermute x0 -> x7, waiting for transfers between devices: none -> 4.97 us  [exchange(): values.append(lax.ppermute(value, axis, pairs))]
    pallas_call x1, Pallas kernels: 3.83 us -> 3.11 us  [per_device(): pl.pallas_call(functools.partial(t_kernel, norm=norm, slots=slots), out_s...]
  transfers between devices with their start and end apart: 1 -> 7, of which waited for: 1 -> 2; matrix products, arithmetic and copies ran while one was open for 0% -> 0% of each run, Pallas kernels for 5% -> 4%
where the time goes in v5:
time: 37.8 us; the launch traced here: 37.5 us
  blocking collectives  12.1 us (32%)
  starting transfers between devices  11.5 us (30%)
  Pallas kernels  8.19 us (22%)
  waiting for transfers between devices  4.97 us (13%)
  between operations  0.74 us (2%)
    ppermute x7, starting transfers between devices, exchange(): values.append(lax.ppermute(value, axis, pairs))  11.5 us
    all_gather x1, blocking collectives, per_device(): packed = lax.all_gather(packed, 'row', axis=2, tiled=True)  6.69 us
    all_gather x1, blocking collectives, per_device(): shares = lax.all_gather(potential, 'row')  5.36 us
    ppermute x7, waiting for transfers between devices, exchange(): values.append(lax.ppermute(value, axis, pairs))  4.97 us
    pallas_call x1, Pallas kernels, per_device(): pl.pallas_call(functools.partial(t_kernel, norm=norm, slots=slots), out_s...  3.11 us
    pallas_call x1, Pallas kernels, per_device(): pl.pallas_call(s_tiles_kernel, out_shape=jax.ShapeDtypeStruct((rows_t, co...  1.64 us
    pallas_call x1, Pallas kernels, per_device(): pl.pallas_call(pack_kernel, out_shape=jax.ShapeDtypeStruct((slots + 2, ex...  1.5 us
    pallas_call x1, Pallas kernels, per_device(): pl.pallas_call(functools.partial(sweep_kernel, slots=slots, part_count=co...  1.33 us
  transfers between devices with their start and end apart: 7, of which 2 were waited for; matrix products, arithmetic and copies ran while one was open for 0% of the time, Pallas kernels for 4%

profile of v5, /device:TPU:0, one launch (start us, length us, event | category | flops | bytes accessed | tf_op | source)
XLA Modules:
  0.0 37.5 jit_solution(4614237296884481241)
XLA Ops:
  0.6 0.0 copy-start.4
  0.6 1.5 %shard_map.113 = bf16[6,16,128]{2,1,0:T(8,128)(2,1)} custom-call(bf16[4,16,128]{2,1,0:T(8,128)(2,1)} %history_ref.1, s32[4,8]{1,0:T(4,128)} %bitcast.7, s32[4,8]{1,0:T(4,128)} %bitcast.9, f32[1,1024]{1,0:T(1,128)} %bitcast.5, f32[4,1024]{1,0:T(4,128)} %refs_10_.1, s32[4,1024]{1,0:T(4,128)} %refs_11_.1), custom_call_target="tpu_custom_call" | custom-call | tf_op jit(solution)/shard_map/pallas_call | solution.py:345
  2.1 0.0 copy-start.3
  2.1 0.0 copy-start.6
  2.1 0.0 copy-start.7
  2.1 6.7 %all_gather.9.packed_ref.refs_8_ = bf16[6,16,512]{2,1,0:T(8,128)(2,1)S(1)} all-gather(bf16[6,16,128]{2,1,0:T(8,128)(2,1)} %shard_map.113), channel_id=1, replica_groups=mesh['row'=4,'col'=8] {'row'}, dimensions={2}, use_global_device_ids=true | all-gather | bytes 122880 | tf_op jit(solution)/shard_map/all_gather | solution.py:352
  8.8 0.0 copy-done.4
  8.8 0.0 copy-done.3
  8.8 0.0 copy-done.6
  8.8 0.0 copy-done.7
  8.9 3.1 %shard_map.114.refs_0_ = bf16[16,1152]{1,0:T(8,128)(2,1)S(1)} custom-call(bf16[6,16,512]{2,1,0:T(8,128)(2,1)S(1)} %all_gather.9.packed_ref.refs_8_, f32[3,4096]{1,0:T(4,128)S(1)} %copy-done.4, f32[4,4096]{1,0:T(4,128)S(1)} %copy-done.3, s32[4,8]{1,0:T(4,128)S(1)} %bitcast.8, s32[4,8]{1,0:T(4,128)S(1)} %bitcast.10), custom_call_target="tpu_custom_call" | custom-call | tf_op jit(solution)/shard_map/pallas_call | solution.py:354
  12.0 0.0 copy-start
  12.0 0.0 copy-start.1
  12.0 0.0 copy-start.2
  12.0 0.0 copy-start.5
  12.0 2.0 %collective-permute-start.6 = (bf16[16,1152]{1,0:T(8,128)(2,1)S(1)}, bf16[16,1152]{1,0:T(8,128)(2,1)S(1)}, u32[]{:S(2)}, u32[]{:S(2)}) collective-permute-start(bf16[16,1152]{1,0:T(8,128)(2,1)S(1)} %shard_map.114.refs_0_), channel_id=1, source_target_pairs={{0,1},{1,0},{2,3},{3,2},{4,5},{5,4},{6,7},{7,6},{8,9},{9,8},{10,11... | collective-permute-start | bytes 110600 | tf_op jit(solution)/shard_map/ppermute | solution.py:320
  14.1 1.6 %collective-permute-start.5 = (bf16[16,1152]{1,0:T(8,128)(2,1)S(1)}, bf16[16,1152]{1,0:T(8,128)(2,1)S(1)}, u32[]{:S(2)}, u32[]{:S(2)}) collective-permute-start(bf16[16,1152]{1,0:T(8,128)(2,1)S(1)} %shard_map.114.refs_0_), channel_id=1, source_target_pairs={{0,2},{1,3},{2,0},{3,1},{4,6},{5,7},{6,4},{7,5},{8,10},{9,11},{10,... | collective-permute-start | bytes 110600 | tf_op jit(solution)/shard_map/ppermute | solution.py:320
  15.6 0.0 collective-permute-start.4
  15.7 3.0 %collective-permute-start.3 = (bf16[16,1152]{1,0:T(8,128)(2,1)S(1)}, bf16[16,1152]{1,0:T(8,128)(2,1)S(1)}, u32[]{:S(2)}, u32[]{:S(2)}) collective-permute-start(bf16[16,1152]{1,0:T(8,128)(2,1)S(1)} %shard_map.114.refs_0_), channel_id=1, source_target_pairs={{0,4},{1,5},{2,6},{3,7},{4,0},{5,1},{6,2},{7,3},{8,12},{9,13},{10,... | collective-permute-start | bytes 110600 | tf_op jit(solution)/shard_map/ppermute | solution.py:320
  18.6 1.3 %collective-permute-start.2 = (bf16[16,1152]{1,0:T(8,128)(2,1)S(1)}, bf16[16,1152]{1,0:T(8,128)(2,1)S(1)}, u32[]{:S(2)}, u32[]{:S(2)}) collective-permute-start(bf16[16,1152]{1,0:T(8,128)(2,1)S(1)} %shard_map.114.refs_0_), channel_id=1, source_target_pairs={{0,5},{1,4},{2,7},{3,6},{4,1},{5,0},{6,3},{7,2},{8,13},{9,12},{10,... | collective-permute-start | bytes 110600 | tf_op jit(solution)/shard_map/ppermute | solution.py:320
  19.9 0.0 collective-permute-done.6.refs_7_
  19.9 3.6 %collective-permute-start.1 = (bf16[16,1152]{1,0:T(8,128)(2,1)S(1)}, bf16[16,1152]{1,0:T(8,128)(2,1)S(1)}, u32[]{:S(2)}, u32[]{:S(2)}) collective-permute-start(bf16[16,1152]{1,0:T(8,128)(2,1)S(1)} %shard_map.114.refs_0_), channel_id=1, source_target_pairs={{0,6},{1,7},{2,4},{3,5},{4,2},{5,3},{6,0},{7,1},{8,14},{9,15},{10,... | collective-permute-start | bytes 110600 | tf_op jit(solution)/shard_map/ppermute | solution.py:320
  23.5 0.0 collective-permute-done.5.refs_6_
  23.5 0.0 collective-permute-start
  23.5 1.6 %shard_map.115.refs_12_ = bf16[1024,512]{1,0:T(8,128)(2,1)S(1)} custom-call(f32[3,4096]{1,0:T(4,128)S(1)} %copy-done.4), custom_call_target="tpu_custom_call" | custom-call | flops 6291456 | bytes 1048576 | tf_op jit(solution)/shard_map/pallas_call | solution.py:370
  25.2 0.0 collective-permute-done.4.refs_5_
  25.2 0.0 collective-permute-done.3.refs_4_
  25.2 0.0 collective-permute-done.2.refs_3_
  25.2 0.7 %collective-permute-done.1.refs_2_ = bf16[16,1152]{1,0:T(8,128)(2,1)S(1)} collective-permute-done((bf16[16,1152]{1,0:T(8,128)(2,1)S(1)}, bf16[16,1152]{1,0:T(8,128)(2,1)S(1)}, u32[]{:S(2)}, u32[]{:S(2)}) %collective-permute-start.1) | collective-permute-done | bytes 36896 | tf_op jit(solution)/shard_map/ppermute | solution.py:320
  26.0 4.2 %collective-permute-done.refs_1_ = bf16[16,1152]{1,0:T(8,128)(2,1)S(1)} collective-permute-done((bf16[16,1152]{1,0:T(8,128)(2,1)S(1)}, bf16[16,1152]{1,0:T(8,128)(2,1)S(1)}, u32[]{:S(2)}, u32[]{:S(2)}) %collective-permute-start) | collective-permute-done | bytes 36896 | tf_op jit(solution)/shard_map/ppermute | solution.py:320
  30.2 0.0 copy-done
  30.2 0.0 copy-done.1
  30.2 0.0 copy-done.2
  30.2 0.0 copy-done.5
  30.2 1.3 %shard_map.116 = (f32[16,128]{1,0:T(8,128)}, bf16[4,16,128]{2,1,0:T(8,128)(2,1)S(1)}) custom-call(bf16[16,1152]{1,0:T(8,128)(2,1)S(1)} %shard_map.114.refs_0_, bf16[16,1152]{1,0:T(8,128)(2,1)S(1)} %collective-permute-done.refs_1_, bf16[16,1152]{1,0:T(8,128)(2,1)S(1)} %collective-permute-done.1.refs_2_, bf16[16,1152]{1,0:T(8,128)(2,1)S(1)} %collective-permute-done.2.refs_3_, ...), custom_call_target="tpu_custom_call" | custom-call | tf_op jit(solution)/shard_map/pallas_call | solution.py:380
  31.5 0.0 copy-start.8
  31.5 5.4 %all-gather = bf16[16,16,128]{2,1,0:T(8,128)(2,1)S(1)} all-gather(bf16[4,16,128]{2,1,0:T(8,128)(2,1)S(1)} %get-tuple-element.8), channel_id=2, replica_groups=mesh['row'=4,'col'=8] {'row'}, dimensions={0}, use_global_device_ids=true | all-gather | bytes 81920 | tf_op jit(solution)/shard_map/all_gather | solution.py:394
  36.9 0.0 copy-done.8
  36.9 0.6 %shard_map.117 = f32[16,128]{1,0:T(8,128)} custom-call(bf16[4,4,16,128]{3,2,1,0:T(8,128)(2,1)S(1)} %bitcast.4, f32[16,128]{1,0:T(8,128)S(1)} %copy-done.8), custom_call_target="tpu_custom_call" | custom-call | tf_op jit(solution)/shard_map/pallas_call | solution.py:395
Async XLA Ops:
  0.6 8.2 %copy-start.4 = (f32[3,4096]{1,0:T(4,128)S(1)}, f32[3,4096]{1,0:T(4,128)}, u32[]{:S(2)}) copy-start(f32[3,4096]{1,0:T(4,128)} %centroids_ref.2) | copy-start | bytes 147460
  2.1 6.7 %copy-start.3 = (f32[4,4096]{1,0:T(4,128)S(1)}, f32[4,4096]{1,0:T(4,128)}, u32[]{:S(2)}) copy-start(f32[4,4096]{1,0:T(4,128)} %moments_ref.1) | copy-start | bytes 196612
  2.1 6.7 %copy-start.6 = (s32[8,4]{0,1:T(4,128)S(1)}, s32[8,4]{0,1:T(4,128)}, u32[]{:S(2)}) copy-start(s32[8,4]{0,1:T(4,128)} %param.15) | copy-start | bytes 388
  2.1 6.7 %copy-start.7 = (s32[8,4]{0,1:T(4,128)S(1)}, s32[8,4]{0,1:T(4,128)}, u32[]{:S(2)}) copy-start(s32[8,4]{0,1:T(4,128)} %param.16) | copy-start | bytes 388
  12.0 18.2 %copy-start = (f32[4,1024]{1,0:T(4,128)S(1)}, f32[4,1024]{1,0:T(4,128)}, u32[]{:S(2)}) copy-start(f32[4,1024]{1,0:T(4,128)} %refs_10_.1) | copy-start | bytes 49156
  12.0 18.2 %copy-start.1 = (s32[4,1024]{1,0:T(4,128)S(1)}, s32[4,1024]{1,0:T(4,128)}, u32[]{:S(2)}) copy-start(s32[4,1024]{1,0:T(4,128)} %refs_11_.1) | copy-start | bytes 49156
  12.0 18.2 %copy-start.2 = (f32[3,4096]{1,0:T(4,128)S(1)}, f32[3,4096]{1,0:T(4,128)}, u32[]{:S(2)}) copy-start(f32[3,4096]{1,0:T(4,128)} %refs_13_.1) | copy-start | bytes 147460
  12.0 18.2 %copy-start.5 = (f32[1024]{0:T(1024)S(1)}, f32[1024]{0:T(1024)}, u32[]{:S(2)}) copy-start(f32[1024]{0:T(1024)} %param.18) | copy-start | bytes 12292
  12.0 7.9 %collective-permute-start.6 = (bf16[16,1152]{1,0:T(8,128)(2,1)S(1)}, bf16[16,1152]{1,0:T(8,128)(2,1)S(1)}, u32[]{:S(2)}, u32[]{:S(2)}) collective-permute-start(bf16[16,1152]{1,0:T(8,128)(2,1)S(1)} %shard_map.114.refs_0_), channel_id=1, source_target_pairs={{0,1},{1,0},{2,3},{3,2},{4,5},{5,4},{6,7},{7,6},{8,9},{9,8},{10,11... | collective-permute-start | bytes 110600 | tf_op jit(solution)/shard_map/ppermute | solution.py:320
  14.1 9.5 %collective-permute-start.5 = (bf16[16,1152]{1,0:T(8,128)(2,1)S(1)}, bf16[16,1152]{1,0:T(8,128)(2,1)S(1)}, u32[]{:S(2)}, u32[]{:S(2)}) collective-permute-start(bf16[16,1152]{1,0:T(8,128)(2,1)S(1)} %shard_map.114.refs_0_), channel_id=1, source_target_pairs={{0,2},{1,3},{2,0},{3,1},{4,6},{5,7},{6,4},{7,5},{8,10},{9,11},{10,... | collective-permute-start | bytes 110600 | tf_op jit(solution)/shard_map/ppermute | solution.py:320
  15.6 9.5 %collective-permute-start.4 = (bf16[16,1152]{1,0:T(8,128)(2,1)S(1)}, bf16[16,1152]{1,0:T(8,128)(2,1)S(1)}, u32[]{:S(2)}, u32[]{:S(2)}) collective-permute-start(bf16[16,1152]{1,0:T(8,128)(2,1)S(1)} %shard_map.114.refs_0_), channel_id=1, source_target_pairs={{0,3},{1,2},{2,1},{3,0},{4,7},{5,6},{6,5},{7,4},{8,11},{9,10},{10,... | collective-permute-start | bytes 110600 | tf_op jit(solution)/shard_map/ppermute | solution.py:320
  15.7 9.6 %collective-permute-start.3 = (bf16[16,1152]{1,0:T(8,128)(2,1)S(1)}, bf16[16,1152]{1,0:T(8,128)(2,1)S(1)}, u32[]{:S(2)}, u32[]{:S(2)}) collective-permute-start(bf16[16,1152]{1,0:T(8,128)(2,1)S(1)} %shard_map.114.refs_0_), channel_id=1, source_target_pairs={{0,4},{1,5},{2,6},{3,7},{4,0},{5,1},{6,2},{7,3},{8,12},{9,13},{10,... | collective-permute-start | bytes 110600 | tf_op jit(solution)/shard_map/ppermute | solution.py:320
  18.6 6.6 %collective-permute-start.2 = (bf16[16,1152]{1,0:T(8,128)(2,1)S(1)}, bf16[16,1152]{1,0:T(8,128)(2,1)S(1)}, u32[]{:S(2)}, u32[]{:S(2)}) collective-permute-start(bf16[16,1152]{1,0:T(8,128)(2,1)S(1)} %shard_map.114.refs_0_), channel_id=1, source_target_pairs={{0,5},{1,4},{2,7},{3,6},{4,1},{5,0},{6,3},{7,2},{8,13},{9,12},{10,... | collective-permute-start | bytes 110600 | tf_op jit(solution)/shard_map/ppermute | solution.py:320
  19.9 6.0 %collective-permute-start.1 = (bf16[16,1152]{1,0:T(8,128)(2,1)S(1)}, bf16[16,1152]{1,0:T(8,128)(2,1)S(1)}, u32[]{:S(2)}, u32[]{:S(2)}) collective-permute-start(bf16[16,1152]{1,0:T(8,128)(2,1)S(1)} %shard_map.114.refs_0_), channel_id=1, source_target_pairs={{0,6},{1,7},{2,4},{3,5},{4,2},{5,3},{6,0},{7,1},{8,14},{9,15},{10,... | collective-permute-start | bytes 110600 | tf_op jit(solution)/shard_map/ppermute | solution.py:320
  23.5 6.7 %collective-permute-start = (bf16[16,1152]{1,0:T(8,128)(2,1)S(1)}, bf16[16,1152]{1,0:T(8,128)(2,1)S(1)}, u32[]{:S(2)}, u32[]{:S(2)}) collective-permute-start(bf16[16,1152]{1,0:T(8,128)(2,1)S(1)} %shard_map.114.refs_0_), channel_id=1, source_target_pairs={{0,7},{1,6},{2,5},{3,4},{4,3},{5,2},{6,1},{7,0},{8,15},{9,14},{10,... | collective-permute-start | bytes 110600 | tf_op jit(solution)/shard_map/ppermute | solution.py:320
  31.5 5.4 %copy-start.8 = (f32[16,128]{1,0:T(8,128)S(1)}, f32[16,128]{1,0:T(8,128)}, u32[]{:S(2)}) copy-start(f32[16,128]{1,0:T(8,128)} %incident_ref.1) | copy-start | bytes 24580

commit v6 on v5

--- a/solution.py
+++ b/solution.py
@@ -311,16 +311,6 @@
     out_ref[...] = incident_ref[...] - total * norm
 
 
-def exchange(value, axis):
-    count = lax.axis_size(axis)
-    pairwise = count & (count - 1) == 0
-    values = [value]
-    for step in range(count - 1, 0, -1):
-        pairs = [(i, i ^ step if pairwise else (i + step) % count) for i in range(count)]
-        values.append(lax.ppermute(value, axis, pairs))
-    return values
-
-
 def per_device(
     history,
     incident,
@@ -333,7 +323,6 @@
     gram_diag,
     gram_off,
 ):
-    col_devices = lax.axis_size("col")
     slots, excitations, shard_len = history.shape
     p_tiles, q_tiles = shell.shape
     rows_t = gram_diag.shape[0]
@@ -364,7 +353,7 @@
         compiler_params=grant((excitations, rows_t), (slots + 2, moments.shape[0] * excitations, cols_t), (5, cols_t, LANES), moments.shape, centroids.shape),
     )(packed, centroids, moments, shell, near_mask)
     parts, late_centroids = lax.optimization_barrier((parts, centroids))
-    parts = exchange(parts, "col")
+    parts = lax.psum(parts, "col")
 
     entries = rows_t * cols_t
     s_tiles = pl.pallas_call(
@@ -378,19 +367,19 @@
     )(late_centroids)
 
     own_dual, potential = pl.pallas_call(
-        functools.partial(sweep_kernel, slots=slots, part_count=col_devices),
+        functools.partial(sweep_kernel, slots=slots, part_count=1),
         out_shape=(
             jax.ShapeDtypeStruct((excitations, shard_len), jnp.float32),
             jax.ShapeDtypeStruct((q_tiles, excitations, LANES), jnp.bfloat16),
         ),
-        in_specs=[VMEM] * (col_devices + 6),
+        in_specs=[VMEM] * 7,
         out_specs=(VMEM, VMEM),
         scratch_shapes=[
             pltpu.VMEM((p_tiles, excitations, LANES), jnp.float32),
             pltpu.VMEM((dual_moments.shape[0] * excitations, rows_t), jnp.bfloat16),
         ],
-        compiler_params=grant((col_devices, excitations, rows_t), (rows_t, cols_t // 2), (excitations, 8 * rows_t)),
-    )(*parts, packed, gram_diag, gram_off, neighbours, s_tiles, dual_moments)
+        compiler_params=grant((excitations, rows_t), (rows_t, cols_t // 2), (excitations, 8 * rows_t)),
+    )(parts, packed, gram_diag, gram_off, neighbours, s_tiles, dual_moments)
     shares = lax.all_gather(potential, "row")
     march_rhs = pl.pallas_call(
         functools.partial(final_kernel, norm=norm),

time: 37.8 us -> 59.4 us (1.57)
  blocking collectives: 12.1 us -> 50.2 us
  starting transfers between devices: 11.5 us -> 0 us
  waiting for transfers between devices: 4.97 us -> 0 us
    psum x0 -> x1, blocking collectives: none -> 38.2 us  [per_device(): parts = lax.psum(parts, 'col')]
    ppermute x7 -> x0, starting transfers between devices: 11.5 us -> none  [exchange(): values.append(lax.ppermute(value, axis, pairs))]
    ppermute x7 -> x0, waiting for transfers between devices: 4.97 us -> none  [exchange(): values.append(lax.ppermute(value, axis, pairs))]
  transfers between devices with their start and end apart: 7 -> 0, of which waited for: 2 -> 0; matrix products, arithmetic and copies ran while one was open for 0% -> 0% of each run, Pallas kernels for 4% -> 0%
where the time goes in v6:
time: 59.4 us; the launch traced here: 59.2 us
  blocking collectives  50.2 us (85%)
  Pallas kernels  8.17 us (14%)
  between operations  0.72 us (1%)
    psum x1, blocking collectives, per_device(): parts = lax.psum(parts, 'col')  38.2 us
    all_gather x1, blocking collectives, per_device(): packed = lax.all_gather(packed, 'row', axis=2, tiled=True)  6.69 us
    all_gather x1, blocking collectives, per_device(): shares = lax.all_gather(potential, 'row')  5.36 us
    pallas_call x1, Pallas kernels, per_device(): pl.pallas_call(functools.partial(t_kernel, norm=norm, slots=slots), out_s...  3.11 us
    pallas_call x1, Pallas kernels, per_device(): pl.pallas_call(s_tiles_kernel, out_shape=jax.ShapeDtypeStruct((rows_t, co...  1.66 us
    pallas_call x1, Pallas kernels, per_device(): pl.pallas_call(pack_kernel, out_shape=jax.ShapeDtypeStruct((slots + 2, ex...  1.49 us
    pallas_call x1, Pallas kernels, per_device(): pl.pallas_call(functools.partial(sweep_kernel, slots=slots, part_count=1)...  1.3 us

profile of v6, /device:TPU:0, one launch (start us, length us, event | category | flops | bytes accessed | tf_op | source)
XLA Modules:
  0.0 59.2 jit_solution(10954945530285628457)
XLA Ops:
  0.6 0.0 copy-start.4
  0.6 1.5 %shard_map.113 = bf16[6,16,128]{2,1,0:T(8,128)(2,1)} custom-call(bf16[4,16,128]{2,1,0:T(8,128)(2,1)} %history_ref.1, s32[4,8]{1,0:T(4,128)} %bitcast.7, s32[4,8]{1,0:T(4,128)} %bitcast.9, f32[1,1024]{1,0:T(1,128)} %bitcast.5, f32[4,1024]{1,0:T(4,128)} %refs_3_.1, s32[4,1024]{1,0:T(4,128)} %refs_4_.1), custom_call_target="tpu_custom_call" | custom-call | tf_op jit(solution)/shard_map/pallas_call | solution.py:334
  2.1 0.0 copy-start.3
  2.1 0.0 copy-start.6
  2.1 0.0 copy-start.7
  2.1 6.7 %all_gather.9.packed_ref.refs_1_ = bf16[6,16,512]{2,1,0:T(8,128)(2,1)S(1)} all-gather(bf16[6,16,128]{2,1,0:T(8,128)(2,1)} %shard_map.113), channel_id=1, replica_groups=mesh['row'=4,'col'=8] {'row'}, dimensions={2}, use_global_device_ids=true | all-gather | bytes 122880 | tf_op jit(solution)/shard_map/all_gather | solution.py:341
  8.8 0.0 copy-done.4
  8.8 0.0 copy-done.3
  8.8 0.0 copy-done.6
  8.8 0.0 copy-done.7
  8.8 3.1 %shard_map.114 = bf16[16,1152]{1,0:T(8,128)(2,1)S(1)} custom-call(bf16[6,16,512]{2,1,0:T(8,128)(2,1)S(1)} %all_gather.9.packed_ref.refs_1_, f32[3,4096]{1,0:T(4,128)S(1)} %copy-done.4, f32[4,4096]{1,0:T(4,128)S(1)} %copy-done.3, s32[4,8]{1,0:T(4,128)S(1)} %bitcast.8, s32[4,8]{1,0:T(4,128)S(1)} %bitcast.10), custom_call_target="tpu_custom_call" | custom-call | tf_op jit(solution)/shard_map/pallas_call | solution.py:343
  12.0 38.2 %psum.7.refs_0_ = bf16[16,1152]{1,0:T(8,128)(2,1)S(1)} all-reduce(bf16[16,1152]{1,0:T(8,128)(2,1)S(1)} %shard_map.114), channel_id=1, replica_groups=mesh['row'=4,'col'=8] {'col'}, use_global_device_ids=true, to_apply=%region_0.0 | all-reduce | flops 18432 | bytes 73728 | tf_op jit(solution)/shard_map/psum | solution.py:356
  50.2 0.0 copy-start
  50.2 0.0 copy-start.1
  50.2 0.0 copy-start.2
  50.2 0.0 copy-start.5
  50.2 1.7 %shard_map.115.refs_5_ = bf16[1024,512]{1,0:T(8,128)(2,1)S(1)} custom-call(f32[3,4096]{1,0:T(4,128)S(1)} %copy-done.4), custom_call_target="tpu_custom_call" | custom-call | flops 6291456 | bytes 1048576 | tf_op jit(solution)/shard_map/pallas_call | solution.py:359
  51.9 0.0 copy-done
  51.9 0.0 copy-done.1
  51.9 0.0 copy-done.2
  51.9 0.0 copy-done.5
  51.9 1.3 %shard_map.116 = (f32[16,128]{1,0:T(8,128)}, bf16[4,16,128]{2,1,0:T(8,128)(2,1)S(1)}) custom-call(bf16[16,1152]{1,0:T(8,128)(2,1)S(1)} %psum.7.refs_0_, bf16[6,16,512]{2,1,0:T(8,128)(2,1)S(1)} %all_gather.9.packed_ref.refs_1_, f32[1,1024]{1,0:T(1,128)S(1)} %bitcast.6, f32[4,1024]{1,0:T(4,128)S(1)} %copy-done, s32[4,1024]{1,0:T(4,128)S(1)} %copy-done.1, ...), custom_call_target="tpu_custom_call" | custom-call | tf_op jit(solution)/shard_map/pallas_call | solution.py:369
  53.2 0.0 copy-start.8
  53.2 5.4 %all-gather = bf16[16,16,128]{2,1,0:T(8,128)(2,1)S(1)} all-gather(bf16[4,16,128]{2,1,0:T(8,128)(2,1)S(1)} %get-tuple-element.8), channel_id=2, replica_groups=mesh['row'=4,'col'=8] {'row'}, dimensions={0}, use_global_device_ids=true | all-gather | bytes 81920 | tf_op jit(solution)/shard_map/all_gather | solution.py:383
  58.6 0.0 copy-done.8
  58.6 0.6 %shard_map.117 = f32[16,128]{1,0:T(8,128)} custom-call(bf16[4,4,16,128]{3,2,1,0:T(8,128)(2,1)S(1)} %bitcast.4, f32[16,128]{1,0:T(8,128)S(1)} %copy-done.8), custom_call_target="tpu_custom_call" | custom-call | tf_op jit(solution)/shard_map/pallas_call | solution.py:384
Async XLA Ops:
  0.6 8.2 %copy-start.4 = (f32[3,4096]{1,0:T(4,128)S(1)}, f32[3,4096]{1,0:T(4,128)}, u32[]{:S(2)}) copy-start(f32[3,4096]{1,0:T(4,128)} %centroids_ref.2) | copy-start | bytes 147460
  2.1 6.7 %copy-start.3 = (f32[4,4096]{1,0:T(4,128)S(1)}, f32[4,4096]{1,0:T(4,128)}, u32[]{:S(2)}) copy-start(f32[4,4096]{1,0:T(4,128)} %moments_ref.1) | copy-start | bytes 196612
  2.1 6.7 %copy-start.6 = (s32[8,4]{0,1:T(4,128)S(1)}, s32[8,4]{0,1:T(4,128)}, u32[]{:S(2)}) copy-start(s32[8,4]{0,1:T(4,128)} %param.15) | copy-start | bytes 388
  2.1 6.7 %copy-start.7 = (s32[8,4]{0,1:T(4,128)S(1)}, s32[8,4]{0,1:T(4,128)}, u32[]{:S(2)}) copy-start(s32[8,4]{0,1:T(4,128)} %param.16) | copy-start | bytes 388
  50.2 1.7 %copy-start = (f32[4,1024]{1,0:T(4,128)S(1)}, f32[4,1024]{1,0:T(4,128)}, u32[]{:S(2)}) copy-start(f32[4,1024]{1,0:T(4,128)} %refs_3_.1) | copy-start | bytes 49156
  50.2 1.7 %copy-start.1 = (s32[4,1024]{1,0:T(4,128)S(1)}, s32[4,1024]{1,0:T(4,128)}, u32[]{:S(2)}) copy-start(s32[4,1024]{1,0:T(4,128)} %refs_4_.1) | copy-start | bytes 49156
  50.2 1.7 %copy-start.2 = (f32[3,4096]{1,0:T(4,128)S(1)}, f32[3,4096]{1,0:T(4,128)}, u32[]{:S(2)}) copy-start(f32[3,4096]{1,0:T(4,128)} %refs_6_.1) | copy-start | bytes 147460
  50.2 1.7 %copy-start.5 = (f32[1024]{0:T(1024)S(1)}, f32[1024]{0:T(1024)}, u32[]{:S(2)}) copy-start(f32[1024]{0:T(1024)} %param.18) | copy-start | bytes 12292
  53.2 5.4 %copy-start.8 = (f32[16,128]{1,0:T(8,128)S(1)}, f32[16,128]{1,0:T(8,128)}, u32[]{:S(2)}) copy-start(f32[16,128]{1,0:T(8,128)} %incident_ref.1) | copy-start | bytes 24580

commit v7 on v5

--- a/solution.py
+++ b/solution.py
@@ -311,14 +311,23 @@
     out_ref[...] = incident_ref[...] - total * norm
 
 
+def swap(value, axis, step):
+    count = lax.axis_size(axis)
+    if count & (count - 1) == 0:
+        pairs = [(i, i ^ step) for i in range(count)]
+    else:
+        pairs = [(i, (i + step) % count) for i in range(count)]
+    return lax.ppermute(value, axis, pairs)
+
+
 def exchange(value, axis):
     count = lax.axis_size(axis)
-    pairwise = count & (count - 1) == 0
-    values = [value]
-    for step in range(count - 1, 0, -1):
-        pairs = [(i, i ^ step if pairwise else (i + step) % count) for i in range(count)]
-        values.append(lax.ppermute(value, axis, pairs))
-    return values
+    stride = 1
+    if count > 2 and count & (count - 1) == 0:
+        other = swap(value, axis, 1)
+        value = (value.astype(jnp.float32) + other.astype(jnp.float32)).astype(value.dtype)
+        stride = 2
+    return [value] + [swap(value, axis, step) for step in range(count - stride, 0, -stride)]
 
 
 def per_device(
@@ -378,12 +387,12 @@
     )(late_centroids)
 
     own_dual, potential = pl.pallas_call(
-        functools.partial(sweep_kernel, slots=slots, part_count=col_devices),
+        functools.partial(sweep_kernel, slots=slots, part_count=len(parts)),
         out_shape=(
             jax.ShapeDtypeStruct((excitations, shard_len), jnp.float32),
             jax.ShapeDtypeStruct((q_tiles, excitations, LANES), jnp.bfloat16),
         ),
-        in_specs=[VMEM] * (col_devices + 6),
+        in_specs=[VMEM] * (len(parts) + 6),
         out_specs=(VMEM, VMEM),
         scratch_shapes=[
             pltpu.VMEM((p_tiles, excitations, LANES), jnp.float32),

time: 37.8 us -> 34.1 us (0.902)
  starting transfers between devices: 11.5 us -> 6.73 us
  waiting for transfers between devices: 4.97 us -> 6.08 us
    ppermute x7 -> x4, starting transfers between devices: 11.5 us -> 6.73 us  [swap(): return lax.ppermute(value, axis, pairs)]
    ppermute x7 -> x4, waiting for transfers between devices: 4.97 us -> 6.08 us  [swap(): return lax.ppermute(value, axis, pairs)]
  transfers between devices with their start and end apart: 7 -> 4, of which waited for: 2 -> 3; matrix products, arithmetic and copies ran while one was open for 0% -> 0% of each run, Pallas kernels for 4% -> 5%
where the time goes in v7:
time: 34.1 us; the launch traced here: 33.8 us
  blocking collectives  12.1 us (35%)
  Pallas kernels  8.17 us (24%)
  starting transfers between devices  6.73 us (20%)
  waiting for transfers between devices  6.08 us (18%)
  between operations  0.73 us (2%)
    ppermute x4, starting transfers between devices, swap(): return lax.ppermute(value, axis, pairs)  6.73 us
    all_gather x1, blocking collectives, per_device(): packed = lax.all_gather(packed, 'row', axis=2, tiled=True)  6.69 us
    ppermute x4, waiting for transfers between devices, swap(): return lax.ppermute(value, axis, pairs)  6.08 us
    all_gather x1, blocking collectives, per_device(): shares = lax.all_gather(potential, 'row')  5.36 us
    pallas_call x1, Pallas kernels, per_device(): pl.pallas_call(functools.partial(t_kernel, norm=norm, slots=slots), out_s...  3.11 us
    pallas_call x1, Pallas kernels, per_device(): pl.pallas_call(s_tiles_kernel, out_shape=jax.ShapeDtypeStruct((rows_t, co...  1.64 us
    pallas_call x1, Pallas kernels, per_device(): pl.pallas_call(pack_kernel, out_shape=jax.ShapeDtypeStruct((slots + 2, ex...  1.5 us
    pallas_call x1, Pallas kernels, per_device(): pl.pallas_call(functools.partial(sweep_kernel, slots=slots, part_count=le...  1.31 us
  transfers between devices with their start and end apart: 4, of which 3 were waited for; matrix products, arithmetic and copies ran while one was open for 0% of the time, Pallas kernels for 5%

profile of v7, /device:TPU:0, one launch (start us, length us, event | category | flops | bytes accessed | tf_op | source)
XLA Modules:
  0.0 33.8 jit_solution(7220796702328740709)
XLA Ops:
  0.6 0.0 copy-start.4
  0.6 1.5 %shard_map.113 = bf16[6,16,128]{2,1,0:T(8,128)(2,1)} custom-call(bf16[4,16,128]{2,1,0:T(8,128)(2,1)} %history_ref.1, s32[4,8]{1,0:T(4,128)} %bitcast.7, s32[4,8]{1,0:T(4,128)} %bitcast.9, f32[1,1024]{1,0:T(1,128)} %bitcast.5, f32[4,1024]{1,0:T(4,128)} %refs_6_.1, s32[4,1024]{1,0:T(4,128)} %refs_7_.1), custom_call_target="tpu_custom_call" | custom-call | tf_op jit(solution)/shard_map/pallas_call | solution.py:354
  2.1 0.0 copy-start.3
  2.1 0.0 copy-start.6
  2.1 0.0 copy-start.7
  2.1 6.7 %all_gather.9.packed_ref.refs_4_ = bf16[6,16,512]{2,1,0:T(8,128)(2,1)S(1)} all-gather(bf16[6,16,128]{2,1,0:T(8,128)(2,1)} %shard_map.113), channel_id=1, replica_groups=mesh['row'=4,'col'=8] {'row'}, dimensions={2}, use_global_device_ids=true | all-gather | bytes 122880 | tf_op jit(solution)/shard_map/all_gather | solution.py:361
  8.8 0.0 copy-done.4
  8.8 0.0 copy-done.3
  8.8 0.0 copy-done.6
  8.8 0.0 copy-done.7
  8.9 3.1 %shard_map.114 = bf16[16,1152]{1,0:T(8,128)(2,1)S(1)} custom-call(bf16[6,16,512]{2,1,0:T(8,128)(2,1)S(1)} %all_gather.9.packed_ref.refs_4_, f32[3,4096]{1,0:T(4,128)S(1)} %copy-done.4, f32[4,4096]{1,0:T(4,128)S(1)} %copy-done.3, s32[4,8]{1,0:T(4,128)S(1)} %bitcast.8, s32[4,8]{1,0:T(4,128)S(1)} %bitcast.10), custom_call_target="tpu_custom_call" | custom-call | tf_op jit(solution)/shard_map/pallas_call | solution.py:363
  12.0 2.0 %collective-permute-start = (bf16[16,1152]{1,0:T(8,128)(2,1)S(1)}, bf16[16,1152]{1,0:T(8,128)(2,1)S(1)}, u32[]{:S(2)}, u32[]{:S(2)}) collective-permute-start(bf16[16,1152]{1,0:T(8,128)(2,1)S(1)} %shard_map.114), channel_id=1, source_target_pairs={{0,1},{1,0},{2,3},{3,2},{4,5},{5,4},{6,7},{7,6},{8,9},{9,8},{10,11... | collective-permute-start | bytes 110600 | tf_op jit(solution)/shard_map/ppermute | solution.py:320
  14.0 2.0 %collective-permute-done = bf16[16,1152]{1,0:T(8,128)(2,1)S(1)} collective-permute-done((bf16[16,1152]{1,0:T(8,128)(2,1)S(1)}, bf16[16,1152]{1,0:T(8,128)(2,1)S(1)}, u32[]{:S(2)}, u32[]{:S(2)}) %collective-permute-start) | collective-permute-done | bytes 36896 | tf_op jit(solution)/shard_map/ppermute | solution.py:320
  16.0 0.0 copy-start
  16.0 0.0 copy-start.1
  16.0 0.0 copy-start.2
  16.1 0.0 copy-start.5
  16.1 2.1 %collective-permute-start.3 = (bf16[16,1152]{1,0:T(8,128)(2,1)S(1)}, bf16[16,1152]{1,0:T(8,128)(2,1)S(1)}, u32[]{:S(2)}, u32[]{:S(2)}) collective-permute-start(bf16[16,1152]{1,0:T(8,128)(2,1)S(1)} %add_convert_fusion.refs_0_), channel_id=1, source_target_pairs={{0,2},{1,3},{2,0},{3,1},{4,6},{5,7},{6,4},{7,5},{8,10},{9,11},{10,... | collective-permute-start | bytes 110600 | tf_op jit(solution)/shard_map/ppermute | solution.py:320
  18.2 2.6 %collective-permute-start.2 = (bf16[16,1152]{1,0:T(8,128)(2,1)S(1)}, bf16[16,1152]{1,0:T(8,128)(2,1)S(1)}, u32[]{:S(2)}, u32[]{:S(2)}) collective-permute-start(bf16[16,1152]{1,0:T(8,128)(2,1)S(1)} %add_convert_fusion.refs_0_), channel_id=1, source_target_pairs={{0,4},{1,5},{2,6},{3,7},{4,0},{5,1},{6,2},{7,3},{8,12},{9,13},{10,... | collective-permute-start | bytes 110600 | tf_op jit(solution)/shard_map/ppermute | solution.py:320
  20.8 0.0 collective-permute-start.1
  20.8 1.6 %shard_map.115.refs_8_ = bf16[1024,512]{1,0:T(8,128)(2,1)S(1)} custom-call(f32[3,4096]{1,0:T(4,128)S(1)} %copy-done.4), custom_call_target="tpu_custom_call" | custom-call | flops 6291456 | bytes 1048576 | tf_op jit(solution)/shard_map/pallas_call | solution.py:379
  22.4 0.0 collective-permute-done.3.refs_3_
  22.4 0.9 %collective-permute-done.2.refs_2_ = bf16[16,1152]{1,0:T(8,128)(2,1)S(1)} collective-permute-done((bf16[16,1152]{1,0:T(8,128)(2,1)S(1)}, bf16[16,1152]{1,0:T(8,128)(2,1)S(1)}, u32[]{:S(2)}, u32[]{:S(2)}) %collective-permute-start.2) | collective-permute-done | bytes 36896 | tf_op jit(solution)/shard_map/ppermute | solution.py:320
  23.4 3.1 %collective-permute-done.1.refs_1_ = bf16[16,1152]{1,0:T(8,128)(2,1)S(1)} collective-permute-done((bf16[16,1152]{1,0:T(8,128)(2,1)S(1)}, bf16[16,1152]{1,0:T(8,128)(2,1)S(1)}, u32[]{:S(2)}, u32[]{:S(2)}) %collective-permute-start.1) | collective-permute-done | bytes 36896 | tf_op jit(solution)/shard_map/ppermute | solution.py:320
  26.5 0.0 copy-done
  26.5 0.0 copy-done.1
  26.5 0.0 copy-done.2
  26.5 0.0 copy-done.5
  26.5 1.3 %shard_map.116 = (f32[16,128]{1,0:T(8,128)}, bf16[4,16,128]{2,1,0:T(8,128)(2,1)S(1)}) custom-call(bf16[16,1152]{1,0:T(8,128)(2,1)S(1)} %add_convert_fusion.refs_0_, bf16[16,1152]{1,0:T(8,128)(2,1)S(1)} %collective-permute-done.1.refs_1_, bf16[16,1152]{1,0:T(8,128)(2,1)S(1)} %collective-permute-done.2.refs_2_, ...), custom_call_target="tpu_custom_call" | custom-call | tf_op jit(solution)/shard_map/pallas_call | solution.py:389
  27.8 0.0 copy-start.8
  27.8 5.4 %all-gather = bf16[16,16,128]{2,1,0:T(8,128)(2,1)S(1)} all-gather(bf16[4,16,128]{2,1,0:T(8,128)(2,1)S(1)} %get-tuple-element.8), channel_id=2, replica_groups=mesh['row'=4,'col'=8] {'row'}, dimensions={0}, use_global_device_ids=true | all-gather | bytes 81920 | tf_op jit(solution)/shard_map/all_gather | solution.py:403
  33.2 0.0 copy-done.8
  33.2 0.6 %shard_map.117 = f32[16,128]{1,0:T(8,128)} custom-call(bf16[4,4,16,128]{3,2,1,0:T(8,128)(2,1)S(1)} %bitcast.4, f32[16,128]{1,0:T(8,128)S(1)} %copy-done.8), custom_call_target="tpu_custom_call" | custom-call | tf_op jit(solution)/shard_map/pallas_call | solution.py:404
  (1 shorter events, 0.0 us)
Async XLA Ops:
  0.6 8.2 %copy-start.4 = (f32[3,4096]{1,0:T(4,128)S(1)}, f32[3,4096]{1,0:T(4,128)}, u32[]{:S(2)}) copy-start(f32[3,4096]{1,0:T(4,128)} %centroids_ref.2) | copy-start | bytes 147460
  2.1 6.7 %copy-start.3 = (f32[4,4096]{1,0:T(4,128)S(1)}, f32[4,4096]{1,0:T(4,128)}, u32[]{:S(2)}) copy-start(f32[4,4096]{1,0:T(4,128)} %moments_ref.1) | copy-start | bytes 196612
  2.1 6.7 %copy-start.6 = (s32[8,4]{0,1:T(4,128)S(1)}, s32[8,4]{0,1:T(4,128)}, u32[]{:S(2)}) copy-start(s32[8,4]{0,1:T(4,128)} %param.15) | copy-start | bytes 388
  2.1 6.7 %copy-start.7 = (s32[8,4]{0,1:T(4,128)S(1)}, s32[8,4]{0,1:T(4,128)}, u32[]{:S(2)}) copy-start(s32[8,4]{0,1:T(4,128)} %param.16) | copy-start | bytes 388
  12.0 4.0 %collective-permute-start = (bf16[16,1152]{1,0:T(8,128)(2,1)S(1)}, bf16[16,1152]{1,0:T(8,128)(2,1)S(1)}, u32[]{:S(2)}, u32[]{:S(2)}) collective-permute-start(bf16[16,1152]{1,0:T(8,128)(2,1)S(1)} %shard_map.114), channel_id=1, source_target_pairs={{0,1},{1,0},{2,3},{3,2},{4,5},{5,4},{6,7},{7,6},{8,9},{9,8},{10,11... | collective-permute-start | bytes 110600 | tf_op jit(solution)/shard_map/ppermute | solution.py:320
  16.0 10.5 %copy-start = (f32[4,1024]{1,0:T(4,128)S(1)}, f32[4,1024]{1,0:T(4,128)}, u32[]{:S(2)}) copy-start(f32[4,1024]{1,0:T(4,128)} %refs_6_.1) | copy-start | bytes 49156
  16.0 10.5 %copy-start.1 = (s32[4,1024]{1,0:T(4,128)S(1)}, s32[4,1024]{1,0:T(4,128)}, u32[]{:S(2)}) copy-start(s32[4,1024]{1,0:T(4,128)} %refs_7_.1) | copy-start | bytes 49156
  16.0 10.5 %copy-start.2 = (f32[3,4096]{1,0:T(4,128)S(1)}, f32[3,4096]{1,0:T(4,128)}, u32[]{:S(2)}) copy-start(f32[3,4096]{1,0:T(4,128)} %refs_9_.1) | copy-start | bytes 147460
  16.1 10.5 %copy-start.5 = (f32[1024]{0:T(1024)S(1)}, f32[1024]{0:T(1024)}, u32[]{:S(2)}) copy-start(f32[1024]{0:T(1024)} %param.18) | copy-start | bytes 12292
  16.1 6.3 %collective-permute-start.3 = (bf16[16,1152]{1,0:T(8,128)(2,1)S(1)}, bf16[16,1152]{1,0:T(8,128)(2,1)S(1)}, u32[]{:S(2)}, u32[]{:S(2)}) collective-permute-start(bf16[16,1152]{1,0:T(8,128)(2,1)S(1)} %add_convert_fusion.refs_0_), channel_id=1, source_target_pairs={{0,2},{1,3},{2,0},{3,1},{4,6},{5,7},{6,4},{7,5},{8,10},{9,11},{10,... | collective-permute-start | bytes 110600 | tf_op jit(solution)/shard_map/ppermute | solution.py:320
  18.2 5.2 %collective-permute-start.2 = (bf16[16,1152]{1,0:T(8,128)(2,1)S(1)}, bf16[16,1152]{1,0:T(8,128)(2,1)S(1)}, u32[]{:S(2)}, u32[]{:S(2)}) collective-permute-start(bf16[16,1152]{1,0:T(8,128)(2,1)S(1)} %add_convert_fusion.refs_0_), channel_id=1, source_target_pairs={{0,4},{1,5},{2,6},{3,7},{4,0},{5,1},{6,2},{7,3},{8,12},{9,13},{10,... | collective-permute-start | bytes 110600 | tf_op jit(solution)/shard_map/ppermute | solution.py:320
  20.8 5.8 %collective-permute-start.1 = (bf16[16,1152]{1,0:T(8,128)(2,1)S(1)}, bf16[16,1152]{1,0:T(8,128)(2,1)S(1)}, u32[]{:S(2)}, u32[]{:S(2)}) collective-permute-start(bf16[16,1152]{1,0:T(8,128)(2,1)S(1)} %add_convert_fusion.refs_0_), channel_id=1, source_target_pairs={{0,6},{1,7},{2,4},{3,5},{4,2},{5,3},{6,0},{7,1},{8,14},{9,15},{10,... | collective-permute-start | bytes 110600 | tf_op jit(solution)/shard_map/ppermute | solution.py:320
  27.8 5.4 %copy-start.8 = (f32[16,128]{1,0:T(8,128)S(1)}, f32[16,128]{1,0:T(8,128)}, u32[]{:S(2)}) copy-start(f32[16,128]{1,0:T(8,128)} %incident_ref.1) | copy-start | bytes 24580

commit v8 on v7

--- a/solution.py
+++ b/solution.py
@@ -322,12 +322,14 @@
 
 def exchange(value, axis):
     count = lax.axis_size(axis)
-    stride = 1
-    if count > 2 and count & (count - 1) == 0:
-        other = swap(value, axis, 1)
+    if count & (count - 1):
+        return [value] + [swap(value, axis, step) for step in range(1, count)]
+    step = 1
+    while 2 * step < count:
+        other = swap(value, axis, step)
         value = (value.astype(jnp.float32) + other.astype(jnp.float32)).astype(value.dtype)
-        stride = 2
-    return [value] + [swap(value, axis, step) for step in range(count - stride, 0, -stride)]
+        step *= 2
+    return [value, swap(value, axis, step)] if count > 1 else [value]
 
 
 def per_device(
@@ -372,8 +374,8 @@
         ],
         compiler_params=grant((excitations, rows_t), (slots + 2, moments.shape[0] * excitations, cols_t), (5, cols_t, LANES), moments.shape, centroids.shape),
     )(packed, centroids, moments, shell, near_mask)
-    parts, late_centroids = lax.optimization_barrier((parts, centroids))
     parts = exchange(parts, "col")
+    last_share, late_centroids = lax.optimization_barrier((parts[0], centroids))
 
     entries = rows_t * cols_t
     s_tiles = pl.pallas_call(
@@ -399,7 +401,7 @@
             pltpu.VMEM((dual_moments.shape[0] * excitations, rows_t), jnp.bfloat16),
         ],
         compiler_params=grant((col_devices, excitations, rows_t), (rows_t, cols_t // 2), (excitations, 8 * rows_t)),
-    )(*parts, packed, gram_diag, gram_off, neighbours, s_tiles, dual_moments)
+    )(last_share, *parts[1:], packed, gram_diag, gram_off, neighbours, s_tiles, dual_moments)
     shares = lax.all_gather(potential, "row")
     march_rhs = pl.pallas_call(
         functools.partial(final_kernel, norm=norm),

time: 34.1 us -> 32.7 us (0.959)
  waiting for transfers between devices: 6.08 us -> 4.21 us
  starting transfers between devices: 6.73 us -> 7.24 us
    ppermute x4 -> x3, waiting for transfers between devices: 6.08 us -> 4.21 us  [swap(): return lax.ppermute(value, axis, pairs)]
    ppermute x4 -> x3, starting transfers between devices: 6.73 us -> 7.24 us  [swap(): return lax.ppermute(value, axis, pairs)]
  transfers between devices with their start and end apart: 4 -> 3, of which waited for: 3 -> 3; matrix products, arithmetic and copies ran while one was open for 0% -> 0% of each run, Pallas kernels for 5% -> 5%
where the time goes in v8:
time: 32.7 us; the launch traced here: 32.5 us
  blocking collectives  12.1 us (37%)
  Pallas kernels  8.16 us (25%)
  starting transfers between devices  7.24 us (22%)
  waiting for transfers between devices  4.21 us (13%)
  between operations  0.72 us (2%)
    ppermute x3, starting transfers between devices, swap(): return lax.ppermute(value, axis, pairs)  7.24 us
    all_gather x1, blocking collectives, per_device(): packed = lax.all_gather(packed, 'row', axis=2, tiled=True)  6.69 us
    all_gather x1, blocking collectives, per_device(): shares = lax.all_gather(potential, 'row')  5.36 us
    ppermute x3, waiting for transfers between devices, swap(): return lax.ppermute(value, axis, pairs)  4.21 us
    pallas_call x1, Pallas kernels, per_device(): pl.pallas_call(functools.partial(t_kernel, norm=norm, slots=slots), out_s...  3.11 us
    pallas_call x1, Pallas kernels, per_device(): pl.pallas_call(s_tiles_kernel, out_shape=jax.ShapeDtypeStruct((rows_t, co...  1.64 us
    pallas_call x1, Pallas kernels, per_device(): pl.pallas_call(pack_kernel, out_shape=jax.ShapeDtypeStruct((slots + 2, ex...  1.49 us
    pallas_call x1, Pallas kernels, per_device(): pl.pallas_call(functools.partial(sweep_kernel, slots=slots, part_count=le...  1.31 us
  transfers between devices with their start and end apart: 3, of which 3 were waited for; matrix products, arithmetic and copies ran while one was open for 0% of the time, Pallas kernels for 5%

profile of v8, /device:TPU:0, one launch (start us, length us, event | category | flops | bytes accessed | tf_op | source)
XLA Modules:
  0.0 32.5 jit_solution(14356454217528085735)
XLA Ops:
  0.6 0.0 copy-start.4
  0.6 1.5 %shard_map.113 = bf16[6,16,128]{2,1,0:T(8,128)(2,1)} custom-call(bf16[4,16,128]{2,1,0:T(8,128)(2,1)} %history_ref.1, s32[4,8]{1,0:T(4,128)} %bitcast.7, s32[4,8]{1,0:T(4,128)} %bitcast.9, f32[1,1024]{1,0:T(1,128)} %bitcast.5, f32[4,1024]{1,0:T(4,128)} %refs_4_.1, s32[4,1024]{1,0:T(4,128)} %refs_5_.1), custom_call_target="tpu_custom_call" | custom-call | tf_op jit(solution)/shard_map/pallas_call | solution.py:356
  2.1 0.0 copy-start.3
  2.1 0.0 copy-start.6
  2.1 0.0 copy-start.7
  2.1 6.7 %all_gather.9.packed_ref.refs_2_ = bf16[6,16,512]{2,1,0:T(8,128)(2,1)S(1)} all-gather(bf16[6,16,128]{2,1,0:T(8,128)(2,1)} %shard_map.113), channel_id=1, replica_groups=mesh['row'=4,'col'=8] {'row'}, dimensions={2}, use_global_device_ids=true | all-gather | bytes 122880 | tf_op jit(solution)/shard_map/all_gather | solution.py:363
  8.8 0.0 copy-done.4
  8.8 0.0 copy-done.3
  8.8 0.0 copy-done.6
  8.8 0.0 copy-done.7
  8.8 3.1 %shard_map.114 = bf16[16,1152]{1,0:T(8,128)(2,1)S(1)} custom-call(bf16[6,16,512]{2,1,0:T(8,128)(2,1)S(1)} %all_gather.9.packed_ref.refs_2_, f32[3,4096]{1,0:T(4,128)S(1)} %copy-done.4, f32[4,4096]{1,0:T(4,128)S(1)} %copy-done.3, s32[4,8]{1,0:T(4,128)S(1)} %bitcast.8, s32[4,8]{1,0:T(4,128)S(1)} %bitcast.10), custom_call_target="tpu_custom_call" | custom-call | tf_op jit(solution)/shard_map/pallas_call | solution.py:365
  12.0 2.0 %collective-permute-start = (bf16[16,1152]{1,0:T(8,128)(2,1)S(1)}, bf16[16,1152]{1,0:T(8,128)(2,1)S(1)}, u32[]{:S(2)}, u32[]{:S(2)}) collective-permute-start(bf16[16,1152]{1,0:T(8,128)(2,1)S(1)} %shard_map.114), channel_id=1, source_target_pairs={{0,1},{1,0},{2,3},{3,2},{4,5},{5,4},{6,7},{7,6},{8,9},{9,8},{10,11... | collective-permute-start | bytes 110600 | tf_op jit(solution)/shard_map/ppermute | solution.py:320
  14.0 2.0 %collective-permute-done = bf16[16,1152]{1,0:T(8,128)(2,1)S(1)} collective-permute-done((bf16[16,1152]{1,0:T(8,128)(2,1)S(1)}, bf16[16,1152]{1,0:T(8,128)(2,1)S(1)}, u32[]{:S(2)}, u32[]{:S(2)}) %collective-permute-start) | collective-permute-done | bytes 36896 | tf_op jit(solution)/shard_map/ppermute | solution.py:320
  16.0 2.1 %collective-permute-start.1 = (bf16[16,1152]{1,0:T(8,128)(2,1)S(1)}, bf16[16,1152]{1,0:T(8,128)(2,1)S(1)}, u32[]{:S(2)}, u32[]{:S(2)}) collective-permute-start(bf16[16,1152]{1,0:T(8,128)(2,1)S(1)} %add_convert_fusion.1), channel_id=1, source_target_pairs={{0,2},{1,3},{2,0},{3,1},{4,6},{5,7},{6,4},{7,5},{8,10},{9,11},{10,... | collective-permute-start | bytes 110600 | tf_op jit(solution)/shard_map/ppermute | solution.py:320
  18.1 1.9 %collective-permute-done.1 = bf16[16,1152]{1,0:T(8,128)(2,1)S(1)} collective-permute-done((bf16[16,1152]{1,0:T(8,128)(2,1)S(1)}, bf16[16,1152]{1,0:T(8,128)(2,1)S(1)}, u32[]{:S(2)}, u32[]{:S(2)}) %collective-permute-start.1) | collective-permute-done | bytes 36896 | tf_op jit(solution)/shard_map/ppermute | solution.py:320
  20.1 0.0 copy-start
  20.1 0.0 copy-start.1
  20.1 0.0 copy-start.2
  20.1 0.0 copy-start.5
  20.1 3.1 %collective-permute-start.2 = (bf16[16,1152]{1,0:T(8,128)(2,1)S(1)}, bf16[16,1152]{1,0:T(8,128)(2,1)S(1)}, u32[]{:S(2)}, u32[]{:S(2)}) collective-permute-start(bf16[16,1152]{1,0:T(8,128)(2,1)S(1)} %add_convert_fusion.refs_0_), channel_id=1, source_target_pairs={{0,4},{1,5},{2,6},{3,7},{4,0},{5,1},{6,2},{7,3},{8,12},{9,13},{10,... | collective-permute-start | bytes 110600 | tf_op jit(solution)/shard_map/ppermute | solution.py:320
  23.2 1.6 %shard_map.115.refs_6_ = bf16[1024,512]{1,0:T(8,128)(2,1)S(1)} custom-call(f32[3,4096]{1,0:T(4,128)S(1)} %copy-done.4), custom_call_target="tpu_custom_call" | custom-call | flops 6291456 | bytes 1048576 | tf_op jit(solution)/shard_map/pallas_call | solution.py:381
  24.9 0.3 collective-permute-done.2.refs_1_
  25.2 0.0 copy-done
  25.2 0.0 copy-done.1
  25.2 0.0 copy-done.2
  25.2 0.0 copy-done.5
  25.2 1.3 %shard_map.116 = (f32[16,128]{1,0:T(8,128)}, bf16[4,16,128]{2,1,0:T(8,128)(2,1)S(1)}) custom-call(bf16[16,1152]{1,0:T(8,128)(2,1)S(1)} %add_convert_fusion.refs_0_, bf16[16,1152]{1,0:T(8,128)(2,1)S(1)} %collective-permute-done.2.refs_1_, bf16[6,16,512]{2,1,0:T(8,128)(2,1)S(1)} %all_gather.9.packed_ref.refs_2_, f32[1,1024]{1,0:T(1,128)S(1)} %bitcast.6, ...), custom_call_target="tpu_custom_call" | custom-call | tf_op jit(solution)/shard_map/pallas_call | solution.py:391
  26.5 0.0 copy-start.8
  26.5 5.4 %all-gather = bf16[16,16,128]{2,1,0:T(8,128)(2,1)S(1)} all-gather(bf16[4,16,128]{2,1,0:T(8,128)(2,1)S(1)} %get-tuple-element.8), channel_id=2, replica_groups=mesh['row'=4,'col'=8] {'row'}, dimensions={0}, use_global_device_ids=true | all-gather | bytes 81920 | tf_op jit(solution)/shard_map/all_gather | solution.py:405
  31.8 0.0 copy-done.8
  31.8 0.6 %shard_map.117 = f32[16,128]{1,0:T(8,128)} custom-call(bf16[4,4,16,128]{3,2,1,0:T(8,128)(2,1)S(1)} %bitcast.4, f32[16,128]{1,0:T(8,128)S(1)} %copy-done.8), custom_call_target="tpu_custom_call" | custom-call | tf_op jit(solution)/shard_map/pallas_call | solution.py:406
  (2 shorter events, 0.0 us)
Async XLA Ops:
  0.6 8.2 %copy-start.4 = (f32[3,4096]{1,0:T(4,128)S(1)}, f32[3,4096]{1,0:T(4,128)}, u32[]{:S(2)}) copy-start(f32[3,4096]{1,0:T(4,128)} %centroids_ref.2) | copy-start | bytes 147460
  2.1 6.7 %copy-start.3 = (f32[4,4096]{1,0:T(4,128)S(1)}, f32[4,4096]{1,0:T(4,128)}, u32[]{:S(2)}) copy-start(f32[4,4096]{1,0:T(4,128)} %moments_ref.1) | copy-start | bytes 196612
  2.1 6.7 %copy-start.6 = (s32[8,4]{0,1:T(4,128)S(1)}, s32[8,4]{0,1:T(4,128)}, u32[]{:S(2)}) copy-start(s32[8,4]{0,1:T(4,128)} %param.15) | copy-start | bytes 388
  2.1 6.7 %copy-start.7 = (s32[8,4]{0,1:T(4,128)S(1)}, s32[8,4]{0,1:T(4,128)}, u32[]{:S(2)}) copy-start(s32[8,4]{0,1:T(4,128)} %param.16) | copy-start | bytes 388
  12.0 4.0 %collective-permute-start = (bf16[16,1152]{1,0:T(8,128)(2,1)S(1)}, bf16[16,1152]{1,0:T(8,128)(2,1)S(1)}, u32[]{:S(2)}, u32[]{:S(2)}) collective-permute-start(bf16[16,1152]{1,0:T(8,128)(2,1)S(1)} %shard_map.114), channel_id=1, source_target_pairs={{0,1},{1,0},{2,3},{3,2},{4,5},{5,4},{6,7},{7,6},{8,9},{9,8},{10,11... | collective-permute-start | bytes 110600 | tf_op jit(solution)/shard_map/ppermute | solution.py:320
  16.0 4.0 %collective-permute-start.1 = (bf16[16,1152]{1,0:T(8,128)(2,1)S(1)}, bf16[16,1152]{1,0:T(8,128)(2,1)S(1)}, u32[]{:S(2)}, u32[]{:S(2)}) collective-permute-start(bf16[16,1152]{1,0:T(8,128)(2,1)S(1)} %add_convert_fusion.1), channel_id=1, source_target_pairs={{0,2},{1,3},{2,0},{3,1},{4,6},{5,7},{6,4},{7,5},{8,10},{9,11},{10,... | collective-permute-start | bytes 110600 | tf_op jit(solution)/shard_map/ppermute | solution.py:320
  20.1 5.1 %copy-start = (f32[4,1024]{1,0:T(4,128)S(1)}, f32[4,1024]{1,0:T(4,128)}, u32[]{:S(2)}) copy-start(f32[4,1024]{1,0:T(4,128)} %refs_4_.1) | copy-start | bytes 49156
  20.1 5.1 %copy-start.1 = (s32[4,1024]{1,0:T(4,128)S(1)}, s32[4,1024]{1,0:T(4,128)}, u32[]{:S(2)}) copy-start(s32[4,1024]{1,0:T(4,128)} %refs_5_.1) | copy-start | bytes 49156
  20.1 5.1 %copy-start.2 = (f32[3,4096]{1,0:T(4,128)S(1)}, f32[3,4096]{1,0:T(4,128)}, u32[]{:S(2)}) copy-start(f32[3,4096]{1,0:T(4,128)} %refs_7_.1) | copy-start | bytes 147460
  20.1 5.1 %copy-start.5 = (f32[1024]{0:T(1024)S(1)}, f32[1024]{0:T(1024)}, u32[]{:S(2)}) copy-start(f32[1024]{0:T(1024)} %param.18) | copy-start | bytes 12292
  20.1 5.0 %collective-permute-start.2 = (bf16[16,1152]{1,0:T(8,128)(2,1)S(1)}, bf16[16,1152]{1,0:T(8,128)(2,1)S(1)}, u32[]{:S(2)}, u32[]{:S(2)}) collective-permute-start(bf16[16,1152]{1,0:T(8,128)(2,1)S(1)} %add_convert_fusion.refs_0_), channel_id=1, source_target_pairs={{0,4},{1,5},{2,6},{3,7},{4,0},{5,1},{6,2},{7,3},{8,12},{9,13},{10,... | collective-permute-start | bytes 110600 | tf_op jit(solution)/shard_map/ppermute | solution.py:320
  26.5 5.4 %copy-start.8 = (f32[16,128]{1,0:T(8,128)S(1)}, f32[16,128]{1,0:T(8,128)}, u32[]{:S(2)}) copy-start(f32[16,128]{1,0:T(8,128)} %incident_ref.1) | copy-start | bytes 24580

commit v9 on v8

v9 whole, which is shorter than its diff:
```python
import functools
import math

import jax
import jax.numpy as jnp
from jax import lax
from jax.experimental import pallas as pl
from jax.experimental.pallas import tpu as pltpu
from jax.sharding import PartitionSpec as P

SWEEPS = 2

SOFT_T = 0.05
SOFT_S = 0.1
NEAR_GAIN = 2.0
NEAR_REACH = 0.5

LANES = 128
HALF = LANES // 2
CHUNK = 64

VMEM = pl.BlockSpec(memory_space=pltpu.VMEM)
SMEM = pl.BlockSpec(memory_space=pltpu.SMEM)
LOG2_E = 1.4426950408889634
TINY = 1e-30
MIB = 1024 * 1024


def grant(*shapes):
    total = 0
    for shape in shapes:
        size = 4
        for extent in shape[:-2] + (-(-shape[-2] // 8) * 8, shape[-1]):
            size *= extent
        total += size
    return pltpu.CompilerParams(vmem_limit_bytes=min(56 * MIB, 2 * total + 2 * MIB))


def root(square):
    square = jnp.maximum(square, TINY)
    return square * lax.rsqrt(square)


def inverse(value):
    return pl.reciprocal(value, approx=True)


def lane_ids(rows=1):
    return lax.broadcasted_iota(jnp.int32, (rows, LANES), 1)


def tile_at(start):
    return pl.ds(pl.multiple_of(start, LANES), LANES)


def edges(ref, row, length):
    first = ref[row : row + 1, :LANES]
    last = ref[row : row + 1, length - LANES :]
    return jnp.where(lane_ids() < HALF, first, last)


def split3(value):
    high = value.astype(jnp.bfloat16).astype(jnp.float32)
    rest = value - high
    middle = rest.astype(jnp.bfloat16).astype(jnp.float32)
    return [high, middle, rest - middle]


def stack_rows(rows, height):
    row_ids = lax.broadcasted_iota(jnp.int32, (height, LANES), 0)
    out = jnp.zeros((height, LANES), jnp.float32)
    for position, row in enumerate(rows):
        out = jnp.where(row_ids == position, row, out)
    return out


def pack_kernel(history_ref, shell_ref, near_ref, diag_ref, off_ref, links_ref, out_ref):
    slots, excitations = history_ref.shape[:2]
    length = diag_ref.shape[1]
    tiles = shell_ref.shape[1]
    lanes = lane_ids()
    rows = []
    for tile in (0, tiles - 1):
        code = jnp.zeros((1, LANES), jnp.float32)
        for j in range(shell_ref.shape[0]):
            value = (shell_ref[j, tile] + slots * near_ref[j, tile]).astype(jnp.float32)
            code = jnp.where(lanes == j, value, code)
        rows.append(code)
    here = lax.axis_index("row") * length + jnp.where(lanes < HALF, lanes, length - LANES + lanes)
    for m in range(links_ref.shape[0]):
        rows.append((edges(links_ref, m, length) - here).astype(jnp.float32))
    rows += split3(edges(diag_ref, 0, length))
    coupling = []
    for m in range(off_ref.shape[0]):
        coupling += split3(edges(off_ref, m, length))
    out_ref[:slots] = history_ref[...]
    out_ref[slots] = stack_rows(rows, excitations).astype(jnp.bfloat16)
    out_ref[slots + 1] = stack_rows(coupling, excitations).astype(jnp.bfloat16)


def target_of(me, step, count):
    return me ^ step if count & (count - 1) == 0 else lax.rem(me + step, count)


def source_of(me, step, count):
    return me ^ step if count & (count - 1) == 0 else lax.rem(me + count - step, count)


def step_from(me, source, count):
    return me ^ source if count & (count - 1) == 0 else lax.rem(me + count - source, count)


def entries_t(line, column, gains):
    dx, dy, dz = [line[axis] - column[axis] for axis in range(3)]
    spacing = root(dx * dx + dy * dy + dz * dz)
    far, near = inverse(spacing + SOFT_T), jnp.exp2(spacing * (-LOG2_E / NEAR_REACH))
    return [(far + gain * near).astype(jnp.bfloat16) if gain is not None else far.astype(jnp.bfloat16) for gain in gains]


def column_coords(centroids_ref, start, store):
    for axis in range(3):
        line = centroids_ref[axis : axis + 1, tile_at(start)]
        store(axis, jnp.broadcast_to(line, (LANES, LANES)).T)


def halo_line(ref, row, row_start, length):
    total = ref.shape[1]
    right_start = lax.rem(row_start + length, total)
    left_start = lax.rem(row_start + total - LANES, total)
    return jnp.where(
        lane_ids() < HALF, ref[row : row + 1, tile_at(right_start)], ref[row : row + 1, tile_at(left_start)]
    )


def t_tiles_kernel(centroids_ref, near_ref, out_ref, column_ref):
    q_tiles, p_tiles = near_ref.shape
    me = lax.axis_index("row")
    length = p_tiles * LANES
    row_start = me * length
    col_start = lax.axis_index("col") * (q_tiles * LANES)
    sources = [source_of(me, i, q_tiles) for i in range(q_tiles)]
    for i in range(q_tiles):

        def store(axis, value, i=i):
            column_ref[axis, i * LANES : (i + 1) * LANES, :] = value

        column_coords(centroids_ref, col_start + sources[i] * LANES, store)

    def fill(first, line, gains_of):
        for i in range(q_tiles):
            gains = gains_of(sources[i])
            for k in range(LANES // CHUNK):
                at = slice(i * LANES + k * CHUNK, i * LANES + (k + 1) * CHUNK)
                for offset, tile in enumerate(entries_t(line, [column_ref[axis, at, :] for axis in range(3)], gains)):
                    out_ref[first + offset, at, :] = tile

    group = max(1, 16 // q_tiles)
    while p_tiles % group:
        group -= 1

    def one_group(g, carry):
        for k in range(group):
            t = g * group + k
            line = [centroids_ref[axis : axis + 1, tile_at(row_start + t * LANES)] for axis in range(3)]
            fill(t, line, lambda j: [NEAR_GAIN * near_ref[j, t].astype(jnp.float32)])
        return carry

    lax.fori_loop(0, p_tiles // group, one_group, 0)
    line = [halo_line(centroids_ref, axis, row_start, length) for axis in range(3)]
    fill(p_tiles, line, lambda j: [None, NEAR_GAIN])


def t_kernel(*refs, norm, slots, count):
    packed = refs[:count]
    tiles_ref, moments_ref, shell_ref = refs[count : count + 3]
    out_ref, halo_ref, scaled_ref, edge_ref = refs[count + 3 :]
    q_tiles, p_tiles = shell_ref.shape
    excitations = out_ref.shape[0]
    kinds = moments_ref.shape[0]
    me = lax.axis_index("row")
    length = p_tiles * LANES
    row_start = me * length
    col_start = lax.axis_index("col") * (q_tiles * LANES)
    low = lane_ids() < HALF

    for i in range(count):
        edge_ref[i] = packed[i][slots:].astype(jnp.float32)
    right = edge_ref[step_from(me, lax.rem(me + 1, count), count)]
    left = edge_ref[step_from(me, lax.rem(me + count - 1, count), count)]
    halo_ref[...] = jnp.where(low[None], right, left)
    codes = right[0, 0:1], left[0, 1:2]
    nears = [jnp.where(code >= slots, 1.0, 0.0) for code in codes]
    picks = [code - slots * near for code, near in zip(codes, nears)]

    sources = [source_of(me, i, count) for i in range(count)]
    lanes = lane_ids()
    halo_tiles = []
    for i in range(count):
        at = slice(i * LANES, (i + 1) * LANES)
        weights = [moments_ref[a : a + 1, tile_at(col_start + sources[i] * LANES)] for a in range(kinds)]
        values = [packed[i][s].astype(jnp.float32) for s in range(slots)]
        here = lanes == sources[i]
        for pick in picks:
            choice = jnp.sum(jnp.where(here, pick, 0.0), axis=1, keepdims=True)
            value = values[0]
            for s in range(1, slots):
                value = jnp.where(choice == s, values[s], value)
            values.append(value)
        for s, value in enumerate(values):
            for a in range(kinds):
                scaled_ref[s, a * excitations : (a + 1) * excitations, at] = (weights[a] * value).astype(jnp.bfloat16)
        near_right, near_left = [jnp.sum(jnp.where(here, near, 0.0), axis=1, keepdims=True) for near in nears]
        near = jnp.where(low, near_right, near_left)
        halo_tiles.append(
            jnp.where(near > 0.5, tiles_ref[p_tiles + 1, at].astype(jnp.float32), tiles_ref[p_tiles, at].astype(jnp.float32))
            .astype(jnp.bfloat16)
        )

    def weighted(product, weights):
        field = weights[0] * product[:excitations]
        for a in range(1, kinds):
            term = weights[a] * product[a * excitations : (a + 1) * excitations]
            field = field + term if a < kinds - 1 else field - term
        return (field * norm).astype(jnp.bfloat16)

    def one_tile(t):
        lhs = jnp.concatenate(
            [scaled_ref[shell_ref[sources[i], t], :, i * LANES : (i + 1) * LANES] for i in range(count)], axis=1
        )
        weights = [moments_ref[a : a + 1, tile_at(row_start + t * LANES)] for a in range(kinds)]
        product = jnp.dot(lhs, tiles_ref[t], preferred_element_type=jnp.float32)
        out_ref[:, tile_at(t * LANES)] = weighted(product, weights)

    group = max(1, 32 // q_tiles)
    while p_tiles % group:
        group -= 1

    def one_group(g, carry):
        for k in range(group):
            one_tile(g * group + k)
        return carry

    if group == p_tiles:
        one_group(0, 0)
    else:
        lax.fori_loop(0, p_tiles // group, one_group, 0)
    halo_tile = jnp.concatenate(halo_tiles, axis=0)
    product = jnp.where(
        low,
        jnp.dot(scaled_ref[slots], halo_tile, preferred_element_type=jnp.float32),
        jnp.dot(scaled_ref[slots + 1], halo_tile, preferred_element_type=jnp.float32),
    )
    out_ref[:, length:] = weighted(product, [halo_line(moments_ref, a, row_start, length) for a in range(kinds)])


def s_tiles_kernel(centroids_ref, out_ref, column_ref):
    length, width = out_ref.shape
    row_start = lax.axis_index("row") * length
    col_start = lax.axis_index("col") * width

    def one_tile(t, carry):
        def store(axis, value):
            column_ref[axis] = value

        column_coords(centroids_ref, row_start + t * LANES, store)
        for k in range(width // LANES):
            line = [centroids_ref[axis : axis + 1, tile_at(col_start + k * LANES)] for axis in range(3)]
            for piece in range(LANES // CHUNK):
                at = slice(piece * CHUNK, (piece + 1) * CHUNK)
                dx = line[0] - column_ref[0, at, :]
                dy = line[1] - column_ref[1, at, :]
                dz = line[2] - column_ref[2, at, :]
                spacing = root(dx * dx + dy * dy + dz * dz)
                rows = pl.ds(pl.multiple_of(t * LANES + piece * CHUNK, CHUNK), CHUNK)
                out_ref[rows, k * LANES : (k + 1) * LANES] = inverse(spacing + SOFT_S).astype(jnp.bfloat16)
        return carry

    lax.fori_loop(0, length // LANES, one_tile, 0)


def sweep_kernel(*refs, slots, part_count, count):
    parts = refs[:part_count]
    halo_ref, diag_ref, off_ref, links_ref, tiles_ref, dual_moments_ref = refs[part_count : part_count + 6]
    dual_ref, *out_refs = refs[part_count + 6 : -3]
    iter_ref, scaled_ref, share_ref = refs[-3:]
    length = diag_ref.shape[1]
    tiles = length // LANES
    excitations = parts[0].shape[0]
    link_count = links_ref.shape[0]
    kinds = dual_moments_ref.shape[0]
    row_start = lax.axis_index("row") * length
    col_start = lax.axis_index("col") * tiles_ref.shape[1]
    lanes = lane_ids()
    low = lanes < HALF

    def halo(plane, row):
        return halo_ref[plane, row : row + 1]

    def sum3(plane, row):
        return halo(plane, row) + halo(plane, row + 1) + halo(plane, row + 2)

    def tile(t):
        return slice(t * LANES, (t + 1) * LANES)

    field, diag = [], []
    for t in range(tiles + 1):
        total = parts[0][:, tile(t)].astype(jnp.float32)
        for part in parts[1:]:
            total = total + part[:, tile(t)].astype(jnp.float32)
        field.append(total)
        diag.append(diag_ref[:, tile(t)] if t < tiles else sum3(0, 2 + link_count))

    dual = [f / d for f, d in zip(field, diag)]
    for sweep_id in range(SWEEPS):
        last = sweep_id == SWEEPS - 1
        updated = []
        for t in range(tiles if last else tiles + 1):
            around = jnp.where(low, dual[(t + 1) % (tiles + 1)], dual[t - 1])
            coupled = jnp.zeros_like(field[t])
            for m in range(link_count):
                if t < tiles:
                    source = links_ref[m : m + 1, tile(t)] - (row_start + t * LANES)
                    gram = off_ref[m : m + 1, tile(t)]
                else:
                    source = halo(0, 2 + m).astype(jnp.int32) + lanes
                    gram = sum3(1, 3 * m)
                inside = (source >= 0) & (source < LANES)
                index = jnp.broadcast_to(source & (LANES - 1), (excitations, LANES))
                here = jnp.take_along_axis(dual[t], index, axis=1)
                beside = jnp.take_along_axis(around, index, axis=1)
                coupled = coupled + gram * jnp.where(inside, here, beside)
            updated.append((field[t] - coupled) / diag[t])
        dual = updated

    for t in range(tiles):
        iter_ref[t] = dual[t]
        for a in range(kinds):
            weight = dual_moments_ref[a : a + 1, tile_at(row_start + t * LANES)]
            scaled_ref[a * excitations : (a + 1) * excitations, tile(t)] = (weight * dual[t]).astype(jnp.bfloat16)
    dual_ref[...] = iter_ref[lax.axis_index("col")]
    product = jnp.dot(scaled_ref[...], tiles_ref[...], preferred_element_type=jnp.float32)
    for k in range(count):
        term = jnp.zeros((excitations, LANES), jnp.float32)
        for a in range(kinds):
            weight = dual_moments_ref[a : a + 1, tile_at(col_start + k * LANES)]
            term = term + weight * product[a * excitations : (a + 1) * excitations, tile(k)]
        share_ref[k] = term
    me = lax.axis_index("row")
    for step, out_ref in enumerate(out_refs):
        out_ref[...] = share_ref[target_of(me, step, count)].astype(out_ref.dtype)


def final_kernel(*refs, norm):
    *share_refs, incident_ref, out_ref = refs
    total = share_refs[0][...].astype(jnp.float32)
    for share_ref in share_refs[1:]:
        total = total + share_ref[...].astype(jnp.float32)
    out_ref[...] = incident_ref[...] - total * norm


def swap(value, axis, step):
    count = lax.axis_size(axis)
    if count & (count - 1) == 0:
        pairs = [(i, i ^ step) for i in range(count)]
    else:
        pairs = [(i, (i + step) % count) for i in range(count)]
    return lax.ppermute(value, axis, pairs)


def exchange(value, axis):
    count = lax.axis_size(axis)
    if count & (count - 1):
        return [value] + [swap(value, axis, step) for step in range(1, count)]
    step = 1
    while 2 * step < count:
        other = swap(value, axis, step)
        value = (value.astype(jnp.float32) + other.astype(jnp.float32)).astype(value.dtype)
        step *= 2
    return [value, swap(value, axis, step)] if count > 1 else [value]


def late(value, after):
    return lax.optimization_barrier((value, after))[0]


def per_device(
    history,
    incident,
    centroids,
    moments,
    dual_moments,
    shell,
    near_mask,
    neighbours,
    gram_diag,
    gram_off,
):
    col_devices = lax.axis_size("col")
    slots, excitations, shard_len = history.shape
    p_tiles, q_tiles = shell.shape
    rows_t = gram_diag.shape[0]
    cols_t = q_tiles * LANES
    norm = 1.0 / math.sqrt(centroids.shape[1])
    shell, near_mask = shell.T, near_mask.T
    gram_diag = gram_diag.reshape(1, rows_t)

    packed = pl.pallas_call(
        pack_kernel,
        out_shape=jax.ShapeDtypeStruct((slots + 2, excitations, shard_len), jnp.bfloat16),
        in_specs=[VMEM, SMEM, SMEM, VMEM, VMEM, VMEM],
        out_specs=VMEM,
        compiler_params=pltpu.CompilerParams(vmem_limit_bytes=56 * MIB),
    )(history, shell, near_mask, gram_diag, gram_off, neighbours)
    count = lax.axis_size("row")
    everyone = [packed] + [swap(packed, "row", step) for step in range(count - 1, 0, -1)][::-1]
    entries = rows_t * cols_t
    t_tiles = pl.pallas_call(
        t_tiles_kernel,
        out_shape=jax.ShapeDtypeStruct((p_tiles + 2, cols_t, LANES), jnp.bfloat16),
        in_specs=[VMEM, SMEM],
        out_specs=VMEM,
        scratch_shapes=[pltpu.VMEM((3, cols_t, LANES), jnp.float32)],
        compiler_params=grant((p_tiles + 8, cols_t // 2, LANES), centroids.shape),
        cost_estimate=pl.CostEstimate(flops=16 * entries, bytes_accessed=2 * entries, transcendentals=3 * entries),
    )(late(centroids, packed), near_mask)

    parts, halo = pl.pallas_call(
        functools.partial(t_kernel, norm=norm, slots=slots, count=count),
        out_shape=(
            jax.ShapeDtypeStruct((excitations, rows_t + LANES), jnp.bfloat16),
            jax.ShapeDtypeStruct((2, excitations, LANES), jnp.float32),
        ),
        in_specs=[VMEM] * (count + 2) + [SMEM],
        out_specs=(VMEM, VMEM),
        scratch_shapes=[
            pltpu.VMEM((slots + 2, moments.shape[0] * excitations, cols_t), jnp.bfloat16),
            pltpu.VMEM((count, 2, excitations, LANES), jnp.float32),
        ],
        compiler_params=grant(
            (p_tiles + 2, cols_t // 2, LANES),
            (excitations, rows_t),
            (slots + 2, moments.shape[0] * excitations, cols_t),
            moments.shape,
        ),
    )(*everyone, t_tiles, moments, shell)
    parts = exchange(parts, "col")
    s_tiles = pl.pallas_call(
        s_tiles_kernel,
        out_shape=jax.ShapeDtypeStruct((rows_t, cols_t), jnp.bfloat16),
        in_specs=[VMEM],
        out_specs=VMEM,
        scratch_shapes=[pltpu.VMEM((3, LANES, LANES), jnp.float32)],
        compiler_params=grant((rows_t, cols_t // 2), centroids.shape),
        cost_estimate=pl.CostEstimate(flops=12 * entries, bytes_accessed=2 * entries, transcendentals=2 * entries),
    )(late(centroids, parts[0]))

    own_dual, *shares = pl.pallas_call(
        functools.partial(sweep_kernel, slots=slots, part_count=len(parts), count=count),
        out_shape=[jax.ShapeDtypeStruct((excitations, shard_len), jnp.float32)] * 2
        + [jax.ShapeDtypeStruct((excitations, shard_len), jnp.bfloat16)] * (count - 1),
        in_specs=[VMEM] * (len(parts) + 6),
        out_specs=[VMEM] * (count + 1),
        scratch_shapes=[
            pltpu.VMEM((p_tiles, excitations, LANES), jnp.float32),
            pltpu.VMEM((dual_moments.shape[0] * excitations, rows_t), jnp.bfloat16),
            pltpu.VMEM((q_tiles, excitations, LANES), jnp.float32),
        ],
        compiler_params=grant((col_devices, excitations, rows_t), (rows_t, cols_t // 2), (excitations, 8 * rows_t)),
    )(*parts, halo, gram_diag, gram_off, neighbours, s_tiles, dual_moments)
    for step in range(count - 1, 0, -1):
        shares[step] = swap(shares[step], "row", step)
    march_rhs = pl.pallas_call(
        functools.partial(final_kernel, norm=norm),
        out_shape=jax.ShapeDtypeStruct(incident.shape, jnp.float32),
        in_specs=[VMEM] * (count + 1),
        out_specs=VMEM,
        compiler_params=grant((count, excitations, shard_len)),
    )(*shares, incident)
    return (march_rhs, own_dual)


def solution(mesh):
    placed = (
        P(None, None, ("col", "row")),
        P(None, ("col", "row")),
        P(),
        P(),
        P(),
        P("row", "col"),
        P("row", "col"),
        P(None, "row"),
        P("row"),
        P(None, "row"),
    )
    return jax.shard_map(
        per_device,
        mesh=mesh,
        in_specs=placed,
        out_specs=(P(None, ("col", "row")), P(None, ("row", "col"))),
        check_vma=False,
    )
```

time: 32.7 us -> 30.1 us (0.920)
  blocking collectives: 12.1 us -> 0 us
  starting transfers between devices: 7.24 us -> 11.7 us
  waiting for transfers between devices: 4.21 us -> 7.57 us
  local copies, waits for them, and re-layouts: 0.04 us -> 1.57 us
    all_gather x2 -> x0, blocking collectives: 12.1 us -> none  [the longest x1 6.69 us: per_device(): packed = lax.all_gather(packed, 'row', axis=2, tiled=True)]
    ppermute x3 -> x9, starting transfers between devices: 7.24 us -> 11.7 us  [swap(): return lax.ppermute(value, axis, pairs)]
    ppermute x3 -> x9, waiting for transfers between devices: 4.21 us -> 7.57 us  [swap(): return lax.ppermute(value, axis, pairs)]
    unnamed x18 -> x22, local copies, waits for them, and re-layouts: 0.04 us -> 1.57 us
    pallas_call x1 -> x2, Pallas kernels: 3.11 us -> 3.26 us  [the longest x1 2.23 us: per_device(): pl.pallas_call(t_tiles_kernel, out_shape=jax.ShapeDtypeStruct((p_tiles +...]
  transfers between devices with their start and end apart: 3 -> 9, of which waited for: 3 -> 5; matrix products, arithmetic and copies ran while one was open for 0% -> 0% of each run, Pallas kernels for 5% -> 13%
where the time goes in v9:
time: 30.1 us; the launch traced here: 29.9 us
  starting transfers between devices  11.7 us (39%)
  Pallas kernels  8.31 us (28%)
  waiting for transfers between devices  7.57 us (25%)
  local copies, waits for them, and re-layouts  1.57 us (5%)
  between operations  0.78 us (3%)
    ppermute x9, starting transfers between devices, swap(): return lax.ppermute(value, axis, pairs)  11.7 us
    ppermute x9, waiting for transfers between devices, swap(): return lax.ppermute(value, axis, pairs)  7.57 us
    pallas_call x1, Pallas kernels, per_device(): pl.pallas_call(t_tiles_kernel, out_shape=jax.ShapeDtypeStruct((p_tiles +...  2.23 us
    pallas_call x1, Pallas kernels, per_device(): pl.pallas_call(s_tiles_kernel, out_shape=jax.ShapeDtypeStruct((rows_t, co...  1.64 us
    unnamed x22, local copies, waits for them, and re-layouts  1.57 us
    pallas_call x1, Pallas kernels, per_device(): pl.pallas_call(pack_kernel, out_shape=jax.ShapeDtypeStruct((slots + 2, ex...  1.5 us
    pallas_call x1, Pallas kernels, per_device(): pl.pallas_call(functools.partial(sweep_kernel, slots=slots, part_count=le...  1.3 us
    pallas_call x1, Pallas kernels, per_device(): pl.pallas_call(functools.partial(t_kernel, norm=norm, slots=slots, count=...  1.03 us
  transfers between devices with their start and end apart: 9, of which 5 were waited for; matrix products, arithmetic and copies ran while one was open for 0% of the time, Pallas kernels for 13%

profile of v9, /device:TPU:0, one launch (start us, length us, event | category | flops | bytes accessed | tf_op | source)
XLA Modules:
  0.0 29.9 jit_solution(5395885479149751111)
XLA Ops:
  0.6 1.5 %shard_map.113.refs_0_ = bf16[6,16,128]{2,1,0:T(8,128)(2,1)} custom-call(bf16[4,16,128]{2,1,0:T(8,128)(2,1)} %history_ref.1, s32[4,8]{1,0:T(4,128)} %bitcast.5, s32[4,8]{1,0:T(4,128)} %bitcast.7, f32[1,1024]{1,0:T(1,128)} %bitcast.3, f32[4,1024]{1,0:T(4,128)} %refs_4_.2, s32[4,1024]{1,0:T(4,128)} %refs_5_.3), custom_call_target="tpu_custom_call" | custom-call | tf_op jit(solution)/shard_map/pallas_call | solution.py:407
  2.1 0.0 copy-start
  2.1 0.0 copy-start.3
  2.1 0.0 copy-start.6
  2.1 2.4 %collective-permute-start.2 = (bf16[6,16,128]{2,1,0:T(8,128)(2,1)}, bf16[6,16,128]{2,1,0:T(8,128)(2,1)S(1)}, u32[]{:S(2)}, u32[]{:S(2)}) collective-permute-start(bf16[6,16,128]{2,1,0:T(8,128)(2,1)} %shard_map.113.refs_0_), channel_id=1, source_target_pairs={{0,24},{8,16},{16,8},{24,0},{1,25},{9,17},{17,9},{25,1},{2,26},{10... | collective-permute-start | bytes 73736 | tf_op jit(solution)/shard_map/ppermute | solution.py:367
  4.6 0.6 %collective-permute-start.1 = (bf16[6,16,128]{2,1,0:T(8,128)(2,1)}, bf16[6,16,128]{2,1,0:T(8,128)(2,1)S(1)}, u32[]{:S(2)}, u32[]{:S(2)}) collective-permute-start(bf16[6,16,128]{2,1,0:T(8,128)(2,1)} %shard_map.113.refs_0_), channel_id=1, source_target_pairs={{0,16},{8,24},{16,0},{24,8},{1,17},{9,25},{17,1},{25,9},{2,18},{10... | collective-permute-start | bytes 73736 | tf_op jit(solution)/shard_map/ppermute | solution.py:367
  5.2 0.0 collective-permute-start
  5.3 0.0 copy-start.8
  5.3 0.7 %copy-done.8 = s32[8,4]{0,1:T(4,128)S(1)} copy-done((s32[8,4]{0,1:T(4,128)S(1)}, s32[8,4]{0,1:T(4,128)}, u32[]{:S(2)}) %copy-start.8) | copy-done | bytes 152
  5.9 0.0 copy-start.9
  5.9 0.8 %copy-done.9 = f32[3,4096]{1,0:T(4,128)S(1)} copy-done((f32[3,4096]{1,0:T(4,128)S(1)}, f32[3,4096]{1,0:T(4,128)}, u32[]{:S(2)}) %copy-start.9) | copy-done | bytes 49176
  6.8 2.2 %shard_map.114.refs_4_ = bf16[10,512,128]{2,1,0:T(8,128)(2,1)S(1)} custom-call(f32[3,4096]{1,0:T(4,128)S(1)} %copy-done.9, s32[4,8]{1,0:T(4,128)S(1)} %bitcast.8), custom_call_target="tpu_custom_call" | custom-call | flops 8388608 | bytes 1048576 | tf_op jit(solution)/shard_map/pallas_call | solution.py:417
  9.0 0.0 copy-start.10
  9.0 0.0 collective-permute-done.2.refs_3_
  9.0 0.0 collective-permute-done.1.refs_2_
  9.1 0.0 collective-permute-done.refs_1_
  9.1 0.0 copy-done
  9.1 0.0 copy-done.3
  9.1 0.0 copy-done.6
  9.1 1.0 %shard_map.115 = (bf16[16,1152]{1,0:T(8,128)(2,1)S(1)}, f32[2,16,128]{2,1,0:T(8,128)S(1)}) custom-call(bf16[6,16,128]{2,1,0:T(8,128)(2,1)S(1)} %copy-done, bf16[6,16,128]{2,1,0:T(8,128)(2,1)S(1)} %collective-permute-done.refs_1_, bf16[6,16,128]{2,1,0:T(8,128)(2,1)S(1)} %collective-permute-done.1.refs_2_, ...), custom_call_target="tpu_custom_call" | custom-call | tf_op jit(solution)/shard_map/pallas_call | solution.py:427
  10.1 0.0 copy-start.1
  10.1 0.0 copy-start.2
  10.1 0.0 copy-start.4
  10.2 0.0 copy-start.5
  10.2 1.8 %collective-permute-start.3 = (bf16[16,1152]{1,0:T(8,128)(2,1)S(1)}, bf16[16,1152]{1,0:T(8,128)(2,1)S(1)}, u32[]{:S(2)}, u32[]{:S(2)}) collective-permute-start(bf16[16,1152]{1,0:T(8,128)(2,1)S(1)} %get-tuple-element.12), channel_id=1, source_target_pairs={{0,1},{1,0},{2,3},{3,2},{4,5},{5,4},{6,7},{7,6},{8,9},{9,8},{10,11... | collective-permute-start | bytes 110600 | tf_op jit(solution)/shard_map/ppermute | solution.py:367
  12.0 2.2 %collective-permute-done.3 = bf16[16,1152]{1,0:T(8,128)(2,1)S(1)} collective-permute-done((bf16[16,1152]{1,0:T(8,128)(2,1)S(1)}, bf16[16,1152]{1,0:T(8,128)(2,1)S(1)}, u32[]{:S(2)}, u32[]{:S(2)}) %collective-permute-start.3) | collective-permute-done | bytes 36896 | tf_op jit(solution)/shard_map/ppermute | solution.py:367
  14.2 1.9 %collective-permute-start.4 = (bf16[16,1152]{1,0:T(8,128)(2,1)S(1)}, bf16[16,1152]{1,0:T(8,128)(2,1)S(1)}, u32[]{:S(2)}, u32[]{:S(2)}) collective-permute-start(bf16[16,1152]{1,0:T(8,128)(2,1)S(1)} %add_convert_fusion.1), channel_id=1, source_target_pairs={{0,2},{1,3},{2,0},{3,1},{4,6},{5,7},{6,4},{7,5},{8,10},{9,11},{10,... | collective-permute-start | bytes 110600 | tf_op jit(solution)/shard_map/ppermute | solution.py:367
  16.1 2.1 %collective-permute-done.4 = bf16[16,1152]{1,0:T(8,128)(2,1)S(1)} collective-permute-done((bf16[16,1152]{1,0:T(8,128)(2,1)S(1)}, bf16[16,1152]{1,0:T(8,128)(2,1)S(1)}, u32[]{:S(2)}, u32[]{:S(2)}) %collective-permute-start.4) | collective-permute-done | bytes 36896 | tf_op jit(solution)/shard_map/ppermute | solution.py:367
  18.3 0.0 copy-start.7
  18.3 2.9 %collective-permute-start.5 = (bf16[16,1152]{1,0:T(8,128)(2,1)S(1)}, bf16[16,1152]{1,0:T(8,128)(2,1)S(1)}, u32[]{:S(2)}, u32[]{:S(2)}) collective-permute-start(bf16[16,1152]{1,0:T(8,128)(2,1)S(1)} %add_convert_fusion.refs_0_), channel_id=1, source_target_pairs={{0,4},{1,5},{2,6},{3,7},{4,0},{5,1},{6,2},{7,3},{8,12},{9,13},{10,... | collective-permute-start | bytes 110600 | tf_op jit(solution)/shard_map/ppermute | solution.py:367
  21.2 0.0 copy-done.10
  21.2 1.6 %shard_map.116.refs_6_ = bf16[1024,512]{1,0:T(8,128)(2,1)S(1)} custom-call(f32[3,4096]{1,0:T(4,128)S(1)} %copy-done.10), custom_call_target="tpu_custom_call" | custom-call | flops 6291456 | bytes 1048576 | tf_op jit(solution)/shard_map/pallas_call | solution.py:447
  22.8 0.4 %collective-permute-done.5.refs_1_ = bf16[16,1152]{1,0:T(8,128)(2,1)S(1)} collective-permute-done((bf16[16,1152]{1,0:T(8,128)(2,1)S(1)}, bf16[16,1152]{1,0:T(8,128)(2,1)S(1)}, u32[]{:S(2)}, u32[]{:S(2)}) %collective-permute-start.5) | collective-permute-done | bytes 36896 | tf_op jit(solution)/shard_map/ppermute | solution.py:367
  23.2 0.0 copy-done.1
  23.2 0.0 copy-done.2
  23.2 0.0 copy-done.4
  23.2 0.0 copy-done.5
  23.2 1.3 %shard_map.117 = (f32[16,128]{1,0:T(8,128)}, f32[16,128]{1,0:T(8,128)S(1)}, bf16[16,128]{1,0:T(8,128)(2,1)S(1)}, bf16[16,128]{1,0:T(8,128)(2,1)S(1)}, bf16[16,128]{1,0:T(8,128)(2,1)S(1)}) custom-call(bf16[16,1152]{1,0:T(8,128)(2,1)S(1)} %add_convert_fusion.refs_0_, bf16[16,1152]{1,0:T(8,128)(2,1)S(1)} %collective-permute-done.5.refs_1_, ...), custom_call_target="tpu_custom_call" | custom-call | tf_op jit(solution)/shard_map/pallas_call | solution.py:457
  24.5 0.0 collective-permute-start.6
  24.5 1.7 %collective-permute-start.7 = (bf16[16,128]{1,0:T(8,128)(2,1)S(1)}, bf16[16,128]{1,0:T(8,128)(2,1)S(1)}, u32[]{:S(2)}, u32[]{:S(2)}) collective-permute-start(bf16[16,128]{1,0:T(8,128)(2,1)S(1)} %get-tuple-element.17), channel_id=1, source_target_pairs={{0,16},{8,24},{16,0},{24,8},{1,17},{9,25},{17,1},{25,9},{2,18},{10... | collective-permute-start | bytes 12296 | tf_op jit(solution)/shard_map/ppermute | solution.py:367
  26.3 0.1 collective-permute-start.8
  26.4 0.0 collective-permute-done.6.refs_1_
  26.4 1.7 %collective-permute-done.7.refs_2_ = bf16[16,128]{1,0:T(8,128)(2,1)S(1)} collective-permute-done((bf16[16,128]{1,0:T(8,128)(2,1)S(1)}, bf16[16,128]{1,0:T(8,128)(2,1)S(1)}, u32[]{:S(2)}, u32[]{:S(2)}) %collective-permute-start.7) | collective-permute-done | bytes 4128 | tf_op jit(solution)/shard_map/ppermute | solution.py:367
  28.1 1.2 %collective-permute-done.8.refs_3_ = bf16[16,128]{1,0:T(8,128)(2,1)S(1)} collective-permute-done((bf16[16,128]{1,0:T(8,128)(2,1)S(1)}, bf16[16,128]{1,0:T(8,128)(2,1)S(1)}, u32[]{:S(2)}, u32[]{:S(2)}) %collective-permute-start.8) | collective-permute-done | bytes 4128 | tf_op jit(solution)/shard_map/ppermute | solution.py:367
  29.3 0.0 copy-done.7
  29.3 0.6 %shard_map.118 = f32[16,128]{1,0:T(8,128)} custom-call(f32[16,128]{1,0:T(8,128)S(1)} %get-tuple-element.15.refs_0_, bf16[16,128]{1,0:T(8,128)(2,1)S(1)} %collective-permute-done.6.refs_1_, bf16[16,128]{1,0:T(8,128)(2,1)S(1)} %collective-permute-done.7.refs_2_, bf16[16,128]{1,0:T(8,128)(2,1)S(1)} %collective-permute-done.8.refs_3_, f32[16,128]{1,0:T(8,128)S(1)} %copy-done.7), custom_call_target="tpu_custom_call" | custom-call | tf_op jit(solution)/shard_map/pallas_call | solution.py:472
  (2 shorter events, 0.0 us)
Async XLA Ops:
  2.1 6.9 %copy-start = (bf16[6,16,128]{2,1,0:T(8,128)(2,1)S(1)}, bf16[6,16,128]{2,1,0:T(8,128)(2,1)}, u32[]{:S(2)}) copy-start(bf16[6,16,128]{2,1,0:T(8,128)(2,1)} %shard_map.113.refs_0_) | copy-start | bytes 73732
  2.1 6.9 %copy-start.3 = (f32[4,4096]{1,0:T(4,128)S(1)}, f32[4,4096]{1,0:T(4,128)}, u32[]{:S(2)}) copy-start(f32[4,4096]{1,0:T(4,128)} %refs_5_.2) | copy-start | bytes 196612
  2.1 7.0 %copy-start.6 = (s32[8,4]{0,1:T(4,128)S(1)}, s32[8,4]{0,1:T(4,128)}, u32[]{:S(2)}) copy-start(s32[8,4]{0,1:T(4,128)} %param.15) | copy-start | bytes 388
  2.1 6.9 %collective-permute-start.2 = (bf16[6,16,128]{2,1,0:T(8,128)(2,1)}, bf16[6,16,128]{2,1,0:T(8,128)(2,1)S(1)}, u32[]{:S(2)}, u32[]{:S(2)}) collective-permute-start(bf16[6,16,128]{2,1,0:T(8,128)(2,1)} %shard_map.113.refs_0_), channel_id=1, source_target_pairs={{0,24},{8,16},{16,8},{24,0},{1,25},{9,17},{17,9},{25,1},{2,26},{10... | collective-permute-start | bytes 73736 | tf_op jit(solution)/shard_map/ppermute | solution.py:367
  4.6 4.5 %collective-permute-start.1 = (bf16[6,16,128]{2,1,0:T(8,128)(2,1)}, bf16[6,16,128]{2,1,0:T(8,128)(2,1)S(1)}, u32[]{:S(2)}, u32[]{:S(2)}) collective-permute-start(bf16[6,16,128]{2,1,0:T(8,128)(2,1)} %shard_map.113.refs_0_), channel_id=1, source_target_pairs={{0,16},{8,24},{16,0},{24,8},{1,17},{9,25},{17,1},{25,9},{2,18},{10... | collective-permute-start | bytes 73736 | tf_op jit(solution)/shard_map/ppermute | solution.py:367
  5.2 3.8 %collective-permute-start = (bf16[6,16,128]{2,1,0:T(8,128)(2,1)}, bf16[6,16,128]{2,1,0:T(8,128)(2,1)S(1)}, u32[]{:S(2)}, u32[]{:S(2)}) collective-permute-start(bf16[6,16,128]{2,1,0:T(8,128)(2,1)} %shard_map.113.refs_0_), channel_id=1, source_target_pairs={{0,8},{8,0},{16,24},{24,16},{1,9},{9,1},{17,25},{25,17},{2,10},{10... | collective-permute-start | bytes 73736 | tf_op jit(solution)/shard_map/ppermute | solution.py:367
  5.3 0.7 %copy-start.8 = (s32[8,4]{0,1:T(4,128)S(1)}, s32[8,4]{0,1:T(4,128)}, u32[]{:S(2)}) copy-start(s32[8,4]{0,1:T(4,128)} %param.16) | copy-start | bytes 388
  5.9 0.8 %copy-start.9 = (f32[3,4096]{1,0:T(4,128)S(1)}, f32[3,4096]{1,0:T(4,128)}, u32[]{:S(2)}) copy-start(f32[3,4096]{1,0:T(4,128)} %centroids_ref.1) | copy-start | bytes 147460
  9.0 12.2 %copy-start.10 = (f32[3,4096]{1,0:T(4,128)S(1)}, f32[3,4096]{1,0:T(4,128)}, u32[]{:S(2)}) copy-start(f32[3,4096]{1,0:T(4,128)} %centroids_ref.1) | copy-start | bytes 147460
  10.1 13.1 %copy-start.1 = (f32[4,1024]{1,0:T(4,128)S(1)}, f32[4,1024]{1,0:T(4,128)}, u32[]{:S(2)}) copy-start(f32[4,1024]{1,0:T(4,128)} %refs_4_.2) | copy-start | bytes 49156
  10.1 13.1 %copy-start.2 = (s32[4,1024]{1,0:T(4,128)S(1)}, s32[4,1024]{1,0:T(4,128)}, u32[]{:S(2)}) copy-start(s32[4,1024]{1,0:T(4,128)} %refs_5_.3) | copy-start | bytes 49156
  10.1 13.0 %copy-start.4 = (f32[3,4096]{1,0:T(4,128)S(1)}, f32[3,4096]{1,0:T(4,128)}, u32[]{:S(2)}) copy-start(f32[3,4096]{1,0:T(4,128)} %refs_7_.1) | copy-start | bytes 147460
  10.2 13.0 %copy-start.5 = (f32[1024]{0:T(1024)S(1)}, f32[1024]{0:T(1024)}, u32[]{:S(2)}) copy-start(f32[1024]{0:T(1024)} %param.18) | copy-start | bytes 12292
  10.2 4.0 %collective-permute-start.3 = (bf16[16,1152]{1,0:T(8,128)(2,1)S(1)}, bf16[16,1152]{1,0:T(8,128)(2,1)S(1)}, u32[]{:S(2)}, u32[]{:S(2)}) collective-permute-start(bf16[16,1152]{1,0:T(8,128)(2,1)S(1)} %get-tuple-element.12), channel_id=1, source_target_pairs={{0,1},{1,0},{2,3},{3,2},{4,5},{5,4},{6,7},{7,6},{8,9},{9,8},{10,11... | collective-permute-start | bytes 110600 | tf_op jit(solution)/shard_map/ppermute | solution.py:367
  14.2 4.0 %collective-permute-start.4 = (bf16[16,1152]{1,0:T(8,128)(2,1)S(1)}, bf16[16,1152]{1,0:T(8,128)(2,1)S(1)}, u32[]{:S(2)}, u32[]{:S(2)}) collective-permute-start(bf16[16,1152]{1,0:T(8,128)(2,1)S(1)} %add_convert_fusion.1), channel_id=1, source_target_pairs={{0,2},{1,3},{2,0},{3,1},{4,6},{5,7},{6,4},{7,5},{8,10},{9,11},{10,... | collective-permute-start | bytes 110600 | tf_op jit(solution)/shard_map/ppermute | solution.py:367
  18.3 11.0 %copy-start.7 = (f32[16,128]{1,0:T(8,128)S(1)}, f32[16,128]{1,0:T(8,128)}, u32[]{:S(2)}) copy-start(f32[16,128]{1,0:T(8,128)} %refs_4_.3) | copy-start | bytes 24580
  18.3 4.9 %collective-permute-start.5 = (bf16[16,1152]{1,0:T(8,128)(2,1)S(1)}, bf16[16,1152]{1,0:T(8,128)(2,1)S(1)}, u32[]{:S(2)}, u32[]{:S(2)}) collective-permute-start(bf16[16,1152]{1,0:T(8,128)(2,1)S(1)} %add_convert_fusion.refs_0_), channel_id=1, source_target_pairs={{0,4},{1,5},{2,6},{3,7},{4,0},{5,1},{6,2},{7,3},{8,12},{9,13},{10,... | collective-permute-start | bytes 110600 | tf_op jit(solution)/shard_map/ppermute | solution.py:367
  24.5 1.9 %collective-permute-start.6 = (bf16[16,128]{1,0:T(8,128)(2,1)S(1)}, bf16[16,128]{1,0:T(8,128)(2,1)S(1)}, u32[]{:S(2)}, u32[]{:S(2)}) collective-permute-start(bf16[16,128]{1,0:T(8,128)(2,1)S(1)} %get-tuple-element.16), channel_id=1, source_target_pairs={{0,8},{8,0},{16,24},{24,16},{1,9},{9,1},{17,25},{25,17},{2,10},{10... | collective-permute-start | bytes 12296 | tf_op jit(solution)/shard_map/ppermute | solution.py:367
  24.5 3.6 %collective-permute-start.7 = (bf16[16,128]{1,0:T(8,128)(2,1)S(1)}, bf16[16,128]{1,0:T(8,128)(2,1)S(1)}, u32[]{:S(2)}, u32[]{:S(2)}) collective-permute-start(bf16[16,128]{1,0:T(8,128)(2,1)S(1)} %get-tuple-element.17), channel_id=1, source_target_pairs={{0,16},{8,24},{16,0},{24,8},{1,17},{9,25},{17,1},{25,9},{2,18},{10... | collective-permute-start | bytes 12296 | tf_op jit(solution)/shard_map/ppermute | solution.py:367
  26.3 3.0 %collective-permute-start.8 = (bf16[16,128]{1,0:T(8,128)(2,1)S(1)}, bf16[16,128]{1,0:T(8,128)(2,1)S(1)}, u32[]{:S(2)}, u32[]{:S(2)}) collective-permute-start(bf16[16,128]{1,0:T(8,128)(2,1)S(1)} %get-tuple-element.18), channel_id=1, source_target_pairs={{0,24},{8,16},{16,8},{24,0},{1,25},{9,17},{17,9},{25,1},{2,26},{10... | collective-permute-start | bytes 12296 | tf_op jit(solution)/shard_map/ppermute | solution.py:367

commit v10 on v9

--- a/solution.py
+++ b/solution.py
@@ -74,7 +74,7 @@
     return out
 
 
-def pack_kernel(history_ref, shell_ref, near_ref, diag_ref, off_ref, links_ref, out_ref):
+def pack_kernel(history_ref, shell_ref, near_ref, diag_ref, off_ref, links_ref, out_ref, token_ref):
     slots, excitations = history_ref.shape[:2]
     length = diag_ref.shape[1]
     tiles = shell_ref.shape[1]
@@ -96,6 +96,7 @@
     out_ref[:slots] = history_ref[...]
     out_ref[slots] = stack_rows(rows, excitations).astype(jnp.bfloat16)
     out_ref[slots + 1] = stack_rows(coupling, excitations).astype(jnp.bfloat16)
+    token_ref[...] = jnp.zeros_like(token_ref)
 
 
 def target_of(me, step, count):
@@ -132,7 +133,8 @@
     )
 
 
-def t_tiles_kernel(centroids_ref, near_ref, out_ref, column_ref):
+def t_tiles_kernel(token_ref, centroids_ref, near_ref, out_ref, column_ref):
+    del token_ref
     q_tiles, p_tiles = near_ref.shape
     me = lax.axis_index("row")
     length = p_tiles * LANES
@@ -369,14 +371,16 @@
 
 def exchange(value, axis):
     count = lax.axis_size(axis)
-    if count & (count - 1):
+    if count == 1 or count & (count - 1):
         return [value] + [swap(value, axis, step) for step in range(1, count)]
     step = 1
-    while 2 * step < count:
-        other = swap(value, axis, step)
-        value = (value.astype(jnp.float32) + other.astype(jnp.float32)).astype(value.dtype)
-        step *= 2
-    return [value, swap(value, axis, step)] if count > 1 else [value]
+    while step < count:
+        radix = min(4, count // step)
+        values = [value] + [swap(value, axis, step * k) for k in range(1, radix)]
+        step *= radix
+        if step < count:
+            value = sum(part.astype(jnp.float32) for part in values).astype(value.dtype)
+    return values
 
 
 def late(value, after):
@@ -404,11 +408,14 @@
     shell, near_mask = shell.T, near_mask.T
     gram_diag = gram_diag.reshape(1, rows_t)
 
-    packed = pl.pallas_call(
+    packed, token = pl.pallas_call(
         pack_kernel,
-        out_shape=jax.ShapeDtypeStruct((slots + 2, excitations, shard_len), jnp.bfloat16),
+        out_shape=(
+            jax.ShapeDtypeStruct((slots + 2, excitations, shard_len), jnp.bfloat16),
+            jax.ShapeDtypeStruct((8, LANES), jnp.float32),
+        ),
         in_specs=[VMEM, SMEM, SMEM, VMEM, VMEM, VMEM],
-        out_specs=VMEM,
+        out_specs=(VMEM, VMEM),
         compiler_params=pltpu.CompilerParams(vmem_limit_bytes=56 * MIB),
     )(history, shell, near_mask, gram_diag, gram_off, neighbours)
     count = lax.axis_size("row")
@@ -417,12 +424,12 @@
     t_tiles = pl.pallas_call(
         t_tiles_kernel,
         out_shape=jax.ShapeDtypeStruct((p_tiles + 2, cols_t, LANES), jnp.bfloat16),
-        in_specs=[VMEM, SMEM],
+        in_specs=[pl.BlockSpec(memory_space=pl.ANY), VMEM, SMEM],
         out_specs=VMEM,
         scratch_shapes=[pltpu.VMEM((3, cols_t, LANES), jnp.float32)],
         compiler_params=grant((p_tiles + 8, cols_t // 2, LANES), centroids.shape),
         cost_estimate=pl.CostEstimate(flops=16 * entries, bytes_accessed=2 * entries, transcendentals=3 * entries),
-    )(late(centroids, packed), near_mask)
+    )(token, centroids, near_mask)
 
     parts, halo = pl.pallas_call(
         functools.partial(t_kernel, norm=norm, slots=slots, count=count),
@@ -467,7 +474,7 @@
         ],
         compiler_params=grant((col_devices, excitations, rows_t), (rows_t, cols_t // 2), (excitations, 8 * rows_t)),
     )(*parts, halo, gram_diag, gram_off, neighbours, s_tiles, dual_moments)
-    for step in range(count - 1, 0, -1):
+    for step in sorted(range(1, count), key=lambda step: (1 - step % 2, step)):
         shares[step] = swap(shares[step], "row", step)
     march_rhs = pl.pallas_call(
         functools.partial(final_kernel, norm=norm),

time: 30.1 us -> 29.8 us (0.990)
  local copies, waits for them, and re-layouts: 1.57 us -> 2.26 us
  starting transfers between devices: 11.7 us -> 11.1 us
  waiting for transfers between devices: 7.57 us -> 6.99 us
    unnamed x22 -> x24, local copies, waits for them, and re-layouts: 1.57 us -> 2.26 us
    ppermute x9 -> x10, waiting for transfers between devices: 7.57 us -> 6.99 us  [swap(): return lax.ppermute(value, axis, pairs)]
    ppermute x9 -> x10, starting transfers between devices: 11.7 us -> 11.1 us  [swap(): return lax.ppermute(value, axis, pairs)]
  transfers between devices with their start and end apart: 9 -> 10, of which waited for: 5 -> 6; matrix products, arithmetic and copies ran while one was open for 0% -> 0% of each run, Pallas kernels for 13% -> 13%
where the time goes in v10:
time: 29.8 us; the launch traced here: 29.5 us
  starting transfers between devices  11.1 us (37%)
  Pallas kernels  8.35 us (28%)
  waiting for transfers between devices  6.99 us (23%)
  local copies, waits for them, and re-layouts  2.26 us (8%)
  between operations  0.77 us (3%)
    ppermute x10, starting transfers between devices, swap(): return lax.ppermute(value, axis, pairs)  11.1 us
    ppermute x10, waiting for transfers between devices, swap(): return lax.ppermute(value, axis, pairs)  6.99 us
    unnamed x24, local copies, waits for them, and re-layouts  2.26 us
    pallas_call x1, Pallas kernels, per_device(): pl.pallas_call(t_tiles_kernel, out_shape=jax.ShapeDtypeStruct((p_tiles +...  2.23 us
    pallas_call x1, Pallas kernels, per_device(): pl.pallas_call(s_tiles_kernel, out_shape=jax.ShapeDtypeStruct((rows_t, co...  1.64 us
    pallas_call x1, Pallas kernels, per_device(): pl.pallas_call(pack_kernel, out_shape=(jax.ShapeDtypeStruct((slots + 2, e...  1.52 us
    pallas_call x1, Pallas kernels, per_device(): pl.pallas_call(functools.partial(sweep_kernel, slots=slots, part_count=le...  1.32 us
    pallas_call x1, Pallas kernels, per_device(): pl.pallas_call(functools.partial(t_kernel, norm=norm, slots=slots, count=...  1.04 us
  transfers between devices with their start and end apart: 10, of which 6 were waited for; matrix products, arithmetic and copies ran while one was open for 0% of the time, Pallas kernels for 13%

profile of v10, /device:TPU:0, one launch (start us, length us, event | category | flops | bytes accessed | tf_op | source)
XLA Modules:
  0.0 29.5 jit_solution(18115697517976553225)
XLA Ops:
  0.6 1.5 %shard_map.113 = (bf16[6,16,128]{2,1,0:T(8,128)(2,1)}, f32[8,128]{1,0:T(8,128)}) custom-call(bf16[4,16,128]{2,1,0:T(8,128)(2,1)} %history_ref.1, s32[4,8]{1,0:T(4,128)} %bitcast.5, s32[4,8]{1,0:T(4,128)} %bitcast.7, f32[1,1024]{1,0:T(1,128)} %bitcast.3, f32[4,1024]{1,0:T(4,128)} %refs_4_.2, s32[4,1024]{1,0:T(4,128)} %refs_5_.3), custom_call_target="tpu_custom_call" | custom-call | tf_op jit(solution)/shard_map/pallas_call | solution.py:411
  2.1 2.4 %collective-permute-start.2 = (bf16[6,16,128]{2,1,0:T(8,128)(2,1)}, bf16[6,16,128]{2,1,0:T(8,128)(2,1)S(1)}, u32[]{:S(2)}, u32[]{:S(2)}) collective-permute-start(bf16[6,16,128]{2,1,0:T(8,128)(2,1)} %get-tuple-element.12.refs_0_), channel_id=1, source_target_pairs={{0,24},{8,16},{16,8},{24,0},{1,25},{9,17},{17,9},{25,1},{2,26},{10... | collective-permute-start | bytes 73736 | tf_op jit(solution)/shard_map/ppermute | solution.py:369
  4.5 0.6 %collective-permute-start.1 = (bf16[6,16,128]{2,1,0:T(8,128)(2,1)}, bf16[6,16,128]{2,1,0:T(8,128)(2,1)S(1)}, u32[]{:S(2)}, u32[]{:S(2)}) collective-permute-start(bf16[6,16,128]{2,1,0:T(8,128)(2,1)} %get-tuple-element.12.refs_0_), channel_id=1, source_target_pairs={{0,16},{8,24},{16,0},{24,8},{1,17},{9,25},{17,1},{25,9},{2,18},{10... | collective-permute-start | bytes 73736 | tf_op jit(solution)/shard_map/ppermute | solution.py:369
  5.1 0.1 collective-permute-start
  5.2 0.0 copy-start.8
  5.2 0.7 %copy-done.8 = s32[8,4]{0,1:T(4,128)S(1)} copy-done((s32[8,4]{0,1:T(4,128)S(1)}, s32[8,4]{0,1:T(4,128)}, u32[]{:S(2)}) %copy-start.8) | copy-done | bytes 152
  5.9 0.0 copy-start.9
  5.9 0.8 %copy-done.9 = f32[3,4096]{1,0:T(4,128)S(1)} copy-done((f32[3,4096]{1,0:T(4,128)S(1)}, f32[3,4096]{1,0:T(4,128)}, u32[]{:S(2)}) %copy-start.9) | copy-done | bytes 49176
  6.7 0.0 copy-start.11
  6.7 0.7 %copy-done.11 = f32[8,128]{1,0:T(8,128)S(1)} copy-done((f32[8,128]{1,0:T(8,128)S(1)}, f32[8,128]{1,0:T(8,128)}, u32[]{:S(2)}) %copy-start.11) | copy-done | bytes 4120
  7.4 0.0 copy-start.2
  7.4 0.0 copy-start.4
  7.4 0.0 copy-start.6
  7.4 2.2 %shard_map.114.refs_4_ = bf16[10,512,128]{2,1,0:T(8,128)(2,1)S(1)} custom-call(f32[8,128]{1,0:T(8,128)S(1)} %copy-done.11, f32[3,4096]{1,0:T(4,128)S(1)} %copy-done.9, s32[4,8]{1,0:T(4,128)S(1)} %bitcast.8), custom_call_target="tpu_custom_call" | custom-call | flops 8388608 | bytes 1048576 | tf_op jit(solution)/shard_map/pallas_call | solution.py:424
  9.7 0.0 copy-start.10
  9.7 0.0 collective-permute-done.2.refs_3_
  9.7 0.0 collective-permute-done.1.refs_2_
  9.7 0.0 collective-permute-done.refs_1_
  9.7 0.0 copy-done.2
  9.7 0.0 copy-done.4
  9.7 0.0 copy-done.6
  9.7 1.0 %shard_map.115 = (bf16[16,1152]{1,0:T(8,128)(2,1)S(1)}, f32[2,16,128]{2,1,0:T(8,128)S(1)}) custom-call(bf16[6,16,128]{2,1,0:T(8,128)(2,1)S(1)} %copy-done.4, bf16[6,16,128]{2,1,0:T(8,128)(2,1)S(1)} %collective-permute-done.refs_1_, bf16[6,16,128]{2,1,0:T(8,128)(2,1)S(1)} %collective-permute-done.1.refs_2_, ...), custom_call_target="tpu_custom_call" | custom-call | tf_op jit(solution)/shard_map/pallas_call | solution.py:434
  10.8 0.0 copy-start
  10.8 0.0 copy-start.1
  10.8 0.0 copy-start.3
  10.8 0.0 copy-start.5
  10.8 2.8 %collective-permute-start.5 = (bf16[16,1152]{1,0:T(8,128)(2,1)S(1)}, bf16[16,1152]{1,0:T(8,128)(2,1)S(1)}, u32[]{:S(2)}, u32[]{:S(2)}) collective-permute-start(bf16[16,1152]{1,0:T(8,128)(2,1)S(1)} %get-tuple-element.14), channel_id=1, source_target_pairs={{0,3},{1,2},{2,1},{3,0},{4,7},{5,6},{6,5},{7,4},{8,11},{9,10},{10,... | collective-permute-start | bytes 110600 | tf_op jit(solution)/shard_map/ppermute | solution.py:369
  13.7 0.5 %collective-permute-start.4 = (bf16[16,1152]{1,0:T(8,128)(2,1)S(1)}, bf16[16,1152]{1,0:T(8,128)(2,1)S(1)}, u32[]{:S(2)}, u32[]{:S(2)}) collective-permute-start(bf16[16,1152]{1,0:T(8,128)(2,1)S(1)} %get-tuple-element.14), channel_id=1, source_target_pairs={{0,2},{1,3},{2,0},{3,1},{4,6},{5,7},{6,4},{7,5},{8,10},{9,11},{10,... | collective-permute-start | bytes 110600 | tf_op jit(solution)/shard_map/ppermute | solution.py:369
  14.1 0.3 collective-permute-start.3
  14.4 1.4 %collective-permute-done.5 = bf16[16,1152]{1,0:T(8,128)(2,1)S(1)} collective-permute-done((bf16[16,1152]{1,0:T(8,128)(2,1)S(1)}, bf16[16,1152]{1,0:T(8,128)(2,1)S(1)}, u32[]{:S(2)}, u32[]{:S(2)}) %collective-permute-start.5) | collective-permute-done | bytes 36896 | tf_op jit(solution)/shard_map/ppermute | solution.py:369
  15.7 1.9 %collective-permute-done.4 = bf16[16,1152]{1,0:T(8,128)(2,1)S(1)} collective-permute-done((bf16[16,1152]{1,0:T(8,128)(2,1)S(1)}, bf16[16,1152]{1,0:T(8,128)(2,1)S(1)}, u32[]{:S(2)}, u32[]{:S(2)}) %collective-permute-start.4) | collective-permute-done | bytes 36896 | tf_op jit(solution)/shard_map/ppermute | solution.py:369
  17.6 0.5 %collective-permute-done.3 = bf16[16,1152]{1,0:T(8,128)(2,1)S(1)} collective-permute-done((bf16[16,1152]{1,0:T(8,128)(2,1)S(1)}, bf16[16,1152]{1,0:T(8,128)(2,1)S(1)}, u32[]{:S(2)}, u32[]{:S(2)}) %collective-permute-start.3) | collective-permute-done | bytes 36896 | tf_op jit(solution)/shard_map/ppermute | solution.py:369
  18.1 0.0 copy-start.7
  18.1 2.7 %collective-permute-start.6 = (bf16[16,1152]{1,0:T(8,128)(2,1)S(1)}, bf16[16,1152]{1,0:T(8,128)(2,1)S(1)}, u32[]{:S(2)}, u32[]{:S(2)}) collective-permute-start(bf16[16,1152]{1,0:T(8,128)(2,1)S(1)} %add_convert_fusion.refs_0_), channel_id=1, source_target_pairs={{0,4},{1,5},{2,6},{3,7},{4,0},{5,1},{6,2},{7,3},{8,12},{9,13},{10,... | collective-permute-start | bytes 110600 | tf_op jit(solution)/shard_map/ppermute | solution.py:369
  20.8 0.0 copy-done.10
  20.8 1.6 %shard_map.116.refs_6_ = bf16[1024,512]{1,0:T(8,128)(2,1)S(1)} custom-call(f32[3,4096]{1,0:T(4,128)S(1)} %copy-done.10), custom_call_target="tpu_custom_call" | custom-call | flops 6291456 | bytes 1048576 | tf_op jit(solution)/shard_map/pallas_call | solution.py:454
  22.4 0.6 %collective-permute-done.6.refs_1_ = bf16[16,1152]{1,0:T(8,128)(2,1)S(1)} collective-permute-done((bf16[16,1152]{1,0:T(8,128)(2,1)S(1)}, bf16[16,1152]{1,0:T(8,128)(2,1)S(1)}, u32[]{:S(2)}, u32[]{:S(2)}) %collective-permute-start.6) | collective-permute-done | bytes 36896 | tf_op jit(solution)/shard_map/ppermute | solution.py:369
  23.0 0.0 copy-done
  23.0 0.0 copy-done.1
  23.1 0.0 copy-done.3
  23.1 0.0 copy-done.5
  23.1 1.3 %shard_map.117 = (f32[16,128]{1,0:T(8,128)}, f32[16,128]{1,0:T(8,128)S(1)}, bf16[16,128]{1,0:T(8,128)(2,1)S(1)}, bf16[16,128]{1,0:T(8,128)(2,1)S(1)}, bf16[16,128]{1,0:T(8,128)(2,1)S(1)}) custom-call(bf16[16,1152]{1,0:T(8,128)(2,1)S(1)} %add_convert_fusion.refs_0_, bf16[16,1152]{1,0:T(8,128)(2,1)S(1)} %collective-permute-done.6.refs_1_, ...), custom_call_target="tpu_custom_call" | custom-call | tf_op jit(solution)/shard_map/pallas_call | solution.py:464
  24.4 0.0 collective-permute-start.7
  24.4 1.5 %collective-permute-start.8 = (bf16[16,128]{1,0:T(8,128)(2,1)S(1)}, bf16[16,128]{1,0:T(8,128)(2,1)S(1)}, u32[]{:S(2)}, u32[]{:S(2)}) collective-permute-start(bf16[16,128]{1,0:T(8,128)(2,1)S(1)} %get-tuple-element.19), channel_id=1, source_target_pairs={{0,16},{8,24},{16,0},{24,8},{1,17},{9,25},{17,1},{25,9},{2,18},{10... | collective-permute-start | bytes 12296 | tf_op jit(solution)/shard_map/ppermute | solution.py:369
  25.9 0.4 %collective-permute-start.9 = (bf16[16,128]{1,0:T(8,128)(2,1)S(1)}, bf16[16,128]{1,0:T(8,128)(2,1)S(1)}, u32[]{:S(2)}, u32[]{:S(2)}) collective-permute-start(bf16[16,128]{1,0:T(8,128)(2,1)S(1)} %get-tuple-element.20), channel_id=1, source_target_pairs={{0,24},{8,16},{16,8},{24,0},{1,25},{9,17},{17,9},{25,1},{2,26},{10... | collective-permute-start | bytes 12296 | tf_op jit(solution)/shard_map/ppermute | solution.py:369
  26.2 0.0 collective-permute-done.7.refs_1_
  26.2 1.7 %collective-permute-done.8.refs_2_ = bf16[16,128]{1,0:T(8,128)(2,1)S(1)} collective-permute-done((bf16[16,128]{1,0:T(8,128)(2,1)S(1)}, bf16[16,128]{1,0:T(8,128)(2,1)S(1)}, u32[]{:S(2)}, u32[]{:S(2)}) %collective-permute-start.8) | collective-permute-done | bytes 4128 | tf_op jit(solution)/shard_map/ppermute | solution.py:369
  28.0 0.9 %collective-permute-done.9.refs_3_ = bf16[16,128]{1,0:T(8,128)(2,1)S(1)} collective-permute-done((bf16[16,128]{1,0:T(8,128)(2,1)S(1)}, bf16[16,128]{1,0:T(8,128)(2,1)S(1)}, u32[]{:S(2)}, u32[]{:S(2)}) %collective-permute-start.9) | collective-permute-done | bytes 4128 | tf_op jit(solution)/shard_map/ppermute | solution.py:369
  28.9 0.0 copy-done.7
  28.9 0.6 %shard_map.118 = f32[16,128]{1,0:T(8,128)} custom-call(f32[16,128]{1,0:T(8,128)S(1)} %get-tuple-element.17.refs_0_, bf16[16,128]{1,0:T(8,128)(2,1)S(1)} %collective-permute-done.7.refs_1_, bf16[16,128]{1,0:T(8,128)(2,1)S(1)} %collective-permute-done.8.refs_2_, bf16[16,128]{1,0:T(8,128)(2,1)S(1)} %collective-permute-done.9.refs_3_, f32[16,128]{1,0:T(8,128)S(1)} %copy-done.7), custom_call_target="tpu_custom_call" | custom-call | tf_op jit(solution)/shard_map/pallas_call | solution.py:479
  (1 shorter events, 0.0 us)
Async XLA Ops:
  2.1 7.5 %collective-permute-start.2 = (bf16[6,16,128]{2,1,0:T(8,128)(2,1)}, bf16[6,16,128]{2,1,0:T(8,128)(2,1)S(1)}, u32[]{:S(2)}, u32[]{:S(2)}) collective-permute-start(bf16[6,16,128]{2,1,0:T(8,128)(2,1)} %get-tuple-element.12.refs_0_), channel_id=1, source_target_pairs={{0,24},{8,16},{16,8},{24,0},{1,25},{9,17},{17,9},{25,1},{2,26},{10... | collective-permute-start | bytes 73736 | tf_op jit(solution)/shard_map/ppermute | solution.py:369
  4.5 5.2 %collective-permute-start.1 = (bf16[6,16,128]{2,1,0:T(8,128)(2,1)}, bf16[6,16,128]{2,1,0:T(8,128)(2,1)S(1)}, u32[]{:S(2)}, u32[]{:S(2)}) collective-permute-start(bf16[6,16,128]{2,1,0:T(8,128)(2,1)} %get-tuple-element.12.refs_0_), channel_id=1, source_target_pairs={{0,16},{8,24},{16,0},{24,8},{1,17},{9,25},{17,1},{25,9},{2,18},{10... | collective-permute-start | bytes 73736 | tf_op jit(solution)/shard_map/ppermute | solution.py:369
  5.1 4.6 %collective-permute-start = (bf16[6,16,128]{2,1,0:T(8,128)(2,1)}, bf16[6,16,128]{2,1,0:T(8,128)(2,1)S(1)}, u32[]{:S(2)}, u32[]{:S(2)}) collective-permute-start(bf16[6,16,128]{2,1,0:T(8,128)(2,1)} %get-tuple-element.12.refs_0_), channel_id=1, source_target_pairs={{0,8},{8,0},{16,24},{24,16},{1,9},{9,1},{17,25},{25,17},{2,10},{10... | collective-permute-start | bytes 73736 | tf_op jit(solution)/shard_map/ppermute | solution.py:369
  5.2 0.7 %copy-start.8 = (s32[8,4]{0,1:T(4,128)S(1)}, s32[8,4]{0,1:T(4,128)}, u32[]{:S(2)}) copy-start(s32[8,4]{0,1:T(4,128)} %param.16) | copy-start | bytes 388
  5.9 0.8 %copy-start.9 = (f32[3,4096]{1,0:T(4,128)S(1)}, f32[3,4096]{1,0:T(4,128)}, u32[]{:S(2)}) copy-start(f32[3,4096]{1,0:T(4,128)} %centroids_ref.2) | copy-start | bytes 147460
  6.7 0.7 %copy-start.11 = (f32[8,128]{1,0:T(8,128)S(1)}, f32[8,128]{1,0:T(8,128)}, u32[]{:S(2)}) copy-start(f32[8,128]{1,0:T(8,128)} %get-tuple-element.13.token_ref) | copy-start | bytes 12292
  7.4 2.3 %copy-start.2 = (f32[4,4096]{1,0:T(4,128)S(1)}, f32[4,4096]{1,0:T(4,128)}, u32[]{:S(2)}) copy-start(f32[4,4096]{1,0:T(4,128)} %refs_5_.2) | copy-start | bytes 196612
  7.4 2.3 %copy-start.4 = (bf16[6,16,128]{2,1,0:T(8,128)(2,1)S(1)}, bf16[6,16,128]{2,1,0:T(8,128)(2,1)}, u32[]{:S(2)}) copy-start(bf16[6,16,128]{2,1,0:T(8,128)(2,1)} %get-tuple-element.12.refs_0_) | copy-start | bytes 73732
  7.4 2.3 %copy-start.6 = (s32[8,4]{0,1:T(4,128)S(1)}, s32[8,4]{0,1:T(4,128)}, u32[]{:S(2)}) copy-start(s32[8,4]{0,1:T(4,128)} %param.15) | copy-start | bytes 388
  9.7 11.1 %copy-start.10 = (f32[3,4096]{1,0:T(4,128)S(1)}, f32[3,4096]{1,0:T(4,128)}, u32[]{:S(2)}) copy-start(f32[3,4096]{1,0:T(4,128)} %centroids_ref.2) | copy-start | bytes 147460
  10.8 12.3 %copy-start = (f32[4,1024]{1,0:T(4,128)S(1)}, f32[4,1024]{1,0:T(4,128)}, u32[]{:S(2)}) copy-start(f32[4,1024]{1,0:T(4,128)} %refs_4_.2) | copy-start | bytes 49156
  10.8 12.3 %copy-start.1 = (s32[4,1024]{1,0:T(4,128)S(1)}, s32[4,1024]{1,0:T(4,128)}, u32[]{:S(2)}) copy-start(s32[4,1024]{1,0:T(4,128)} %refs_5_.3) | copy-start | bytes 49156
  10.8 12.3 %copy-start.3 = (f32[3,4096]{1,0:T(4,128)S(1)}, f32[3,4096]{1,0:T(4,128)}, u32[]{:S(2)}) copy-start(f32[3,4096]{1,0:T(4,128)} %refs_7_.1) | copy-start | bytes 147460
  10.8 12.2 %copy-start.5 = (f32[1024]{0:T(1024)S(1)}, f32[1024]{0:T(1024)}, u32[]{:S(2)}) copy-start(f32[1024]{0:T(1024)} %param.18) | copy-start | bytes 12292
  10.8 4.9 %collective-permute-start.5 = (bf16[16,1152]{1,0:T(8,128)(2,1)S(1)}, bf16[16,1152]{1,0:T(8,128)(2,1)S(1)}, u32[]{:S(2)}, u32[]{:S(2)}) collective-permute-start(bf16[16,1152]{1,0:T(8,128)(2,1)S(1)} %get-tuple-element.14), channel_id=1, source_target_pairs={{0,3},{1,2},{2,1},{3,0},{4,7},{5,6},{6,5},{7,4},{8,11},{9,10},{10,... | collective-permute-start | bytes 110600 | tf_op jit(solution)/shard_map/ppermute | solution.py:369
  13.7 4.0 %collective-permute-start.4 = (bf16[16,1152]{1,0:T(8,128)(2,1)S(1)}, bf16[16,1152]{1,0:T(8,128)(2,1)S(1)}, u32[]{:S(2)}, u32[]{:S(2)}) collective-permute-start(bf16[16,1152]{1,0:T(8,128)(2,1)S(1)} %get-tuple-element.14), channel_id=1, source_target_pairs={{0,2},{1,3},{2,0},{3,1},{4,6},{5,7},{6,4},{7,5},{8,10},{9,11},{10,... | collective-permute-start | bytes 110600 | tf_op jit(solution)/shard_map/ppermute | solution.py:369
  14.1 4.0 %collective-permute-start.3 = (bf16[16,1152]{1,0:T(8,128)(2,1)S(1)}, bf16[16,1152]{1,0:T(8,128)(2,1)S(1)}, u32[]{:S(2)}, u32[]{:S(2)}) collective-permute-start(bf16[16,1152]{1,0:T(8,128)(2,1)S(1)} %get-tuple-element.14), channel_id=1, source_target_pairs={{0,1},{1,0},{2,3},{3,2},{4,5},{5,4},{6,7},{7,6},{8,9},{9,8},{10,11... | collective-permute-start | bytes 110600 | tf_op jit(solution)/shard_map/ppermute | solution.py:369
  18.1 10.8 %copy-start.7 = (f32[16,128]{1,0:T(8,128)S(1)}, f32[16,128]{1,0:T(8,128)}, u32[]{:S(2)}) copy-start(f32[16,128]{1,0:T(8,128)} %refs_4_.3) | copy-start | bytes 24580
  18.1 4.9 %collective-permute-start.6 = (bf16[16,1152]{1,0:T(8,128)(2,1)S(1)}, bf16[16,1152]{1,0:T(8,128)(2,1)S(1)}, u32[]{:S(2)}, u32[]{:S(2)}) collective-permute-start(bf16[16,1152]{1,0:T(8,128)(2,1)S(1)} %add_convert_fusion.refs_0_), channel_id=1, source_target_pairs={{0,4},{1,5},{2,6},{3,7},{4,0},{5,1},{6,2},{7,3},{8,12},{9,13},{10,... | collective-permute-start | bytes 110600 | tf_op jit(solution)/shard_map/ppermute | solution.py:369
  24.4 1.9 %collective-permute-start.7 = (bf16[16,128]{1,0:T(8,128)(2,1)S(1)}, bf16[16,128]{1,0:T(8,128)(2,1)S(1)}, u32[]{:S(2)}, u32[]{:S(2)}) collective-permute-start(bf16[16,128]{1,0:T(8,128)(2,1)S(1)} %get-tuple-element.18), channel_id=1, source_target_pairs={{0,8},{8,0},{16,24},{24,16},{1,9},{9,1},{17,25},{25,17},{2,10},{10... | collective-permute-start | bytes 12296 | tf_op jit(solution)/shard_map/ppermute | solution.py:369
  24.4 3.6 %collective-permute-start.8 = (bf16[16,128]{1,0:T(8,128)(2,1)S(1)}, bf16[16,128]{1,0:T(8,128)(2,1)S(1)}, u32[]{:S(2)}, u32[]{:S(2)}) collective-permute-start(bf16[16,128]{1,0:T(8,128)(2,1)S(1)} %get-tuple-element.19), channel_id=1, source_target_pairs={{0,16},{8,24},{16,0},{24,8},{1,17},{9,25},{17,1},{25,9},{2,18},{10... | collective-permute-start | bytes 12296 | tf_op jit(solution)/shard_map/ppermute | solution.py:369
  25.9 3.0 %collective-permute-start.9 = (bf16[16,128]{1,0:T(8,128)(2,1)S(1)}, bf16[16,128]{1,0:T(8,128)(2,1)S(1)}, u32[]{:S(2)}, u32[]{:S(2)}) collective-permute-start(bf16[16,128]{1,0:T(8,128)(2,1)S(1)} %get-tuple-element.20), channel_id=1, source_target_pairs={{0,24},{8,16},{16,8},{24,0},{1,25},{9,17},{17,9},{25,1},{2,26},{10... | collective-permute-start | bytes 12296 | tf_op jit(solution)/shard_map/ppermute | solution.py:369

commit v11 on v10

--- a/solution.py
+++ b/solution.py
@@ -74,7 +74,7 @@
     return out
 
 
-def pack_kernel(history_ref, shell_ref, near_ref, diag_ref, off_ref, links_ref, out_ref, token_ref):
+def pack_kernel(history_ref, shell_ref, near_ref, diag_ref, off_ref, links_ref, centroids_ref, out_ref, lines_ref):
     slots, excitations = history_ref.shape[:2]
     length = diag_ref.shape[1]
     tiles = shell_ref.shape[1]
@@ -96,7 +96,27 @@
     out_ref[:slots] = history_ref[...]
     out_ref[slots] = stack_rows(rows, excitations).astype(jnp.bfloat16)
     out_ref[slots + 1] = stack_rows(coupling, excitations).astype(jnp.bfloat16)
-    token_ref[...] = jnp.zeros_like(token_ref)
+    me = lax.axis_index("row")
+    row_start = me * length
+    q_tiles = shell_ref.shape[0]
+    col_start = lax.axis_index("col") * (q_tiles * LANES)
+    sources = [source_of(me, i, q_tiles) for i in range(q_tiles)]
+    for t in range(tiles):
+        for axis in range(3):
+            lines_ref[3 * t + axis] = centroids_ref[axis, tile_at(row_start + t * LANES)]
+    row = 3 * tiles
+    for axis in range(3):
+        lines_ref[row + axis : row + axis + 1] = halo_line(centroids_ref, axis, row_start, length)
+    row += 3
+    for i in range(q_tiles):
+        for axis in range(3):
+            lines_ref[row + axis] = centroids_ref[axis, tile_at(col_start + sources[i] * LANES)]
+        row += 3
+    for t in range(tiles):
+        for i in range(q_tiles):
+            gain = NEAR_GAIN * near_ref[sources[i], t].astype(jnp.float32)
+            lines_ref[row : row + 1] = jnp.full((1, LANES), gain, jnp.float32)
+            row += 1
 
 
 def target_of(me, step, count):
@@ -118,10 +138,8 @@
     return [(far + gain * near).astype(jnp.bfloat16) if gain is not None else far.astype(jnp.bfloat16) for gain in gains]
 
 
-def column_coords(centroids_ref, start, store):
-    for axis in range(3):
-        line = centroids_ref[axis : axis + 1, tile_at(start)]
-        store(axis, jnp.broadcast_to(line, (LANES, LANES)).T)
+def columns(line):
+    return jnp.broadcast_to(line, (LANES, LANES)).T
 
 
 def halo_line(ref, row, row_start, length):
@@ -133,24 +151,18 @@
     )
 
 
-def t_tiles_kernel(token_ref, centroids_ref, near_ref, out_ref, column_ref):
-    del token_ref
-    q_tiles, p_tiles = near_ref.shape
-    me = lax.axis_index("row")
-    length = p_tiles * LANES
-    row_start = me * length
-    col_start = lax.axis_index("col") * (q_tiles * LANES)
-    sources = [source_of(me, i, q_tiles) for i in range(q_tiles)]
+def t_tiles_kernel(lines_ref, out_ref, column_ref, p_tiles, q_tiles):
+    first_column = 3 * (p_tiles + 1)
+    first_gain = first_column + 3 * q_tiles
     for i in range(q_tiles):
-
-        def store(axis, value, i=i):
-            column_ref[axis, i * LANES : (i + 1) * LANES, :] = value
-
-        column_coords(centroids_ref, col_start + sources[i] * LANES, store)
-
-    def fill(first, line, gains_of):
+        for axis in range(3):
+            row = first_column + 3 * i + axis
+            column_ref[axis, i * LANES : (i + 1) * LANES, :] = columns(lines_ref[row : row + 1])
+
+    def fill(first, gains_of):
+        line = [lines_ref[pl.ds(3 * first + axis, 1)] for axis in range(3)]
         for i in range(q_tiles):
-            gains = gains_of(sources[i])
+            gains = gains_of(i)
             for k in range(LANES // CHUNK):
                 at = slice(i * LANES + k * CHUNK, i * LANES + (k + 1) * CHUNK)
                 for offset, tile in enumerate(entries_t(line, [column_ref[axis, at, :] for axis in range(3)], gains)):
@@ -163,13 +175,11 @@
     def one_group(g, carry):
         for k in range(group):
             t = g * group + k
-            line = [centroids_ref[axis : axis + 1, tile_at(row_start + t * LANES)] for axis in range(3)]
-            fill(t, line, lambda j: [NEAR_GAIN * near_ref[j, t].astype(jnp.float32)])
+            fill(t, lambda i: [lines_ref[pl.ds(first_gain + t * q_tiles + i, 1)]])
         return carry
 
     lax.fori_loop(0, p_tiles // group, one_group, 0)
-    line = [halo_line(centroids_ref, axis, row_start, length) for axis in range(3)]
-    fill(p_tiles, line, lambda j: [None, NEAR_GAIN])
+    fill(p_tiles, lambda i: [None, NEAR_GAIN])
 
 
 def t_kernel(*refs, norm, slots, count):
@@ -261,10 +271,8 @@
     col_start = lax.axis_index("col") * width
 
     def one_tile(t, carry):
-        def store(axis, value):
-            column_ref[axis] = value
-
-        column_coords(centroids_ref, row_start + t * LANES, store)
+        for axis in range(3):
+            column_ref[axis] = columns(centroids_ref[axis : axis + 1, tile_at(row_start + t * LANES)])
         for k in range(width // LANES):
             line = [centroids_ref[axis : axis + 1, tile_at(col_start + k * LANES)] for axis in range(3)]
             for piece in range(LANES // CHUNK):
@@ -379,7 +387,7 @@
         values = [value] + [swap(value, axis, step * k) for k in range(1, radix)]
         step *= radix
         if step < count:
-            value = sum(part.astype(jnp.float32) for part in values).astype(value.dtype)
+            value = sum(part.astype(jnp.float32) for part in values[::-1]).astype(value.dtype)
     return values
 
 
@@ -408,28 +416,29 @@
     shell, near_mask = shell.T, near_mask.T
     gram_diag = gram_diag.reshape(1, rows_t)
 
-    packed, token = pl.pallas_call(
+    line_rows = -(-(3 * (p_tiles + 1 + q_tiles) + p_tiles * q_tiles) // 8) * 8
+    packed, lines = pl.pallas_call(
         pack_kernel,
         out_shape=(
             jax.ShapeDtypeStruct((slots + 2, excitations, shard_len), jnp.bfloat16),
-            jax.ShapeDtypeStruct((8, LANES), jnp.float32),
+            jax.ShapeDtypeStruct((line_rows, LANES), jnp.float32),
         ),
-        in_specs=[VMEM, SMEM, SMEM, VMEM, VMEM, VMEM],
+        in_specs=[VMEM, SMEM, SMEM, VMEM, VMEM, VMEM, VMEM],
         out_specs=(VMEM, VMEM),
         compiler_params=pltpu.CompilerParams(vmem_limit_bytes=56 * MIB),
-    )(history, shell, near_mask, gram_diag, gram_off, neighbours)
+    )(history, shell, near_mask, gram_diag, gram_off, neighbours, centroids)
     count = lax.axis_size("row")
     everyone = [packed] + [swap(packed, "row", step) for step in range(count - 1, 0, -1)][::-1]
     entries = rows_t * cols_t
     t_tiles = pl.pallas_call(
-        t_tiles_kernel,
+        functools.partial(t_tiles_kernel, p_tiles=p_tiles, q_tiles=q_tiles),
         out_shape=jax.ShapeDtypeStruct((p_tiles + 2, cols_t, LANES), jnp.bfloat16),
-        in_specs=[pl.BlockSpec(memory_space=pl.ANY), VMEM, SMEM],
+        in_specs=[VMEM],
         out_specs=VMEM,
         scratch_shapes=[pltpu.VMEM((3, cols_t, LANES), jnp.float32)],
         compiler_params=grant((p_tiles + 8, cols_t // 2, LANES), centroids.shape),
         cost_estimate=pl.CostEstimate(flops=16 * entries, bytes_accessed=2 * entries, transcendentals=3 * entries),
-    )(token, centroids, near_mask)
+    )(lines)
 
     parts, halo = pl.pallas_call(
         functools.partial(t_kernel, norm=norm, slots=slots, count=count),

time: 29.8 us -> 29.1 us (0.977)
  local copies, waits for them, and re-layouts: 2.26 us -> 0.82 us
  waiting for transfers between devices: 6.99 us -> 7.92 us
  Pallas kernels: 8.35 us -> 7.85 us
  starting transfers between devices: 11.1 us -> 11.5 us
    unnamed x24 -> x20, local copies, waits for them, and re-layouts: 2.26 us -> 0.82 us
    ppermute x10, waiting for transfers between devices: 6.99 us -> 7.92 us  [swap(): return lax.ppermute(value, axis, pairs)]
    pallas_call x1, Pallas kernels: 2.23 us -> 1.64 us  [per_device(): pl.pallas_call(functools.partial(t_tiles_kernel, p_tiles=p_tiles, q_tiles...]
    ppermute x10, starting transfers between devices: 11.1 us -> 11.5 us  [swap(): return lax.ppermute(value, axis, pairs)]
  transfers between devices with their start and end apart: 10 -> 10, of which waited for: 6 -> 7; matrix products, arithmetic and copies ran while one was open for 0% -> 0% of each run, Pallas kernels for 13% -> 11%
where the time goes in v11:
time: 29.1 us; the launch traced here: 28.9 us
  starting transfers between devices  11.5 us (40%)
  waiting for transfers between devices  7.92 us (27%)
  Pallas kernels  7.85 us (27%)
  local copies, waits for them, and re-layouts  0.82 us (3%)
  between operations  0.75 us (3%)
    ppermute x10, starting transfers between devices, swap(): return lax.ppermute(value, axis, pairs)  11.5 us
    ppermute x10, waiting for transfers between devices, swap(): return lax.ppermute(value, axis, pairs)  7.92 us
    pallas_call x1, Pallas kernels, per_device(): pl.pallas_call(s_tiles_kernel, out_shape=jax.ShapeDtypeStruct((rows_t, co...  1.65 us
    pallas_call x1, Pallas kernels, per_device(): pl.pallas_call(functools.partial(t_tiles_kernel, p_tiles=p_tiles, q_tiles...  1.64 us
    pallas_call x1, Pallas kernels, per_device(): pl.pallas_call(pack_kernel, out_shape=(jax.ShapeDtypeStruct((slots + 2, e...  1.61 us
    pallas_call x1, Pallas kernels, per_device(): pl.pallas_call(functools.partial(sweep_kernel, slots=slots, part_count=le...  1.32 us
    pallas_call x1, Pallas kernels, per_device(): pl.pallas_call(functools.partial(t_kernel, norm=norm, slots=slots, count=...  1.04 us
    unnamed x20, local copies, waits for them, and re-layouts  0.82 us
  transfers between devices with their start and end apart: 10, of which 7 were waited for; matrix products, arithmetic and copies ran while one was open for 0% of the time, Pallas kernels for 11%

profile of v11, /device:TPU:0, one launch (start us, length us, event | category | flops | bytes accessed | tf_op | source)
XLA Modules:
  0.0 28.9 jit_solution(7257495678542978664)
XLA Ops:
  0.6 1.6 %shard_map.113 = (bf16[6,16,128]{2,1,0:T(8,128)(2,1)}, f32[72,128]{1,0:T(8,128)}) custom-call(bf16[4,16,128]{2,1,0:T(8,128)(2,1)} %history_ref.1, s32[4,8]{1,0:T(4,128)} %bitcast.5, s32[4,8]{1,0:T(4,128)} %bitcast.7, f32[1,1024]{1,0:T(1,128)} %bitcast.3, f32[4,1024]{1,0:T(4,128)} %refs_4_.2, s32[4,1024]{1,0:T(4,128)} %refs_5_.3, f32[3,4096]{1,0:T(4,128)} %centroids_ref.2), custom_call_target="tpu_custom_call" | custom-call | tf_op jit(solution)/shard_map/pallas_call | solution.py:420
  2.2 2.4 %collective-permute-start.2 = (bf16[6,16,128]{2,1,0:T(8,128)(2,1)}, bf16[6,16,128]{2,1,0:T(8,128)(2,1)S(1)}, u32[]{:S(2)}, u32[]{:S(2)}) collective-permute-start(bf16[6,16,128]{2,1,0:T(8,128)(2,1)} %get-tuple-element.12.refs_0_), channel_id=1, source_target_pairs={{0,24},{8,16},{16,8},{24,0},{1,25},{9,17},{17,9},{25,1},{2,26},{10... | collective-permute-start | bytes 73736 | tf_op jit(solution)/shard_map/ppermute | solution.py:377
  4.6 0.6 %collective-permute-start.1 = (bf16[6,16,128]{2,1,0:T(8,128)(2,1)}, bf16[6,16,128]{2,1,0:T(8,128)(2,1)S(1)}, u32[]{:S(2)}, u32[]{:S(2)}) collective-permute-start(bf16[6,16,128]{2,1,0:T(8,128)(2,1)} %get-tuple-element.12.refs_0_), channel_id=1, source_target_pairs={{0,16},{8,24},{16,0},{24,8},{1,17},{9,25},{17,1},{25,9},{2,18},{10... | collective-permute-start | bytes 73736 | tf_op jit(solution)/shard_map/ppermute | solution.py:377
  5.2 0.1 collective-permute-start
  5.3 0.0 copy-start.9
  5.3 0.8 %copy-done.9 = f32[72,128]{1,0:T(8,128)S(1)} copy-done((f32[72,128]{1,0:T(8,128)S(1)}, f32[72,128]{1,0:T(8,128)}, u32[]{:S(2)}) %copy-start.9) | copy-done | bytes 36888
  6.1 0.0 copy-start.2
  6.1 0.0 copy-start.5
  6.1 0.0 copy-start.7
  6.1 1.6 %shard_map.114.refs_4_ = bf16[10,512,128]{2,1,0:T(8,128)(2,1)S(1)} custom-call(f32[72,128]{1,0:T(8,128)S(1)} %copy-done.9), custom_call_target="tpu_custom_call" | custom-call | flops 8388608 | bytes 1048576 | tf_op jit(solution)/shard_map/pallas_call | solution.py:433
  7.7 0.0 copy-start.4
  7.7 0.0 collective-permute-done.2.refs_3_
  7.7 0.9 %collective-permute-done.1.refs_2_ = bf16[6,16,128]{2,1,0:T(8,128)(2,1)S(1)} collective-permute-done((bf16[6,16,128]{2,1,0:T(8,128)(2,1)}, bf16[6,16,128]{2,1,0:T(8,128)(2,1)S(1)}, u32[]{:S(2)}, u32[]{:S(2)}) %collective-permute-start.1) | collective-permute-done | bytes 24608 | tf_op jit(solution)/shard_map/ppermute | solution.py:377
  8.7 0.0 collective-permute-done.refs_1_
  8.7 0.0 copy-done.2
  8.7 0.0 copy-done.5
  8.7 0.0 copy-done.7
  8.7 1.0 %shard_map.115 = (bf16[16,1152]{1,0:T(8,128)(2,1)S(1)}, f32[2,16,128]{2,1,0:T(8,128)S(1)}) custom-call(bf16[6,16,128]{2,1,0:T(8,128)(2,1)S(1)} %copy-done.5, bf16[6,16,128]{2,1,0:T(8,128)(2,1)S(1)} %collective-permute-done.refs_1_, bf16[6,16,128]{2,1,0:T(8,128)(2,1)S(1)} %collective-permute-done.1.refs_2_, ...), custom_call_target="tpu_custom_call" | custom-call | tf_op jit(solution)/shard_map/pallas_call | solution.py:443
  9.7 0.0 copy-start
  9.7 0.0 copy-start.1
  9.7 0.0 copy-start.3
  9.8 0.0 copy-start.6
  9.8 1.6 %collective-permute-start.5 = (bf16[16,1152]{1,0:T(8,128)(2,1)S(1)}, bf16[16,1152]{1,0:T(8,128)(2,1)S(1)}, u32[]{:S(2)}, u32[]{:S(2)}) collective-permute-start(bf16[16,1152]{1,0:T(8,128)(2,1)S(1)} %get-tuple-element.14), channel_id=1, source_target_pairs={{0,1},{1,0},{2,3},{3,2},{4,5},{5,4},{6,7},{7,6},{8,9},{9,8},{10,11... | collective-permute-start | bytes 110600 | tf_op jit(solution)/shard_map/ppermute | solution.py:377
  11.4 1.6 %collective-permute-start.4 = (bf16[16,1152]{1,0:T(8,128)(2,1)S(1)}, bf16[16,1152]{1,0:T(8,128)(2,1)S(1)}, u32[]{:S(2)}, u32[]{:S(2)}) collective-permute-start(bf16[16,1152]{1,0:T(8,128)(2,1)S(1)} %get-tuple-element.14), channel_id=1, source_target_pairs={{0,2},{1,3},{2,0},{3,1},{4,6},{5,7},{6,4},{7,5},{8,10},{9,11},{10,... | collective-permute-start | bytes 110600 | tf_op jit(solution)/shard_map/ppermute | solution.py:377
  12.9 0.4 %collective-permute-start.3 = (bf16[16,1152]{1,0:T(8,128)(2,1)S(1)}, bf16[16,1152]{1,0:T(8,128)(2,1)S(1)}, u32[]{:S(2)}, u32[]{:S(2)}) collective-permute-start(bf16[16,1152]{1,0:T(8,128)(2,1)S(1)} %get-tuple-element.14), channel_id=1, source_target_pairs={{0,3},{1,2},{2,1},{3,0},{4,7},{5,6},{6,5},{7,4},{8,11},{9,10},{10,... | collective-permute-start | bytes 110600 | tf_op jit(solution)/shard_map/ppermute | solution.py:377
  13.3 0.5 %collective-permute-done.5 = bf16[16,1152]{1,0:T(8,128)(2,1)S(1)} collective-permute-done((bf16[16,1152]{1,0:T(8,128)(2,1)S(1)}, bf16[16,1152]{1,0:T(8,128)(2,1)S(1)}, u32[]{:S(2)}, u32[]{:S(2)}) %collective-permute-start.5) | collective-permute-done | bytes 36896 | tf_op jit(solution)/shard_map/ppermute | solution.py:377
  13.8 1.5 %collective-permute-done.4 = bf16[16,1152]{1,0:T(8,128)(2,1)S(1)} collective-permute-done((bf16[16,1152]{1,0:T(8,128)(2,1)S(1)}, bf16[16,1152]{1,0:T(8,128)(2,1)S(1)}, u32[]{:S(2)}, u32[]{:S(2)}) %collective-permute-start.4) | collective-permute-done | bytes 36896 | tf_op jit(solution)/shard_map/ppermute | solution.py:377
  15.3 2.5 %collective-permute-done.3 = bf16[16,1152]{1,0:T(8,128)(2,1)S(1)} collective-permute-done((bf16[16,1152]{1,0:T(8,128)(2,1)S(1)}, bf16[16,1152]{1,0:T(8,128)(2,1)S(1)}, u32[]{:S(2)}, u32[]{:S(2)}) %collective-permute-start.3) | collective-permute-done | bytes 36896 | tf_op jit(solution)/shard_map/ppermute | solution.py:377
  17.8 0.0 copy-start.8
  17.8 3.0 %collective-permute-start.6 = (bf16[16,1152]{1,0:T(8,128)(2,1)S(1)}, bf16[16,1152]{1,0:T(8,128)(2,1)S(1)}, u32[]{:S(2)}, u32[]{:S(2)}) collective-permute-start(bf16[16,1152]{1,0:T(8,128)(2,1)S(1)} %add_convert_fusion.refs_0_), channel_id=1, source_target_pairs={{0,4},{1,5},{2,6},{3,7},{4,0},{5,1},{6,2},{7,3},{8,12},{9,13},{10,... | collective-permute-start | bytes 110600 | tf_op jit(solution)/shard_map/ppermute | solution.py:377
  20.9 0.0 copy-done.4
  20.9 1.6 %shard_map.116.refs_6_ = bf16[1024,512]{1,0:T(8,128)(2,1)S(1)} custom-call(f32[3,4096]{1,0:T(4,128)S(1)} %copy-done.4), custom_call_target="tpu_custom_call" | custom-call | flops 6291456 | bytes 1048576 | tf_op jit(solution)/shard_map/pallas_call | solution.py:463
  22.5 0.5 %collective-permute-done.6.refs_1_ = bf16[16,1152]{1,0:T(8,128)(2,1)S(1)} collective-permute-done((bf16[16,1152]{1,0:T(8,128)(2,1)S(1)}, bf16[16,1152]{1,0:T(8,128)(2,1)S(1)}, u32[]{:S(2)}, u32[]{:S(2)}) %collective-permute-start.6) | collective-permute-done | bytes 36896 | tf_op jit(solution)/shard_map/ppermute | solution.py:377
  23.0 0.0 copy-done
  23.0 0.0 copy-done.1
  23.0 0.0 copy-done.3
  23.0 0.0 copy-done.6
  23.1 1.3 %shard_map.117 = (f32[16,128]{1,0:T(8,128)}, f32[16,128]{1,0:T(8,128)S(1)}, bf16[16,128]{1,0:T(8,128)(2,1)S(1)}, bf16[16,128]{1,0:T(8,128)(2,1)S(1)}, bf16[16,128]{1,0:T(8,128)(2,1)S(1)}) custom-call(bf16[16,1152]{1,0:T(8,128)(2,1)S(1)} %add_convert_fusion.refs_0_, bf16[16,1152]{1,0:T(8,128)(2,1)S(1)} %collective-permute-done.6.refs_1_, ...), custom_call_target="tpu_custom_call" | custom-call | tf_op jit(solution)/shard_map/pallas_call | solution.py:473
  24.4 0.0 collective-permute-start.7
  24.4 0.9 %collective-permute-start.8 = (bf16[16,128]{1,0:T(8,128)(2,1)S(1)}, bf16[16,128]{1,0:T(8,128)(2,1)S(1)}, u32[]{:S(2)}, u32[]{:S(2)}) collective-permute-start(bf16[16,128]{1,0:T(8,128)(2,1)S(1)} %get-tuple-element.19), channel_id=1, source_target_pairs={{0,16},{8,24},{16,0},{24,8},{1,17},{9,25},{17,1},{25,9},{2,18},{10... | collective-permute-start | bytes 12296 | tf_op jit(solution)/shard_map/ppermute | solution.py:377
  25.2 1.0 %collective-permute-start.9 = (bf16[16,128]{1,0:T(8,128)(2,1)S(1)}, bf16[16,128]{1,0:T(8,128)(2,1)S(1)}, u32[]{:S(2)}, u32[]{:S(2)}) collective-permute-start(bf16[16,128]{1,0:T(8,128)(2,1)S(1)} %get-tuple-element.20), channel_id=1, source_target_pairs={{0,24},{8,16},{16,8},{24,0},{1,25},{9,17},{17,9},{25,1},{2,26},{10... | collective-permute-start | bytes 12296 | tf_op jit(solution)/shard_map/ppermute | solution.py:377
  26.2 0.0 collective-permute-done.7.refs_1_
  26.2 1.7 %collective-permute-done.8.refs_2_ = bf16[16,128]{1,0:T(8,128)(2,1)S(1)} collective-permute-done((bf16[16,128]{1,0:T(8,128)(2,1)S(1)}, bf16[16,128]{1,0:T(8,128)(2,1)S(1)}, u32[]{:S(2)}, u32[]{:S(2)}) %collective-permute-start.8) | collective-permute-done | bytes 4128 | tf_op jit(solution)/shard_map/ppermute | solution.py:377
  28.0 0.3 collective-permute-done.9.refs_3_
  28.3 0.0 copy-done.8
  28.3 0.6 %shard_map.118 = f32[16,128]{1,0:T(8,128)} custom-call(f32[16,128]{1,0:T(8,128)S(1)} %get-tuple-element.17.refs_0_, bf16[16,128]{1,0:T(8,128)(2,1)S(1)} %collective-permute-done.7.refs_1_, bf16[16,128]{1,0:T(8,128)(2,1)S(1)} %collective-permute-done.8.refs_2_, bf16[16,128]{1,0:T(8,128)(2,1)S(1)} %collective-permute-done.9.refs_3_, f32[16,128]{1,0:T(8,128)S(1)} %copy-done.8), custom_call_target="tpu_custom_call" | custom-call | tf_op jit(solution)/shard_map/pallas_call | solution.py:488
  (1 shorter events, 0.0 us)
Async XLA Ops:
  2.2 5.5 %collective-permute-start.2 = (bf16[6,16,128]{2,1,0:T(8,128)(2,1)}, bf16[6,16,128]{2,1,0:T(8,128)(2,1)S(1)}, u32[]{:S(2)}, u32[]{:S(2)}) collective-permute-start(bf16[6,16,128]{2,1,0:T(8,128)(2,1)} %get-tuple-element.12.refs_0_), channel_id=1, source_target_pairs={{0,24},{8,16},{16,8},{24,0},{1,25},{9,17},{17,9},{25,1},{2,26},{10... | collective-permute-start | bytes 73736 | tf_op jit(solution)/shard_map/ppermute | solution.py:377
  4.6 4.0 %collective-permute-start.1 = (bf16[6,16,128]{2,1,0:T(8,128)(2,1)}, bf16[6,16,128]{2,1,0:T(8,128)(2,1)S(1)}, u32[]{:S(2)}, u32[]{:S(2)}) collective-permute-start(bf16[6,16,128]{2,1,0:T(8,128)(2,1)} %get-tuple-element.12.refs_0_), channel_id=1, source_target_pairs={{0,16},{8,24},{16,0},{24,8},{1,17},{9,25},{17,1},{25,9},{2,18},{10... | collective-permute-start | bytes 73736 | tf_op jit(solution)/shard_map/ppermute | solution.py:377
  5.2 3.4 %collective-permute-start = (bf16[6,16,128]{2,1,0:T(8,128)(2,1)}, bf16[6,16,128]{2,1,0:T(8,128)(2,1)S(1)}, u32[]{:S(2)}, u32[]{:S(2)}) collective-permute-start(bf16[6,16,128]{2,1,0:T(8,128)(2,1)} %get-tuple-element.12.refs_0_), channel_id=1, source_target_pairs={{0,8},{8,0},{16,24},{24,16},{1,9},{9,1},{17,25},{25,17},{2,10},{10... | collective-permute-start | bytes 73736 | tf_op jit(solution)/shard_map/ppermute | solution.py:377
  5.3 0.8 %copy-start.9 = (f32[72,128]{1,0:T(8,128)S(1)}, f32[72,128]{1,0:T(8,128)}, u32[]{:S(2)}) copy-start(f32[72,128]{1,0:T(8,128)} %get-tuple-element.13.lines_ref) | copy-start | bytes 110596
  6.1 2.6 %copy-start.2 = (f32[4,4096]{1,0:T(4,128)S(1)}, f32[4,4096]{1,0:T(4,128)}, u32[]{:S(2)}) copy-start(f32[4,4096]{1,0:T(4,128)} %refs_5_.2) | copy-start | bytes 196612
  6.1 2.6 %copy-start.5 = (bf16[6,16,128]{2,1,0:T(8,128)(2,1)S(1)}, bf16[6,16,128]{2,1,0:T(8,128)(2,1)}, u32[]{:S(2)}) copy-start(bf16[6,16,128]{2,1,0:T(8,128)(2,1)} %get-tuple-element.12.refs_0_) | copy-start | bytes 73732
  6.1 2.6 %copy-start.7 = (s32[8,4]{0,1:T(4,128)S(1)}, s32[8,4]{0,1:T(4,128)}, u32[]{:S(2)}) copy-start(s32[8,4]{0,1:T(4,128)} %param.15) | copy-start | bytes 388
  7.7 13.2 %copy-start.4 = (f32[3,4096]{1,0:T(4,128)S(1)}, f32[3,4096]{1,0:T(4,128)}, u32[]{:S(2)}) copy-start(f32[3,4096]{1,0:T(4,128)} %centroids_ref.2) | copy-start | bytes 147460
  9.7 13.3 %copy-start = (f32[4,1024]{1,0:T(4,128)S(1)}, f32[4,1024]{1,0:T(4,128)}, u32[]{:S(2)}) copy-start(f32[4,1024]{1,0:T(4,128)} %refs_4_.2) | copy-start | bytes 49156
  9.7 13.3 %copy-start.1 = (s32[4,1024]{1,0:T(4,128)S(1)}, s32[4,1024]{1,0:T(4,128)}, u32[]{:S(2)}) copy-start(s32[4,1024]{1,0:T(4,128)} %refs_5_.3) | copy-start | bytes 49156
  9.7 13.3 %copy-start.3 = (f32[3,4096]{1,0:T(4,128)S(1)}, f32[3,4096]{1,0:T(4,128)}, u32[]{:S(2)}) copy-start(f32[3,4096]{1,0:T(4,128)} %refs_7_.1) | copy-start | bytes 147460
  9.8 13.3 %copy-start.6 = (f32[1024]{0:T(1024)S(1)}, f32[1024]{0:T(1024)}, u32[]{:S(2)}) copy-start(f32[1024]{0:T(1024)} %param.18) | copy-start | bytes 12292
  9.8 4.0 %collective-permute-start.5 = (bf16[16,1152]{1,0:T(8,128)(2,1)S(1)}, bf16[16,1152]{1,0:T(8,128)(2,1)S(1)}, u32[]{:S(2)}, u32[]{:S(2)}) collective-permute-start(bf16[16,1152]{1,0:T(8,128)(2,1)S(1)} %get-tuple-element.14), channel_id=1, source_target_pairs={{0,1},{1,0},{2,3},{3,2},{4,5},{5,4},{6,7},{7,6},{8,9},{9,8},{10,11... | collective-permute-start | bytes 110600 | tf_op jit(solution)/shard_map/ppermute | solution.py:377
  11.4 4.0 %collective-permute-start.4 = (bf16[16,1152]{1,0:T(8,128)(2,1)S(1)}, bf16[16,1152]{1,0:T(8,128)(2,1)S(1)}, u32[]{:S(2)}, u32[]{:S(2)}) collective-permute-start(bf16[16,1152]{1,0:T(8,128)(2,1)S(1)} %get-tuple-element.14), channel_id=1, source_target_pairs={{0,2},{1,3},{2,0},{3,1},{4,6},{5,7},{6,4},{7,5},{8,10},{9,11},{10,... | collective-permute-start | bytes 110600 | tf_op jit(solution)/shard_map/ppermute | solution.py:377
  12.9 4.9 %collective-permute-start.3 = (bf16[16,1152]{1,0:T(8,128)(2,1)S(1)}, bf16[16,1152]{1,0:T(8,128)(2,1)S(1)}, u32[]{:S(2)}, u32[]{:S(2)}) collective-permute-start(bf16[16,1152]{1,0:T(8,128)(2,1)S(1)} %get-tuple-element.14), channel_id=1, source_target_pairs={{0,3},{1,2},{2,1},{3,0},{4,7},{5,6},{6,5},{7,4},{8,11},{9,10},{10,... | collective-permute-start | bytes 110600 | tf_op jit(solution)/shard_map/ppermute | solution.py:377
  17.8 10.4 %copy-start.8 = (f32[16,128]{1,0:T(8,128)S(1)}, f32[16,128]{1,0:T(8,128)}, u32[]{:S(2)}) copy-start(f32[16,128]{1,0:T(8,128)} %refs_4_.3) | copy-start | bytes 24580
  17.8 5.2 %collective-permute-start.6 = (bf16[16,1152]{1,0:T(8,128)(2,1)S(1)}, bf16[16,1152]{1,0:T(8,128)(2,1)S(1)}, u32[]{:S(2)}, u32[]{:S(2)}) collective-permute-start(bf16[16,1152]{1,0:T(8,128)(2,1)S(1)} %add_convert_fusion.refs_0_), channel_id=1, source_target_pairs={{0,4},{1,5},{2,6},{3,7},{4,0},{5,1},{6,2},{7,3},{8,12},{9,13},{10,... | collective-permute-start | bytes 110600 | tf_op jit(solution)/shard_map/ppermute | solution.py:377
  24.4 1.9 %collective-permute-start.7 = (bf16[16,128]{1,0:T(8,128)(2,1)S(1)}, bf16[16,128]{1,0:T(8,128)(2,1)S(1)}, u32[]{:S(2)}, u32[]{:S(2)}) collective-permute-start(bf16[16,128]{1,0:T(8,128)(2,1)S(1)} %get-tuple-element.18), channel_id=1, source_target_pairs={{0,8},{8,0},{16,24},{24,16},{1,9},{9,1},{17,25},{25,17},{2,10},{10... | collective-permute-start | bytes 12296 | tf_op jit(solution)/shard_map/ppermute | solution.py:377
  24.4 3.6 %collective-permute-start.8 = (bf16[16,128]{1,0:T(8,128)(2,1)S(1)}, bf16[16,128]{1,0:T(8,128)(2,1)S(1)}, u32[]{:S(2)}, u32[]{:S(2)}) collective-permute-start(bf16[16,128]{1,0:T(8,128)(2,1)S(1)} %get-tuple-element.19), channel_id=1, source_target_pairs={{0,16},{8,24},{16,0},{24,8},{1,17},{9,25},{17,1},{25,9},{2,18},{10... | collective-permute-start | bytes 12296 | tf_op jit(solution)/shard_map/ppermute | solution.py:377
  25.2 3.0 %collective-permute-start.9 = (bf16[16,128]{1,0:T(8,128)(2,1)S(1)}, bf16[16,128]{1,0:T(8,128)(2,1)S(1)}, u32[]{:S(2)}, u32[]{:S(2)}) collective-permute-start(bf16[16,128]{1,0:T(8,128)(2,1)S(1)} %get-tuple-element.20), channel_id=1, source_target_pairs={{0,24},{8,16},{16,8},{24,0},{1,25},{9,17},{17,9},{25,1},{2,26},{10... | collective-permute-start | bytes 12296 | tf_op jit(solution)/shard_map/ppermute | solution.py:377

commit v12 on v11

--- a/solution.py
+++ b/solution.py
@@ -183,7 +183,7 @@
 
 
 def t_kernel(*refs, norm, slots, count):
-    packed = refs[:count]
+    packed = [refs[order_of(count).index(step)] for step in range(count)]
     tiles_ref, moments_ref, shell_ref = refs[count : count + 3]
     out_ref, halo_ref, scaled_ref, edge_ref = refs[count + 3 :]
     q_tiles, p_tiles = shell_ref.shape
@@ -377,6 +377,10 @@
     return lax.ppermute(value, axis, pairs)
 
 
+def order_of(count):
+    return (0, 1, 3, 2) if count == 4 else tuple(range(count))
+
+
 def exchange(value, axis):
     count = lax.axis_size(axis)
     if count == 1 or count & (count - 1):
@@ -387,7 +391,7 @@
         values = [value] + [swap(value, axis, step * k) for k in range(1, radix)]
         step *= radix
         if step < count:
-            value = sum(part.astype(jnp.float32) for part in values[::-1]).astype(value.dtype)
+            value = sum(values[k].astype(jnp.float32) for k in order_of(radix)).astype(value.dtype)
     return values
 
 
@@ -458,7 +462,7 @@
             (slots + 2, moments.shape[0] * excitations, cols_t),
             moments.shape,
         ),
-    )(*everyone, t_tiles, moments, shell)
+    )(*[everyone[step] for step in order_of(count)], t_tiles, moments, shell)
     parts = exchange(parts, "col")
     s_tiles = pl.pallas_call(
         s_tiles_kernel,

time: 29.1 us -> 28.1 us (0.966)
  waiting for transfers between devices: 7.92 us -> 7.26 us
  starting transfers between devices: 11.5 us -> 11.2 us
    ppermute x10, waiting for transfers between devices: 7.92 us -> 7.26 us  [swap(): return lax.ppermute(value, axis, pairs)]
    ppermute x10, starting transfers between devices: 11.5 us -> 11.2 us  [swap(): return lax.ppermute(value, axis, pairs)]
  transfers between devices with their start and end apart: 10 -> 10, of which waited for: 7 -> 7; matrix products, arithmetic and copies ran while one was open for 0% -> 0% of each run, Pallas kernels for 11% -> 12%
where the time goes in v12:
time: 28.1 us; the launch traced here: 27.9 us
  starting transfers between devices  11.2 us (40%)
  Pallas kernels  7.85 us (28%)
  waiting for transfers between devices  7.26 us (26%)
  local copies, waits for them, and re-layouts  0.82 us (3%)
  between operations  0.75 us (3%)
    ppermute x10, starting transfers between devices, swap(): return lax.ppermute(value, axis, pairs)  11.2 us
    ppermute x10, waiting for transfers between devices, swap(): return lax.ppermute(value, axis, pairs)  7.26 us
    pallas_call x1, Pallas kernels, per_device(): pl.pallas_call(s_tiles_kernel, out_shape=jax.ShapeDtypeStruct((rows_t, co...  1.65 us
    pallas_call x1, Pallas kernels, per_device(): pl.pallas_call(functools.partial(t_tiles_kernel, p_tiles=p_tiles, q_tiles...  1.64 us
    pallas_call x1, Pallas kernels, per_device(): pl.pallas_call(pack_kernel, out_shape=(jax.ShapeDtypeStruct((slots + 2, e...  1.61 us
    pallas_call x1, Pallas kernels, per_device(): pl.pallas_call(functools.partial(sweep_kernel, slots=slots, part_count=le...  1.31 us
    pallas_call x1, Pallas kernels, per_device(): pl.pallas_call(functools.partial(t_kernel, norm=norm, slots=slots, count=...  1.04 us
    unnamed x20, local copies, waits for them, and re-layouts  0.82 us
  transfers between devices with their start and end apart: 10, of which 7 were waited for; matrix products, arithmetic and copies ran while one was open for 0% of the time, Pallas kernels for 12%

profile of v12, /device:TPU:0, one launch (start us, length us, event | category | flops | bytes accessed | tf_op | source)
XLA Modules:
  0.0 27.9 jit_solution(15214806607587339674)
XLA Ops:
  0.6 1.6 %shard_map.113 = (bf16[6,16,128]{2,1,0:T(8,128)(2,1)}, f32[72,128]{1,0:T(8,128)}) custom-call(bf16[4,16,128]{2,1,0:T(8,128)(2,1)} %history_ref.1, s32[4,8]{1,0:T(4,128)} %bitcast.5, s32[4,8]{1,0:T(4,128)} %bitcast.7, f32[1,1024]{1,0:T(1,128)} %bitcast.3, f32[4,1024]{1,0:T(4,128)} %refs_4_.2, s32[4,1024]{1,0:T(4,128)} %refs_5_.3, f32[3,4096]{1,0:T(4,128)} %centroids_ref.2), custom_call_target="tpu_custom_call" | custom-call | tf_op jit(solution)/shard_map/pallas_call | solution.py:424
  2.2 2.9 %collective-permute-start.2 = (bf16[6,16,128]{2,1,0:T(8,128)(2,1)}, bf16[6,16,128]{2,1,0:T(8,128)(2,1)S(1)}, u32[]{:S(2)}, u32[]{:S(2)}) collective-permute-start(bf16[6,16,128]{2,1,0:T(8,128)(2,1)} %get-tuple-element.12.refs_0_), channel_id=1, source_target_pairs={{0,16},{8,24},{16,0},{24,8},{1,17},{9,25},{17,1},{25,9},{2,18},{10... | collective-permute-start | bytes 73736 | tf_op jit(solution)/shard_map/ppermute | solution.py:377
  5.2 0.0 collective-permute-start.1
  5.2 0.1 collective-permute-start
  5.3 0.0 copy-start.9
  5.3 0.8 %copy-done.9 = f32[72,128]{1,0:T(8,128)S(1)} copy-done((f32[72,128]{1,0:T(8,128)S(1)}, f32[72,128]{1,0:T(8,128)}, u32[]{:S(2)}) %copy-start.9) | copy-done | bytes 36888
  6.1 0.0 copy-start.2
  6.1 0.0 copy-start.5
  6.1 0.0 copy-start.7
  6.1 1.6 %shard_map.114.refs_4_ = bf16[10,512,128]{2,1,0:T(8,128)(2,1)S(1)} custom-call(f32[72,128]{1,0:T(8,128)S(1)} %copy-done.9), custom_call_target="tpu_custom_call" | custom-call | flops 8388608 | bytes 1048576 | tf_op jit(solution)/shard_map/pallas_call | solution.py:437
  7.7 0.0 copy-start.4
  7.8 0.0 collective-permute-done.2.refs_3_
  7.8 0.9 %collective-permute-done.1.refs_2_ = bf16[6,16,128]{2,1,0:T(8,128)(2,1)S(1)} collective-permute-done((bf16[6,16,128]{2,1,0:T(8,128)(2,1)}, bf16[6,16,128]{2,1,0:T(8,128)(2,1)S(1)}, u32[]{:S(2)}, u32[]{:S(2)}) %collective-permute-start.1) | collective-permute-done | bytes 24608 | tf_op jit(solution)/shard_map/ppermute | solution.py:377
  8.6 0.0 collective-permute-done.refs_1_
  8.6 0.0 copy-done.2
  8.6 0.0 copy-done.5
  8.7 0.0 copy-done.7
  8.7 1.0 %shard_map.115 = (bf16[16,1152]{1,0:T(8,128)(2,1)S(1)}, f32[2,16,128]{2,1,0:T(8,128)S(1)}) custom-call(bf16[6,16,128]{2,1,0:T(8,128)(2,1)S(1)} %copy-done.5, bf16[6,16,128]{2,1,0:T(8,128)(2,1)S(1)} %collective-permute-done.refs_1_, bf16[6,16,128]{2,1,0:T(8,128)(2,1)S(1)} %collective-permute-done.1.refs_2_, ...), custom_call_target="tpu_custom_call" | custom-call | tf_op jit(solution)/shard_map/pallas_call | solution.py:447
  9.7 0.0 copy-start
  9.7 0.0 copy-start.1
  9.7 0.0 copy-start.3
  9.7 0.0 copy-start.6
  9.8 1.6 %collective-permute-start.5 = (bf16[16,1152]{1,0:T(8,128)(2,1)S(1)}, bf16[16,1152]{1,0:T(8,128)(2,1)S(1)}, u32[]{:S(2)}, u32[]{:S(2)}) collective-permute-start(bf16[16,1152]{1,0:T(8,128)(2,1)S(1)} %get-tuple-element.14), channel_id=1, source_target_pairs={{0,2},{1,3},{2,0},{3,1},{4,6},{5,7},{6,4},{7,5},{8,10},{9,11},{10,... | collective-permute-start | bytes 110600 | tf_op jit(solution)/shard_map/ppermute | solution.py:377
  11.4 1.4 %collective-permute-start.4 = (bf16[16,1152]{1,0:T(8,128)(2,1)S(1)}, bf16[16,1152]{1,0:T(8,128)(2,1)S(1)}, u32[]{:S(2)}, u32[]{:S(2)}) collective-permute-start(bf16[16,1152]{1,0:T(8,128)(2,1)S(1)} %get-tuple-element.14), channel_id=1, source_target_pairs={{0,3},{1,2},{2,1},{3,0},{4,7},{5,6},{6,5},{7,4},{8,11},{9,10},{10,... | collective-permute-start | bytes 110600 | tf_op jit(solution)/shard_map/ppermute | solution.py:377
  12.8 0.5 %collective-permute-start.3 = (bf16[16,1152]{1,0:T(8,128)(2,1)S(1)}, bf16[16,1152]{1,0:T(8,128)(2,1)S(1)}, u32[]{:S(2)}, u32[]{:S(2)}) collective-permute-start(bf16[16,1152]{1,0:T(8,128)(2,1)S(1)} %get-tuple-element.14), channel_id=1, source_target_pairs={{0,1},{1,0},{2,3},{3,2},{4,5},{5,4},{6,7},{7,6},{8,9},{9,8},{10,11... | collective-permute-start | bytes 110600 | tf_op jit(solution)/shard_map/ppermute | solution.py:377
  13.3 0.5 %collective-permute-done.5 = bf16[16,1152]{1,0:T(8,128)(2,1)S(1)} collective-permute-done((bf16[16,1152]{1,0:T(8,128)(2,1)S(1)}, bf16[16,1152]{1,0:T(8,128)(2,1)S(1)}, u32[]{:S(2)}, u32[]{:S(2)}) %collective-permute-start.5) | collective-permute-done | bytes 36896 | tf_op jit(solution)/shard_map/ppermute | solution.py:377
  13.8 2.5 %collective-permute-done.4 = bf16[16,1152]{1,0:T(8,128)(2,1)S(1)} collective-permute-done((bf16[16,1152]{1,0:T(8,128)(2,1)S(1)}, bf16[16,1152]{1,0:T(8,128)(2,1)S(1)}, u32[]{:S(2)}, u32[]{:S(2)}) %collective-permute-start.4) | collective-permute-done | bytes 36896 | tf_op jit(solution)/shard_map/ppermute | solution.py:377
  16.3 0.5 %collective-permute-done.3 = bf16[16,1152]{1,0:T(8,128)(2,1)S(1)} collective-permute-done((bf16[16,1152]{1,0:T(8,128)(2,1)S(1)}, bf16[16,1152]{1,0:T(8,128)(2,1)S(1)}, u32[]{:S(2)}, u32[]{:S(2)}) %collective-permute-start.3) | collective-permute-done | bytes 36896 | tf_op jit(solution)/shard_map/ppermute | solution.py:377
  16.8 0.0 copy-start.8
  16.8 2.7 %collective-permute-start.6 = (bf16[16,1152]{1,0:T(8,128)(2,1)S(1)}, bf16[16,1152]{1,0:T(8,128)(2,1)S(1)}, u32[]{:S(2)}, u32[]{:S(2)}) collective-permute-start(bf16[16,1152]{1,0:T(8,128)(2,1)S(1)} %add_convert_fusion.refs_0_), channel_id=1, source_target_pairs={{0,4},{1,5},{2,6},{3,7},{4,0},{5,1},{6,2},{7,3},{8,12},{9,13},{10,... | collective-permute-start | bytes 110600 | tf_op jit(solution)/shard_map/ppermute | solution.py:377
  19.5 0.0 copy-done.4
  19.5 1.6 %shard_map.116.refs_6_ = bf16[1024,512]{1,0:T(8,128)(2,1)S(1)} custom-call(f32[3,4096]{1,0:T(4,128)S(1)} %copy-done.4), custom_call_target="tpu_custom_call" | custom-call | flops 6291456 | bytes 1048576 | tf_op jit(solution)/shard_map/pallas_call | solution.py:467
  21.1 0.6 %collective-permute-done.6.refs_1_ = bf16[16,1152]{1,0:T(8,128)(2,1)S(1)} collective-permute-done((bf16[16,1152]{1,0:T(8,128)(2,1)S(1)}, bf16[16,1152]{1,0:T(8,128)(2,1)S(1)}, u32[]{:S(2)}, u32[]{:S(2)}) %collective-permute-start.6) | collective-permute-done | bytes 36896 | tf_op jit(solution)/shard_map/ppermute | solution.py:377
  21.7 0.0 copy-done
  21.7 0.0 copy-done.1
  21.7 0.0 copy-done.3
  21.7 0.0 copy-done.6
  21.7 1.3 %shard_map.117 = (f32[16,128]{1,0:T(8,128)}, f32[16,128]{1,0:T(8,128)S(1)}, bf16[16,128]{1,0:T(8,128)(2,1)S(1)}, bf16[16,128]{1,0:T(8,128)(2,1)S(1)}, bf16[16,128]{1,0:T(8,128)(2,1)S(1)}) custom-call(bf16[16,1152]{1,0:T(8,128)(2,1)S(1)} %add_convert_fusion.refs_0_, bf16[16,1152]{1,0:T(8,128)(2,1)S(1)} %collective-permute-done.6.refs_1_, ...), custom_call_target="tpu_custom_call" | custom-call | tf_op jit(solution)/shard_map/pallas_call | solution.py:477
  23.1 0.0 collective-permute-start.7
  23.1 1.2 %collective-permute-start.8 = (bf16[16,128]{1,0:T(8,128)(2,1)S(1)}, bf16[16,128]{1,0:T(8,128)(2,1)S(1)}, u32[]{:S(2)}, u32[]{:S(2)}) collective-permute-start(bf16[16,128]{1,0:T(8,128)(2,1)S(1)} %get-tuple-element.19), channel_id=1, source_target_pairs={{0,16},{8,24},{16,0},{24,8},{1,17},{9,25},{17,1},{25,9},{2,18},{10... | collective-permute-start | bytes 12296 | tf_op jit(solution)/shard_map/ppermute | solution.py:377
  24.2 0.7 %collective-permute-start.9 = (bf16[16,128]{1,0:T(8,128)(2,1)S(1)}, bf16[16,128]{1,0:T(8,128)(2,1)S(1)}, u32[]{:S(2)}, u32[]{:S(2)}) collective-permute-start(bf16[16,128]{1,0:T(8,128)(2,1)S(1)} %get-tuple-element.20), channel_id=1, source_target_pairs={{0,24},{8,16},{16,8},{24,0},{1,25},{9,17},{17,9},{25,1},{2,26},{10... | collective-permute-start | bytes 12296 | tf_op jit(solution)/shard_map/ppermute | solution.py:377
  24.9 0.0 collective-permute-done.7.refs_1_
  24.9 1.7 %collective-permute-done.8.refs_2_ = bf16[16,128]{1,0:T(8,128)(2,1)S(1)} collective-permute-done((bf16[16,128]{1,0:T(8,128)(2,1)S(1)}, bf16[16,128]{1,0:T(8,128)(2,1)S(1)}, u32[]{:S(2)}, u32[]{:S(2)}) %collective-permute-start.8) | collective-permute-done | bytes 4128 | tf_op jit(solution)/shard_map/ppermute | solution.py:377
  26.7 0.6 %collective-permute-done.9.refs_3_ = bf16[16,128]{1,0:T(8,128)(2,1)S(1)} collective-permute-done((bf16[16,128]{1,0:T(8,128)(2,1)S(1)}, bf16[16,128]{1,0:T(8,128)(2,1)S(1)}, u32[]{:S(2)}, u32[]{:S(2)}) %collective-permute-start.9) | collective-permute-done | bytes 4128 | tf_op jit(solution)/shard_map/ppermute | solution.py:377
  27.2 0.0 copy-done.8
  27.2 0.6 %shard_map.118 = f32[16,128]{1,0:T(8,128)} custom-call(f32[16,128]{1,0:T(8,128)S(1)} %get-tuple-element.17.refs_0_, bf16[16,128]{1,0:T(8,128)(2,1)S(1)} %collective-permute-done.7.refs_1_, bf16[16,128]{1,0:T(8,128)(2,1)S(1)} %collective-permute-done.8.refs_2_, bf16[16,128]{1,0:T(8,128)(2,1)S(1)} %collective-permute-done.9.refs_3_, f32[16,128]{1,0:T(8,128)S(1)} %copy-done.8), custom_call_target="tpu_custom_call" | custom-call | tf_op jit(solution)/shard_map/pallas_call | solution.py:492
  (1 shorter events, 0.0 us)
Async XLA Ops:
  2.2 5.5 %collective-permute-start.2 = (bf16[6,16,128]{2,1,0:T(8,128)(2,1)}, bf16[6,16,128]{2,1,0:T(8,128)(2,1)S(1)}, u32[]{:S(2)}, u32[]{:S(2)}) collective-permute-start(bf16[6,16,128]{2,1,0:T(8,128)(2,1)} %get-tuple-element.12.refs_0_), channel_id=1, source_target_pairs={{0,16},{8,24},{16,0},{24,8},{1,17},{9,25},{17,1},{25,9},{2,18},{10... | collective-permute-start | bytes 73736 | tf_op jit(solution)/shard_map/ppermute | solution.py:377
  5.2 3.5 %collective-permute-start.1 = (bf16[6,16,128]{2,1,0:T(8,128)(2,1)}, bf16[6,16,128]{2,1,0:T(8,128)(2,1)S(1)}, u32[]{:S(2)}, u32[]{:S(2)}) collective-permute-start(bf16[6,16,128]{2,1,0:T(8,128)(2,1)} %get-tuple-element.12.refs_0_), channel_id=1, source_target_pairs={{0,24},{8,16},{16,8},{24,0},{1,25},{9,17},{17,9},{25,1},{2,26},{10... | collective-permute-start | bytes 73736 | tf_op jit(solution)/shard_map/ppermute | solution.py:377
  5.2 3.5 %collective-permute-start = (bf16[6,16,128]{2,1,0:T(8,128)(2,1)}, bf16[6,16,128]{2,1,0:T(8,128)(2,1)S(1)}, u32[]{:S(2)}, u32[]{:S(2)}) collective-permute-start(bf16[6,16,128]{2,1,0:T(8,128)(2,1)} %get-tuple-element.12.refs_0_), channel_id=1, source_target_pairs={{0,8},{8,0},{16,24},{24,16},{1,9},{9,1},{17,25},{25,17},{2,10},{10... | collective-permute-start | bytes 73736 | tf_op jit(solution)/shard_map/ppermute | solution.py:377
  5.3 0.8 %copy-start.9 = (f32[72,128]{1,0:T(8,128)S(1)}, f32[72,128]{1,0:T(8,128)}, u32[]{:S(2)}) copy-start(f32[72,128]{1,0:T(8,128)} %get-tuple-element.13.lines_ref) | copy-start | bytes 110596
  6.1 2.6 %copy-start.2 = (f32[4,4096]{1,0:T(4,128)S(1)}, f32[4,4096]{1,0:T(4,128)}, u32[]{:S(2)}) copy-start(f32[4,4096]{1,0:T(4,128)} %refs_5_.2) | copy-start | bytes 196612
  6.1 2.6 %copy-start.5 = (bf16[6,16,128]{2,1,0:T(8,128)(2,1)S(1)}, bf16[6,16,128]{2,1,0:T(8,128)(2,1)}, u32[]{:S(2)}) copy-start(bf16[6,16,128]{2,1,0:T(8,128)(2,1)} %get-tuple-element.12.refs_0_) | copy-start | bytes 73732
  6.1 2.6 %copy-start.7 = (s32[8,4]{0,1:T(4,128)S(1)}, s32[8,4]{0,1:T(4,128)}, u32[]{:S(2)}) copy-start(s32[8,4]{0,1:T(4,128)} %param.15) | copy-start | bytes 388
  7.7 11.7 %copy-start.4 = (f32[3,4096]{1,0:T(4,128)S(1)}, f32[3,4096]{1,0:T(4,128)}, u32[]{:S(2)}) copy-start(f32[3,4096]{1,0:T(4,128)} %centroids_ref.2) | copy-start | bytes 147460
  9.7 12.0 %copy-start = (f32[4,1024]{1,0:T(4,128)S(1)}, f32[4,1024]{1,0:T(4,128)}, u32[]{:S(2)}) copy-start(f32[4,1024]{1,0:T(4,128)} %refs_4_.2) | copy-start | bytes 49156
  9.7 12.0 %copy-start.1 = (s32[4,1024]{1,0:T(4,128)S(1)}, s32[4,1024]{1,0:T(4,128)}, u32[]{:S(2)}) copy-start(s32[4,1024]{1,0:T(4,128)} %refs_5_.3) | copy-start | bytes 49156
  9.7 12.0 %copy-start.3 = (f32[3,4096]{1,0:T(4,128)S(1)}, f32[3,4096]{1,0:T(4,128)}, u32[]{:S(2)}) copy-start(f32[3,4096]{1,0:T(4,128)} %refs_7_.1) | copy-start | bytes 147460
  9.7 12.0 %copy-start.6 = (f32[1024]{0:T(1024)S(1)}, f32[1024]{0:T(1024)}, u32[]{:S(2)}) copy-start(f32[1024]{0:T(1024)} %param.18) | copy-start | bytes 12292
  9.8 4.0 %collective-permute-start.5 = (bf16[16,1152]{1,0:T(8,128)(2,1)S(1)}, bf16[16,1152]{1,0:T(8,128)(2,1)S(1)}, u32[]{:S(2)}, u32[]{:S(2)}) collective-permute-start(bf16[16,1152]{1,0:T(8,128)(2,1)S(1)} %get-tuple-element.14), channel_id=1, source_target_pairs={{0,2},{1,3},{2,0},{3,1},{4,6},{5,7},{6,4},{7,5},{8,10},{9,11},{10,... | collective-permute-start | bytes 110600 | tf_op jit(solution)/shard_map/ppermute | solution.py:377
  11.4 4.9 %collective-permute-start.4 = (bf16[16,1152]{1,0:T(8,128)(2,1)S(1)}, bf16[16,1152]{1,0:T(8,128)(2,1)S(1)}, u32[]{:S(2)}, u32[]{:S(2)}) collective-permute-start(bf16[16,1152]{1,0:T(8,128)(2,1)S(1)} %get-tuple-element.14), channel_id=1, source_target_pairs={{0,3},{1,2},{2,1},{3,0},{4,7},{5,6},{6,5},{7,4},{8,11},{9,10},{10,... | collective-permute-start | bytes 110600 | tf_op jit(solution)/shard_map/ppermute | solution.py:377
  12.8 4.0 %collective-permute-start.3 = (bf16[16,1152]{1,0:T(8,128)(2,1)S(1)}, bf16[16,1152]{1,0:T(8,128)(2,1)S(1)}, u32[]{:S(2)}, u32[]{:S(2)}) collective-permute-start(bf16[16,1152]{1,0:T(8,128)(2,1)S(1)} %get-tuple-element.14), channel_id=1, source_target_pairs={{0,1},{1,0},{2,3},{3,2},{4,5},{5,4},{6,7},{7,6},{8,9},{9,8},{10,11... | collective-permute-start | bytes 110600 | tf_op jit(solution)/shard_map/ppermute | solution.py:377
  16.8 10.5 %copy-start.8 = (f32[16,128]{1,0:T(8,128)S(1)}, f32[16,128]{1,0:T(8,128)}, u32[]{:S(2)}) copy-start(f32[16,128]{1,0:T(8,128)} %refs_4_.3) | copy-start | bytes 24580
  16.8 4.9 %collective-permute-start.6 = (bf16[16,1152]{1,0:T(8,128)(2,1)S(1)}, bf16[16,1152]{1,0:T(8,128)(2,1)S(1)}, u32[]{:S(2)}, u32[]{:S(2)}) collective-permute-start(bf16[16,1152]{1,0:T(8,128)(2,1)S(1)} %add_convert_fusion.refs_0_), channel_id=1, source_target_pairs={{0,4},{1,5},{2,6},{3,7},{4,0},{5,1},{6,2},{7,3},{8,12},{9,13},{10,... | collective-permute-start | bytes 110600 | tf_op jit(solution)/shard_map/ppermute | solution.py:377
  23.1 1.9 %collective-permute-start.7 = (bf16[16,128]{1,0:T(8,128)(2,1)S(1)}, bf16[16,128]{1,0:T(8,128)(2,1)S(1)}, u32[]{:S(2)}, u32[]{:S(2)}) collective-permute-start(bf16[16,128]{1,0:T(8,128)(2,1)S(1)} %get-tuple-element.18), channel_id=1, source_target_pairs={{0,8},{8,0},{16,24},{24,16},{1,9},{9,1},{17,25},{25,17},{2,10},{10... | collective-permute-start | bytes 12296 | tf_op jit(solution)/shard_map/ppermute | solution.py:377
  23.1 3.6 %collective-permute-start.8 = (bf16[16,128]{1,0:T(8,128)(2,1)S(1)}, bf16[16,128]{1,0:T(8,128)(2,1)S(1)}, u32[]{:S(2)}, u32[]{:S(2)}) collective-permute-start(bf16[16,128]{1,0:T(8,128)(2,1)S(1)} %get-tuple-element.19), channel_id=1, source_target_pairs={{0,16},{8,24},{16,0},{24,8},{1,17},{9,25},{17,1},{25,9},{2,18},{10... | collective-permute-start | bytes 12296 | tf_op jit(solution)/shard_map/ppermute | solution.py:377
  24.2 3.0 %collective-permute-start.9 = (bf16[16,128]{1,0:T(8,128)(2,1)S(1)}, bf16[16,128]{1,0:T(8,128)(2,1)S(1)}, u32[]{:S(2)}, u32[]{:S(2)}) collective-permute-start(bf16[16,128]{1,0:T(8,128)(2,1)S(1)} %get-tuple-element.20), channel_id=1, source_target_pairs={{0,24},{8,16},{16,8},{24,0},{1,25},{9,17},{17,9},{25,1},{2,26},{10... | collective-permute-start | bytes 12296 | tf_op jit(solution)/shard_map/ppermute | solution.py:377

commit v13 on v12

--- a/solution.py
+++ b/solution.py
@@ -356,7 +356,7 @@
             term = term + weight * product[a * excitations : (a + 1) * excitations, tile(k)]
         share_ref[k] = term
     me = lax.axis_index("row")
-    for step, out_ref in enumerate(out_refs):
+    for step, out_ref in zip(last_steps(count), out_refs):
         out_ref[...] = share_ref[target_of(me, step, count)].astype(out_ref.dtype)
 
 
@@ -379,6 +379,10 @@
 
 def order_of(count):
     return (0, 1, 3, 2) if count == 4 else tuple(range(count))
+
+
+def last_steps(count):
+    return (0,) + tuple(range(count - 1, 0, -1))
 
 
 def exchange(value, axis):
@@ -487,8 +491,7 @@
         ],
         compiler_params=grant((col_devices, excitations, rows_t), (rows_t, cols_t // 2), (excitations, 8 * rows_t)),
     )(*parts, halo, gram_diag, gram_off, neighbours, s_tiles, dual_moments)
-    for step in sorted(range(1, count), key=lambda step: (1 - step % 2, step)):
-        shares[step] = swap(shares[step], "row", step)
+    shares = shares[:1] + [swap(share, "row", step) for step, share in zip(last_steps(count)[1:], shares[1:])]
     march_rhs = pl.pallas_call(
         functools.partial(final_kernel, norm=norm),
         out_shape=jax.ShapeDtypeStruct(incident.shape, jnp.float32),

time: 28.1 us -> 27.5 us (0.979)
  waiting for transfers between devices: 7.26 us -> 6.72 us
    ppermute x10, waiting for transfers between devices: 7.26 us -> 6.72 us  [swap(): return lax.ppermute(value, axis, pairs)]
where the time goes in v13:
time: 27.5 us; the launch traced here: 27.3 us
  starting transfers between devices  11.2 us (41%)
  Pallas kernels  7.86 us (29%)
  waiting for transfers between devices  6.72 us (24%)
  local copies, waits for them, and re-layouts  0.82 us (3%)
  between operations  0.75 us (3%)
    ppermute x10, starting transfers between devices, swap(): return lax.ppermute(value, axis, pairs)  11.2 us
    ppermute x10, waiting for transfers between devices, swap(): return lax.ppermute(value, axis, pairs)  6.72 us
    pallas_call x1, Pallas kernels, per_device(): pl.pallas_call(s_tiles_kernel, out_shape=jax.ShapeDtypeStruct((rows_t, co...  1.65 us
    pallas_call x1, Pallas kernels, per_device(): pl.pallas_call(functools.partial(t_tiles_kernel, p_tiles=p_tiles, q_tiles...  1.64 us
    pallas_call x1, Pallas kernels, per_device(): pl.pallas_call(pack_kernel, out_shape=(jax.ShapeDtypeStruct((slots + 2, e...  1.61 us
    pallas_call x1, Pallas kernels, per_device(): pl.pallas_call(functools.partial(sweep_kernel, slots=slots, part_count=le...  1.32 us
    pallas_call x1, Pallas kernels, per_device(): pl.pallas_call(functools.partial(t_kernel, norm=norm, slots=slots, count=...  1.04 us
    unnamed x20, local copies, waits for them, and re-layouts  0.82 us
  transfers between devices with their start and end apart: 10, of which 7 were waited for; matrix products, arithmetic and copies ran while one was open for 0% of the time, Pallas kernels for 12%

profile of v13, /device:TPU:0, one launch (start us, length us, event | category | flops | bytes accessed | tf_op | source)
XLA Modules:
  0.0 27.3 jit_solution(2260524811454656108)
XLA Ops:
  0.6 1.6 %shard_map.113 = (bf16[6,16,128]{2,1,0:T(8,128)(2,1)}, f32[72,128]{1,0:T(8,128)}) custom-call(bf16[4,16,128]{2,1,0:T(8,128)(2,1)} %history_ref.1, s32[4,8]{1,0:T(4,128)} %bitcast.5, s32[4,8]{1,0:T(4,128)} %bitcast.7, f32[1,1024]{1,0:T(1,128)} %bitcast.3, f32[4,1024]{1,0:T(4,128)} %refs_4_.2, s32[4,1024]{1,0:T(4,128)} %refs_5_.3, f32[3,4096]{1,0:T(4,128)} %centroids_ref.2), custom_call_target="tpu_custom_call" | custom-call | tf_op jit(solution)/shard_map/pallas_call | solution.py:428
  2.2 2.9 %collective-permute-start.2 = (bf16[6,16,128]{2,1,0:T(8,128)(2,1)}, bf16[6,16,128]{2,1,0:T(8,128)(2,1)S(1)}, u32[]{:S(2)}, u32[]{:S(2)}) collective-permute-start(bf16[6,16,128]{2,1,0:T(8,128)(2,1)} %get-tuple-element.12.refs_0_), channel_id=1, source_target_pairs={{0,16},{8,24},{16,0},{24,8},{1,17},{9,25},{17,1},{25,9},{2,18},{10... | collective-permute-start | bytes 73736 | tf_op jit(solution)/shard_map/ppermute | solution.py:377
  5.2 0.0 collective-permute-start.1
  5.2 0.1 collective-permute-start
  5.3 0.0 copy-start.9
  5.3 0.8 %copy-done.9 = f32[72,128]{1,0:T(8,128)S(1)} copy-done((f32[72,128]{1,0:T(8,128)S(1)}, f32[72,128]{1,0:T(8,128)}, u32[]{:S(2)}) %copy-start.9) | copy-done | bytes 36888
  6.1 0.0 copy-start.2
  6.1 0.0 copy-start.5
  6.1 0.0 copy-start.7
  6.1 1.6 %shard_map.114.refs_4_ = bf16[10,512,128]{2,1,0:T(8,128)(2,1)S(1)} custom-call(f32[72,128]{1,0:T(8,128)S(1)} %copy-done.9), custom_call_target="tpu_custom_call" | custom-call | flops 8388608 | bytes 1048576 | tf_op jit(solution)/shard_map/pallas_call | solution.py:441
  7.7 0.0 copy-start.4
  7.8 0.0 collective-permute-done.2.refs_3_
  7.8 0.9 %collective-permute-done.1.refs_2_ = bf16[6,16,128]{2,1,0:T(8,128)(2,1)S(1)} collective-permute-done((bf16[6,16,128]{2,1,0:T(8,128)(2,1)}, bf16[6,16,128]{2,1,0:T(8,128)(2,1)S(1)}, u32[]{:S(2)}, u32[]{:S(2)}) %collective-permute-start.1) | collective-permute-done | bytes 24608 | tf_op jit(solution)/shard_map/ppermute | solution.py:377
  8.6 0.0 collective-permute-done.refs_1_
  8.6 0.0 copy-done.2
  8.6 0.0 copy-done.5
  8.7 0.0 copy-done.7
  8.7 1.0 %shard_map.115 = (bf16[16,1152]{1,0:T(8,128)(2,1)S(1)}, f32[2,16,128]{2,1,0:T(8,128)S(1)}) custom-call(bf16[6,16,128]{2,1,0:T(8,128)(2,1)S(1)} %copy-done.5, bf16[6,16,128]{2,1,0:T(8,128)(2,1)S(1)} %collective-permute-done.refs_1_, bf16[6,16,128]{2,1,0:T(8,128)(2,1)S(1)} %collective-permute-done.1.refs_2_, ...), custom_call_target="tpu_custom_call" | custom-call | tf_op jit(solution)/shard_map/pallas_call | solution.py:451
  9.7 0.0 copy-start
  9.7 0.0 copy-start.1
  9.7 0.0 copy-start.3
  9.7 0.0 copy-start.6
  9.8 1.6 %collective-permute-start.5 = (bf16[16,1152]{1,0:T(8,128)(2,1)S(1)}, bf16[16,1152]{1,0:T(8,128)(2,1)S(1)}, u32[]{:S(2)}, u32[]{:S(2)}) collective-permute-start(bf16[16,1152]{1,0:T(8,128)(2,1)S(1)} %get-tuple-element.14), channel_id=1, source_target_pairs={{0,2},{1,3},{2,0},{3,1},{4,6},{5,7},{6,4},{7,5},{8,10},{9,11},{10,... | collective-permute-start | bytes 110600 | tf_op jit(solution)/shard_map/ppermute | solution.py:377
  11.4 1.4 %collective-permute-start.4 = (bf16[16,1152]{1,0:T(8,128)(2,1)S(1)}, bf16[16,1152]{1,0:T(8,128)(2,1)S(1)}, u32[]{:S(2)}, u32[]{:S(2)}) collective-permute-start(bf16[16,1152]{1,0:T(8,128)(2,1)S(1)} %get-tuple-element.14), channel_id=1, source_target_pairs={{0,3},{1,2},{2,1},{3,0},{4,7},{5,6},{6,5},{7,4},{8,11},{9,10},{10,... | collective-permute-start | bytes 110600 | tf_op jit(solution)/shard_map/ppermute | solution.py:377
  12.8 0.5 %collective-permute-start.3 = (bf16[16,1152]{1,0:T(8,128)(2,1)S(1)}, bf16[16,1152]{1,0:T(8,128)(2,1)S(1)}, u32[]{:S(2)}, u32[]{:S(2)}) collective-permute-start(bf16[16,1152]{1,0:T(8,128)(2,1)S(1)} %get-tuple-element.14), channel_id=1, source_target_pairs={{0,1},{1,0},{2,3},{3,2},{4,5},{5,4},{6,7},{7,6},{8,9},{9,8},{10,11... | collective-permute-start | bytes 110600 | tf_op jit(solution)/shard_map/ppermute | solution.py:377
  13.3 0.5 %collective-permute-done.5 = bf16[16,1152]{1,0:T(8,128)(2,1)S(1)} collective-permute-done((bf16[16,1152]{1,0:T(8,128)(2,1)S(1)}, bf16[16,1152]{1,0:T(8,128)(2,1)S(1)}, u32[]{:S(2)}, u32[]{:S(2)}) %collective-permute-start.5) | collective-permute-done | bytes 36896 | tf_op jit(solution)/shard_map/ppermute | solution.py:377
  13.8 2.5 %collective-permute-done.4 = bf16[16,1152]{1,0:T(8,128)(2,1)S(1)} collective-permute-done((bf16[16,1152]{1,0:T(8,128)(2,1)S(1)}, bf16[16,1152]{1,0:T(8,128)(2,1)S(1)}, u32[]{:S(2)}, u32[]{:S(2)}) %collective-permute-start.4) | collective-permute-done | bytes 36896 | tf_op jit(solution)/shard_map/ppermute | solution.py:377
  16.3 0.5 %collective-permute-done.3 = bf16[16,1152]{1,0:T(8,128)(2,1)S(1)} collective-permute-done((bf16[16,1152]{1,0:T(8,128)(2,1)S(1)}, bf16[16,1152]{1,0:T(8,128)(2,1)S(1)}, u32[]{:S(2)}, u32[]{:S(2)}) %collective-permute-start.3) | collective-permute-done | bytes 36896 | tf_op jit(solution)/shard_map/ppermute | solution.py:377
  16.8 0.0 copy-start.8
  16.8 2.7 %collective-permute-start.6 = (bf16[16,1152]{1,0:T(8,128)(2,1)S(1)}, bf16[16,1152]{1,0:T(8,128)(2,1)S(1)}, u32[]{:S(2)}, u32[]{:S(2)}) collective-permute-start(bf16[16,1152]{1,0:T(8,128)(2,1)S(1)} %add_convert_fusion.refs_0_), channel_id=1, source_target_pairs={{0,4},{1,5},{2,6},{3,7},{4,0},{5,1},{6,2},{7,3},{8,12},{9,13},{10,... | collective-permute-start | bytes 110600 | tf_op jit(solution)/shard_map/ppermute | solution.py:377
  19.5 0.0 copy-done.4
  19.5 1.6 %shard_map.116.refs_6_ = bf16[1024,512]{1,0:T(8,128)(2,1)S(1)} custom-call(f32[3,4096]{1,0:T(4,128)S(1)} %copy-done.4), custom_call_target="tpu_custom_call" | custom-call | flops 6291456 | bytes 1048576 | tf_op jit(solution)/shard_map/pallas_call | solution.py:471
  21.1 0.6 %collective-permute-done.6.refs_1_ = bf16[16,1152]{1,0:T(8,128)(2,1)S(1)} collective-permute-done((bf16[16,1152]{1,0:T(8,128)(2,1)S(1)}, bf16[16,1152]{1,0:T(8,128)(2,1)S(1)}, u32[]{:S(2)}, u32[]{:S(2)}) %collective-permute-start.6) | collective-permute-done | bytes 36896 | tf_op jit(solution)/shard_map/ppermute | solution.py:377
  21.7 0.0 copy-done
  21.7 0.0 copy-done.1
  21.7 0.0 copy-done.3
  21.7 0.0 copy-done.6
  21.7 1.3 %shard_map.117 = (f32[16,128]{1,0:T(8,128)}, f32[16,128]{1,0:T(8,128)S(1)}, bf16[16,128]{1,0:T(8,128)(2,1)S(1)}, bf16[16,128]{1,0:T(8,128)(2,1)S(1)}, bf16[16,128]{1,0:T(8,128)(2,1)S(1)}) custom-call(bf16[16,1152]{1,0:T(8,128)(2,1)S(1)} %add_convert_fusion.refs_0_, bf16[16,1152]{1,0:T(8,128)(2,1)S(1)} %collective-permute-done.6.refs_1_, ...), custom_call_target="tpu_custom_call" | custom-call | tf_op jit(solution)/shard_map/pallas_call | solution.py:481
  23.1 0.0 collective-permute-start.7
  23.1 1.2 %collective-permute-start.8 = (bf16[16,128]{1,0:T(8,128)(2,1)S(1)}, bf16[16,128]{1,0:T(8,128)(2,1)S(1)}, u32[]{:S(2)}, u32[]{:S(2)}) collective-permute-start(bf16[16,128]{1,0:T(8,128)(2,1)S(1)} %get-tuple-element.19), channel_id=1, source_target_pairs={{0,16},{8,24},{16,0},{24,8},{1,17},{9,25},{17,1},{25,9},{2,18},{10... | collective-permute-start | bytes 12296 | tf_op jit(solution)/shard_map/ppermute | solution.py:377
  24.2 0.7 %collective-permute-start.9 = (bf16[16,128]{1,0:T(8,128)(2,1)S(1)}, bf16[16,128]{1,0:T(8,128)(2,1)S(1)}, u32[]{:S(2)}, u32[]{:S(2)}) collective-permute-start(bf16[16,128]{1,0:T(8,128)(2,1)S(1)} %get-tuple-element.20), channel_id=1, source_target_pairs={{0,8},{8,0},{16,24},{24,16},{1,9},{9,1},{17,25},{25,17},{2,10},{10... | collective-permute-start | bytes 12296 | tf_op jit(solution)/shard_map/ppermute | solution.py:377
  24.9 1.2 %collective-permute-done.7.refs_1_ = bf16[16,128]{1,0:T(8,128)(2,1)S(1)} collective-permute-done((bf16[16,128]{1,0:T(8,128)(2,1)S(1)}, bf16[16,128]{1,0:T(8,128)(2,1)S(1)}, u32[]{:S(2)}, u32[]{:S(2)}) %collective-permute-start.7) | collective-permute-done | bytes 4128 | tf_op jit(solution)/shard_map/ppermute | solution.py:377
  26.1 0.6 %collective-permute-done.8.refs_2_ = bf16[16,128]{1,0:T(8,128)(2,1)S(1)} collective-permute-done((bf16[16,128]{1,0:T(8,128)(2,1)S(1)}, bf16[16,128]{1,0:T(8,128)(2,1)S(1)}, u32[]{:S(2)}, u32[]{:S(2)}) %collective-permute-start.8) | collective-permute-done | bytes 4128 | tf_op jit(solution)/shard_map/ppermute | solution.py:377
  26.7 0.0 collective-permute-done.9.refs_3_
  26.7 0.0 copy-done.8
  26.7 0.6 %shard_map.118 = f32[16,128]{1,0:T(8,128)} custom-call(f32[16,128]{1,0:T(8,128)S(1)} %get-tuple-element.17.refs_0_, bf16[16,128]{1,0:T(8,128)(2,1)S(1)} %collective-permute-done.7.refs_1_, bf16[16,128]{1,0:T(8,128)(2,1)S(1)} %collective-permute-done.8.refs_2_, bf16[16,128]{1,0:T(8,128)(2,1)S(1)} %collective-permute-done.9.refs_3_, f32[16,128]{1,0:T(8,128)S(1)} %copy-done.8), custom_call_target="tpu_custom_call" | custom-call | tf_op jit(solution)/shard_map/pallas_call | solution.py:495
  (1 shorter events, 0.0 us)
Async XLA Ops:
  2.2 5.5 %collective-permute-start.2 = (bf16[6,16,128]{2,1,0:T(8,128)(2,1)}, bf16[6,16,128]{2,1,0:T(8,128)(2,1)S(1)}, u32[]{:S(2)}, u32[]{:S(2)}) collective-permute-start(bf16[6,16,128]{2,1,0:T(8,128)(2,1)} %get-tuple-element.12.refs_0_), channel_id=1, source_target_pairs={{0,16},{8,24},{16,0},{24,8},{1,17},{9,25},{17,1},{25,9},{2,18},{10... | collective-permute-start | bytes 73736 | tf_op jit(solution)/shard_map/ppermute | solution.py:377
  5.2 3.5 %collective-permute-start.1 = (bf16[6,16,128]{2,1,0:T(8,128)(2,1)}, bf16[6,16,128]{2,1,0:T(8,128)(2,1)S(1)}, u32[]{:S(2)}, u32[]{:S(2)}) collective-permute-start(bf16[6,16,128]{2,1,0:T(8,128)(2,1)} %get-tuple-element.12.refs_0_), channel_id=1, source_target_pairs={{0,24},{8,16},{16,8},{24,0},{1,25},{9,17},{17,9},{25,1},{2,26},{10... | collective-permute-start | bytes 73736 | tf_op jit(solution)/shard_map/ppermute | solution.py:377
  5.2 3.5 %collective-permute-start = (bf16[6,16,128]{2,1,0:T(8,128)(2,1)}, bf16[6,16,128]{2,1,0:T(8,128)(2,1)S(1)}, u32[]{:S(2)}, u32[]{:S(2)}) collective-permute-start(bf16[6,16,128]{2,1,0:T(8,128)(2,1)} %get-tuple-element.12.refs_0_), channel_id=1, source_target_pairs={{0,8},{8,0},{16,24},{24,16},{1,9},{9,1},{17,25},{25,17},{2,10},{10... | collective-permute-start | bytes 73736 | tf_op jit(solution)/shard_map/ppermute | solution.py:377
  5.3 0.8 %copy-start.9 = (f32[72,128]{1,0:T(8,128)S(1)}, f32[72,128]{1,0:T(8,128)}, u32[]{:S(2)}) copy-start(f32[72,128]{1,0:T(8,128)} %get-tuple-element.13.lines_ref) | copy-start | bytes 110596
  6.1 2.6 %copy-start.2 = (f32[4,4096]{1,0:T(4,128)S(1)}, f32[4,4096]{1,0:T(4,128)}, u32[]{:S(2)}) copy-start(f32[4,4096]{1,0:T(4,128)} %refs_5_.2) | copy-start | bytes 196612
  6.1 2.6 %copy-start.5 = (bf16[6,16,128]{2,1,0:T(8,128)(2,1)S(1)}, bf16[6,16,128]{2,1,0:T(8,128)(2,1)}, u32[]{:S(2)}) copy-start(bf16[6,16,128]{2,1,0:T(8,128)(2,1)} %get-tuple-element.12.refs_0_) | copy-start | bytes 73732
  6.1 2.6 %copy-start.7 = (s32[8,4]{0,1:T(4,128)S(1)}, s32[8,4]{0,1:T(4,128)}, u32[]{:S(2)}) copy-start(s32[8,4]{0,1:T(4,128)} %param.15) | copy-start | bytes 388
  7.7 11.7 %copy-start.4 = (f32[3,4096]{1,0:T(4,128)S(1)}, f32[3,4096]{1,0:T(4,128)}, u32[]{:S(2)}) copy-start(f32[3,4096]{1,0:T(4,128)} %centroids_ref.2) | copy-start | bytes 147460
  9.7 12.0 %copy-start = (f32[4,1024]{1,0:T(4,128)S(1)}, f32[4,1024]{1,0:T(4,128)}, u32[]{:S(2)}) copy-start(f32[4,1024]{1,0:T(4,128)} %refs_4_.2) | copy-start | bytes 49156
  9.7 12.0 %copy-start.1 = (s32[4,1024]{1,0:T(4,128)S(1)}, s32[4,1024]{1,0:T(4,128)}, u32[]{:S(2)}) copy-start(s32[4,1024]{1,0:T(4,128)} %refs_5_.3) | copy-start | bytes 49156
  9.7 12.0 %copy-start.3 = (f32[3,4096]{1,0:T(4,128)S(1)}, f32[3,4096]{1,0:T(4,128)}, u32[]{:S(2)}) copy-start(f32[3,4096]{1,0:T(4,128)} %refs_7_.1) | copy-start | bytes 147460
  9.7 12.0 %copy-start.6 = (f32[1024]{0:T(1024)S(1)}, f32[1024]{0:T(1024)}, u32[]{:S(2)}) copy-start(f32[1024]{0:T(1024)} %param.18) | copy-start | bytes 12292
  9.8 4.0 %collective-permute-start.5 = (bf16[16,1152]{1,0:T(8,128)(2,1)S(1)}, bf16[16,1152]{1,0:T(8,128)(2,1)S(1)}, u32[]{:S(2)}, u32[]{:S(2)}) collective-permute-start(bf16[16,1152]{1,0:T(8,128)(2,1)S(1)} %get-tuple-element.14), channel_id=1, source_target_pairs={{0,2},{1,3},{2,0},{3,1},{4,6},{5,7},{6,4},{7,5},{8,10},{9,11},{10,... | collective-permute-start | bytes 110600 | tf_op jit(solution)/shard_map/ppermute | solution.py:377
  11.4 4.9 %collective-permute-start.4 = (bf16[16,1152]{1,0:T(8,128)(2,1)S(1)}, bf16[16,1152]{1,0:T(8,128)(2,1)S(1)}, u32[]{:S(2)}, u32[]{:S(2)}) collective-permute-start(bf16[16,1152]{1,0:T(8,128)(2,1)S(1)} %get-tuple-element.14), channel_id=1, source_target_pairs={{0,3},{1,2},{2,1},{3,0},{4,7},{5,6},{6,5},{7,4},{8,11},{9,10},{10,... | collective-permute-start | bytes 110600 | tf_op jit(solution)/shard_map/ppermute | solution.py:377
  12.8 4.0 %collective-permute-start.3 = (bf16[16,1152]{1,0:T(8,128)(2,1)S(1)}, bf16[16,1152]{1,0:T(8,128)(2,1)S(1)}, u32[]{:S(2)}, u32[]{:S(2)}) collective-permute-start(bf16[16,1152]{1,0:T(8,128)(2,1)S(1)} %get-tuple-element.14), channel_id=1, source_target_pairs={{0,1},{1,0},{2,3},{3,2},{4,5},{5,4},{6,7},{7,6},{8,9},{9,8},{10,11... | collective-permute-start | bytes 110600 | tf_op jit(solution)/shard_map/ppermute | solution.py:377
  16.8 9.9 %copy-start.8 = (f32[16,128]{1,0:T(8,128)S(1)}, f32[16,128]{1,0:T(8,128)}, u32[]{:S(2)}) copy-start(f32[16,128]{1,0:T(8,128)} %refs_4_.3) | copy-start | bytes 24580
  16.8 4.9 %collective-permute-start.6 = (bf16[16,1152]{1,0:T(8,128)(2,1)S(1)}, bf16[16,1152]{1,0:T(8,128)(2,1)S(1)}, u32[]{:S(2)}, u32[]{:S(2)}) collective-permute-start(bf16[16,1152]{1,0:T(8,128)(2,1)S(1)} %add_convert_fusion.refs_0_), channel_id=1, source_target_pairs={{0,4},{1,5},{2,6},{3,7},{4,0},{5,1},{6,2},{7,3},{8,12},{9,13},{10,... | collective-permute-start | bytes 110600 | tf_op jit(solution)/shard_map/ppermute | solution.py:377
  23.1 3.0 %collective-permute-start.7 = (bf16[16,128]{1,0:T(8,128)(2,1)S(1)}, bf16[16,128]{1,0:T(8,128)(2,1)S(1)}, u32[]{:S(2)}, u32[]{:S(2)}) collective-permute-start(bf16[16,128]{1,0:T(8,128)(2,1)S(1)} %get-tuple-element.18), channel_id=1, source_target_pairs={{0,24},{8,16},{16,8},{24,0},{1,25},{9,17},{17,9},{25,1},{2,26},{10... | collective-permute-start | bytes 12296 | tf_op jit(solution)/shard_map/ppermute | solution.py:377
  23.1 3.6 %collective-permute-start.8 = (bf16[16,128]{1,0:T(8,128)(2,1)S(1)}, bf16[16,128]{1,0:T(8,128)(2,1)S(1)}, u32[]{:S(2)}, u32[]{:S(2)}) collective-permute-start(bf16[16,128]{1,0:T(8,128)(2,1)S(1)} %get-tuple-element.19), channel_id=1, source_target_pairs={{0,16},{8,24},{16,0},{24,8},{1,17},{9,25},{17,1},{25,9},{2,18},{10... | collective-permute-start | bytes 12296 | tf_op jit(solution)/shard_map/ppermute | solution.py:377
  24.2 2.5 %collective-permute-start.9 = (bf16[16,128]{1,0:T(8,128)(2,1)S(1)}, bf16[16,128]{1,0:T(8,128)(2,1)S(1)}, u32[]{:S(2)}, u32[]{:S(2)}) collective-permute-start(bf16[16,128]{1,0:T(8,128)(2,1)S(1)} %get-tuple-element.20), channel_id=1, source_target_pairs={{0,8},{8,0},{16,24},{24,16},{1,9},{9,1},{17,25},{25,17},{2,10},{10... | collective-permute-start | bytes 12296 | tf_op jit(solution)/shard_map/ppermute | solution.py:377

commit v14 on v13

--- a/solution.py
+++ b/solution.py
@@ -21,6 +21,7 @@
 
 VMEM = pl.BlockSpec(memory_space=pltpu.VMEM)
 SMEM = pl.BlockSpec(memory_space=pltpu.SMEM)
+ANY = pl.BlockSpec(memory_space=pl.ANY)
 LOG2_E = 1.4426950408889634
 TINY = 1e-30
 MIB = 1024 * 1024
@@ -59,11 +60,9 @@
     return jnp.where(lane_ids() < HALF, first, last)
 
 
-def split3(value):
+def split2(value):
     high = value.astype(jnp.bfloat16).astype(jnp.float32)
-    rest = value - high
-    middle = rest.astype(jnp.bfloat16).astype(jnp.float32)
-    return [high, middle, rest - middle]
+    return [high, value - high]
 
 
 def stack_rows(rows, height):
@@ -74,8 +73,30 @@
     return out
 
 
-def pack_kernel(history_ref, shell_ref, near_ref, diag_ref, off_ref, links_ref, centroids_ref, out_ref, lines_ref):
-    slots, excitations = history_ref.shape[:2]
+def pack_kernel(
+    history_in, shell_in, near_in, diag_in, off_in, links_in, centroids_in, out_any, lines_any,
+    shell_ref, near_ref, diag_ref, off_ref, links_ref, centroids_ref, edge_ref, lines_ref, sems,
+):
+    slots, excitations = history_in.shape[:2]
+    pairs = (
+        (centroids_in, centroids_ref),
+        (near_in, near_ref),
+        (shell_in, shell_ref),
+        (links_in, links_ref),
+        (diag_in, diag_ref),
+        (off_in, off_ref),
+        (history_in, out_any.at[pl.ds(0, slots)]),
+        (edge_ref, out_any.at[pl.ds(slots, 1)]),
+        (lines_ref, lines_any),
+    )
+    *reads, history_copy, edge_copy, lines_copy = [
+        pltpu.make_async_copy(source, target, sems.at[k]) for k, (source, target) in enumerate(pairs)
+    ]
+    for read in reads:
+        read.start()
+    history_copy.start()
+    for read in reads:
+        read.wait()
     length = diag_ref.shape[1]
     tiles = shell_ref.shape[1]
     lanes = lane_ids()
@@ -89,13 +110,11 @@
     here = lax.axis_index("row") * length + jnp.where(lanes < HALF, lanes, length - LANES + lanes)
     for m in range(links_ref.shape[0]):
         rows.append((edges(links_ref, m, length) - here).astype(jnp.float32))
-    rows += split3(edges(diag_ref, 0, length))
-    coupling = []
+    rows += split2(edges(diag_ref, 0, length))
     for m in range(off_ref.shape[0]):
-        coupling += split3(edges(off_ref, m, length))
-    out_ref[:slots] = history_ref[...]
-    out_ref[slots] = stack_rows(rows, excitations).astype(jnp.bfloat16)
-    out_ref[slots + 1] = stack_rows(coupling, excitations).astype(jnp.bfloat16)
+        rows += split2(edges(off_ref, m, length))
+    edge_ref[0] = stack_rows(rows, excitations).astype(jnp.bfloat16)
+    edge_copy.start()
     me = lax.axis_index("row")
     row_start = me * length
     q_tiles = shell_ref.shape[0]
@@ -117,6 +136,10 @@
             gain = NEAR_GAIN * near_ref[sources[i], t].astype(jnp.float32)
             lines_ref[row : row + 1] = jnp.full((1, LANES), gain, jnp.float32)
             row += 1
+    lines_copy.start()
+    history_copy.wait()
+    edge_copy.wait()
+    lines_copy.wait()
 
 
 def target_of(me, step, count):
@@ -303,11 +326,11 @@
     lanes = lane_ids()
     low = lanes < HALF
 
-    def halo(plane, row):
-        return halo_ref[plane, row : row + 1]
-
-    def sum3(plane, row):
-        return halo(plane, row) + halo(plane, row + 1) + halo(plane, row + 2)
+    def halo(row):
+        return halo_ref[0, row : row + 1]
+
+    def sum2(row):
+        return halo(row) + halo(row + 1)
 
     def tile(t):
         return slice(t * LANES, (t + 1) * LANES)
@@ -318,7 +341,7 @@
         for part in parts[1:]:
             total = total + part[:, tile(t)].astype(jnp.float32)
         field.append(total)
-        diag.append(diag_ref[:, tile(t)] if t < tiles else sum3(0, 2 + link_count))
+        diag.append(diag_ref[:, tile(t)] if t < tiles else sum2(2 + link_count))
 
     dual = [f / d for f, d in zip(field, diag)]
     for sweep_id in range(SWEEPS):
@@ -332,8 +355,8 @@
                     source = links_ref[m : m + 1, tile(t)] - (row_start + t * LANES)
                     gram = off_ref[m : m + 1, tile(t)]
                 else:
-                    source = halo(0, 2 + m).astype(jnp.int32) + lanes
-                    gram = sum3(1, 3 * m)
+                    source = halo(2 + m).astype(jnp.int32) + lanes
+                    gram = sum2(4 + link_count + 2 * m)
                 inside = (source >= 0) & (source < LANES)
                 index = jnp.broadcast_to(source & (LANES - 1), (excitations, LANES))
                 here = jnp.take_along_axis(dual[t], index, axis=1)
@@ -428,11 +451,22 @@
     packed, lines = pl.pallas_call(
         pack_kernel,
         out_shape=(
-            jax.ShapeDtypeStruct((slots + 2, excitations, shard_len), jnp.bfloat16),
+            jax.ShapeDtypeStruct((slots + 1, excitations, shard_len), jnp.bfloat16),
             jax.ShapeDtypeStruct((line_rows, LANES), jnp.float32),
         ),
-        in_specs=[VMEM, SMEM, SMEM, VMEM, VMEM, VMEM, VMEM],
-        out_specs=(VMEM, VMEM),
+        in_specs=[ANY] * 7,
+        out_specs=(ANY, ANY),
+        scratch_shapes=[
+            pltpu.SMEM(shell.shape, jnp.int32),
+            pltpu.SMEM(shell.shape, jnp.int32),
+            pltpu.VMEM(gram_diag.shape, jnp.float32),
+            pltpu.VMEM(gram_off.shape, jnp.float32),
+            pltpu.VMEM(neighbours.shape, jnp.int32),
+            pltpu.VMEM(centroids.shape, jnp.float32),
+            pltpu.VMEM((1, excitations, LANES), jnp.bfloat16),
+            pltpu.VMEM((line_rows, LANES), jnp.float32),
+            pltpu.SemaphoreType.DMA((9,)),
+        ],
         compiler_params=pltpu.CompilerParams(vmem_limit_bytes=56 * MIB),
     )(history, shell, near_mask, gram_diag, gram_off, neighbours, centroids)
     count = lax.axis_size("row")
@@ -452,13 +486,13 @@
         functools.partial(t_kernel, norm=norm, slots=slots, count=count),
         out_shape=(
             jax.ShapeDtypeStruct((excitations, rows_t + LANES), jnp.bfloat16),
-            jax.ShapeDtypeStruct((2, excitations, LANES), jnp.float32),
+            jax.ShapeDtypeStruct((1, excitations, LANES), jnp.float32),
         ),
         in_specs=[VMEM] * (count + 2) + [SMEM],
         out_specs=(VMEM, VMEM),
         scratch_shapes=[
             pltpu.VMEM((slots + 2, moments.shape[0] * excitations, cols_t), jnp.bfloat16),
-            pltpu.VMEM((count, 2, excitations, LANES), jnp.float32),
+            pltpu.VMEM((count, 1, excitations, LANES), jnp.float32),
         ],
         compiler_params=grant(
             (p_tiles + 2, cols_t // 2, LANES),

time: 27.5 us -> 27.7 us (level)
  no operation moved by 1% of the time
where the time goes in v14:
time: 27.7 us; the launch traced here: 27.4 us
  starting transfers between devices  11.3 us (41%)
  Pallas kernels  7.95 us (29%)
  waiting for transfers between devices  6.64 us (24%)
  local copies, waits for them, and re-layouts  0.82 us (3%)
  between operations  0.75 us (3%)
    ppermute x10, starting transfers between devices, swap(): return lax.ppermute(value, axis, pairs)  11.3 us
    ppermute x10, waiting for transfers between devices, swap(): return lax.ppermute(value, axis, pairs)  6.64 us
    pallas_call x1, Pallas kernels, per_device(): pl.pallas_call(pack_kernel, out_shape=(jax.ShapeDtypeStruct((slots + 1, e...  1.69 us
    pallas_call x1, Pallas kernels, per_device(): pl.pallas_call(s_tiles_kernel, out_shape=jax.ShapeDtypeStruct((rows_t, co...  1.65 us
    pallas_call x1, Pallas kernels, per_device(): pl.pallas_call(functools.partial(t_tiles_kernel, p_tiles=p_tiles, q_tiles...  1.64 us
    pallas_call x1, Pallas kernels, per_device(): pl.pallas_call(functools.partial(sweep_kernel, slots=slots, part_count=le...  1.31 us
    pallas_call x1, Pallas kernels, per_device(): pl.pallas_call(functools.partial(t_kernel, norm=norm, slots=slots, count=...  1.05 us
    unnamed x20, local copies, waits for them, and re-layouts  0.82 us
  transfers between devices with their start and end apart: 10, of which 7 were waited for; matrix products, arithmetic and copies ran while one was open for 0% of the time, Pallas kernels for 12%

profile of v14, /device:TPU:0, one launch (start us, length us, event | category | flops | bytes accessed | tf_op | source)
XLA Modules:
  0.0 27.4 jit_solution(14398014195492384056)
XLA Ops:
  0.6 1.7 %shard_map.113 = (bf16[5,16,128]{2,1,0:T(8,128)(2,1)}, f32[72,128]{1,0:T(8,128)}) custom-call(bf16[4,16,128]{2,1,0:T(8,128)(2,1)} %history_in.1, s32[4,8]{1,0:T(4,128)} %bitcast.5, s32[4,8]{1,0:T(4,128)} %bitcast.7, f32[1,1024]{1,0:T(1,128)} %bitcast.3, f32[4,1024]{1,0:T(4,128)} %refs_4_.2, s32[4,1024]{1,0:T(4,128)} %refs_5_.3, f32[3,4096]{1,0:T(4,128)} %centroids_ref), custom_call_target="tpu_custom_call" | custom-call | tf_op jit(solution)/shard_map/pallas_call | solution.py:451
  2.3 3.0 %collective-permute-start.2 = (bf16[5,16,128]{2,1,0:T(8,128)(2,1)}, bf16[5,16,128]{2,1,0:T(8,128)(2,1)S(1)}, u32[]{:S(2)}, u32[]{:S(2)}) collective-permute-start(bf16[5,16,128]{2,1,0:T(8,128)(2,1)} %get-tuple-element.12.refs_0_), channel_id=1, source_target_pairs={{0,16},{8,24},{16,0},{24,8},{1,17},{9,25},{17,1},{25,9},{2,18},{10... | collective-permute-start | bytes 61448 | tf_op jit(solution)/shard_map/ppermute | solution.py:400
  5.3 0.0 collective-permute-start.1
  5.3 0.2 collective-permute-start
  5.5 0.0 copy-start.9
  5.5 0.8 %copy-done.9 = f32[72,128]{1,0:T(8,128)S(1)} copy-done((f32[72,128]{1,0:T(8,128)S(1)}, f32[72,128]{1,0:T(8,128)}, u32[]{:S(2)}) %copy-start.9) | copy-done | bytes 36888
  6.3 0.0 copy-start.2
  6.3 0.0 copy-start.5
  6.3 0.0 copy-start.7
  6.3 1.6 %shard_map.114.refs_4_ = bf16[10,512,128]{2,1,0:T(8,128)(2,1)S(1)} custom-call(f32[72,128]{1,0:T(8,128)S(1)} %copy-done.9), custom_call_target="tpu_custom_call" | custom-call | flops 8388608 | bytes 1048576 | tf_op jit(solution)/shard_map/pallas_call | solution.py:475
  7.9 0.0 copy-start.4
  8.0 0.0 collective-permute-done.2.refs_3_
  8.0 0.8 %collective-permute-done.1.refs_2_ = bf16[5,16,128]{2,1,0:T(8,128)(2,1)S(1)} collective-permute-done((bf16[5,16,128]{2,1,0:T(8,128)(2,1)}, bf16[5,16,128]{2,1,0:T(8,128)(2,1)S(1)}, u32[]{:S(2)}, u32[]{:S(2)}) %collective-permute-start.1) | collective-permute-done | bytes 20512 | tf_op jit(solution)/shard_map/ppermute | solution.py:400
  8.7 0.0 collective-permute-done.refs_1_
  8.8 0.0 copy-done.2
  8.8 0.0 copy-done.5
  8.8 0.0 copy-done.7
  8.8 1.1 %shard_map.115 = (bf16[16,1152]{1,0:T(8,128)(2,1)S(1)}, f32[1,16,128]{2,1,0:T(8,128)S(1)}) custom-call(bf16[5,16,128]{2,1,0:T(8,128)(2,1)S(1)} %copy-done.5, bf16[5,16,128]{2,1,0:T(8,128)(2,1)S(1)} %collective-permute-done.refs_1_, bf16[5,16,128]{2,1,0:T(8,128)(2,1)S(1)} %collective-permute-done.1.refs_2_, ...), custom_call_target="tpu_custom_call" | custom-call | tf_op jit(solution)/shard_map/pallas_call | solution.py:485
  9.8 0.0 copy-start
  9.8 0.0 copy-start.1
  9.9 0.0 copy-start.3
  9.9 0.0 copy-start.6
  9.9 1.6 %collective-permute-start.5 = (bf16[16,1152]{1,0:T(8,128)(2,1)S(1)}, bf16[16,1152]{1,0:T(8,128)(2,1)S(1)}, u32[]{:S(2)}, u32[]{:S(2)}) collective-permute-start(bf16[16,1152]{1,0:T(8,128)(2,1)S(1)} %get-tuple-element.14), channel_id=1, source_target_pairs={{0,2},{1,3},{2,0},{3,1},{4,6},{5,7},{6,4},{7,5},{8,10},{9,11},{10,... | collective-permute-start | bytes 110600 | tf_op jit(solution)/shard_map/ppermute | solution.py:400
  11.5 1.4 %collective-permute-start.4 = (bf16[16,1152]{1,0:T(8,128)(2,1)S(1)}, bf16[16,1152]{1,0:T(8,128)(2,1)S(1)}, u32[]{:S(2)}, u32[]{:S(2)}) collective-permute-start(bf16[16,1152]{1,0:T(8,128)(2,1)S(1)} %get-tuple-element.14), channel_id=1, source_target_pairs={{0,3},{1,2},{2,1},{3,0},{4,7},{5,6},{6,5},{7,4},{8,11},{9,10},{10,... | collective-permute-start | bytes 110600 | tf_op jit(solution)/shard_map/ppermute | solution.py:400
  12.9 0.5 %collective-permute-start.3 = (bf16[16,1152]{1,0:T(8,128)(2,1)S(1)}, bf16[16,1152]{1,0:T(8,128)(2,1)S(1)}, u32[]{:S(2)}, u32[]{:S(2)}) collective-permute-start(bf16[16,1152]{1,0:T(8,128)(2,1)S(1)} %get-tuple-element.14), channel_id=1, source_target_pairs={{0,1},{1,0},{2,3},{3,2},{4,5},{5,4},{6,7},{7,6},{8,9},{9,8},{10,11... | collective-permute-start | bytes 110600 | tf_op jit(solution)/shard_map/ppermute | solution.py:400
  13.4 0.5 %collective-permute-done.5 = bf16[16,1152]{1,0:T(8,128)(2,1)S(1)} collective-permute-done((bf16[16,1152]{1,0:T(8,128)(2,1)S(1)}, bf16[16,1152]{1,0:T(8,128)(2,1)S(1)}, u32[]{:S(2)}, u32[]{:S(2)}) %collective-permute-start.5) | collective-permute-done | bytes 36896 | tf_op jit(solution)/shard_map/ppermute | solution.py:400
  13.9 2.5 %collective-permute-done.4 = bf16[16,1152]{1,0:T(8,128)(2,1)S(1)} collective-permute-done((bf16[16,1152]{1,0:T(8,128)(2,1)S(1)}, bf16[16,1152]{1,0:T(8,128)(2,1)S(1)}, u32[]{:S(2)}, u32[]{:S(2)}) %collective-permute-start.4) | collective-permute-done | bytes 36896 | tf_op jit(solution)/shard_map/ppermute | solution.py:400
  16.4 0.5 %collective-permute-done.3 = bf16[16,1152]{1,0:T(8,128)(2,1)S(1)} collective-permute-done((bf16[16,1152]{1,0:T(8,128)(2,1)S(1)}, bf16[16,1152]{1,0:T(8,128)(2,1)S(1)}, u32[]{:S(2)}, u32[]{:S(2)}) %collective-permute-start.3) | collective-permute-done | bytes 36896 | tf_op jit(solution)/shard_map/ppermute | solution.py:400
  16.9 0.0 copy-start.8
  16.9 2.6 %collective-permute-start.6 = (bf16[16,1152]{1,0:T(8,128)(2,1)S(1)}, bf16[16,1152]{1,0:T(8,128)(2,1)S(1)}, u32[]{:S(2)}, u32[]{:S(2)}) collective-permute-start(bf16[16,1152]{1,0:T(8,128)(2,1)S(1)} %add_convert_fusion.refs_0_), channel_id=1, source_target_pairs={{0,4},{1,5},{2,6},{3,7},{4,0},{5,1},{6,2},{7,3},{8,12},{9,13},{10,... | collective-permute-start | bytes 110600 | tf_op jit(solution)/shard_map/ppermute | solution.py:400
  19.6 0.0 copy-done.4
  19.6 1.6 %shard_map.116.refs_6_ = bf16[1024,512]{1,0:T(8,128)(2,1)S(1)} custom-call(f32[3,4096]{1,0:T(4,128)S(1)} %copy-done.4), custom_call_target="tpu_custom_call" | custom-call | flops 6291456 | bytes 1048576 | tf_op jit(solution)/shard_map/pallas_call | solution.py:505
  21.2 0.6 %collective-permute-done.6.refs_1_ = bf16[16,1152]{1,0:T(8,128)(2,1)S(1)} collective-permute-done((bf16[16,1152]{1,0:T(8,128)(2,1)S(1)}, bf16[16,1152]{1,0:T(8,128)(2,1)S(1)}, u32[]{:S(2)}, u32[]{:S(2)}) %collective-permute-start.6) | collective-permute-done | bytes 36896 | tf_op jit(solution)/shard_map/ppermute | solution.py:400
  21.8 0.0 copy-done
  21.9 0.0 copy-done.1
  21.9 0.0 copy-done.3
  21.9 0.0 copy-done.6
  21.9 1.3 %shard_map.117 = (f32[16,128]{1,0:T(8,128)}, f32[16,128]{1,0:T(8,128)S(1)}, bf16[16,128]{1,0:T(8,128)(2,1)S(1)}, bf16[16,128]{1,0:T(8,128)(2,1)S(1)}, bf16[16,128]{1,0:T(8,128)(2,1)S(1)}) custom-call(bf16[16,1152]{1,0:T(8,128)(2,1)S(1)} %add_convert_fusion.refs_0_, bf16[16,1152]{1,0:T(8,128)(2,1)S(1)} %collective-permute-done.6.refs_1_, ...), custom_call_target="tpu_custom_call" | custom-call | tf_op jit(solution)/shard_map/pallas_call | solution.py:515
  23.2 0.0 collective-permute-start.7
  23.2 1.2 %collective-permute-start.8 = (bf16[16,128]{1,0:T(8,128)(2,1)S(1)}, bf16[16,128]{1,0:T(8,128)(2,1)S(1)}, u32[]{:S(2)}, u32[]{:S(2)}) collective-permute-start(bf16[16,128]{1,0:T(8,128)(2,1)S(1)} %get-tuple-element.19), channel_id=1, source_target_pairs={{0,16},{8,24},{16,0},{24,8},{1,17},{9,25},{17,1},{25,9},{2,18},{10... | collective-permute-start | bytes 12296 | tf_op jit(solution)/shard_map/ppermute | solution.py:400
  24.4 0.6 %collective-permute-start.9 = (bf16[16,128]{1,0:T(8,128)(2,1)S(1)}, bf16[16,128]{1,0:T(8,128)(2,1)S(1)}, u32[]{:S(2)}, u32[]{:S(2)}) collective-permute-start(bf16[16,128]{1,0:T(8,128)(2,1)S(1)} %get-tuple-element.20), channel_id=1, source_target_pairs={{0,8},{8,0},{16,24},{24,16},{1,9},{9,1},{17,25},{25,17},{2,10},{10... | collective-permute-start | bytes 12296 | tf_op jit(solution)/shard_map/ppermute | solution.py:400
  25.0 1.2 %collective-permute-done.7.refs_1_ = bf16[16,128]{1,0:T(8,128)(2,1)S(1)} collective-permute-done((bf16[16,128]{1,0:T(8,128)(2,1)S(1)}, bf16[16,128]{1,0:T(8,128)(2,1)S(1)}, u32[]{:S(2)}, u32[]{:S(2)}) %collective-permute-start.7) | collective-permute-done | bytes 4128 | tf_op jit(solution)/shard_map/ppermute | solution.py:400
  26.2 0.6 %collective-permute-done.8.refs_2_ = bf16[16,128]{1,0:T(8,128)(2,1)S(1)} collective-permute-done((bf16[16,128]{1,0:T(8,128)(2,1)S(1)}, bf16[16,128]{1,0:T(8,128)(2,1)S(1)}, u32[]{:S(2)}, u32[]{:S(2)}) %collective-permute-start.8) | collective-permute-done | bytes 4128 | tf_op jit(solution)/shard_map/ppermute | solution.py:400
  26.8 0.0 collective-permute-done.9.refs_3_
  26.8 0.0 copy-done.8
  26.8 0.6 %shard_map.118 = f32[16,128]{1,0:T(8,128)} custom-call(f32[16,128]{1,0:T(8,128)S(1)} %get-tuple-element.17.refs_0_, bf16[16,128]{1,0:T(8,128)(2,1)S(1)} %collective-permute-done.7.refs_1_, bf16[16,128]{1,0:T(8,128)(2,1)S(1)} %collective-permute-done.8.refs_2_, bf16[16,128]{1,0:T(8,128)(2,1)S(1)} %collective-permute-done.9.refs_3_, f32[16,128]{1,0:T(8,128)S(1)} %copy-done.8), custom_call_target="tpu_custom_call" | custom-call | tf_op jit(solution)/shard_map/pallas_call | solution.py:529
  (1 shorter events, 0.0 us)
Async XLA Ops:
  2.3 5.6 %collective-permute-start.2 = (bf16[5,16,128]{2,1,0:T(8,128)(2,1)}, bf16[5,16,128]{2,1,0:T(8,128)(2,1)S(1)}, u32[]{:S(2)}, u32[]{:S(2)}) collective-permute-start(bf16[5,16,128]{2,1,0:T(8,128)(2,1)} %get-tuple-element.12.refs_0_), channel_id=1, source_target_pairs={{0,16},{8,24},{16,0},{24,8},{1,17},{9,25},{17,1},{25,9},{2,18},{10... | collective-permute-start | bytes 61448 | tf_op jit(solution)/shard_map/ppermute | solution.py:400
  5.3 3.4 %collective-permute-start.1 = (bf16[5,16,128]{2,1,0:T(8,128)(2,1)}, bf16[5,16,128]{2,1,0:T(8,128)(2,1)S(1)}, u32[]{:S(2)}, u32[]{:S(2)}) collective-permute-start(bf16[5,16,128]{2,1,0:T(8,128)(2,1)} %get-tuple-element.12.refs_0_), channel_id=1, source_target_pairs={{0,24},{8,16},{16,8},{24,0},{1,25},{9,17},{17,9},{25,1},{2,26},{10... | collective-permute-start | bytes 61448 | tf_op jit(solution)/shard_map/ppermute | solution.py:400
  5.3 3.4 %collective-permute-start = (bf16[5,16,128]{2,1,0:T(8,128)(2,1)}, bf16[5,16,128]{2,1,0:T(8,128)(2,1)S(1)}, u32[]{:S(2)}, u32[]{:S(2)}) collective-permute-start(bf16[5,16,128]{2,1,0:T(8,128)(2,1)} %get-tuple-element.12.refs_0_), channel_id=1, source_target_pairs={{0,8},{8,0},{16,24},{24,16},{1,9},{9,1},{17,25},{25,17},{2,10},{10... | collective-permute-start | bytes 61448 | tf_op jit(solution)/shard_map/ppermute | solution.py:400
  5.5 0.8 %copy-start.9 = (f32[72,128]{1,0:T(8,128)S(1)}, f32[72,128]{1,0:T(8,128)}, u32[]{:S(2)}) copy-start(f32[72,128]{1,0:T(8,128)} %get-tuple-element.13.lines_ref) | copy-start | bytes 110596
  6.3 2.5 %copy-start.2 = (f32[4,4096]{1,0:T(4,128)S(1)}, f32[4,4096]{1,0:T(4,128)}, u32[]{:S(2)}) copy-start(f32[4,4096]{1,0:T(4,128)} %refs_5_.2) | copy-start | bytes 196612
  6.3 2.5 %copy-start.5 = (bf16[5,16,128]{2,1,0:T(8,128)(2,1)S(1)}, bf16[5,16,128]{2,1,0:T(8,128)(2,1)}, u32[]{:S(2)}) copy-start(bf16[5,16,128]{2,1,0:T(8,128)(2,1)} %get-tuple-element.12.refs_0_) | copy-start | bytes 61444
  6.3 2.5 %copy-start.7 = (s32[8,4]{0,1:T(4,128)S(1)}, s32[8,4]{0,1:T(4,128)}, u32[]{:S(2)}) copy-start(s32[8,4]{0,1:T(4,128)} %param.15) | copy-start | bytes 388
  7.9 11.6 %copy-start.4 = (f32[3,4096]{1,0:T(4,128)S(1)}, f32[3,4096]{1,0:T(4,128)}, u32[]{:S(2)}) copy-start(f32[3,4096]{1,0:T(4,128)} %centroids_ref) | copy-start | bytes 147460
  9.8 12.0 %copy-start = (f32[4,1024]{1,0:T(4,128)S(1)}, f32[4,1024]{1,0:T(4,128)}, u32[]{:S(2)}) copy-start(f32[4,1024]{1,0:T(4,128)} %refs_4_.2) | copy-start | bytes 49156
  9.8 12.0 %copy-start.1 = (s32[4,1024]{1,0:T(4,128)S(1)}, s32[4,1024]{1,0:T(4,128)}, u32[]{:S(2)}) copy-start(s32[4,1024]{1,0:T(4,128)} %refs_5_.3) | copy-start | bytes 49156
  9.9 12.0 %copy-start.3 = (f32[3,4096]{1,0:T(4,128)S(1)}, f32[3,4096]{1,0:T(4,128)}, u32[]{:S(2)}) copy-start(f32[3,4096]{1,0:T(4,128)} %refs_7_.1) | copy-start | bytes 147460
  9.9 12.0 %copy-start.6 = (f32[1024]{0:T(1024)S(1)}, f32[1024]{0:T(1024)}, u32[]{:S(2)}) copy-start(f32[1024]{0:T(1024)} %param.18) | copy-start | bytes 12292
  9.9 4.0 %collective-permute-start.5 = (bf16[16,1152]{1,0:T(8,128)(2,1)S(1)}, bf16[16,1152]{1,0:T(8,128)(2,1)S(1)}, u32[]{:S(2)}, u32[]{:S(2)}) collective-permute-start(bf16[16,1152]{1,0:T(8,128)(2,1)S(1)} %get-tuple-element.14), channel_id=1, source_target_pairs={{0,2},{1,3},{2,0},{3,1},{4,6},{5,7},{6,4},{7,5},{8,10},{9,11},{10,... | collective-permute-start | bytes 110600 | tf_op jit(solution)/shard_map/ppermute | solution.py:400
  11.5 4.9 %collective-permute-start.4 = (bf16[16,1152]{1,0:T(8,128)(2,1)S(1)}, bf16[16,1152]{1,0:T(8,128)(2,1)S(1)}, u32[]{:S(2)}, u32[]{:S(2)}) collective-permute-start(bf16[16,1152]{1,0:T(8,128)(2,1)S(1)} %get-tuple-element.14), channel_id=1, source_target_pairs={{0,3},{1,2},{2,1},{3,0},{4,7},{5,6},{6,5},{7,4},{8,11},{9,10},{10,... | collective-permute-start | bytes 110600 | tf_op jit(solution)/shard_map/ppermute | solution.py:400
  12.9 4.0 %collective-permute-start.3 = (bf16[16,1152]{1,0:T(8,128)(2,1)S(1)}, bf16[16,1152]{1,0:T(8,128)(2,1)S(1)}, u32[]{:S(2)}, u32[]{:S(2)}) collective-permute-start(bf16[16,1152]{1,0:T(8,128)(2,1)S(1)} %get-tuple-element.14), channel_id=1, source_target_pairs={{0,1},{1,0},{2,3},{3,2},{4,5},{5,4},{6,7},{7,6},{8,9},{9,8},{10,11... | collective-permute-start | bytes 110600 | tf_op jit(solution)/shard_map/ppermute | solution.py:400
  16.9 9.9 %copy-start.8 = (f32[16,128]{1,0:T(8,128)S(1)}, f32[16,128]{1,0:T(8,128)}, u32[]{:S(2)}) copy-start(f32[16,128]{1,0:T(8,128)} %refs_4_.3) | copy-start | bytes 24580
  16.9 4.9 %collective-permute-start.6 = (bf16[16,1152]{1,0:T(8,128)(2,1)S(1)}, bf16[16,1152]{1,0:T(8,128)(2,1)S(1)}, u32[]{:S(2)}, u32[]{:S(2)}) collective-permute-start(bf16[16,1152]{1,0:T(8,128)(2,1)S(1)} %add_convert_fusion.refs_0_), channel_id=1, source_target_pairs={{0,4},{1,5},{2,6},{3,7},{4,0},{5,1},{6,2},{7,3},{8,12},{9,13},{10,... | collective-permute-start | bytes 110600 | tf_op jit(solution)/shard_map/ppermute | solution.py:400
  23.2 3.0 %collective-permute-start.7 = (bf16[16,128]{1,0:T(8,128)(2,1)S(1)}, bf16[16,128]{1,0:T(8,128)(2,1)S(1)}, u32[]{:S(2)}, u32[]{:S(2)}) collective-permute-start(bf16[16,128]{1,0:T(8,128)(2,1)S(1)} %get-tuple-element.18), channel_id=1, source_target_pairs={{0,24},{8,16},{16,8},{24,0},{1,25},{9,17},{17,9},{25,1},{2,26},{10... | collective-permute-start | bytes 12296 | tf_op jit(solution)/shard_map/ppermute | solution.py:400
  23.2 3.6 %collective-permute-start.8 = (bf16[16,128]{1,0:T(8,128)(2,1)S(1)}, bf16[16,128]{1,0:T(8,128)(2,1)S(1)}, u32[]{:S(2)}, u32[]{:S(2)}) collective-permute-start(bf16[16,128]{1,0:T(8,128)(2,1)S(1)} %get-tuple-element.19), channel_id=1, source_target_pairs={{0,16},{8,24},{16,0},{24,8},{1,17},{9,25},{17,1},{25,9},{2,18},{10... | collective-permute-start | bytes 12296 | tf_op jit(solution)/shard_map/ppermute | solution.py:400
  24.4 2.4 %collective-permute-start.9 = (bf16[16,128]{1,0:T(8,128)(2,1)S(1)}, bf16[16,128]{1,0:T(8,128)(2,1)S(1)}, u32[]{:S(2)}, u32[]{:S(2)}) collective-permute-start(bf16[16,128]{1,0:T(8,128)(2,1)S(1)} %get-tuple-element.20), channel_id=1, source_target_pairs={{0,8},{8,0},{16,24},{24,16},{1,9},{9,1},{17,25},{25,17},{2,10},{10... | collective-permute-start | bytes 12296 | tf_op jit(solution)/shard_map/ppermute | solution.py:400

commit v15 on v13

--- a/solution.py
+++ b/solution.py
@@ -59,11 +59,9 @@
     return jnp.where(lane_ids() < HALF, first, last)
 
 
-def split3(value):
+def split2(value):
     high = value.astype(jnp.bfloat16).astype(jnp.float32)
-    rest = value - high
-    middle = rest.astype(jnp.bfloat16).astype(jnp.float32)
-    return [high, middle, rest - middle]
+    return [high, value - high]
 
 
 def stack_rows(rows, height):
@@ -89,13 +87,11 @@
     here = lax.axis_index("row") * length + jnp.where(lanes < HALF, lanes, length - LANES + lanes)
     for m in range(links_ref.shape[0]):
         rows.append((edges(links_ref, m, length) - here).astype(jnp.float32))
-    rows += split3(edges(diag_ref, 0, length))
-    coupling = []
+    rows += split2(edges(diag_ref, 0, length))
     for m in range(off_ref.shape[0]):
-        coupling += split3(edges(off_ref, m, length))
+        rows += split2(edges(off_ref, m, length))
     out_ref[:slots] = history_ref[...]
     out_ref[slots] = stack_rows(rows, excitations).astype(jnp.bfloat16)
-    out_ref[slots + 1] = stack_rows(coupling, excitations).astype(jnp.bfloat16)
     me = lax.axis_index("row")
     row_start = me * length
     q_tiles = shell_ref.shape[0]
@@ -303,11 +299,11 @@
     lanes = lane_ids()
     low = lanes < HALF
 
-    def halo(plane, row):
-        return halo_ref[plane, row : row + 1]
-
-    def sum3(plane, row):
-        return halo(plane, row) + halo(plane, row + 1) + halo(plane, row + 2)
+    def halo(row):
+        return halo_ref[0, row : row + 1]
+
+    def sum2(row):
+        return halo(row) + halo(row + 1)
 
     def tile(t):
         return slice(t * LANES, (t + 1) * LANES)
@@ -318,7 +314,7 @@
         for part in parts[1:]:
             total = total + part[:, tile(t)].astype(jnp.float32)
         field.append(total)
-        diag.append(diag_ref[:, tile(t)] if t < tiles else sum3(0, 2 + link_count))
+        diag.append(diag_ref[:, tile(t)] if t < tiles else sum2(2 + link_count))
 
     dual = [f / d for f, d in zip(field, diag)]
     for sweep_id in range(SWEEPS):
@@ -332,8 +328,8 @@
                     source = links_ref[m : m + 1, tile(t)] - (row_start + t * LANES)
                     gram = off_ref[m : m + 1, tile(t)]
                 else:
-                    source = halo(0, 2 + m).astype(jnp.int32) + lanes
-                    gram = sum3(1, 3 * m)
+                    source = halo(2 + m).astype(jnp.int32) + lanes
+                    gram = sum2(4 + link_count + 2 * m)
                 inside = (source >= 0) & (source < LANES)
                 index = jnp.broadcast_to(source & (LANES - 1), (excitations, LANES))
                 here = jnp.take_along_axis(dual[t], index, axis=1)
@@ -361,11 +357,12 @@
 
 
 def final_kernel(*refs, norm):
-    *share_refs, incident_ref, out_ref = refs
+    *share_refs, dual_in_ref, incident_ref, out_ref, dual_ref = refs
     total = share_refs[0][...].astype(jnp.float32)
     for share_ref in share_refs[1:]:
         total = total + share_ref[...].astype(jnp.float32)
     out_ref[...] = incident_ref[...] - total * norm
+    dual_ref[...] = dual_in_ref[...]
 
 
 def swap(value, axis, step):
@@ -428,7 +425,7 @@
     packed, lines = pl.pallas_call(
         pack_kernel,
         out_shape=(
-            jax.ShapeDtypeStruct((slots + 2, excitations, shard_len), jnp.bfloat16),
+            jax.ShapeDtypeStruct((slots + 1, excitations, shard_len), jnp.bfloat16),
             jax.ShapeDtypeStruct((line_rows, LANES), jnp.float32),
         ),
         in_specs=[VMEM, SMEM, SMEM, VMEM, VMEM, VMEM, VMEM],
@@ -452,13 +449,13 @@
         functools.partial(t_kernel, norm=norm, slots=slots, count=count),
         out_shape=(
             jax.ShapeDtypeStruct((excitations, rows_t + LANES), jnp.bfloat16),
-            jax.ShapeDtypeStruct((2, excitations, LANES), jnp.float32),
+            jax.ShapeDtypeStruct((1, excitations, LANES), jnp.float32),
         ),
         in_specs=[VMEM] * (count + 2) + [SMEM],
         out_specs=(VMEM, VMEM),
         scratch_shapes=[
             pltpu.VMEM((slots + 2, moments.shape[0] * excitations, cols_t), jnp.bfloat16),
-            pltpu.VMEM((count, 2, excitations, LANES), jnp.float32),
+            pltpu.VMEM((count, 1, excitations, LANES), jnp.float32),
         ],
         compiler_params=grant(
             (p_tiles + 2, cols_t // 2, LANES),
@@ -492,13 +489,13 @@
         compiler_params=grant((col_devices, excitations, rows_t), (rows_t, cols_t // 2), (excitations, 8 * rows_t)),
     )(*parts, halo, gram_diag, gram_off, neighbours, s_tiles, dual_moments)
     shares = shares[:1] + [swap(share, "row", step) for step, share in zip(last_steps(count)[1:], shares[1:])]
-    march_rhs = pl.pallas_call(
+    march_rhs, own_dual = pl.pallas_call(
         functools.partial(final_kernel, norm=norm),
-        out_shape=jax.ShapeDtypeStruct(incident.shape, jnp.float32),
-        in_specs=[VMEM] * (count + 1),
-        out_specs=VMEM,
+        out_shape=[jax.ShapeDtypeStruct(incident.shape, jnp.float32)] * 2,
+        in_specs=[VMEM] * (count + 2),
+        out_specs=[VMEM, VMEM],
         compiler_params=grant((count, excitations, shard_len)),
-    )(*shares, incident)
+    )(*shares, own_dual, incident)
     return (march_rhs, own_dual)
 
 

time: 27.5 us -> 27.1 us (0.985)
  Pallas kernels: 7.86 us -> 7.39 us
    pallas_call x1, Pallas kernels: 1.32 us -> 0.83 us  [per_device(): pl.pallas_call(functools.partial(sweep_kernel, slots=slots, part_count=le...]
where the time goes in v15:
time: 27.1 us; the launch traced here: 26.9 us
  starting transfers between devices  11.2 us (41%)
  Pallas kernels  7.39 us (27%)
  waiting for transfers between devices  6.72 us (25%)
  local copies, waits for them, and re-layouts  0.82 us (3%)
  between operations  0.76 us (3%)
    ppermute x10, starting transfers between devices, swap(): return lax.ppermute(value, axis, pairs)  11.2 us
    ppermute x10, waiting for transfers between devices, swap(): return lax.ppermute(value, axis, pairs)  6.72 us
    pallas_call x1, Pallas kernels, per_device(): pl.pallas_call(s_tiles_kernel, out_shape=jax.ShapeDtypeStruct((rows_t, co...  1.65 us
    pallas_call x1, Pallas kernels, per_device(): pl.pallas_call(functools.partial(t_tiles_kernel, p_tiles=p_tiles, q_tiles...  1.64 us
    pallas_call x1, Pallas kernels, per_device(): pl.pallas_call(pack_kernel, out_shape=(jax.ShapeDtypeStruct((slots + 1, e...  1.61 us
    pallas_call x1, Pallas kernels, per_device(): pl.pallas_call(functools.partial(t_kernel, norm=norm, slots=slots, count=...  1.05 us
    pallas_call x1, Pallas kernels, per_device(): pl.pallas_call(functools.partial(sweep_kernel, slots=slots, part_count=le...  0.83 us
    unnamed x20, local copies, waits for them, and re-layouts  0.82 us
  transfers between devices with their start and end apart: 10, of which 7 were waited for; matrix products, arithmetic and copies ran while one was open for 0% of the time, Pallas kernels for 12%

profile of v15, /device:TPU:0, one launch (start us, length us, event | category | flops | bytes accessed | tf_op | source)
XLA Modules:
  0.0 26.9 jit_solution(8694525685423083228)
XLA Ops:
  0.6 1.6 %shard_map.113 = (bf16[5,16,128]{2,1,0:T(8,128)(2,1)}, f32[72,128]{1,0:T(8,128)}) custom-call(bf16[4,16,128]{2,1,0:T(8,128)(2,1)} %history_ref.1, s32[4,8]{1,0:T(4,128)} %bitcast.5, s32[4,8]{1,0:T(4,128)} %bitcast.7, f32[1,1024]{1,0:T(1,128)} %bitcast.3, f32[4,1024]{1,0:T(4,128)} %refs_4_.1, s32[4,1024]{1,0:T(4,128)} %refs_5_.4, f32[3,4096]{1,0:T(4,128)} %centroids_ref.2), custom_call_target="tpu_custom_call" | custom-call | tf_op jit(solution)/shard_map/pallas_call | solution.py:425
  2.2 2.9 %collective-permute-start.2 = (bf16[5,16,128]{2,1,0:T(8,128)(2,1)}, bf16[5,16,128]{2,1,0:T(8,128)(2,1)S(1)}, u32[]{:S(2)}, u32[]{:S(2)}) collective-permute-start(bf16[5,16,128]{2,1,0:T(8,128)(2,1)} %get-tuple-element.12.refs_0_), channel_id=1, source_target_pairs={{0,16},{8,24},{16,0},{24,8},{1,17},{9,25},{17,1},{25,9},{2,18},{10... | collective-permute-start | bytes 61448 | tf_op jit(solution)/shard_map/ppermute | solution.py:374
  5.2 0.0 collective-permute-start.1
  5.2 0.1 collective-permute-start
  5.3 0.0 copy-start.9
  5.3 0.8 %copy-done.9 = f32[72,128]{1,0:T(8,128)S(1)} copy-done((f32[72,128]{1,0:T(8,128)S(1)}, f32[72,128]{1,0:T(8,128)}, u32[]{:S(2)}) %copy-start.9) | copy-done | bytes 36888
  6.1 0.0 copy-start.2
  6.1 0.0 copy-start.5
  6.1 0.0 copy-start.7
  6.1 1.6 %shard_map.114.refs_4_ = bf16[10,512,128]{2,1,0:T(8,128)(2,1)S(1)} custom-call(f32[72,128]{1,0:T(8,128)S(1)} %copy-done.9), custom_call_target="tpu_custom_call" | custom-call | flops 8388608 | bytes 1048576 | tf_op jit(solution)/shard_map/pallas_call | solution.py:438
  7.7 0.0 copy-start.4
  7.8 0.0 collective-permute-done.2.refs_3_
  7.8 0.8 %collective-permute-done.1.refs_2_ = bf16[5,16,128]{2,1,0:T(8,128)(2,1)S(1)} collective-permute-done((bf16[5,16,128]{2,1,0:T(8,128)(2,1)}, bf16[5,16,128]{2,1,0:T(8,128)(2,1)S(1)}, u32[]{:S(2)}, u32[]{:S(2)}) %collective-permute-start.1) | collective-permute-done | bytes 20512 | tf_op jit(solution)/shard_map/ppermute | solution.py:374
  8.6 0.0 collective-permute-done.refs_1_
  8.6 0.0 copy-done.2
  8.6 0.0 copy-done.5
  8.6 0.0 copy-done.7
  8.6 1.1 %shard_map.115 = (bf16[16,1152]{1,0:T(8,128)(2,1)S(1)}, f32[1,16,128]{2,1,0:T(8,128)S(1)}) custom-call(bf16[5,16,128]{2,1,0:T(8,128)(2,1)S(1)} %copy-done.5, bf16[5,16,128]{2,1,0:T(8,128)(2,1)S(1)} %collective-permute-done.refs_1_, bf16[5,16,128]{2,1,0:T(8,128)(2,1)S(1)} %collective-permute-done.1.refs_2_, ...), custom_call_target="tpu_custom_call" | custom-call | tf_op jit(solution)/shard_map/pallas_call | solution.py:448
  9.7 0.0 copy-start
  9.7 0.0 copy-start.1
  9.7 0.0 copy-start.3
  9.7 0.0 copy-start.6
  9.7 1.6 %collective-permute-start.5 = (bf16[16,1152]{1,0:T(8,128)(2,1)S(1)}, bf16[16,1152]{1,0:T(8,128)(2,1)S(1)}, u32[]{:S(2)}, u32[]{:S(2)}) collective-permute-start(bf16[16,1152]{1,0:T(8,128)(2,1)S(1)} %get-tuple-element.14), channel_id=1, source_target_pairs={{0,2},{1,3},{2,0},{3,1},{4,6},{5,7},{6,4},{7,5},{8,10},{9,11},{10,... | collective-permute-start | bytes 110600 | tf_op jit(solution)/shard_map/ppermute | solution.py:374
  11.4 1.4 %collective-permute-start.4 = (bf16[16,1152]{1,0:T(8,128)(2,1)S(1)}, bf16[16,1152]{1,0:T(8,128)(2,1)S(1)}, u32[]{:S(2)}, u32[]{:S(2)}) collective-permute-start(bf16[16,1152]{1,0:T(8,128)(2,1)S(1)} %get-tuple-element.14), channel_id=1, source_target_pairs={{0,3},{1,2},{2,1},{3,0},{4,7},{5,6},{6,5},{7,4},{8,11},{9,10},{10,... | collective-permute-start | bytes 110600 | tf_op jit(solution)/shard_map/ppermute | solution.py:374
  12.8 0.5 %collective-permute-start.3 = (bf16[16,1152]{1,0:T(8,128)(2,1)S(1)}, bf16[16,1152]{1,0:T(8,128)(2,1)S(1)}, u32[]{:S(2)}, u32[]{:S(2)}) collective-permute-start(bf16[16,1152]{1,0:T(8,128)(2,1)S(1)} %get-tuple-element.14), channel_id=1, source_target_pairs={{0,1},{1,0},{2,3},{3,2},{4,5},{5,4},{6,7},{7,6},{8,9},{9,8},{10,11... | collective-permute-start | bytes 110600 | tf_op jit(solution)/shard_map/ppermute | solution.py:374
  13.3 0.5 %collective-permute-done.5 = bf16[16,1152]{1,0:T(8,128)(2,1)S(1)} collective-permute-done((bf16[16,1152]{1,0:T(8,128)(2,1)S(1)}, bf16[16,1152]{1,0:T(8,128)(2,1)S(1)}, u32[]{:S(2)}, u32[]{:S(2)}) %collective-permute-start.5) | collective-permute-done | bytes 36896 | tf_op jit(solution)/shard_map/ppermute | solution.py:374
  13.7 2.5 %collective-permute-done.4 = bf16[16,1152]{1,0:T(8,128)(2,1)S(1)} collective-permute-done((bf16[16,1152]{1,0:T(8,128)(2,1)S(1)}, bf16[16,1152]{1,0:T(8,128)(2,1)S(1)}, u32[]{:S(2)}, u32[]{:S(2)}) %collective-permute-start.4) | collective-permute-done | bytes 36896 | tf_op jit(solution)/shard_map/ppermute | solution.py:374
  16.2 0.5 %collective-permute-done.3 = bf16[16,1152]{1,0:T(8,128)(2,1)S(1)} collective-permute-done((bf16[16,1152]{1,0:T(8,128)(2,1)S(1)}, bf16[16,1152]{1,0:T(8,128)(2,1)S(1)}, u32[]{:S(2)}, u32[]{:S(2)}) %collective-permute-start.3) | collective-permute-done | bytes 36896 | tf_op jit(solution)/shard_map/ppermute | solution.py:374
  16.8 0.0 copy-start.8
  16.8 2.7 %collective-permute-start.6 = (bf16[16,1152]{1,0:T(8,128)(2,1)S(1)}, bf16[16,1152]{1,0:T(8,128)(2,1)S(1)}, u32[]{:S(2)}, u32[]{:S(2)}) collective-permute-start(bf16[16,1152]{1,0:T(8,128)(2,1)S(1)} %add_convert_fusion.refs_0_), channel_id=1, source_target_pairs={{0,4},{1,5},{2,6},{3,7},{4,0},{5,1},{6,2},{7,3},{8,12},{9,13},{10,... | collective-permute-start | bytes 110600 | tf_op jit(solution)/shard_map/ppermute | solution.py:374
  19.4 0.0 copy-done.4
  19.4 1.6 %shard_map.116.refs_6_ = bf16[1024,512]{1,0:T(8,128)(2,1)S(1)} custom-call(f32[3,4096]{1,0:T(4,128)S(1)} %copy-done.4), custom_call_target="tpu_custom_call" | custom-call | flops 6291456 | bytes 1048576 | tf_op jit(solution)/shard_map/pallas_call | solution.py:468
  21.1 0.6 %collective-permute-done.6.refs_1_ = bf16[16,1152]{1,0:T(8,128)(2,1)S(1)} collective-permute-done((bf16[16,1152]{1,0:T(8,128)(2,1)S(1)}, bf16[16,1152]{1,0:T(8,128)(2,1)S(1)}, u32[]{:S(2)}, u32[]{:S(2)}) %collective-permute-start.6) | collective-permute-done | bytes 36896 | tf_op jit(solution)/shard_map/ppermute | solution.py:374
  21.7 0.0 copy-done
  21.7 0.0 copy-done.1
  21.7 0.0 copy-done.3
  21.7 0.0 copy-done.6
  21.7 0.8 %shard_map.117 = (f32[16,128]{1,0:T(8,128)S(1)}, f32[16,128]{1,0:T(8,128)S(1)}, bf16[16,128]{1,0:T(8,128)(2,1)S(1)}, bf16[16,128]{1,0:T(8,128)(2,1)S(1)}, bf16[16,128]{1,0:T(8,128)(2,1)S(1)}) custom-call(bf16[16,1152]{1,0:T(8,128)(2,1)S(1)} %add_convert_fusion.refs_0_, bf16[16,1152]{1,0:T(8,128)(2,1)S(1)} %collective-permute-done.6.refs_1_, ...), custom_call_target="tpu_custom_call" | custom-call | tf_op jit(solution)/shard_map/pallas_call | solution.py:478
  22.6 0.1 collective-permute-start.7
  22.6 1.3 %collective-permute-start.8 = (bf16[16,128]{1,0:T(8,128)(2,1)S(1)}, bf16[16,128]{1,0:T(8,128)(2,1)S(1)}, u32[]{:S(2)}, u32[]{:S(2)}) collective-permute-start(bf16[16,128]{1,0:T(8,128)(2,1)S(1)} %get-tuple-element.19), channel_id=1, source_target_pairs={{0,16},{8,24},{16,0},{24,8},{1,17},{9,25},{17,1},{25,9},{2,18},{10... | collective-permute-start | bytes 12296 | tf_op jit(solution)/shard_map/ppermute | solution.py:374
  23.9 0.6 %collective-permute-start.9 = (bf16[16,128]{1,0:T(8,128)(2,1)S(1)}, bf16[16,128]{1,0:T(8,128)(2,1)S(1)}, u32[]{:S(2)}, u32[]{:S(2)}) collective-permute-start(bf16[16,128]{1,0:T(8,128)(2,1)S(1)} %get-tuple-element.20), channel_id=1, source_target_pairs={{0,8},{8,0},{16,24},{24,16},{1,9},{9,1},{17,25},{25,17},{2,10},{10... | collective-permute-start | bytes 12296 | tf_op jit(solution)/shard_map/ppermute | solution.py:374
  24.5 1.2 %collective-permute-done.7.refs_1_ = bf16[16,128]{1,0:T(8,128)(2,1)S(1)} collective-permute-done((bf16[16,128]{1,0:T(8,128)(2,1)S(1)}, bf16[16,128]{1,0:T(8,128)(2,1)S(1)}, u32[]{:S(2)}, u32[]{:S(2)}) %collective-permute-start.7) | collective-permute-done | bytes 4128 | tf_op jit(solution)/shard_map/ppermute | solution.py:374
  25.6 0.7 %collective-permute-done.8.refs_2_ = bf16[16,128]{1,0:T(8,128)(2,1)S(1)} collective-permute-done((bf16[16,128]{1,0:T(8,128)(2,1)S(1)}, bf16[16,128]{1,0:T(8,128)(2,1)S(1)}, u32[]{:S(2)}, u32[]{:S(2)}) %collective-permute-start.8) | collective-permute-done | bytes 4128 | tf_op jit(solution)/shard_map/ppermute | solution.py:374
  26.3 0.0 collective-permute-done.9.refs_3_
  26.3 0.0 copy-done.8
  26.3 0.6 %shard_map.118 = (f32[16,128]{1,0:T(8,128)}, f32[16,128]{1,0:T(8,128)}) custom-call(f32[16,128]{1,0:T(8,128)S(1)} %get-tuple-element.17.refs_0_, bf16[16,128]{1,0:T(8,128)(2,1)S(1)} %collective-permute-done.7.refs_1_, bf16[16,128]{1,0:T(8,128)(2,1)S(1)} %collective-permute-done.8.refs_2_, bf16[16,128]{1,0:T(8,128)(2,1)S(1)} %collective-permute-done.9.refs_3_, ...), custom_call_target="tpu_custom_call" | custom-call | tf_op jit(solution)/shard_map/pallas_call | solution.py:492
  (1 shorter events, 0.0 us)
Async XLA Ops:
  2.2 5.5 %collective-permute-start.2 = (bf16[5,16,128]{2,1,0:T(8,128)(2,1)}, bf16[5,16,128]{2,1,0:T(8,128)(2,1)S(1)}, u32[]{:S(2)}, u32[]{:S(2)}) collective-permute-start(bf16[5,16,128]{2,1,0:T(8,128)(2,1)} %get-tuple-element.12.refs_0_), channel_id=1, source_target_pairs={{0,16},{8,24},{16,0},{24,8},{1,17},{9,25},{17,1},{25,9},{2,18},{10... | collective-permute-start | bytes 61448 | tf_op jit(solution)/shard_map/ppermute | solution.py:374
  5.2 3.4 %collective-permute-start.1 = (bf16[5,16,128]{2,1,0:T(8,128)(2,1)}, bf16[5,16,128]{2,1,0:T(8,128)(2,1)S(1)}, u32[]{:S(2)}, u32[]{:S(2)}) collective-permute-start(bf16[5,16,128]{2,1,0:T(8,128)(2,1)} %get-tuple-element.12.refs_0_), channel_id=1, source_target_pairs={{0,24},{8,16},{16,8},{24,0},{1,25},{9,17},{17,9},{25,1},{2,26},{10... | collective-permute-start | bytes 61448 | tf_op jit(solution)/shard_map/ppermute | solution.py:374
  5.2 3.4 %collective-permute-start = (bf16[5,16,128]{2,1,0:T(8,128)(2,1)}, bf16[5,16,128]{2,1,0:T(8,128)(2,1)S(1)}, u32[]{:S(2)}, u32[]{:S(2)}) collective-permute-start(bf16[5,16,128]{2,1,0:T(8,128)(2,1)} %get-tuple-element.12.refs_0_), channel_id=1, source_target_pairs={{0,8},{8,0},{16,24},{24,16},{1,9},{9,1},{17,25},{25,17},{2,10},{10... | collective-permute-start | bytes 61448 | tf_op jit(solution)/shard_map/ppermute | solution.py:374
  5.3 0.8 %copy-start.9 = (f32[72,128]{1,0:T(8,128)S(1)}, f32[72,128]{1,0:T(8,128)}, u32[]{:S(2)}) copy-start(f32[72,128]{1,0:T(8,128)} %get-tuple-element.13.lines_ref) | copy-start | bytes 110596
  6.1 2.5 %copy-start.2 = (f32[4,4096]{1,0:T(4,128)S(1)}, f32[4,4096]{1,0:T(4,128)}, u32[]{:S(2)}) copy-start(f32[4,4096]{1,0:T(4,128)} %refs_5_.3) | copy-start | bytes 196612
  6.1 2.5 %copy-start.5 = (bf16[5,16,128]{2,1,0:T(8,128)(2,1)S(1)}, bf16[5,16,128]{2,1,0:T(8,128)(2,1)}, u32[]{:S(2)}) copy-start(bf16[5,16,128]{2,1,0:T(8,128)(2,1)} %get-tuple-element.12.refs_0_) | copy-start | bytes 61444
  6.1 2.5 %copy-start.7 = (s32[8,4]{0,1:T(4,128)S(1)}, s32[8,4]{0,1:T(4,128)}, u32[]{:S(2)}) copy-start(s32[8,4]{0,1:T(4,128)} %param.15) | copy-start | bytes 388
  7.7 11.7 %copy-start.4 = (f32[3,4096]{1,0:T(4,128)S(1)}, f32[3,4096]{1,0:T(4,128)}, u32[]{:S(2)}) copy-start(f32[3,4096]{1,0:T(4,128)} %centroids_ref.2) | copy-start | bytes 147460
  9.7 12.0 %copy-start = (f32[4,1024]{1,0:T(4,128)S(1)}, f32[4,1024]{1,0:T(4,128)}, u32[]{:S(2)}) copy-start(f32[4,1024]{1,0:T(4,128)} %refs_4_.1) | copy-start | bytes 49156
  9.7 12.0 %copy-start.1 = (s32[4,1024]{1,0:T(4,128)S(1)}, s32[4,1024]{1,0:T(4,128)}, u32[]{:S(2)}) copy-start(s32[4,1024]{1,0:T(4,128)} %refs_5_.4) | copy-start | bytes 49156
  9.7 12.0 %copy-start.3 = (f32[3,4096]{1,0:T(4,128)S(1)}, f32[3,4096]{1,0:T(4,128)}, u32[]{:S(2)}) copy-start(f32[3,4096]{1,0:T(4,128)} %refs_7_.1) | copy-start | bytes 147460
  9.7 12.0 %copy-start.6 = (f32[1024]{0:T(1024)S(1)}, f32[1024]{0:T(1024)}, u32[]{:S(2)}) copy-start(f32[1024]{0:T(1024)} %param.18) | copy-start | bytes 12292
  9.7 4.0 %collective-permute-start.5 = (bf16[16,1152]{1,0:T(8,128)(2,1)S(1)}, bf16[16,1152]{1,0:T(8,128)(2,1)S(1)}, u32[]{:S(2)}, u32[]{:S(2)}) collective-permute-start(bf16[16,1152]{1,0:T(8,128)(2,1)S(1)} %get-tuple-element.14), channel_id=1, source_target_pairs={{0,2},{1,3},{2,0},{3,1},{4,6},{5,7},{6,4},{7,5},{8,10},{9,11},{10,... | collective-permute-start | bytes 110600 | tf_op jit(solution)/shard_map/ppermute | solution.py:374
  11.4 4.9 %collective-permute-start.4 = (bf16[16,1152]{1,0:T(8,128)(2,1)S(1)}, bf16[16,1152]{1,0:T(8,128)(2,1)S(1)}, u32[]{:S(2)}, u32[]{:S(2)}) collective-permute-start(bf16[16,1152]{1,0:T(8,128)(2,1)S(1)} %get-tuple-element.14), channel_id=1, source_target_pairs={{0,3},{1,2},{2,1},{3,0},{4,7},{5,6},{6,5},{7,4},{8,11},{9,10},{10,... | collective-permute-start | bytes 110600 | tf_op jit(solution)/shard_map/ppermute | solution.py:374
  12.8 4.0 %collective-permute-start.3 = (bf16[16,1152]{1,0:T(8,128)(2,1)S(1)}, bf16[16,1152]{1,0:T(8,128)(2,1)S(1)}, u32[]{:S(2)}, u32[]{:S(2)}) collective-permute-start(bf16[16,1152]{1,0:T(8,128)(2,1)S(1)} %get-tuple-element.14), channel_id=1, source_target_pairs={{0,1},{1,0},{2,3},{3,2},{4,5},{5,4},{6,7},{7,6},{8,9},{9,8},{10,11... | collective-permute-start | bytes 110600 | tf_op jit(solution)/shard_map/ppermute | solution.py:374
  16.8 9.6 %copy-start.8 = (f32[16,128]{1,0:T(8,128)S(1)}, f32[16,128]{1,0:T(8,128)}, u32[]{:S(2)}) copy-start(f32[16,128]{1,0:T(8,128)} %refs_5_.5) | copy-start | bytes 24580
  16.8 4.9 %collective-permute-start.6 = (bf16[16,1152]{1,0:T(8,128)(2,1)S(1)}, bf16[16,1152]{1,0:T(8,128)(2,1)S(1)}, u32[]{:S(2)}, u32[]{:S(2)}) collective-permute-start(bf16[16,1152]{1,0:T(8,128)(2,1)S(1)} %add_convert_fusion.refs_0_), channel_id=1, source_target_pairs={{0,4},{1,5},{2,6},{3,7},{4,0},{5,1},{6,2},{7,3},{8,12},{9,13},{10,... | collective-permute-start | bytes 110600 | tf_op jit(solution)/shard_map/ppermute | solution.py:374
  22.6 3.1 %collective-permute-start.7 = (bf16[16,128]{1,0:T(8,128)(2,1)S(1)}, bf16[16,128]{1,0:T(8,128)(2,1)S(1)}, u32[]{:S(2)}, u32[]{:S(2)}) collective-permute-start(bf16[16,128]{1,0:T(8,128)(2,1)S(1)} %get-tuple-element.18), channel_id=1, source_target_pairs={{0,24},{8,16},{16,8},{24,0},{1,25},{9,17},{17,9},{25,1},{2,26},{10... | collective-permute-start | bytes 12296 | tf_op jit(solution)/shard_map/ppermute | solution.py:374
  22.6 3.7 %collective-permute-start.8 = (bf16[16,128]{1,0:T(8,128)(2,1)S(1)}, bf16[16,128]{1,0:T(8,128)(2,1)S(1)}, u32[]{:S(2)}, u32[]{:S(2)}) collective-permute-start(bf16[16,128]{1,0:T(8,128)(2,1)S(1)} %get-tuple-element.19), channel_id=1, source_target_pairs={{0,16},{8,24},{16,0},{24,8},{1,17},{9,25},{17,1},{25,9},{2,18},{10... | collective-permute-start | bytes 12296 | tf_op jit(solution)/shard_map/ppermute | solution.py:374
  23.9 2.4 %collective-permute-start.9 = (bf16[16,128]{1,0:T(8,128)(2,1)S(1)}, bf16[16,128]{1,0:T(8,128)(2,1)S(1)}, u32[]{:S(2)}, u32[]{:S(2)}) collective-permute-start(bf16[16,128]{1,0:T(8,128)(2,1)S(1)} %get-tuple-element.20), channel_id=1, source_target_pairs={{0,8},{8,0},{16,24},{24,16},{1,9},{9,1},{17,25},{25,17},{2,10},{10... | collective-permute-start | bytes 12296 | tf_op jit(solution)/shard_map/ppermute | solution.py:374

commit v16 on v15

--- a/solution.py
+++ b/solution.py
@@ -180,8 +180,10 @@
 
 def t_kernel(*refs, norm, slots, count):
     packed = [refs[order_of(count).index(step)] for step in range(count)]
-    tiles_ref, moments_ref, shell_ref = refs[count : count + 3]
-    out_ref, halo_ref, scaled_ref, edge_ref = refs[count + 3 :]
+    tiles_ref, moments_ref, shell_in = refs[count : count + 3]
+    out_ref, halo_ref, scaled_ref, edge_ref, shell_ref, sem = refs[count + 3 :]
+    shell_copy = pltpu.make_async_copy(shell_in, shell_ref, sem)
+    shell_copy.start()
     q_tiles, p_tiles = shell_ref.shape
     excitations = out_ref.shape[0]
     kinds = moments_ref.shape[0]
@@ -231,6 +233,14 @@
             field = field + term if a < kinds - 1 else field - term
         return (field * norm).astype(jnp.bfloat16)
 
+    halo_tile = jnp.concatenate(halo_tiles, axis=0)
+    product = jnp.where(
+        low,
+        jnp.dot(scaled_ref[slots], halo_tile, preferred_element_type=jnp.float32),
+        jnp.dot(scaled_ref[slots + 1], halo_tile, preferred_element_type=jnp.float32),
+    )
+    out_ref[:, length:] = weighted(product, [halo_line(moments_ref, a, row_start, length) for a in range(kinds)])
+
     def one_tile(t):
         lhs = jnp.concatenate(
             [scaled_ref[shell_ref[sources[i], t], :, i * LANES : (i + 1) * LANES] for i in range(count)], axis=1
@@ -248,18 +258,11 @@
             one_tile(g * group + k)
         return carry
 
+    shell_copy.wait()
     if group == p_tiles:
         one_group(0, 0)
     else:
         lax.fori_loop(0, p_tiles // group, one_group, 0)
-    halo_tile = jnp.concatenate(halo_tiles, axis=0)
-    product = jnp.where(
-        low,
-        jnp.dot(scaled_ref[slots], halo_tile, preferred_element_type=jnp.float32),
-        jnp.dot(scaled_ref[slots + 1], halo_tile, preferred_element_type=jnp.float32),
-    )
-    out_ref[:, length:] = weighted(product, [halo_line(moments_ref, a, row_start, length) for a in range(kinds)])
-
 
 def s_tiles_kernel(centroids_ref, out_ref, column_ref):
     length, width = out_ref.shape
@@ -451,11 +454,13 @@
             jax.ShapeDtypeStruct((excitations, rows_t + LANES), jnp.bfloat16),
             jax.ShapeDtypeStruct((1, excitations, LANES), jnp.float32),
         ),
-        in_specs=[VMEM] * (count + 2) + [SMEM],
+        in_specs=[VMEM] * (count + 2) + [pl.BlockSpec(memory_space=pl.ANY)],
         out_specs=(VMEM, VMEM),
         scratch_shapes=[
             pltpu.VMEM((slots + 2, moments.shape[0] * excitations, cols_t), jnp.bfloat16),
             pltpu.VMEM((count, 1, excitations, LANES), jnp.float32),
+            pltpu.SMEM(shell.shape, jnp.int32),
+            pltpu.SemaphoreType.DMA,
         ],
         compiler_params=grant(
             (p_tiles + 2, cols_t // 2, LANES),

time: 27.1 us -> 27.1 us (level)
  no operation moved by 1% of the time
where the time goes in v16:
time: 27.1 us; the launch traced here: 26.9 us
  starting transfers between devices  11.2 us (41%)
  Pallas kernels  7.38 us (27%)
  waiting for transfers between devices  6.72 us (25%)
  local copies, waits for them, and re-layouts  0.82 us (3%)
  between operations  0.76 us (3%)
    ppermute x10, starting transfers between devices, swap(): return lax.ppermute(value, axis, pairs)  11.2 us
    ppermute x10, waiting for transfers between devices, swap(): return lax.ppermute(value, axis, pairs)  6.72 us
    pallas_call x1, Pallas kernels, per_device(): pl.pallas_call(s_tiles_kernel, out_shape=jax.ShapeDtypeStruct((rows_t, co...  1.65 us
    pallas_call x1, Pallas kernels, per_device(): pl.pallas_call(functools.partial(t_tiles_kernel, p_tiles=p_tiles, q_tiles...  1.64 us
    pallas_call x1, Pallas kernels, per_device(): pl.pallas_call(pack_kernel, out_shape=(jax.ShapeDtypeStruct((slots + 1, e...  1.61 us
    pallas_call x1, Pallas kernels, per_device(): pl.pallas_call(functools.partial(t_kernel, norm=norm, slots=slots, count=...  1.04 us
    pallas_call x1, Pallas kernels, per_device(): pl.pallas_call(functools.partial(sweep_kernel, slots=slots, part_count=le...  0.84 us
    unnamed x20, local copies, waits for them, and re-layouts  0.82 us
  transfers between devices with their start and end apart: 10, of which 7 were waited for; matrix products, arithmetic and copies ran while one was open for 0% of the time, Pallas kernels for 12%

profile of v16, /device:TPU:0, one launch (start us, length us, event | category | flops | bytes accessed | tf_op | source)
XLA Modules:
  0.0 26.9 jit_solution(4835571848189663025)
XLA Ops:
  0.6 1.6 %shard_map.113 = (bf16[5,16,128]{2,1,0:T(8,128)(2,1)}, f32[72,128]{1,0:T(8,128)}) custom-call(bf16[4,16,128]{2,1,0:T(8,128)(2,1)} %history_ref.1, s32[4,8]{1,0:T(4,128)} %bitcast.5, s32[4,8]{1,0:T(4,128)} %bitcast.7, f32[1,1024]{1,0:T(1,128)} %bitcast.3, f32[4,1024]{1,0:T(4,128)} %refs_4_.1, s32[4,1024]{1,0:T(4,128)} %refs_5_.4, f32[3,4096]{1,0:T(4,128)} %centroids_ref.2), custom_call_target="tpu_custom_call" | custom-call | tf_op jit(solution)/shard_map/pallas_call | solution.py:428
  2.2 2.9 %collective-permute-start.2 = (bf16[5,16,128]{2,1,0:T(8,128)(2,1)}, bf16[5,16,128]{2,1,0:T(8,128)(2,1)S(1)}, u32[]{:S(2)}, u32[]{:S(2)}) collective-permute-start(bf16[5,16,128]{2,1,0:T(8,128)(2,1)} %get-tuple-element.12.refs_0_), channel_id=1, source_target_pairs={{0,16},{8,24},{16,0},{24,8},{1,17},{9,25},{17,1},{25,9},{2,18},{10... | collective-permute-start | bytes 61448 | tf_op jit(solution)/shard_map/ppermute | solution.py:377
  5.2 0.0 collective-permute-start.1
  5.2 0.1 collective-permute-start
  5.3 0.0 copy-start.9
  5.3 0.8 %copy-done.9 = f32[72,128]{1,0:T(8,128)S(1)} copy-done((f32[72,128]{1,0:T(8,128)S(1)}, f32[72,128]{1,0:T(8,128)}, u32[]{:S(2)}) %copy-start.9) | copy-done | bytes 36888
  6.1 0.0 copy-start.2
  6.1 0.0 copy-start.5
  6.1 0.0 copy-start.7
  6.1 1.6 %shard_map.114.refs_4_ = bf16[10,512,128]{2,1,0:T(8,128)(2,1)S(1)} custom-call(f32[72,128]{1,0:T(8,128)S(1)} %copy-done.9), custom_call_target="tpu_custom_call" | custom-call | flops 8388608 | bytes 1048576 | tf_op jit(solution)/shard_map/pallas_call | solution.py:441
  7.7 0.0 copy-start.4
  7.8 0.0 collective-permute-done.2.refs_3_
  7.8 0.8 %collective-permute-done.1.refs_2_ = bf16[5,16,128]{2,1,0:T(8,128)(2,1)S(1)} collective-permute-done((bf16[5,16,128]{2,1,0:T(8,128)(2,1)}, bf16[5,16,128]{2,1,0:T(8,128)(2,1)S(1)}, u32[]{:S(2)}, u32[]{:S(2)}) %collective-permute-start.1) | collective-permute-done | bytes 20512 | tf_op jit(solution)/shard_map/ppermute | solution.py:377
  8.6 0.0 collective-permute-done.refs_1_
  8.6 0.0 copy-done.2
  8.6 0.0 copy-done.5
  8.6 0.0 copy-done.7
  8.6 1.0 %shard_map.115 = (bf16[16,1152]{1,0:T(8,128)(2,1)S(1)}, f32[1,16,128]{2,1,0:T(8,128)S(1)}) custom-call(bf16[5,16,128]{2,1,0:T(8,128)(2,1)S(1)} %copy-done.5, bf16[5,16,128]{2,1,0:T(8,128)(2,1)S(1)} %collective-permute-done.refs_1_, bf16[5,16,128]{2,1,0:T(8,128)(2,1)S(1)} %collective-permute-done.1.refs_2_, ...), custom_call_target="tpu_custom_call" | custom-call | tf_op jit(solution)/shard_map/pallas_call | solution.py:451
  9.7 0.0 copy-start
  9.7 0.0 copy-start.1
  9.7 0.0 copy-start.3
  9.7 0.0 copy-start.6
  9.7 1.6 %collective-permute-start.5 = (bf16[16,1152]{1,0:T(8,128)(2,1)S(1)}, bf16[16,1152]{1,0:T(8,128)(2,1)S(1)}, u32[]{:S(2)}, u32[]{:S(2)}) collective-permute-start(bf16[16,1152]{1,0:T(8,128)(2,1)S(1)} %get-tuple-element.14), channel_id=1, source_target_pairs={{0,2},{1,3},{2,0},{3,1},{4,6},{5,7},{6,4},{7,5},{8,10},{9,11},{10,... | collective-permute-start | bytes 110600 | tf_op jit(solution)/shard_map/ppermute | solution.py:377
  11.4 1.4 %collective-permute-start.4 = (bf16[16,1152]{1,0:T(8,128)(2,1)S(1)}, bf16[16,1152]{1,0:T(8,128)(2,1)S(1)}, u32[]{:S(2)}, u32[]{:S(2)}) collective-permute-start(bf16[16,1152]{1,0:T(8,128)(2,1)S(1)} %get-tuple-element.14), channel_id=1, source_target_pairs={{0,3},{1,2},{2,1},{3,0},{4,7},{5,6},{6,5},{7,4},{8,11},{9,10},{10,... | collective-permute-start | bytes 110600 | tf_op jit(solution)/shard_map/ppermute | solution.py:377
  12.8 0.5 %collective-permute-start.3 = (bf16[16,1152]{1,0:T(8,128)(2,1)S(1)}, bf16[16,1152]{1,0:T(8,128)(2,1)S(1)}, u32[]{:S(2)}, u32[]{:S(2)}) collective-permute-start(bf16[16,1152]{1,0:T(8,128)(2,1)S(1)} %get-tuple-element.14), channel_id=1, source_target_pairs={{0,1},{1,0},{2,3},{3,2},{4,5},{5,4},{6,7},{7,6},{8,9},{9,8},{10,11... | collective-permute-start | bytes 110600 | tf_op jit(solution)/shard_map/ppermute | solution.py:377
  13.3 0.5 %collective-permute-done.5 = bf16[16,1152]{1,0:T(8,128)(2,1)S(1)} collective-permute-done((bf16[16,1152]{1,0:T(8,128)(2,1)S(1)}, bf16[16,1152]{1,0:T(8,128)(2,1)S(1)}, u32[]{:S(2)}, u32[]{:S(2)}) %collective-permute-start.5) | collective-permute-done | bytes 36896 | tf_op jit(solution)/shard_map/ppermute | solution.py:377
  13.7 2.5 %collective-permute-done.4 = bf16[16,1152]{1,0:T(8,128)(2,1)S(1)} collective-permute-done((bf16[16,1152]{1,0:T(8,128)(2,1)S(1)}, bf16[16,1152]{1,0:T(8,128)(2,1)S(1)}, u32[]{:S(2)}, u32[]{:S(2)}) %collective-permute-start.4) | collective-permute-done | bytes 36896 | tf_op jit(solution)/shard_map/ppermute | solution.py:377
  16.2 0.5 %collective-permute-done.3 = bf16[16,1152]{1,0:T(8,128)(2,1)S(1)} collective-permute-done((bf16[16,1152]{1,0:T(8,128)(2,1)S(1)}, bf16[16,1152]{1,0:T(8,128)(2,1)S(1)}, u32[]{:S(2)}, u32[]{:S(2)}) %collective-permute-start.3) | collective-permute-done | bytes 36896 | tf_op jit(solution)/shard_map/ppermute | solution.py:377
  16.7 0.0 copy-start.8
  16.8 2.7 %collective-permute-start.6 = (bf16[16,1152]{1,0:T(8,128)(2,1)S(1)}, bf16[16,1152]{1,0:T(8,128)(2,1)S(1)}, u32[]{:S(2)}, u32[]{:S(2)}) collective-permute-start(bf16[16,1152]{1,0:T(8,128)(2,1)S(1)} %add_convert_fusion.refs_0_), channel_id=1, source_target_pairs={{0,4},{1,5},{2,6},{3,7},{4,0},{5,1},{6,2},{7,3},{8,12},{9,13},{10,... | collective-permute-start | bytes 110600 | tf_op jit(solution)/shard_map/ppermute | solution.py:377
  19.4 0.0 copy-done.4
  19.4 1.6 %shard_map.116.refs_6_ = bf16[1024,512]{1,0:T(8,128)(2,1)S(1)} custom-call(f32[3,4096]{1,0:T(4,128)S(1)} %copy-done.4), custom_call_target="tpu_custom_call" | custom-call | flops 6291456 | bytes 1048576 | tf_op jit(solution)/shard_map/pallas_call | solution.py:473
  21.1 0.6 %collective-permute-done.6.refs_1_ = bf16[16,1152]{1,0:T(8,128)(2,1)S(1)} collective-permute-done((bf16[16,1152]{1,0:T(8,128)(2,1)S(1)}, bf16[16,1152]{1,0:T(8,128)(2,1)S(1)}, u32[]{:S(2)}, u32[]{:S(2)}) %collective-permute-start.6) | collective-permute-done | bytes 36896 | tf_op jit(solution)/shard_map/ppermute | solution.py:377
  21.7 0.0 copy-done
  21.7 0.0 copy-done.1
  21.7 0.0 copy-done.3
  21.7 0.0 copy-done.6
  21.7 0.8 %shard_map.117 = (f32[16,128]{1,0:T(8,128)S(1)}, f32[16,128]{1,0:T(8,128)S(1)}, bf16[16,128]{1,0:T(8,128)(2,1)S(1)}, bf16[16,128]{1,0:T(8,128)(2,1)S(1)}, bf16[16,128]{1,0:T(8,128)(2,1)S(1)}) custom-call(bf16[16,1152]{1,0:T(8,128)(2,1)S(1)} %add_convert_fusion.refs_0_, bf16[16,1152]{1,0:T(8,128)(2,1)S(1)} %collective-permute-done.6.refs_1_, ...), custom_call_target="tpu_custom_call" | custom-call | tf_op jit(solution)/shard_map/pallas_call | solution.py:483
  22.5 0.1 collective-permute-start.7
  22.6 1.3 %collective-permute-start.8 = (bf16[16,128]{1,0:T(8,128)(2,1)S(1)}, bf16[16,128]{1,0:T(8,128)(2,1)S(1)}, u32[]{:S(2)}, u32[]{:S(2)}) collective-permute-start(bf16[16,128]{1,0:T(8,128)(2,1)S(1)} %get-tuple-element.19), channel_id=1, source_target_pairs={{0,16},{8,24},{16,0},{24,8},{1,17},{9,25},{17,1},{25,9},{2,18},{10... | collective-permute-start | bytes 12296 | tf_op jit(solution)/shard_map/ppermute | solution.py:377
  23.9 0.6 %collective-permute-start.9 = (bf16[16,128]{1,0:T(8,128)(2,1)S(1)}, bf16[16,128]{1,0:T(8,128)(2,1)S(1)}, u32[]{:S(2)}, u32[]{:S(2)}) collective-permute-start(bf16[16,128]{1,0:T(8,128)(2,1)S(1)} %get-tuple-element.20), channel_id=1, source_target_pairs={{0,8},{8,0},{16,24},{24,16},{1,9},{9,1},{17,25},{25,17},{2,10},{10... | collective-permute-start | bytes 12296 | tf_op jit(solution)/shard_map/ppermute | solution.py:377
  24.5 1.2 %collective-permute-done.7.refs_1_ = bf16[16,128]{1,0:T(8,128)(2,1)S(1)} collective-permute-done((bf16[16,128]{1,0:T(8,128)(2,1)S(1)}, bf16[16,128]{1,0:T(8,128)(2,1)S(1)}, u32[]{:S(2)}, u32[]{:S(2)}) %collective-permute-start.7) | collective-permute-done | bytes 4128 | tf_op jit(solution)/shard_map/ppermute | solution.py:377
  25.6 0.7 %collective-permute-done.8.refs_2_ = bf16[16,128]{1,0:T(8,128)(2,1)S(1)} collective-permute-done((bf16[16,128]{1,0:T(8,128)(2,1)S(1)}, bf16[16,128]{1,0:T(8,128)(2,1)S(1)}, u32[]{:S(2)}, u32[]{:S(2)}) %collective-permute-start.8) | collective-permute-done | bytes 4128 | tf_op jit(solution)/shard_map/ppermute | solution.py:377
  26.3 0.0 collective-permute-done.9.refs_3_
  26.3 0.0 copy-done.8
  26.3 0.6 %shard_map.118 = (f32[16,128]{1,0:T(8,128)}, f32[16,128]{1,0:T(8,128)}) custom-call(f32[16,128]{1,0:T(8,128)S(1)} %get-tuple-element.17.refs_0_, bf16[16,128]{1,0:T(8,128)(2,1)S(1)} %collective-permute-done.7.refs_1_, bf16[16,128]{1,0:T(8,128)(2,1)S(1)} %collective-permute-done.8.refs_2_, bf16[16,128]{1,0:T(8,128)(2,1)S(1)} %collective-permute-done.9.refs_3_, ...), custom_call_target="tpu_custom_call" | custom-call | tf_op jit(solution)/shard_map/pallas_call | solution.py:497
  (1 shorter events, 0.0 us)
Async XLA Ops:
  2.2 5.5 %collective-permute-start.2 = (bf16[5,16,128]{2,1,0:T(8,128)(2,1)}, bf16[5,16,128]{2,1,0:T(8,128)(2,1)S(1)}, u32[]{:S(2)}, u32[]{:S(2)}) collective-permute-start(bf16[5,16,128]{2,1,0:T(8,128)(2,1)} %get-tuple-element.12.refs_0_), channel_id=1, source_target_pairs={{0,16},{8,24},{16,0},{24,8},{1,17},{9,25},{17,1},{25,9},{2,18},{10... | collective-permute-start | bytes 61448 | tf_op jit(solution)/shard_map/ppermute | solution.py:377
  5.2 3.4 %collective-permute-start.1 = (bf16[5,16,128]{2,1,0:T(8,128)(2,1)}, bf16[5,16,128]{2,1,0:T(8,128)(2,1)S(1)}, u32[]{:S(2)}, u32[]{:S(2)}) collective-permute-start(bf16[5,16,128]{2,1,0:T(8,128)(2,1)} %get-tuple-element.12.refs_0_), channel_id=1, source_target_pairs={{0,24},{8,16},{16,8},{24,0},{1,25},{9,17},{17,9},{25,1},{2,26},{10... | collective-permute-start | bytes 61448 | tf_op jit(solution)/shard_map/ppermute | solution.py:377
  5.2 3.4 %collective-permute-start = (bf16[5,16,128]{2,1,0:T(8,128)(2,1)}, bf16[5,16,128]{2,1,0:T(8,128)(2,1)S(1)}, u32[]{:S(2)}, u32[]{:S(2)}) collective-permute-start(bf16[5,16,128]{2,1,0:T(8,128)(2,1)} %get-tuple-element.12.refs_0_), channel_id=1, source_target_pairs={{0,8},{8,0},{16,24},{24,16},{1,9},{9,1},{17,25},{25,17},{2,10},{10... | collective-permute-start | bytes 61448 | tf_op jit(solution)/shard_map/ppermute | solution.py:377
  5.3 0.8 %copy-start.9 = (f32[72,128]{1,0:T(8,128)S(1)}, f32[72,128]{1,0:T(8,128)}, u32[]{:S(2)}) copy-start(f32[72,128]{1,0:T(8,128)} %get-tuple-element.13.lines_ref) | copy-start | bytes 110596
  6.1 2.5 %copy-start.2 = (f32[4,4096]{1,0:T(4,128)S(1)}, f32[4,4096]{1,0:T(4,128)}, u32[]{:S(2)}) copy-start(f32[4,4096]{1,0:T(4,128)} %refs_5_.3) | copy-start | bytes 196612
  6.1 2.5 %copy-start.5 = (bf16[5,16,128]{2,1,0:T(8,128)(2,1)S(1)}, bf16[5,16,128]{2,1,0:T(8,128)(2,1)}, u32[]{:S(2)}) copy-start(bf16[5,16,128]{2,1,0:T(8,128)(2,1)} %get-tuple-element.12.refs_0_) | copy-start | bytes 61444
  6.1 2.5 %copy-start.7 = (s32[8,4]{0,1:T(4,128)S(1)}, s32[8,4]{0,1:T(4,128)}, u32[]{:S(2)}) copy-start(s32[8,4]{0,1:T(4,128)} %param.15) | copy-start | bytes 388
  7.7 11.7 %copy-start.4 = (f32[3,4096]{1,0:T(4,128)S(1)}, f32[3,4096]{1,0:T(4,128)}, u32[]{:S(2)}) copy-start(f32[3,4096]{1,0:T(4,128)} %centroids_ref.2) | copy-start | bytes 147460
  9.7 12.0 %copy-start = (f32[4,1024]{1,0:T(4,128)S(1)}, f32[4,1024]{1,0:T(4,128)}, u32[]{:S(2)}) copy-start(f32[4,1024]{1,0:T(4,128)} %refs_4_.1) | copy-start | bytes 49156
  9.7 12.0 %copy-start.1 = (s32[4,1024]{1,0:T(4,128)S(1)}, s32[4,1024]{1,0:T(4,128)}, u32[]{:S(2)}) copy-start(s32[4,1024]{1,0:T(4,128)} %refs_5_.4) | copy-start | bytes 49156
  9.7 12.0 %copy-start.3 = (f32[3,4096]{1,0:T(4,128)S(1)}, f32[3,4096]{1,0:T(4,128)}, u32[]{:S(2)}) copy-start(f32[3,4096]{1,0:T(4,128)} %refs_7_.1) | copy-start | bytes 147460
  9.7 12.0 %copy-start.6 = (f32[1024]{0:T(1024)S(1)}, f32[1024]{0:T(1024)}, u32[]{:S(2)}) copy-start(f32[1024]{0:T(1024)} %param.18) | copy-start | bytes 12292
  9.7 4.0 %collective-permute-start.5 = (bf16[16,1152]{1,0:T(8,128)(2,1)S(1)}, bf16[16,1152]{1,0:T(8,128)(2,1)S(1)}, u32[]{:S(2)}, u32[]{:S(2)}) collective-permute-start(bf16[16,1152]{1,0:T(8,128)(2,1)S(1)} %get-tuple-element.14), channel_id=1, source_target_pairs={{0,2},{1,3},{2,0},{3,1},{4,6},{5,7},{6,4},{7,5},{8,10},{9,11},{10,... | collective-permute-start | bytes 110600 | tf_op jit(solution)/shard_map/ppermute | solution.py:377
  11.4 4.9 %collective-permute-start.4 = (bf16[16,1152]{1,0:T(8,128)(2,1)S(1)}, bf16[16,1152]{1,0:T(8,128)(2,1)S(1)}, u32[]{:S(2)}, u32[]{:S(2)}) collective-permute-start(bf16[16,1152]{1,0:T(8,128)(2,1)S(1)} %get-tuple-element.14), channel_id=1, source_target_pairs={{0,3},{1,2},{2,1},{3,0},{4,7},{5,6},{6,5},{7,4},{8,11},{9,10},{10,... | collective-permute-start | bytes 110600 | tf_op jit(solution)/shard_map/ppermute | solution.py:377
  12.8 4.0 %collective-permute-start.3 = (bf16[16,1152]{1,0:T(8,128)(2,1)S(1)}, bf16[16,1152]{1,0:T(8,128)(2,1)S(1)}, u32[]{:S(2)}, u32[]{:S(2)}) collective-permute-start(bf16[16,1152]{1,0:T(8,128)(2,1)S(1)} %get-tuple-element.14), channel_id=1, source_target_pairs={{0,1},{1,0},{2,3},{3,2},{4,5},{5,4},{6,7},{7,6},{8,9},{9,8},{10,11... | collective-permute-start | bytes 110600 | tf_op jit(solution)/shard_map/ppermute | solution.py:377
  16.7 9.6 %copy-start.8 = (f32[16,128]{1,0:T(8,128)S(1)}, f32[16,128]{1,0:T(8,128)}, u32[]{:S(2)}) copy-start(f32[16,128]{1,0:T(8,128)} %refs_5_.5) | copy-start | bytes 24580
  16.8 4.9 %collective-permute-start.6 = (bf16[16,1152]{1,0:T(8,128)(2,1)S(1)}, bf16[16,1152]{1,0:T(8,128)(2,1)S(1)}, u32[]{:S(2)}, u32[]{:S(2)}) collective-permute-start(bf16[16,1152]{1,0:T(8,128)(2,1)S(1)} %add_convert_fusion.refs_0_), channel_id=1, source_target_pairs={{0,4},{1,5},{2,6},{3,7},{4,0},{5,1},{6,2},{7,3},{8,12},{9,13},{10,... | collective-permute-start | bytes 110600 | tf_op jit(solution)/shard_map/ppermute | solution.py:377
  22.5 3.1 %collective-permute-start.7 = (bf16[16,128]{1,0:T(8,128)(2,1)S(1)}, bf16[16,128]{1,0:T(8,128)(2,1)S(1)}, u32[]{:S(2)}, u32[]{:S(2)}) collective-permute-start(bf16[16,128]{1,0:T(8,128)(2,1)S(1)} %get-tuple-element.18), channel_id=1, source_target_pairs={{0,24},{8,16},{16,8},{24,0},{1,25},{9,17},{17,9},{25,1},{2,26},{10... | collective-permute-start | bytes 12296 | tf_op jit(solution)/shard_map/ppermute | solution.py:377
  22.6 3.7 %collective-permute-start.8 = (bf16[16,128]{1,0:T(8,128)(2,1)S(1)}, bf16[16,128]{1,0:T(8,128)(2,1)S(1)}, u32[]{:S(2)}, u32[]{:S(2)}) collective-permute-start(bf16[16,128]{1,0:T(8,128)(2,1)S(1)} %get-tuple-element.19), channel_id=1, source_target_pairs={{0,16},{8,24},{16,0},{24,8},{1,17},{9,25},{17,1},{25,9},{2,18},{10... | collective-permute-start | bytes 12296 | tf_op jit(solution)/shard_map/ppermute | solution.py:377
  23.9 2.4 %collective-permute-start.9 = (bf16[16,128]{1,0:T(8,128)(2,1)S(1)}, bf16[16,128]{1,0:T(8,128)(2,1)S(1)}, u32[]{:S(2)}, u32[]{:S(2)}) collective-permute-start(bf16[16,128]{1,0:T(8,128)(2,1)S(1)} %get-tuple-element.20), channel_id=1, source_target_pairs={{0,8},{8,0},{16,24},{24,16},{1,9},{9,1},{17,25},{25,17},{2,10},{10... | collective-permute-start | bytes 12296 | tf_op jit(solution)/shard_map/ppermute | solution.py:377

commit v17 on v15

--- a/solution.py
+++ b/solution.py
@@ -180,8 +180,10 @@
 
 def t_kernel(*refs, norm, slots, count):
     packed = [refs[order_of(count).index(step)] for step in range(count)]
-    tiles_ref, moments_ref, shell_ref = refs[count : count + 3]
-    out_ref, halo_ref, scaled_ref, edge_ref = refs[count + 3 :]
+    tiles_ref, moments_ref, shell_in = refs[count : count + 3]
+    out_ref, halo_ref, scaled_ref, edge_ref, shell_ref, sem = refs[count + 3 :]
+    shell_copy = pltpu.make_async_copy(shell_in, shell_ref, sem)
+    shell_copy.start()
     q_tiles, p_tiles = shell_ref.shape
     excitations = out_ref.shape[0]
     kinds = moments_ref.shape[0]
@@ -202,21 +204,16 @@
 
     sources = [source_of(me, i, count) for i in range(count)]
     lanes = lane_ids()
-    halo_tiles = []
+    choices, halo_tiles = [], []
     for i in range(count):
         at = slice(i * LANES, (i + 1) * LANES)
         weights = [moments_ref[a : a + 1, tile_at(col_start + sources[i] * LANES)] for a in range(kinds)]
-        values = [packed[i][s].astype(jnp.float32) for s in range(slots)]
-        here = lanes == sources[i]
-        for pick in picks:
-            choice = jnp.sum(jnp.where(here, pick, 0.0), axis=1, keepdims=True)
-            value = values[0]
-            for s in range(1, slots):
-                value = jnp.where(choice == s, values[s], value)
-            values.append(value)
-        for s, value in enumerate(values):
+        for s in range(slots):
+            value = packed[i][s].astype(jnp.float32)
             for a in range(kinds):
                 scaled_ref[s, a * excitations : (a + 1) * excitations, at] = (weights[a] * value).astype(jnp.bfloat16)
+        here = lanes == sources[i]
+        choices.append([jnp.sum(jnp.where(here, pick, 0.0), axis=1, keepdims=True) for pick in picks])
         near_right, near_left = [jnp.sum(jnp.where(here, near, 0.0), axis=1, keepdims=True) for near in nears]
         near = jnp.where(low, near_right, near_left)
         halo_tiles.append(
@@ -248,10 +245,21 @@
             one_tile(g * group + k)
         return carry
 
+    shell_copy.wait()
     if group == p_tiles:
         one_group(0, 0)
     else:
         lax.fori_loop(0, p_tiles // group, one_group, 0)
+    for side in range(2):
+        for i in range(count):
+            choice = choices[i][side]
+            for a in range(kinds):
+                rows = slice(a * excitations, (a + 1) * excitations)
+                at = slice(i * LANES, (i + 1) * LANES)
+                value = scaled_ref[0, rows, at].astype(jnp.float32)
+                for s in range(1, slots):
+                    value = jnp.where(choice == s, scaled_ref[s, rows, at].astype(jnp.float32), value)
+                scaled_ref[slots + side, rows, at] = value.astype(jnp.bfloat16)
     halo_tile = jnp.concatenate(halo_tiles, axis=0)
     product = jnp.where(
         low,
@@ -451,11 +459,13 @@
             jax.ShapeDtypeStruct((excitations, rows_t + LANES), jnp.bfloat16),
             jax.ShapeDtypeStruct((1, excitations, LANES), jnp.float32),
         ),
-        in_specs=[VMEM] * (count + 2) + [SMEM],
+        in_specs=[VMEM] * (count + 2) + [pl.BlockSpec(memory_space=pl.ANY)],
         out_specs=(VMEM, VMEM),
         scratch_shapes=[
             pltpu.VMEM((slots + 2, moments.shape[0] * excitations, cols_t), jnp.bfloat16),
             pltpu.VMEM((count, 1, excitations, LANES), jnp.float32),
+            pltpu.SMEM(shell.shape, jnp.int32),
+            pltpu.SemaphoreType.DMA,
         ],
         compiler_params=grant(
             (p_tiles + 2, cols_t // 2, LANES),

time: 27.1 us -> 27.2 us (level)
  no operation moved by 1% of the time
where the time goes in v17:
time: 27.2 us; the launch traced here: 26.9 us
  starting transfers between devices  11.2 us (41%)
  Pallas kernels  7.4 us (27%)
  waiting for transfers between devices  6.72 us (25%)
  local copies, waits for them, and re-layouts  0.82 us (3%)
  between operations  0.76 us (3%)
    ppermute x10, starting transfers between devices, swap(): return lax.ppermute(value, axis, pairs)  11.2 us
    ppermute x10, waiting for transfers between devices, swap(): return lax.ppermute(value, axis, pairs)  6.72 us
    pallas_call x1, Pallas kernels, per_device(): pl.pallas_call(s_tiles_kernel, out_shape=jax.ShapeDtypeStruct((rows_t, co...  1.65 us
    pallas_call x1, Pallas kernels, per_device(): pl.pallas_call(functools.partial(t_tiles_kernel, p_tiles=p_tiles, q_tiles...  1.64 us
    pallas_call x1, Pallas kernels, per_device(): pl.pallas_call(pack_kernel, out_shape=(jax.ShapeDtypeStruct((slots + 1, e...  1.61 us
    pallas_call x1, Pallas kernels, per_device(): pl.pallas_call(functools.partial(t_kernel, norm=norm, slots=slots, count=...  1.06 us
    pallas_call x1, Pallas kernels, per_device(): pl.pallas_call(functools.partial(sweep_kernel, slots=slots, part_count=le...  0.84 us
    unnamed x20, local copies, waits for them, and re-layouts  0.82 us
  transfers between devices with their start and end apart: 10, of which 7 were waited for; matrix products, arithmetic and copies ran while one was open for 0% of the time, Pallas kernels for 12%

profile of v17, /device:TPU:0, one launch (start us, length us, event | category | flops | bytes accessed | tf_op | source)
XLA Modules:
  0.0 26.9 jit_solution(18230232615349659843)
XLA Ops:
  0.6 1.6 %shard_map.113 = (bf16[5,16,128]{2,1,0:T(8,128)(2,1)}, f32[72,128]{1,0:T(8,128)}) custom-call(bf16[4,16,128]{2,1,0:T(8,128)(2,1)} %history_ref.1, s32[4,8]{1,0:T(4,128)} %bitcast.5, s32[4,8]{1,0:T(4,128)} %bitcast.7, f32[1,1024]{1,0:T(1,128)} %bitcast.3, f32[4,1024]{1,0:T(4,128)} %refs_4_.1, s32[4,1024]{1,0:T(4,128)} %refs_5_.4, f32[3,4096]{1,0:T(4,128)} %centroids_ref.2), custom_call_target="tpu_custom_call" | custom-call | tf_op jit(solution)/shard_map/pallas_call | solution.py:433
  2.2 2.9 %collective-permute-start.2 = (bf16[5,16,128]{2,1,0:T(8,128)(2,1)}, bf16[5,16,128]{2,1,0:T(8,128)(2,1)S(1)}, u32[]{:S(2)}, u32[]{:S(2)}) collective-permute-start(bf16[5,16,128]{2,1,0:T(8,128)(2,1)} %get-tuple-element.12.refs_0_), channel_id=1, source_target_pairs={{0,16},{8,24},{16,0},{24,8},{1,17},{9,25},{17,1},{25,9},{2,18},{10... | collective-permute-start | bytes 61448 | tf_op jit(solution)/shard_map/ppermute | solution.py:382
  5.2 0.0 collective-permute-start.1
  5.2 0.1 collective-permute-start
  5.3 0.0 copy-start.9
  5.3 0.8 %copy-done.9 = f32[72,128]{1,0:T(8,128)S(1)} copy-done((f32[72,128]{1,0:T(8,128)S(1)}, f32[72,128]{1,0:T(8,128)}, u32[]{:S(2)}) %copy-start.9) | copy-done | bytes 36888
  6.1 0.0 copy-start.2
  6.1 0.0 copy-start.5
  6.1 0.0 copy-start.7
  6.1 1.6 %shard_map.114.refs_4_ = bf16[10,512,128]{2,1,0:T(8,128)(2,1)S(1)} custom-call(f32[72,128]{1,0:T(8,128)S(1)} %copy-done.9), custom_call_target="tpu_custom_call" | custom-call | flops 8388608 | bytes 1048576 | tf_op jit(solution)/shard_map/pallas_call | solution.py:446
  7.7 0.0 copy-start.4
  7.8 0.0 collective-permute-done.2.refs_3_
  7.8 0.8 %collective-permute-done.1.refs_2_ = bf16[5,16,128]{2,1,0:T(8,128)(2,1)S(1)} collective-permute-done((bf16[5,16,128]{2,1,0:T(8,128)(2,1)}, bf16[5,16,128]{2,1,0:T(8,128)(2,1)S(1)}, u32[]{:S(2)}, u32[]{:S(2)}) %collective-permute-start.1) | collective-permute-done | bytes 20512 | tf_op jit(solution)/shard_map/ppermute | solution.py:382
  8.6 0.0 collective-permute-done.refs_1_
  8.6 0.0 copy-done.2
  8.6 0.0 copy-done.5
  8.6 0.0 copy-done.7
  8.6 1.1 %shard_map.115 = (bf16[16,1152]{1,0:T(8,128)(2,1)S(1)}, f32[1,16,128]{2,1,0:T(8,128)S(1)}) custom-call(bf16[5,16,128]{2,1,0:T(8,128)(2,1)S(1)} %copy-done.5, bf16[5,16,128]{2,1,0:T(8,128)(2,1)S(1)} %collective-permute-done.refs_1_, bf16[5,16,128]{2,1,0:T(8,128)(2,1)S(1)} %collective-permute-done.1.refs_2_, ...), custom_call_target="tpu_custom_call" | custom-call | tf_op jit(solution)/shard_map/pallas_call | solution.py:456
  9.7 0.0 copy-start
  9.7 0.0 copy-start.1
  9.7 0.0 copy-start.3
  9.7 0.0 copy-start.6
  9.7 1.6 %collective-permute-start.5 = (bf16[16,1152]{1,0:T(8,128)(2,1)S(1)}, bf16[16,1152]{1,0:T(8,128)(2,1)S(1)}, u32[]{:S(2)}, u32[]{:S(2)}) collective-permute-start(bf16[16,1152]{1,0:T(8,128)(2,1)S(1)} %get-tuple-element.14), channel_id=1, source_target_pairs={{0,2},{1,3},{2,0},{3,1},{4,6},{5,7},{6,4},{7,5},{8,10},{9,11},{10,... | collective-permute-start | bytes 110600 | tf_op jit(solution)/shard_map/ppermute | solution.py:382
  11.4 1.4 %collective-permute-start.4 = (bf16[16,1152]{1,0:T(8,128)(2,1)S(1)}, bf16[16,1152]{1,0:T(8,128)(2,1)S(1)}, u32[]{:S(2)}, u32[]{:S(2)}) collective-permute-start(bf16[16,1152]{1,0:T(8,128)(2,1)S(1)} %get-tuple-element.14), channel_id=1, source_target_pairs={{0,3},{1,2},{2,1},{3,0},{4,7},{5,6},{6,5},{7,4},{8,11},{9,10},{10,... | collective-permute-start | bytes 110600 | tf_op jit(solution)/shard_map/ppermute | solution.py:382
  12.8 0.5 %collective-permute-start.3 = (bf16[16,1152]{1,0:T(8,128)(2,1)S(1)}, bf16[16,1152]{1,0:T(8,128)(2,1)S(1)}, u32[]{:S(2)}, u32[]{:S(2)}) collective-permute-start(bf16[16,1152]{1,0:T(8,128)(2,1)S(1)} %get-tuple-element.14), channel_id=1, source_target_pairs={{0,1},{1,0},{2,3},{3,2},{4,5},{5,4},{6,7},{7,6},{8,9},{9,8},{10,11... | collective-permute-start | bytes 110600 | tf_op jit(solution)/shard_map/ppermute | solution.py:382
  13.3 0.5 %collective-permute-done.5 = bf16[16,1152]{1,0:T(8,128)(2,1)S(1)} collective-permute-done((bf16[16,1152]{1,0:T(8,128)(2,1)S(1)}, bf16[16,1152]{1,0:T(8,128)(2,1)S(1)}, u32[]{:S(2)}, u32[]{:S(2)}) %collective-permute-start.5) | collective-permute-done | bytes 36896 | tf_op jit(solution)/shard_map/ppermute | solution.py:382
  13.8 2.5 %collective-permute-done.4 = bf16[16,1152]{1,0:T(8,128)(2,1)S(1)} collective-permute-done((bf16[16,1152]{1,0:T(8,128)(2,1)S(1)}, bf16[16,1152]{1,0:T(8,128)(2,1)S(1)}, u32[]{:S(2)}, u32[]{:S(2)}) %collective-permute-start.4) | collective-permute-done | bytes 36896 | tf_op jit(solution)/shard_map/ppermute | solution.py:382
  16.2 0.5 %collective-permute-done.3 = bf16[16,1152]{1,0:T(8,128)(2,1)S(1)} collective-permute-done((bf16[16,1152]{1,0:T(8,128)(2,1)S(1)}, bf16[16,1152]{1,0:T(8,128)(2,1)S(1)}, u32[]{:S(2)}, u32[]{:S(2)}) %collective-permute-start.3) | collective-permute-done | bytes 36896 | tf_op jit(solution)/shard_map/ppermute | solution.py:382
  16.8 0.0 copy-start.8
  16.8 2.7 %collective-permute-start.6 = (bf16[16,1152]{1,0:T(8,128)(2,1)S(1)}, bf16[16,1152]{1,0:T(8,128)(2,1)S(1)}, u32[]{:S(2)}, u32[]{:S(2)}) collective-permute-start(bf16[16,1152]{1,0:T(8,128)(2,1)S(1)} %add_convert_fusion.refs_0_), channel_id=1, source_target_pairs={{0,4},{1,5},{2,6},{3,7},{4,0},{5,1},{6,2},{7,3},{8,12},{9,13},{10,... | collective-permute-start | bytes 110600 | tf_op jit(solution)/shard_map/ppermute | solution.py:382
  19.4 0.0 copy-done.4
  19.4 1.6 %shard_map.116.refs_6_ = bf16[1024,512]{1,0:T(8,128)(2,1)S(1)} custom-call(f32[3,4096]{1,0:T(4,128)S(1)} %copy-done.4), custom_call_target="tpu_custom_call" | custom-call | flops 6291456 | bytes 1048576 | tf_op jit(solution)/shard_map/pallas_call | solution.py:478
  21.1 0.6 %collective-permute-done.6.refs_1_ = bf16[16,1152]{1,0:T(8,128)(2,1)S(1)} collective-permute-done((bf16[16,1152]{1,0:T(8,128)(2,1)S(1)}, bf16[16,1152]{1,0:T(8,128)(2,1)S(1)}, u32[]{:S(2)}, u32[]{:S(2)}) %collective-permute-start.6) | collective-permute-done | bytes 36896 | tf_op jit(solution)/shard_map/ppermute | solution.py:382
  21.7 0.0 copy-done
  21.7 0.0 copy-done.1
  21.7 0.0 copy-done.3
  21.7 0.0 copy-done.6
  21.7 0.8 %shard_map.117 = (f32[16,128]{1,0:T(8,128)S(1)}, f32[16,128]{1,0:T(8,128)S(1)}, bf16[16,128]{1,0:T(8,128)(2,1)S(1)}, bf16[16,128]{1,0:T(8,128)(2,1)S(1)}, bf16[16,128]{1,0:T(8,128)(2,1)S(1)}) custom-call(bf16[16,1152]{1,0:T(8,128)(2,1)S(1)} %add_convert_fusion.refs_0_, bf16[16,1152]{1,0:T(8,128)(2,1)S(1)} %collective-permute-done.6.refs_1_, ...), custom_call_target="tpu_custom_call" | custom-call | tf_op jit(solution)/shard_map/pallas_call | solution.py:488
  22.6 0.1 collective-permute-start.7
  22.6 1.3 %collective-permute-start.8 = (bf16[16,128]{1,0:T(8,128)(2,1)S(1)}, bf16[16,128]{1,0:T(8,128)(2,1)S(1)}, u32[]{:S(2)}, u32[]{:S(2)}) collective-permute-start(bf16[16,128]{1,0:T(8,128)(2,1)S(1)} %get-tuple-element.19), channel_id=1, source_target_pairs={{0,16},{8,24},{16,0},{24,8},{1,17},{9,25},{17,1},{25,9},{2,18},{10... | collective-permute-start | bytes 12296 | tf_op jit(solution)/shard_map/ppermute | solution.py:382
  23.9 0.6 %collective-permute-start.9 = (bf16[16,128]{1,0:T(8,128)(2,1)S(1)}, bf16[16,128]{1,0:T(8,128)(2,1)S(1)}, u32[]{:S(2)}, u32[]{:S(2)}) collective-permute-start(bf16[16,128]{1,0:T(8,128)(2,1)S(1)} %get-tuple-element.20), channel_id=1, source_target_pairs={{0,8},{8,0},{16,24},{24,16},{1,9},{9,1},{17,25},{25,17},{2,10},{10... | collective-permute-start | bytes 12296 | tf_op jit(solution)/shard_map/ppermute | solution.py:382
  24.5 1.2 %collective-permute-done.7.refs_1_ = bf16[16,128]{1,0:T(8,128)(2,1)S(1)} collective-permute-done((bf16[16,128]{1,0:T(8,128)(2,1)S(1)}, bf16[16,128]{1,0:T(8,128)(2,1)S(1)}, u32[]{:S(2)}, u32[]{:S(2)}) %collective-permute-start.7) | collective-permute-done | bytes 4128 | tf_op jit(solution)/shard_map/ppermute | solution.py:382
  25.7 0.7 %collective-permute-done.8.refs_2_ = bf16[16,128]{1,0:T(8,128)(2,1)S(1)} collective-permute-done((bf16[16,128]{1,0:T(8,128)(2,1)S(1)}, bf16[16,128]{1,0:T(8,128)(2,1)S(1)}, u32[]{:S(2)}, u32[]{:S(2)}) %collective-permute-start.8) | collective-permute-done | bytes 4128 | tf_op jit(solution)/shard_map/ppermute | solution.py:382
  26.3 0.0 collective-permute-done.9.refs_3_
  26.3 0.0 copy-done.8
  26.3 0.6 %shard_map.118 = (f32[16,128]{1,0:T(8,128)}, f32[16,128]{1,0:T(8,128)}) custom-call(f32[16,128]{1,0:T(8,128)S(1)} %get-tuple-element.17.refs_0_, bf16[16,128]{1,0:T(8,128)(2,1)S(1)} %collective-permute-done.7.refs_1_, bf16[16,128]{1,0:T(8,128)(2,1)S(1)} %collective-permute-done.8.refs_2_, bf16[16,128]{1,0:T(8,128)(2,1)S(1)} %collective-permute-done.9.refs_3_, ...), custom_call_target="tpu_custom_call" | custom-call | tf_op jit(solution)/shard_map/pallas_call | solution.py:502
  (1 shorter events, 0.0 us)
Async XLA Ops:
  2.2 5.5 %collective-permute-start.2 = (bf16[5,16,128]{2,1,0:T(8,128)(2,1)}, bf16[5,16,128]{2,1,0:T(8,128)(2,1)S(1)}, u32[]{:S(2)}, u32[]{:S(2)}) collective-permute-start(bf16[5,16,128]{2,1,0:T(8,128)(2,1)} %get-tuple-element.12.refs_0_), channel_id=1, source_target_pairs={{0,16},{8,24},{16,0},{24,8},{1,17},{9,25},{17,1},{25,9},{2,18},{10... | collective-permute-start | bytes 61448 | tf_op jit(solution)/shard_map/ppermute | solution.py:382
  5.2 3.4 %collective-permute-start.1 = (bf16[5,16,128]{2,1,0:T(8,128)(2,1)}, bf16[5,16,128]{2,1,0:T(8,128)(2,1)S(1)}, u32[]{:S(2)}, u32[]{:S(2)}) collective-permute-start(bf16[5,16,128]{2,1,0:T(8,128)(2,1)} %get-tuple-element.12.refs_0_), channel_id=1, source_target_pairs={{0,24},{8,16},{16,8},{24,0},{1,25},{9,17},{17,9},{25,1},{2,26},{10... | collective-permute-start | bytes 61448 | tf_op jit(solution)/shard_map/ppermute | solution.py:382
  5.2 3.4 %collective-permute-start = (bf16[5,16,128]{2,1,0:T(8,128)(2,1)}, bf16[5,16,128]{2,1,0:T(8,128)(2,1)S(1)}, u32[]{:S(2)}, u32[]{:S(2)}) collective-permute-start(bf16[5,16,128]{2,1,0:T(8,128)(2,1)} %get-tuple-element.12.refs_0_), channel_id=1, source_target_pairs={{0,8},{8,0},{16,24},{24,16},{1,9},{9,1},{17,25},{25,17},{2,10},{10... | collective-permute-start | bytes 61448 | tf_op jit(solution)/shard_map/ppermute | solution.py:382
  5.3 0.8 %copy-start.9 = (f32[72,128]{1,0:T(8,128)S(1)}, f32[72,128]{1,0:T(8,128)}, u32[]{:S(2)}) copy-start(f32[72,128]{1,0:T(8,128)} %get-tuple-element.13.lines_ref) | copy-start | bytes 110596
  6.1 2.5 %copy-start.2 = (f32[4,4096]{1,0:T(4,128)S(1)}, f32[4,4096]{1,0:T(4,128)}, u32[]{:S(2)}) copy-start(f32[4,4096]{1,0:T(4,128)} %refs_5_.3) | copy-start | bytes 196612
  6.1 2.5 %copy-start.5 = (bf16[5,16,128]{2,1,0:T(8,128)(2,1)S(1)}, bf16[5,16,128]{2,1,0:T(8,128)(2,1)}, u32[]{:S(2)}) copy-start(bf16[5,16,128]{2,1,0:T(8,128)(2,1)} %get-tuple-element.12.refs_0_) | copy-start | bytes 61444
  6.1 2.5 %copy-start.7 = (s32[8,4]{0,1:T(4,128)S(1)}, s32[8,4]{0,1:T(4,128)}, u32[]{:S(2)}) copy-start(s32[8,4]{0,1:T(4,128)} %param.15) | copy-start | bytes 388
  7.7 11.7 %copy-start.4 = (f32[3,4096]{1,0:T(4,128)S(1)}, f32[3,4096]{1,0:T(4,128)}, u32[]{:S(2)}) copy-start(f32[3,4096]{1,0:T(4,128)} %centroids_ref.2) | copy-start | bytes 147460
  9.7 12.0 %copy-start = (f32[4,1024]{1,0:T(4,128)S(1)}, f32[4,1024]{1,0:T(4,128)}, u32[]{:S(2)}) copy-start(f32[4,1024]{1,0:T(4,128)} %refs_4_.1) | copy-start | bytes 49156
  9.7 12.0 %copy-start.1 = (s32[4,1024]{1,0:T(4,128)S(1)}, s32[4,1024]{1,0:T(4,128)}, u32[]{:S(2)}) copy-start(s32[4,1024]{1,0:T(4,128)} %refs_5_.4) | copy-start | bytes 49156
  9.7 12.0 %copy-start.3 = (f32[3,4096]{1,0:T(4,128)S(1)}, f32[3,4096]{1,0:T(4,128)}, u32[]{:S(2)}) copy-start(f32[3,4096]{1,0:T(4,128)} %refs_7_.1) | copy-start | bytes 147460
  9.7 12.0 %copy-start.6 = (f32[1024]{0:T(1024)S(1)}, f32[1024]{0:T(1024)}, u32[]{:S(2)}) copy-start(f32[1024]{0:T(1024)} %param.18) | copy-start | bytes 12292
  9.7 4.0 %collective-permute-start.5 = (bf16[16,1152]{1,0:T(8,128)(2,1)S(1)}, bf16[16,1152]{1,0:T(8,128)(2,1)S(1)}, u32[]{:S(2)}, u32[]{:S(2)}) collective-permute-start(bf16[16,1152]{1,0:T(8,128)(2,1)S(1)} %get-tuple-element.14), channel_id=1, source_target_pairs={{0,2},{1,3},{2,0},{3,1},{4,6},{5,7},{6,4},{7,5},{8,10},{9,11},{10,... | collective-permute-start | bytes 110600 | tf_op jit(solution)/shard_map/ppermute | solution.py:382
  11.4 4.9 %collective-permute-start.4 = (bf16[16,1152]{1,0:T(8,128)(2,1)S(1)}, bf16[16,1152]{1,0:T(8,128)(2,1)S(1)}, u32[]{:S(2)}, u32[]{:S(2)}) collective-permute-start(bf16[16,1152]{1,0:T(8,128)(2,1)S(1)} %get-tuple-element.14), channel_id=1, source_target_pairs={{0,3},{1,2},{2,1},{3,0},{4,7},{5,6},{6,5},{7,4},{8,11},{9,10},{10,... | collective-permute-start | bytes 110600 | tf_op jit(solution)/shard_map/ppermute | solution.py:382
  12.8 4.0 %collective-permute-start.3 = (bf16[16,1152]{1,0:T(8,128)(2,1)S(1)}, bf16[16,1152]{1,0:T(8,128)(2,1)S(1)}, u32[]{:S(2)}, u32[]{:S(2)}) collective-permute-start(bf16[16,1152]{1,0:T(8,128)(2,1)S(1)} %get-tuple-element.14), channel_id=1, source_target_pairs={{0,1},{1,0},{2,3},{3,2},{4,5},{5,4},{6,7},{7,6},{8,9},{9,8},{10,11... | collective-permute-start | bytes 110600 | tf_op jit(solution)/shard_map/ppermute | solution.py:382
  16.8 9.6 %copy-start.8 = (f32[16,128]{1,0:T(8,128)S(1)}, f32[16,128]{1,0:T(8,128)}, u32[]{:S(2)}) copy-start(f32[16,128]{1,0:T(8,128)} %refs_5_.5) | copy-start | bytes 24580
  16.8 4.9 %collective-permute-start.6 = (bf16[16,1152]{1,0:T(8,128)(2,1)S(1)}, bf16[16,1152]{1,0:T(8,128)(2,1)S(1)}, u32[]{:S(2)}, u32[]{:S(2)}) collective-permute-start(bf16[16,1152]{1,0:T(8,128)(2,1)S(1)} %add_convert_fusion.refs_0_), channel_id=1, source_target_pairs={{0,4},{1,5},{2,6},{3,7},{4,0},{5,1},{6,2},{7,3},{8,12},{9,13},{10,... | collective-permute-start | bytes 110600 | tf_op jit(solution)/shard_map/ppermute | solution.py:382
  22.6 3.1 %collective-permute-start.7 = (bf16[16,128]{1,0:T(8,128)(2,1)S(1)}, bf16[16,128]{1,0:T(8,128)(2,1)S(1)}, u32[]{:S(2)}, u32[]{:S(2)}) collective-permute-start(bf16[16,128]{1,0:T(8,128)(2,1)S(1)} %get-tuple-element.18), channel_id=1, source_target_pairs={{0,24},{8,16},{16,8},{24,0},{1,25},{9,17},{17,9},{25,1},{2,26},{10... | collective-permute-start | bytes 12296 | tf_op jit(solution)/shard_map/ppermute | solution.py:382
  22.6 3.7 %collective-permute-start.8 = (bf16[16,128]{1,0:T(8,128)(2,1)S(1)}, bf16[16,128]{1,0:T(8,128)(2,1)S(1)}, u32[]{:S(2)}, u32[]{:S(2)}) collective-permute-start(bf16[16,128]{1,0:T(8,128)(2,1)S(1)} %get-tuple-element.19), channel_id=1, source_target_pairs={{0,16},{8,24},{16,0},{24,8},{1,17},{9,25},{17,1},{25,9},{2,18},{10... | collective-permute-start | bytes 12296 | tf_op jit(solution)/shard_map/ppermute | solution.py:382
  23.9 2.4 %collective-permute-start.9 = (bf16[16,128]{1,0:T(8,128)(2,1)S(1)}, bf16[16,128]{1,0:T(8,128)(2,1)S(1)}, u32[]{:S(2)}, u32[]{:S(2)}) collective-permute-start(bf16[16,128]{1,0:T(8,128)(2,1)S(1)} %get-tuple-element.20), channel_id=1, source_target_pairs={{0,8},{8,0},{16,24},{24,16},{1,9},{9,1},{17,25},{25,17},{2,10},{10... | collective-permute-start | bytes 12296 | tf_op jit(solution)/shard_map/ppermute | solution.py:382

commit v18 on v16

--- a/solution.py
+++ b/solution.py
@@ -395,7 +395,7 @@
         values = [value] + [swap(value, axis, step * k) for k in range(1, radix)]
         step *= radix
         if step < count:
-            value = sum(values[k].astype(jnp.float32) for k in order_of(radix)).astype(value.dtype)
+            value = sum(part.astype(jnp.float32) for part in values).astype(value.dtype)
     return values
 
 

time: 27.1 us -> 27.1 us (level)
  no operation moved by 1% of the time
where the time goes in v18:
time: 27.1 us; the launch traced here: 26.9 us
  starting transfers between devices  11.2 us (41%)
  Pallas kernels  7.38 us (27%)
  waiting for transfers between devices  6.72 us (25%)
  local copies, waits for them, and re-layouts  0.82 us (3%)
  between operations  0.76 us (3%)
    ppermute x10, starting transfers between devices, swap(): return lax.ppermute(value, axis, pairs)  11.2 us
    ppermute x10, waiting for transfers between devices, swap(): return lax.ppermute(value, axis, pairs)  6.72 us
    pallas_call x1, Pallas kernels, per_device(): pl.pallas_call(s_tiles_kernel, out_shape=jax.ShapeDtypeStruct((rows_t, co...  1.65 us
    pallas_call x1, Pallas kernels, per_device(): pl.pallas_call(functools.partial(t_tiles_kernel, p_tiles=p_tiles, q_tiles...  1.64 us
    pallas_call x1, Pallas kernels, per_device(): pl.pallas_call(pack_kernel, out_shape=(jax.ShapeDtypeStruct((slots + 1, e...  1.61 us
    pallas_call x1, Pallas kernels, per_device(): pl.pallas_call(functools.partial(t_kernel, norm=norm, slots=slots, count=...  1.04 us
    pallas_call x1, Pallas kernels, per_device(): pl.pallas_call(functools.partial(sweep_kernel, slots=slots, part_count=le...  0.84 us
    unnamed x20, local copies, waits for them, and re-layouts  0.82 us
  transfers between devices with their start and end apart: 10, of which 7 were waited for; matrix products, arithmetic and copies ran while one was open for 0% of the time, Pallas kernels for 12%

profile of v18, /device:TPU:0, one launch (start us, length us, event | category | flops | bytes accessed | tf_op | source)
XLA Modules:
  0.0 26.9 jit_solution(8714555580654221226)
XLA Ops:
  0.6 1.6 %shard_map.113 = (bf16[5,16,128]{2,1,0:T(8,128)(2,1)}, f32[72,128]{1,0:T(8,128)}) custom-call(bf16[4,16,128]{2,1,0:T(8,128)(2,1)} %history_ref.1, s32[4,8]{1,0:T(4,128)} %bitcast.5, s32[4,8]{1,0:T(4,128)} %bitcast.7, f32[1,1024]{1,0:T(1,128)} %bitcast.3, f32[4,1024]{1,0:T(4,128)} %refs_4_.1, s32[4,1024]{1,0:T(4,128)} %refs_5_.4, f32[3,4096]{1,0:T(4,128)} %centroids_ref.2), custom_call_target="tpu_custom_call" | custom-call | tf_op jit(solution)/shard_map/pallas_call | solution.py:428
  2.2 2.9 %collective-permute-start.2 = (bf16[5,16,128]{2,1,0:T(8,128)(2,1)}, bf16[5,16,128]{2,1,0:T(8,128)(2,1)S(1)}, u32[]{:S(2)}, u32[]{:S(2)}) collective-permute-start(bf16[5,16,128]{2,1,0:T(8,128)(2,1)} %get-tuple-element.12.refs_0_), channel_id=1, source_target_pairs={{0,16},{8,24},{16,0},{24,8},{1,17},{9,25},{17,1},{25,9},{2,18},{10... | collective-permute-start | bytes 61448 | tf_op jit(solution)/shard_map/ppermute | solution.py:377
  5.2 0.0 collective-permute-start.1
  5.2 0.1 collective-permute-start
  5.3 0.0 copy-start.9
  5.3 0.8 %copy-done.9 = f32[72,128]{1,0:T(8,128)S(1)} copy-done((f32[72,128]{1,0:T(8,128)S(1)}, f32[72,128]{1,0:T(8,128)}, u32[]{:S(2)}) %copy-start.9) | copy-done | bytes 36888
  6.1 0.0 copy-start.2
  6.1 0.0 copy-start.5
  6.1 0.0 copy-start.7
  6.1 1.6 %shard_map.114.refs_4_ = bf16[10,512,128]{2,1,0:T(8,128)(2,1)S(1)} custom-call(f32[72,128]{1,0:T(8,128)S(1)} %copy-done.9), custom_call_target="tpu_custom_call" | custom-call | flops 8388608 | bytes 1048576 | tf_op jit(solution)/shard_map/pallas_call | solution.py:441
  7.7 0.0 copy-start.4
  7.8 0.0 collective-permute-done.2.refs_3_
  7.8 0.8 %collective-permute-done.1.refs_2_ = bf16[5,16,128]{2,1,0:T(8,128)(2,1)S(1)} collective-permute-done((bf16[5,16,128]{2,1,0:T(8,128)(2,1)}, bf16[5,16,128]{2,1,0:T(8,128)(2,1)S(1)}, u32[]{:S(2)}, u32[]{:S(2)}) %collective-permute-start.1) | collective-permute-done | bytes 20512 | tf_op jit(solution)/shard_map/ppermute | solution.py:377
  8.6 0.0 collective-permute-done.refs_1_
  8.6 0.0 copy-done.2
  8.6 0.0 copy-done.5
  8.6 0.0 copy-done.7
  8.6 1.0 %shard_map.115 = (bf16[16,1152]{1,0:T(8,128)(2,1)S(1)}, f32[1,16,128]{2,1,0:T(8,128)S(1)}) custom-call(bf16[5,16,128]{2,1,0:T(8,128)(2,1)S(1)} %copy-done.5, bf16[5,16,128]{2,1,0:T(8,128)(2,1)S(1)} %collective-permute-done.refs_1_, bf16[5,16,128]{2,1,0:T(8,128)(2,1)S(1)} %collective-permute-done.1.refs_2_, ...), custom_call_target="tpu_custom_call" | custom-call | tf_op jit(solution)/shard_map/pallas_call | solution.py:451
  9.7 0.0 copy-start
  9.7 0.0 copy-start.1
  9.7 0.0 copy-start.3
  9.7 0.0 copy-start.6
  9.7 2.6 %collective-permute-start.5 = (bf16[16,1152]{1,0:T(8,128)(2,1)S(1)}, bf16[16,1152]{1,0:T(8,128)(2,1)S(1)}, u32[]{:S(2)}, u32[]{:S(2)}) collective-permute-start(bf16[16,1152]{1,0:T(8,128)(2,1)S(1)} %get-tuple-element.14), channel_id=1, source_target_pairs={{0,3},{1,2},{2,1},{3,0},{4,7},{5,6},{6,5},{7,4},{8,11},{9,10},{10,... | collective-permute-start | bytes 110600 | tf_op jit(solution)/shard_map/ppermute | solution.py:377
  12.3 0.4 %collective-permute-start.4 = (bf16[16,1152]{1,0:T(8,128)(2,1)S(1)}, bf16[16,1152]{1,0:T(8,128)(2,1)S(1)}, u32[]{:S(2)}, u32[]{:S(2)}) collective-permute-start(bf16[16,1152]{1,0:T(8,128)(2,1)S(1)} %get-tuple-element.14), channel_id=1, source_target_pairs={{0,2},{1,3},{2,0},{3,1},{4,6},{5,7},{6,4},{7,5},{8,10},{9,11},{10,... | collective-permute-start | bytes 110600 | tf_op jit(solution)/shard_map/ppermute | solution.py:377
  12.8 0.5 %collective-permute-start.3 = (bf16[16,1152]{1,0:T(8,128)(2,1)S(1)}, bf16[16,1152]{1,0:T(8,128)(2,1)S(1)}, u32[]{:S(2)}, u32[]{:S(2)}) collective-permute-start(bf16[16,1152]{1,0:T(8,128)(2,1)S(1)} %get-tuple-element.14), channel_id=1, source_target_pairs={{0,1},{1,0},{2,3},{3,2},{4,5},{5,4},{6,7},{7,6},{8,9},{9,8},{10,11... | collective-permute-start | bytes 110600 | tf_op jit(solution)/shard_map/ppermute | solution.py:377
  13.3 1.7 %collective-permute-done.5 = bf16[16,1152]{1,0:T(8,128)(2,1)S(1)} collective-permute-done((bf16[16,1152]{1,0:T(8,128)(2,1)S(1)}, bf16[16,1152]{1,0:T(8,128)(2,1)S(1)}, u32[]{:S(2)}, u32[]{:S(2)}) %collective-permute-start.5) | collective-permute-done | bytes 36896 | tf_op jit(solution)/shard_map/ppermute | solution.py:377
  15.0 1.3 %collective-permute-done.4 = bf16[16,1152]{1,0:T(8,128)(2,1)S(1)} collective-permute-done((bf16[16,1152]{1,0:T(8,128)(2,1)S(1)}, bf16[16,1152]{1,0:T(8,128)(2,1)S(1)}, u32[]{:S(2)}, u32[]{:S(2)}) %collective-permute-start.4) | collective-permute-done | bytes 36896 | tf_op jit(solution)/shard_map/ppermute | solution.py:377
  16.3 0.4 %collective-permute-done.3 = bf16[16,1152]{1,0:T(8,128)(2,1)S(1)} collective-permute-done((bf16[16,1152]{1,0:T(8,128)(2,1)S(1)}, bf16[16,1152]{1,0:T(8,128)(2,1)S(1)}, u32[]{:S(2)}, u32[]{:S(2)}) %collective-permute-start.3) | collective-permute-done | bytes 36896 | tf_op jit(solution)/shard_map/ppermute | solution.py:377
  16.7 0.0 copy-start.8
  16.8 2.7 %collective-permute-start.6 = (bf16[16,1152]{1,0:T(8,128)(2,1)S(1)}, bf16[16,1152]{1,0:T(8,128)(2,1)S(1)}, u32[]{:S(2)}, u32[]{:S(2)}) collective-permute-start(bf16[16,1152]{1,0:T(8,128)(2,1)S(1)} %add_convert_fusion.refs_0_), channel_id=1, source_target_pairs={{0,4},{1,5},{2,6},{3,7},{4,0},{5,1},{6,2},{7,3},{8,12},{9,13},{10,... | collective-permute-start | bytes 110600 | tf_op jit(solution)/shard_map/ppermute | solution.py:377
  19.4 0.0 copy-done.4
  19.4 1.6 %shard_map.116.refs_6_ = bf16[1024,512]{1,0:T(8,128)(2,1)S(1)} custom-call(f32[3,4096]{1,0:T(4,128)S(1)} %copy-done.4), custom_call_target="tpu_custom_call" | custom-call | flops 6291456 | bytes 1048576 | tf_op jit(solution)/shard_map/pallas_call | solution.py:473
  21.1 0.6 %collective-permute-done.6.refs_1_ = bf16[16,1152]{1,0:T(8,128)(2,1)S(1)} collective-permute-done((bf16[16,1152]{1,0:T(8,128)(2,1)S(1)}, bf16[16,1152]{1,0:T(8,128)(2,1)S(1)}, u32[]{:S(2)}, u32[]{:S(2)}) %collective-permute-start.6) | collective-permute-done | bytes 36896 | tf_op jit(solution)/shard_map/ppermute | solution.py:377
  21.7 0.0 copy-done
  21.7 0.0 copy-done.1
  21.7 0.0 copy-done.3
  21.7 0.0 copy-done.6
  21.7 0.8 %shard_map.117 = (f32[16,128]{1,0:T(8,128)S(1)}, f32[16,128]{1,0:T(8,128)S(1)}, bf16[16,128]{1,0:T(8,128)(2,1)S(1)}, bf16[16,128]{1,0:T(8,128)(2,1)S(1)}, bf16[16,128]{1,0:T(8,128)(2,1)S(1)}) custom-call(bf16[16,1152]{1,0:T(8,128)(2,1)S(1)} %add_convert_fusion.refs_0_, bf16[16,1152]{1,0:T(8,128)(2,1)S(1)} %collective-permute-done.6.refs_1_, ...), custom_call_target="tpu_custom_call" | custom-call | tf_op jit(solution)/shard_map/pallas_call | solution.py:483
  22.5 0.1 collective-permute-start.7
  22.6 1.3 %collective-permute-start.8 = (bf16[16,128]{1,0:T(8,128)(2,1)S(1)}, bf16[16,128]{1,0:T(8,128)(2,1)S(1)}, u32[]{:S(2)}, u32[]{:S(2)}) collective-permute-start(bf16[16,128]{1,0:T(8,128)(2,1)S(1)} %get-tuple-element.19), channel_id=1, source_target_pairs={{0,16},{8,24},{16,0},{24,8},{1,17},{9,25},{17,1},{25,9},{2,18},{10... | collective-permute-start | bytes 12296 | tf_op jit(solution)/shard_map/ppermute | solution.py:377
  23.9 0.6 %collective-permute-start.9 = (bf16[16,128]{1,0:T(8,128)(2,1)S(1)}, bf16[16,128]{1,0:T(8,128)(2,1)S(1)}, u32[]{:S(2)}, u32[]{:S(2)}) collective-permute-start(bf16[16,128]{1,0:T(8,128)(2,1)S(1)} %get-tuple-element.20), channel_id=1, source_target_pairs={{0,8},{8,0},{16,24},{24,16},{1,9},{9,1},{17,25},{25,17},{2,10},{10... | collective-permute-start | bytes 12296 | tf_op jit(solution)/shard_map/ppermute | solution.py:377
  24.5 1.2 %collective-permute-done.7.refs_1_ = bf16[16,128]{1,0:T(8,128)(2,1)S(1)} collective-permute-done((bf16[16,128]{1,0:T(8,128)(2,1)S(1)}, bf16[16,128]{1,0:T(8,128)(2,1)S(1)}, u32[]{:S(2)}, u32[]{:S(2)}) %collective-permute-start.7) | collective-permute-done | bytes 4128 | tf_op jit(solution)/shard_map/ppermute | solution.py:377
  25.6 0.7 %collective-permute-done.8.refs_2_ = bf16[16,128]{1,0:T(8,128)(2,1)S(1)} collective-permute-done((bf16[16,128]{1,0:T(8,128)(2,1)S(1)}, bf16[16,128]{1,0:T(8,128)(2,1)S(1)}, u32[]{:S(2)}, u32[]{:S(2)}) %collective-permute-start.8) | collective-permute-done | bytes 4128 | tf_op jit(solution)/shard_map/ppermute | solution.py:377
  26.3 0.0 collective-permute-done.9.refs_3_
  26.3 0.0 copy-done.8
  26.3 0.6 %shard_map.118 = (f32[16,128]{1,0:T(8,128)}, f32[16,128]{1,0:T(8,128)}) custom-call(f32[16,128]{1,0:T(8,128)S(1)} %get-tuple-element.17.refs_0_, bf16[16,128]{1,0:T(8,128)(2,1)S(1)} %collective-permute-done.7.refs_1_, bf16[16,128]{1,0:T(8,128)(2,1)S(1)} %collective-permute-done.8.refs_2_, bf16[16,128]{1,0:T(8,128)(2,1)S(1)} %collective-permute-done.9.refs_3_, ...), custom_call_target="tpu_custom_call" | custom-call | tf_op jit(solution)/shard_map/pallas_call | solution.py:497
  (1 shorter events, 0.0 us)
Async XLA Ops:
  2.2 5.5 %collective-permute-start.2 = (bf16[5,16,128]{2,1,0:T(8,128)(2,1)}, bf16[5,16,128]{2,1,0:T(8,128)(2,1)S(1)}, u32[]{:S(2)}, u32[]{:S(2)}) collective-permute-start(bf16[5,16,128]{2,1,0:T(8,128)(2,1)} %get-tuple-element.12.refs_0_), channel_id=1, source_target_pairs={{0,16},{8,24},{16,0},{24,8},{1,17},{9,25},{17,1},{25,9},{2,18},{10... | collective-permute-start | bytes 61448 | tf_op jit(solution)/shard_map/ppermute | solution.py:377
  5.2 3.4 %collective-permute-start.1 = (bf16[5,16,128]{2,1,0:T(8,128)(2,1)}, bf16[5,16,128]{2,1,0:T(8,128)(2,1)S(1)}, u32[]{:S(2)}, u32[]{:S(2)}) collective-permute-start(bf16[5,16,128]{2,1,0:T(8,128)(2,1)} %get-tuple-element.12.refs_0_), channel_id=1, source_target_pairs={{0,24},{8,16},{16,8},{24,0},{1,25},{9,17},{17,9},{25,1},{2,26},{10... | collective-permute-start | bytes 61448 | tf_op jit(solution)/shard_map/ppermute | solution.py:377
  5.2 3.4 %collective-permute-start = (bf16[5,16,128]{2,1,0:T(8,128)(2,1)}, bf16[5,16,128]{2,1,0:T(8,128)(2,1)S(1)}, u32[]{:S(2)}, u32[]{:S(2)}) collective-permute-start(bf16[5,16,128]{2,1,0:T(8,128)(2,1)} %get-tuple-element.12.refs_0_), channel_id=1, source_target_pairs={{0,8},{8,0},{16,24},{24,16},{1,9},{9,1},{17,25},{25,17},{2,10},{10... | collective-permute-start | bytes 61448 | tf_op jit(solution)/shard_map/ppermute | solution.py:377
  5.3 0.8 %copy-start.9 = (f32[72,128]{1,0:T(8,128)S(1)}, f32[72,128]{1,0:T(8,128)}, u32[]{:S(2)}) copy-start(f32[72,128]{1,0:T(8,128)} %get-tuple-element.13.lines_ref) | copy-start | bytes 110596
  6.1 2.5 %copy-start.2 = (f32[4,4096]{1,0:T(4,128)S(1)}, f32[4,4096]{1,0:T(4,128)}, u32[]{:S(2)}) copy-start(f32[4,4096]{1,0:T(4,128)} %refs_5_.3) | copy-start | bytes 196612
  6.1 2.5 %copy-start.5 = (bf16[5,16,128]{2,1,0:T(8,128)(2,1)S(1)}, bf16[5,16,128]{2,1,0:T(8,128)(2,1)}, u32[]{:S(2)}) copy-start(bf16[5,16,128]{2,1,0:T(8,128)(2,1)} %get-tuple-element.12.refs_0_) | copy-start | bytes 61444
  6.1 2.5 %copy-start.7 = (s32[8,4]{0,1:T(4,128)S(1)}, s32[8,4]{0,1:T(4,128)}, u32[]{:S(2)}) copy-start(s32[8,4]{0,1:T(4,128)} %param.15) | copy-start | bytes 388
  7.7 11.7 %copy-start.4 = (f32[3,4096]{1,0:T(4,128)S(1)}, f32[3,4096]{1,0:T(4,128)}, u32[]{:S(2)}) copy-start(f32[3,4096]{1,0:T(4,128)} %centroids_ref.2) | copy-start | bytes 147460
  9.7 12.0 %copy-start = (f32[4,1024]{1,0:T(4,128)S(1)}, f32[4,1024]{1,0:T(4,128)}, u32[]{:S(2)}) copy-start(f32[4,1024]{1,0:T(4,128)} %refs_4_.1) | copy-start | bytes 49156
  9.7 12.0 %copy-start.1 = (s32[4,1024]{1,0:T(4,128)S(1)}, s32[4,1024]{1,0:T(4,128)}, u32[]{:S(2)}) copy-start(s32[4,1024]{1,0:T(4,128)} %refs_5_.4) | copy-start | bytes 49156
  9.7 12.0 %copy-start.3 = (f32[3,4096]{1,0:T(4,128)S(1)}, f32[3,4096]{1,0:T(4,128)}, u32[]{:S(2)}) copy-start(f32[3,4096]{1,0:T(4,128)} %refs_7_.1) | copy-start | bytes 147460
  9.7 12.0 %copy-start.6 = (f32[1024]{0:T(1024)S(1)}, f32[1024]{0:T(1024)}, u32[]{:S(2)}) copy-start(f32[1024]{0:T(1024)} %param.18) | copy-start | bytes 12292
  9.7 5.3 %collective-permute-start.5 = (bf16[16,1152]{1,0:T(8,128)(2,1)S(1)}, bf16[16,1152]{1,0:T(8,128)(2,1)S(1)}, u32[]{:S(2)}, u32[]{:S(2)}) collective-permute-start(bf16[16,1152]{1,0:T(8,128)(2,1)S(1)} %get-tuple-element.14), channel_id=1, source_target_pairs={{0,3},{1,2},{2,1},{3,0},{4,7},{5,6},{6,5},{7,4},{8,11},{9,10},{10,... | collective-permute-start | bytes 110600 | tf_op jit(solution)/shard_map/ppermute | solution.py:377
  12.3 4.0 %collective-permute-start.4 = (bf16[16,1152]{1,0:T(8,128)(2,1)S(1)}, bf16[16,1152]{1,0:T(8,128)(2,1)S(1)}, u32[]{:S(2)}, u32[]{:S(2)}) collective-permute-start(bf16[16,1152]{1,0:T(8,128)(2,1)S(1)} %get-tuple-element.14), channel_id=1, source_target_pairs={{0,2},{1,3},{2,0},{3,1},{4,6},{5,7},{6,4},{7,5},{8,10},{9,11},{10,... | collective-permute-start | bytes 110600 | tf_op jit(solution)/shard_map/ppermute | solution.py:377
  12.8 4.0 %collective-permute-start.3 = (bf16[16,1152]{1,0:T(8,128)(2,1)S(1)}, bf16[16,1152]{1,0:T(8,128)(2,1)S(1)}, u32[]{:S(2)}, u32[]{:S(2)}) collective-permute-start(bf16[16,1152]{1,0:T(8,128)(2,1)S(1)} %get-tuple-element.14), channel_id=1, source_target_pairs={{0,1},{1,0},{2,3},{3,2},{4,5},{5,4},{6,7},{7,6},{8,9},{9,8},{10,11... | collective-permute-start | bytes 110600 | tf_op jit(solution)/shard_map/ppermute | solution.py:377
  16.7 9.6 %copy-start.8 = (f32[16,128]{1,0:T(8,128)S(1)}, f32[16,128]{1,0:T(8,128)}, u32[]{:S(2)}) copy-start(f32[16,128]{1,0:T(8,128)} %refs_5_.5) | copy-start | bytes 24580
  16.8 4.9 %collective-permute-start.6 = (bf16[16,1152]{1,0:T(8,128)(2,1)S(1)}, bf16[16,1152]{1,0:T(8,128)(2,1)S(1)}, u32[]{:S(2)}, u32[]{:S(2)}) collective-permute-start(bf16[16,1152]{1,0:T(8,128)(2,1)S(1)} %add_convert_fusion.refs_0_), channel_id=1, source_target_pairs={{0,4},{1,5},{2,6},{3,7},{4,0},{5,1},{6,2},{7,3},{8,12},{9,13},{10,... | collective-permute-start | bytes 110600 | tf_op jit(solution)/shard_map/ppermute | solution.py:377
  22.5 3.1 %collective-permute-start.7 = (bf16[16,128]{1,0:T(8,128)(2,1)S(1)}, bf16[16,128]{1,0:T(8,128)(2,1)S(1)}, u32[]{:S(2)}, u32[]{:S(2)}) collective-permute-start(bf16[16,128]{1,0:T(8,128)(2,1)S(1)} %get-tuple-element.18), channel_id=1, source_target_pairs={{0,24},{8,16},{16,8},{24,0},{1,25},{9,17},{17,9},{25,1},{2,26},{10... | collective-permute-start | bytes 12296 | tf_op jit(solution)/shard_map/ppermute | solution.py:377
  22.6 3.7 %collective-permute-start.8 = (bf16[16,128]{1,0:T(8,128)(2,1)S(1)}, bf16[16,128]{1,0:T(8,128)(2,1)S(1)}, u32[]{:S(2)}, u32[]{:S(2)}) collective-permute-start(bf16[16,128]{1,0:T(8,128)(2,1)S(1)} %get-tuple-element.19), channel_id=1, source_target_pairs={{0,16},{8,24},{16,0},{24,8},{1,17},{9,25},{17,1},{25,9},{2,18},{10... | collective-permute-start | bytes 12296 | tf_op jit(solution)/shard_map/ppermute | solution.py:377
  23.9 2.4 %collective-permute-start.9 = (bf16[16,128]{1,0:T(8,128)(2,1)S(1)}, bf16[16,128]{1,0:T(8,128)(2,1)S(1)}, u32[]{:S(2)}, u32[]{:S(2)}) collective-permute-start(bf16[16,128]{1,0:T(8,128)(2,1)S(1)} %get-tuple-element.20), channel_id=1, source_target_pairs={{0,8},{8,0},{16,24},{24,16},{1,9},{9,1},{17,25},{25,17},{2,10},{10... | collective-permute-start | bytes 12296 | tf_op jit(solution)/shard_map/ppermute | solution.py:377
